TPU v7x, 32 devices: a whole 2x2x4 slice. The times are simulated.
32 devices in a mesh: groups: 2 (over y), gx: 4 (over z), gy: 2 (over x), gz: 2 (over core).
Axes of the slice: x: 2, y: 2, z: 4, core: 2. Of those that a mesh axis runs over, the one named last changes fastest.
Arguments:
- coarse_fields: float32 [6, 96, 24, 256], P(None, ('groups', 'gx'), 'gy', 'gz'), parts along dimension 1, may hold values from -6 to 6
- permittivity: float32 [96, 24, 256], P(('groups', 'gx'), 'gy', 'gz'), parts along dimension 0, may hold values from 1 to 4.4
- fine_fields: float32 [8, 2, 8, 6, 4096], P(('groups', 'gx'), 'gy', 'gz'), parts along dimension 0, may hold values from -6 to 6
- fine_permittivity: float32 [8, 2, 8, 4096], P(('groups', 'gx'), 'gy', 'gz'), parts along dimension 0, may hold values from 1 to 4.4
- patch_corner: int32 [8, 2, 4, 3], P(('groups', 'gx'), 'gy', 'gz'), parts along dimension 0, may hold values from 1 to 119, as said below
- patch_owner: int32 [8, 4, 2], P(('groups', 'gx')), parts along dimension 0, may hold values from 0 to 3, as said below
Outputs:
- coarse_out: float32 [6, 96, 24, 256], P(None, ('groups', 'gx'), 'gy', 'gz'), parts along dimension 1
- fine_out: float32 [8, 2, 8, 6, 4096], P(('groups', 'gx'), 'gy', 'gz'), parts along dimension 0
There are 2 independent parts, one for each index of `groups`. A program takes and returns all parts, laid end to end along the dimension named above; each array names one. Nothing has to cross between parts.
Inputs may be any that keep to these rules, and one draw needn't show every extreme that they name: `patch_corner`: coordinates x in 1 to 3, y in 1 to 3, and z of patch q of a device in q * 64 + 1 to (q + 1) * 64 - 9; a region with a rim of one cell lies inside its device's block, and two regions never meet. A device's 2 patches have different owners, so each slot of a device holds at most one patch; in every gx slab some device owns a patch of every device of the slab; a slot holds a patch only where patch_owner names that device for a patch of the slot's rank.
All inputs are finite; a program needn't handle non-finite values.
Results may differ from a plain program's by a relative error of at most 0.0003.
Values sent between devices are 32-bit elements; how exact they have to be, the bound alone decides.
No kernel may reach another device: no remote copies, remote signals or barrier semaphores. Data moves between devices by JAX's collectives and lax.ppermute only.
A program may use at most 128 MiB of HBM per device.

v0:
```python
import functools
import jax
import jax.numpy as jnp
import numpy as np
from jax import lax
from jax.experimental import pallas as pl
from jax.experimental.pallas import tpu as pltpu
from jax.sharding import PartitionSpec as P

PF = 16
PAR = 2
HALF = PF // 2
RIM = HALF + 2
PLANES = 9
LINE = PF + 2
LANES = 128
WIDE = 384
BATCH = 4
ROWS_BOX = PLANES * 8
ROWS_REGION = 64
EDGE_ROWS = 40
X_COMPS = (0, 1, 2, 4, 5)
Y_COMPS = (0, 1, 2, 3, 5)
VMEM_BYTES = 48 * 1024 * 1024
F32 = jnp.float32
BF16 = jnp.bfloat16


def grow_table():
    table = np.zeros((PF * PF, WIDE), np.float32)
    for y in range(PF):
        for z in range(PF):
            table[y * PF + z, (y + 1) * LINE + z + 1] = 1.0
    return table


def ghost_table():
    table = np.zeros((LANES, WIDE), np.float32)
    for y in range(LINE):
        for z in range(LINE):
            table[((y + 1) // 2) * RIM + (z + 1) // 2, y * LINE + z] = 1.0
    return table


def mean_table():
    table = np.zeros((2, WIDE, LANES), np.float32)
    for odd in range(2):
        for y in range(PF):
            for z in range(PF):
                lane = odd * HALF * HALF + (y // 2) * HALF + z // 2
                table[odd, (y + 1) * LINE + z + 1, lane] = 0.125
    return table.reshape(2 * WIDE, LANES)


def move(rows, table):
    high = rows.astype(BF16)
    low = (rows - high.astype(F32)).astype(BF16)
    out = jnp.dot(high, table, preferred_element_type=F32)
    return out + jnp.dot(low, table, preferred_element_type=F32)


def lane_iota(shape):
    return lax.broadcasted_iota(jnp.int32, shape, len(shape) - 1)


def whole(memory_space=pltpu.VMEM):
    return pl.BlockSpec(memory_space=memory_space)


def call(kernel, outs, in_specs, scratch=(), flops=1_000_000, size=1_000_000, **extra):
    return pl.pallas_call(
        kernel,
        out_shape=outs,
        in_specs=in_specs,
        out_specs=jax.tree.map(lambda _: whole(), outs),
        scratch_shapes=list(scratch),
        compiler_params=pltpu.CompilerParams(vmem_limit_bytes=VMEM_BYTES),
        cost_estimate=pl.CostEstimate(flops=flops, bytes_accessed=size, transcendentals=0),
        **extra,
    )


def swap_pairs(count, first):
    pairs = []
    for i in range(first, count - 1, 2):
        pairs += [(i, i + 1), (i + 1, i)]
    return pairs


def faces_kernel(block, x_even, x_odd, y_even, y_odd):
    deep, tall = block.shape[1], block.shape[2]
    gx_odd = lax.rem(lax.axis_index("gx"), 2)
    gy_odd = lax.rem(lax.axis_index("gy"), 2)
    for k, c in enumerate(X_COMPS):
        x_even[k] = block[c, (1 - gx_odd) * (deep - 1)]
        x_odd[k] = block[c, gx_odd * (deep - 1)]
    for k, c in enumerate(Y_COMPS):
        for x in range(deep):
            first = block[c, x, 0:1, :]
            last = block[c, x, tall - 1 : tall, :]
            y_even[k, x : x + 1, :] = jnp.where(gy_odd == 0, last, first)
            if y_odd is not None:
                y_odd[k, x : x + 1, :] = jnp.where(gy_odd == 0, first, last)


def leap_kernel(two_y, *refs):
    if two_y:
        block, beside, perm, corner, x_even, x_odd, y_even, y_odd, new, packed, pad, side, mag, rate, fresh = refs
    else:
        block, beside, perm, corner, x_even, x_odd, y_even, new, packed, pad, side, mag, rate, fresh = refs
        y_odd = None
    deep, tall = block.shape[1], block.shape[2]
    full = deep + 2
    gx_odd = lax.rem(lax.axis_index("gx"), 2)
    gy_odd = lax.rem(lax.axis_index("gy"), 2)
    gz = lax.axis_index("gz")
    pad[...] = jnp.zeros_like(pad)
    side[...] = jnp.zeros_like(side)
    rate[...] = jnp.ones_like(rate)
    lane = lane_iota((tall, LANES))
    keep = ((lane == 0) & (gz == 0)) | ((lane == LANES - 1) & (gz == 1))

    def at(c, x):
        return (c * full + x) * 16

    for x in range(deep):
        rate[pl.ds(x * 16 + 1, tall), :] = perm[x]
    for c in range(6):
        for x in range(deep):
            pad[pl.ds(at(c, x + 1) + 1, tall), :] = block[c, x]
            side[pl.ds(at(c, x + 1) + 1, tall), :] = jnp.where(keep, beside[c, x], 0.0)
    for k, c in enumerate(X_COMPS):
        even, odd = x_even[k], x_odd[k]
        pad[pl.ds(at(c, 0) + 1, tall), :] = jnp.where(gx_odd == 0, odd, even)
        if c in (1, 2):
            pad[pl.ds(at(c, full - 1) + 1, tall), :] = jnp.where(gx_odd == 0, even, odd)
    for k, c in enumerate(Y_COMPS):
        for x in range(deep):
            even = y_even[k, x : x + 1, :]
            odd = jnp.zeros_like(even) if y_odd is None else y_odd[k, x : x + 1, :]
            pad[pl.ds(at(c, x + 1), 1), :] = jnp.where(gy_odd == 0, odd, even)
            if c in (0, 2):
                pad[pl.ds(at(c, x + 1) + tall + 1, 1), :] = jnp.where(gy_odd == 0, even, odd)

    def up_y(a):
        return pltpu.roll(a, 15, 0)

    def up_z(a):
        return pltpu.roll(a, 2 * LANES - 1, 1)

    def down_y(a):
        return pltpu.roll(a, 1, 0)

    def down_z(a):
        return pltpu.roll(a, 1, 1)

    def plane(c, x):
        rows = pl.ds(at(c, x), 16)
        return jnp.concatenate([pad[rows, :], side[rows, :]], axis=1)

    def field(c, x):
        return mag[pl.ds((c * (full - 1) + x) * 16, 16), :]

    for x in range(full - 1):
        e0, e1, e2 = plane(0, x), plane(1, x), plane(2, x)
        h0 = plane(3, x) - 0.5 * ((up_y(e2) - e2) - (up_z(e1) - e1))
        h1 = plane(4, x) - 0.5 * ((up_z(e0) - e0) - (plane(2, x + 1) - e2))
        h2 = plane(5, x) - 0.5 * ((plane(1, x + 1) - e1) - (up_y(e0) - e0))
        for c, value in enumerate((h0, h1, h2)):
            mag[pl.ds((c * (full - 1) + x) * 16, 16), :] = value
    for x in range(deep):
        h0, h1, h2 = field(0, x + 1), field(1, x + 1), field(2, x + 1)
        coef = 0.5 / rate[pl.ds(x * 16, 16), :]
        c0 = ((h2 - down_y(h2)) - (h1 - down_z(h1)))[:, 0:LANES]
        c1 = ((h0 - down_z(h0)) - (h2 - field(2, x)))[:, 0:LANES]
        c2 = ((h1 - field(1, x)) - (h0 - down_y(h0)))[:, 0:LANES]
        for c, curl in enumerate((c0, c1, c2)):
            fresh[pl.ds((c * deep + x) * 16, 16), :] = plane(c, x + 1)[:, 0:LANES] + coef * curl
            fresh[pl.ds(((c + 3) * deep + x) * 16, 16), :] = (h0, h1, h2)[c][:, 0:LANES]
    for c in range(6):
        for x in range(deep):
            new[c, x] = fresh[pl.ds((c * deep + x) * 16 + 1, tall), :]
    region_lane = lane_iota((RIM, LANES))
    for q in range(PAR):
        cx, cy, cz = corner[0, 0, q, 0], corner[0, 0, q, 1], corner[0, 0, q, 2]
        for t in range(2):
            base = (q * 2 + t) * ROWS_REGION
            for c in range(6):
                total = jnp.zeros((RIM, LANES), F32)
                for j in range(RIM):
                    if t == 0:
                        rows = pad[pl.ds((c * full + cx) * 16 + cy + j, RIM, stride=16), :]
                    else:
                        rows = fresh[pl.ds((c * deep + cx - 1) * 16 + cy + j, RIM, stride=16), :]
                    shift = lax.rem(j * RIM - (cz - 1) + 2 * LANES, LANES)
                    rows = pltpu.roll(rows, shift, 1)
                    inside = (region_lane >= j * RIM) & (region_lane < (j + 1) * RIM)
                    total = jnp.where(inside, rows, total)
                packed[pl.ds(base + c * RIM, RIM), :] = total
            packed[pl.ds(base + 6 * RIM, ROWS_REGION - 6 * RIM), :] = jnp.zeros((ROWS_REGION - 6 * RIM, LANES), F32)
    base = PAR * 2 * ROWS_REGION
    half = lane_iota((16, LANES)) < LANES // 2
    packed[pl.ds(base, 16), :] = jnp.where(half, plane(0, 0)[:, 0:LANES], plane(2, full - 1)[:, 0:LANES])
    low = jnp.where(gy_odd == 0, jnp.zeros_like(y_even[1]) if y_odd is None else y_odd[1], y_even[1])
    high = jnp.where(gy_odd == 0, y_even[2], jnp.zeros_like(y_even[2]) if y_odd is None else y_odd[2])
    packed[pl.ds(base + 16, 16), :] = jnp.zeros((16, LANES), F32)
    packed[pl.ds(base + 16, deep), :] = jnp.where(lane_iota((deep, LANES)) < LANES // 2, low, high)
    packed[pl.ds(base + 32, 8), :] = jnp.zeros((8, LANES), F32)
    packed[pl.ds(base + 32, 1), :] = pad[pl.ds(at(1, full - 1) + tall, 1), :]
    packed[pl.ds(base + 33, 1), :] = pad[pl.ds(at(0, 0) + 1, 1), :]


def put(ref, g, c, m, value):
    for v in range(WIDE // LANES):
        ref[g, c * 3 + v, m * 8 : (m + 1) * 8, :] = value[:, v * LANES : (v + 1) * LANES]


def get(ref, g, c, m):
    return jnp.concatenate([ref[g, c * 3 + v, m * 8 : (m + 1) * 8, :] for v in range(WIDE // LANES)], axis=1)


def load_kernel(fine, perm, table, box, rate, lhs, wide, coefs):
    groups = fine.shape[2] // BATCH
    for g in range(groups):
        for s in range(BATCH):
            for x in range(PF):
                row = (s * PF + x) * 8
                lhs[row : row + 6, :] = fine[0, 0, g * BATCH + s, :, x * PF * PF : (x + 1) * PF * PF]
                lhs[row + 6 : row + 8, :] = jnp.zeros((2, PF * PF), F32)
        grown = move(lhs[...], table[...])
        for v in range(WIDE // LANES):
            wide[v] = grown[:, v * LANES : (v + 1) * LANES]
        zero = jnp.zeros((8, WIDE), F32)
        for c in range(6):
            put(box, g, c, 0, zero)
            put(box, g, c, PLANES - 1, zero)
            for s in range(BATCH):
                for xh in range(2):
                    source = pl.ds((s * PF + xh * 8) * 8 + c, 8, stride=8)
                    for v in range(WIDE // LANES):
                        target = pl.ds((1 - xh) * 8 + xh * BATCH + s, 8, stride=8)
                        box[g, c * 3 + v, target, :] = wide[v, source, :]
        coefs[...] = jnp.zeros_like(coefs)
        for x in range(PF):
            row = (x % 8 + (1 if x < 8 else 0)) * 8 + (0 if x < 8 else BATCH)
            cells = perm[0, 0, g * BATCH : (g + 1) * BATCH, x * PF * PF : (x + 1) * PF * PF]
            coefs[row : row + BATCH, :] = 0.5 / cells
        rate[g] = move(coefs[...], table[...])


def fine_kernel(regions, box, rate, owners, ghosts, means, out, small, lhs, now, mag, halves):
    groups = box.shape[0]
    rank = lax.axis_index("gy") * lax.axis_size("gz") + lax.axis_index("gz")
    flat = lane_iota((8, WIDE))
    yy = lax.shift_right_logical(flat * 3641, 16)
    zz = flat - yy * LINE
    inner = (yy >= 1) & (yy <= PF) & (zz >= 1) & (zz <= PF)
    upper = lax.broadcasted_iota(jnp.int32, (8, WIDE), 0) >= BATCH

    def inner_of(m):
        if m == 0:
            return inner & upper
        if m == PLANES - 1:
            return inner & jnp.logical_not(upper)
        return inner

    def up_y(a):
        return pltpu.roll(a, WIDE - LINE, 1)

    def up_z(a):
        return pltpu.roll(a, WIDE - 1, 1)

    def down_y(a):
        return pltpu.roll(a, LINE, 1)

    def down_z(a):
        return pltpu.roll(a, 1, 1)

    def rows_of(m):
        return pl.ds(m * 8, 8)

    for g in range(groups):
        for sub in range(2):
            for s in range(BATCH):
                r = g * BATCH + s
                q = jnp.where(owners[0, r, 0] == rank, 0, 1)
                for c in range(6):
                    old = regions[r, pl.ds(q * 2 * ROWS_REGION + c * RIM, RIM), :]
                    if sub == 1:
                        fresh = regions[r, pl.ds((q * 2 + 1) * ROWS_REGION + c * RIM, RIM), :]
                        old = old + 0.5 * (fresh - old)
                    row = c * ROWS_BOX + s
                    lhs[pl.ds(row, 5, stride=16), :] = old[0:5]
                    lhs[pl.ds(row + 8, 4, stride=16), :] = old[1:5]
                    lhs[pl.ds(row + BATCH, 5, stride=16), :] = old[5:10]
                    lhs[pl.ds(row + BATCH + 8, 4, stride=16), :] = old[5:9]
            source = box if sub == 0 else out
            for c in range(6):
                ghost = move(lhs[pl.ds(c * ROWS_BOX, ROWS_BOX), :], ghosts[...])
                for m in range(PLANES):
                    now[c, rows_of(m), :] = jnp.where(
                        inner_of(m), get(source, g, c, m), ghost[m * 8 : (m + 1) * 8]
                    )

            def next_x(c, m):
                if m == PLANES - 1:
                    return pltpu.roll(now[c, rows_of(0), :], BATCH, 0)
                return now[c, rows_of(m + 1), :]

            def last_x(c, m):
                if m == 0:
                    return pltpu.roll(mag[c, rows_of(PLANES - 1), :], BATCH, 0)
                return mag[c, rows_of(m - 1), :]

            for m in range(PLANES):
                e0, e1, e2 = (now[c, rows_of(m), :] for c in range(3))
                h0, h1, h2 = (now[c, rows_of(m), :] for c in range(3, 6))
                mag[0, rows_of(m), :] = h0 - 0.5 * ((up_y(e2) - e2) - (up_z(e1) - e1))
                mag[1, rows_of(m), :] = h1 - 0.5 * ((up_z(e0) - e0) - (next_x(2, m) - e2))
                mag[2, rows_of(m), :] = h2 - 0.5 * ((next_x(1, m) - e1) - (up_y(e0) - e0))
            for m in range(PLANES):
                h0, h1, h2 = (mag[c, rows_of(m), :] for c in range(3))
                coef = rate[g, rows_of(m), :]
                e0, e1, e2 = (now[c, rows_of(m), :] for c in range(3))
                put(out, g, 0, m, e0 + coef * ((h2 - down_y(h2)) - (h1 - down_z(h1))))
                put(out, g, 1, m, e1 + coef * ((h0 - down_z(h0)) - (h2 - last_x(2, m))))
                put(out, g, 2, m, e2 + coef * ((h1 - last_x(1, m)) - (h0 - down_y(h0))))
                for c, value in enumerate((h0, h1, h2)):
                    put(out, g, c + 3, m, value)
        for c in range(6):
            for k in range(4):
                other = jnp.where(upper, get(out, g, c, 2 * k), get(out, g, c, 2 * k + 2))
                pair = get(out, g, c, 2 * k + 1) + other
                halves[pl.ds((c * 2 + k // 2) * 8, 8), (k % 2) * WIDE : (k % 2 + 1) * WIDE] = pair
        small[pl.ds(g * 96, 96), :] = move(halves[...], means[...])


def store_kernel(box, fine, owners, table, out, cells):
    groups = box.shape[0]
    rank = lax.axis_index("gy") * lax.axis_size("gz") + lax.axis_index("gz")
    for g in range(groups):
        for c in range(6):
            rows = jnp.concatenate([box[g, c * 3 + v] for v in range(WIDE // LANES)], axis=1)
            flat = move(rows, table[...])
            for v in range(PF * PF // LANES):
                cells[v, pl.ds(c * ROWS_BOX, ROWS_BOX), :] = flat[:, v * LANES : (v + 1) * LANES]
        for s in range(BATCH):
            slot = g * BATCH + s
            live = (owners[0, slot, 0] == rank) | (owners[0, slot, 1] == rank)
            for x in range(PF):
                row = (x % 8 + (1 if x < 8 else 0)) * 8 + (0 if x < 8 else BATCH) + s
                for v in range(PF * PF // LANES):
                    cut = slice(x * PF * PF + v * LANES, x * PF * PF + (v + 1) * LANES)
                    value = cells[v, pl.ds(row, 6, stride=ROWS_BOX), :]
                    out[0, 0, slot, :, cut] = jnp.where(live, value, fine[0, 0, slot, :, cut])


def fix_kernel(new, perm, edges, out):
    deep, tall = new.shape[1], new.shape[2]
    ranks_y, gy, gz = lax.axis_size("gy"), lax.axis_index("gy"), lax.axis_index("gz")
    rank = gy * 2 + gz
    base = PAR * 2 * ROWS_REGION
    out[...] = new[...]

    def add(c, x, rows, amount):
        out[c, x, rows, :] = out[c, x, rows, :] + 0.25 / perm[x, rows, :] * amount

    lower = edges[jnp.maximum(rank - 2, gz), pl.ds(base + 32, 1), :]
    higher = edges[jnp.minimum(rank + 2, (ranks_y - 1) * 2 + gz), pl.ds(base + 33, 1), :]
    add(0, deep - 1, slice(0, 1), jnp.where(gy > 0, lower, 0.0))
    add(1, 0, slice(tall - 1, tall), jnp.where(gy < ranks_y - 1, higher, 0.0))
    side = gy * 2 + 1 - gz
    lane = lane_iota((tall, LANES))
    tile = edges[side, pl.ds(base + 1, tall), :]
    add(0, deep - 1, slice(0, tall), jnp.where((lane == 0) & (gz == 1), pltpu.roll(tile, 1, 1), 0.0))
    add(2, 0, slice(0, tall), jnp.where((lane == LANES - 1) & (gz == 0), pltpu.roll(tile, LANES - 1, 1), 0.0))
    lane = lane_iota((deep, LANES))
    tile = edges[side, pl.ds(base + 16, deep), :]
    first = jnp.where((lane == LANES - 1) & (gz == 0), pltpu.roll(tile, LANES - 1, 1), 0.0)
    last = jnp.where((lane == 0) & (gz == 1), pltpu.roll(tile, 1, 1), 0.0)
    for x in range(deep):
        add(2, x, slice(0, 1), first[x : x + 1])
        add(1, x, slice(tall - 1, tall), last[x : x + 1])


def place_kernel(new, means, corner, owners, out, spread):
    stretch = means.shape[1]
    rank = lax.axis_index("gy") * lax.axis_size("gz") + lax.axis_index("gz")
    out[...] = new[...]
    lane = lane_iota((HALF, LANES))
    for q in range(PAR):
        cx, cy, cz = corner[0, 0, q, 0], corner[0, 0, q, 1], corner[0, 0, q, 2]
        owner = owners[0, rank, q]
        start = (rank // BATCH) * 96 + lax.rem(rank, BATCH)
        for xh in range(2):
            rows = means[owner, pl.ds(start + xh * BATCH, 12, stride=8), :]
            for odd in range(2):
                for y in range(HALF):
                    shift = lax.rem(cz - y * HALF - odd * HALF * HALF + 2 * LANES, LANES)
                    spread[pl.ds((xh * 2 + odd) * 96 + y, 12, stride=8), :] = pltpu.roll(rows, shift, 1)
        inside = (lane >= cz) & (lane < cz + HALF)
        for c in range(6):
            for x in range(HALF):
                xh, k = x // 4, x % 4
                tile = spread[pl.ds((xh * 2 + k % 2) * 96 + (c * 2 + k // 2) * 8, 8), :]
                spot = out[c, cx + x, pl.ds(cy, HALF), :]
                out[c, cx + x, pl.ds(cy, HALF), :] = jnp.where(inside, tile, spot)


def local(coarse_fields, permittivity, fine_fields, fine_permittivity, patch_corner, patch_owner):
    deep, tall, cols = coarse_fields.shape[1:]
    slots = fine_fields.shape[2]
    groups = slots // BATCH
    count_x, count_y = lax.axis_size("gx"), lax.axis_size("gy")
    two_y = count_y > 2
    smem = whole(pltpu.SMEM)
    vmem = whole()
    shape = jax.ShapeDtypeStruct
    grow = grow_table()

    beside = lax.ppermute(coarse_fields, "gz", swap_pairs(2, 0))
    x_face = shape((5, tall, cols), F32)
    y_face = shape((5, deep, cols), F32)
    if two_y:
        body = faces_kernel
    else:
        body = functools.partial(faces_kernel, y_odd=None)
    faces = call(body, [x_face, x_face, y_face] + [y_face] * two_y, [vmem])(coarse_fields)
    got = [
        lax.ppermute(faces[0], "gx", swap_pairs(count_x, 0)),
        lax.ppermute(faces[1], "gx", swap_pairs(count_x, 1)),
        lax.ppermute(faces[2], "gy", swap_pairs(count_y, 0)),
    ]
    if two_y:
        got.append(lax.ppermute(faces[3], "gy", swap_pairs(count_y, 1)))

    box, rate = call(
        load_kernel,
        [shape((groups, 18, ROWS_BOX, LANES), F32), shape((groups, ROWS_BOX, WIDE), F32)],
        [vmem] * 3,
        [pltpu.VMEM((512, PF * PF), F32), pltpu.VMEM((3, 512, LANES), F32), pltpu.VMEM((ROWS_BOX, PF * PF), F32)],
        size=4_000_000,
    )(fine_fields, fine_permittivity, jnp.asarray(grow, BF16))

    full = deep + 2
    payload = PAR * 2 * ROWS_REGION + EDGE_ROWS
    new, packed = call(
        functools.partial(leap_kernel, two_y),
        [shape(coarse_fields.shape, F32), shape((payload, LANES), F32)],
        [vmem] * 3 + [smem] + [vmem] * len(got),
        [
            pltpu.VMEM((6 * full * 16, LANES), F32),
            pltpu.VMEM((6 * full * 16, LANES), F32),
            pltpu.VMEM((3 * (full - 1) * 16, 2 * LANES), F32),
            pltpu.VMEM((deep * 16, LANES), F32),
            pltpu.VMEM((6 * deep * 16, LANES), F32),
        ],
    )(coarse_fields, beside, permittivity, patch_corner, *got)
    regions = lax.all_gather(packed, ("gy", "gz"))

    box, small = call(
        fine_kernel,
        [shape((groups, 18, ROWS_BOX, LANES), F32), shape((groups * 96, LANES), F32)],
        [vmem] * 3 + [smem] + [vmem] * 2,
        [
            pltpu.VMEM((6 * ROWS_BOX, LANES), F32),
            pltpu.VMEM((6, ROWS_BOX, WIDE), F32),
            pltpu.VMEM((3, ROWS_BOX, WIDE), F32),
            pltpu.VMEM((96, 2 * WIDE), F32),
        ],
    )(regions, box, rate, patch_owner, jnp.asarray(ghost_table(), BF16), jnp.asarray(mean_table(), BF16))
    means = lax.all_gather(small, ("gy", "gz"))

    fine = call(
        store_kernel,
        shape(fine_fields.shape, F32),
        [vmem, vmem, smem, vmem],
        [pltpu.VMEM((2, 6 * ROWS_BOX, LANES), F32)],
        size=4_000_000,
    )(box, fine_fields, patch_owner, jnp.asarray(grow.T, BF16))
    new = call(fix_kernel, shape(coarse_fields.shape, F32), [vmem] * 3)(new, permittivity, regions)
    coarse = call(
        place_kernel,
        shape(coarse_fields.shape, F32),
        [vmem, vmem, smem, smem],
        [pltpu.VMEM((4 * 96, LANES), F32)],
    )(new, means, patch_corner, patch_owner)
    return coarse, fine


def solution(mesh):
    in_specs = (
        P(None, ("groups", "gx"), "gy", "gz"),
        P(("groups", "gx"), "gy", "gz"),
        P(("groups", "gx"), "gy", "gz", None, None),
        P(("groups", "gx"), "gy", "gz", None),
        P(("groups", "gx"), "gy", "gz", None),
        P(("groups", "gx"), None, None),
    )
    out_specs = (P(None, ("groups", "gx"), "gy", "gz"), P(("groups", "gx"), "gy", "gz", None, None))
    return jax.shard_map(local, mesh=mesh, in_specs=in_specs, out_specs=out_specs, check_vma=False)
```

profile of v0, /device:TPU:9, one launch (start us, length us, event | category | flops | bytes accessed | tf_op | source)
XLA Modules:
  0.0 33.1 jit_solution(9648011581058650488)
XLA Ops:
  0.6 0.7 %collective-permute-start = (f32[6,12,12,128]{3,2,1,0:T(8,128)}, f32[6,12,12,128]{3,2,1,0:T(8,128)S(1)}, u32[]{:S(2)}, u32[]{:S(2)}) collective-permute-start(f32[6,12,12,128]{3,2,1,0:T(8,128)} %refs_0_.1), channel_id=1, source_target_pairs={{0,1},{1,0},{2,3},{3,2},{4,5},{5,4},{6,7},{7,6},{8,9},{9,8},{10,11... | collective-permute-start | bytes 1327112 | tf_op jit(solution)/shard_map/ppermute | solution.py:421
  1.4 1.1 %copy-done = f32[6,12,12,128]{3,2,1,0:T(8,128)S(1)} copy-done((f32[6,12,12,128]{3,2,1,0:T(8,128)S(1)}, f32[6,12,12,128]{3,2,1,0:T(8,128)}, u32[]{:S(2)}) %copy-start) | copy-done | bytes 442392
  2.5 0.1 collective-permute-start.1
  2.6 0.0 copy-start.10
  2.6 4.6 %collective-permute-start.2 = (f32[5,12,128]{2,1,0:T(8,128)S(1)}, f32[5,12,128]{2,1,0:T(8,128)S(1)}, u32[]{:S(2)}, u32[]{:S(2)}) collective-permute-start(f32[5,12,128]{2,1,0:T(8,128)S(1)} %get-tuple-element.12), channel_id=1, source_target_pairs={{4,8},{8,4},{5,9},{9,5},{6,10},{10,6},{7,11},{11,7},{20,24},{24,20... | collective-permute-start | bytes 92168 | tf_op jit(solution)/shard_map/ppermute | solution.py:431
  7.2 1.3 %collective-permute-start.3 = (f32[5,12,128]{2,1,0:T(8,128)S(1)}, f32[5,12,128]{2,1,0:T(8,128)S(1)}, u32[]{:S(2)}, u32[]{:S(2)}) collective-permute-start(f32[5,12,128]{2,1,0:T(8,128)S(1)} %get-tuple-element.13), channel_id=1, source_target_pairs={{0,2},{2,0},{1,3},{3,1},{4,6},{6,4},{5,7},{7,5},{8,10},{10,8},{9,1... | collective-permute-start | bytes 92168 | tf_op jit(solution)/shard_map/ppermute | solution.py:432
  8.5 0.1 copy.13.owners
  8.6 0.2 copy.12.fine
  8.8 0.7 %copy-done.5 = bf16[256,384]{1,0:T(8,128)(2,1)S(1)} copy-done((bf16[256,384]{1,0:T(8,128)(2,1)S(1)}, bf16[256,384]{1,0:T(8,128)(2,1)}, u32[]{:S(2)}) %copy-start.5) | copy-done | bytes 196632
  9.5 0.0 copy-done.7
  9.5 0.6 %shard_map.116 = (f32[1,18,72,128]{3,2,1,0:T(8,128)S(1)}, f32[1,72,384]{2,1,0:T(8,128)S(1)}) custom-call(f32[1,1,4,6,4096]{4,3,2,1,0:T(8,128)S(1)} %copy.12.fine, f32[1,1,4,4096]{3,2,1,0:T(4,128)S(1)} %copy-done.7, bf16[256,384]{1,0:T(8,128)(2,1)S(1)} %copy-done.5), custom_call_target="tpu_custom_call" | custom-call | flops 1000000 | bytes 4000000 | tf_op jit(solution)/shard_map/pallas_call | solution.py:437
  10.1 0.0 collective-permute-done.2.refs_5_
  10.2 0.4 %copy-done.1 = f32[6,12,12,128]{3,2,1,0:T(8,128)S(1)} copy-done((f32[6,12,12,128]{3,2,1,0:T(8,128)S(1)}, f32[6,12,12,128]{3,2,1,0:T(8,128)}, u32[]{:S(2)}) %copy-start.1) | copy-done | bytes 442392
  10.6 0.0 copy-done.2
  10.6 1.5 %shard_map.114 = (f32[6,12,12,128]{3,2,1,0:T(8,128)S(1)}, f32[296,128]{1,0:T(8,128)S(1)}) custom-call(f32[6,12,12,128]{3,2,1,0:T(8,128)S(1)} %copy-done.1, f32[6,12,12,128]{3,2,1,0:T(8,128)S(1)} %collective-permute-done.refs_1_, f32[12,12,128]{2,1,0:T(8,128)S(1)} %copy-done.2, s32[1,1,2,3]{3,2,1,0:T(2,128)S(1)} %copy-done.8, ...), custom_call_target="tpu_custom_call" | custom-call | flops 1000000 | bytes 1000000 | tf_op jit(solution)/shard_map/pallas_call | solution.py:447
  12.1 8.7 %all-gather = f32[1184,128]{1,0:T(8,128)S(1)} all-gather(f32[296,128]{1,0:T(8,128)S(1)} %get-tuple-element.15), channel_id=2, replica_groups=mesh['groups'=2,'gx'=4,'gy'=2,'gz'=2] {'gy','gz'}, dimensions={0}, use_global_device_ids=true | all-gather | bytes 757760 | tf_op jit(solution)/shard_map/all_gather | solution.py:459
  20.8 0.1 shard_map.115.new
  20.9 0.8 %copy-done.4 = bf16[768,128]{1,0:T(8,128)(2,1)S(1)} copy-done((bf16[768,128]{1,0:T(8,128)(2,1)S(1)}, bf16[768,128]{1,0:T(8,128)(2,1)}, u32[]{:S(2)}) %copy-start.4) | copy-done | bytes 196632
  21.7 0.1 copy-done.6
  21.8 1.8 %shard_map.117 = (f32[1,18,72,128]{3,2,1,0:T(8,128)S(1)}, f32[96,128]{1,0:T(8,128)S(1)}) custom-call(f32[4,296,128]{2,1,0:T(8,128)S(1)} %bitcast.3, f32[1,18,72,128]{3,2,1,0:T(8,128)S(1)} %get-tuple-element.16.box, f32[1,72,384]{2,1,0:T(8,128)S(1)} %get-tuple-element.17.rate, s32[1,4,2]{2,1,0:T(4,128)S(1)} %copy.13.owners, bf16[128,384]{1,0:T(8,128)(2,1)S(1)} %copy-done.6, ...), custom_call_target="tpu_custom_call" | custom-call | flops 1000000 | bytes 1000000 | tf_op jit(solution)/shard_map/pallas_call | solution.py:461
  23.7 1.2 %shard_map.119 = f32[1,1,4,6,4096]{4,3,2,1,0:T(8,128)S(1)} custom-call(f32[1,18,72,128]{3,2,1,0:T(8,128)S(1)} %get-tuple-element.19.box, f32[1,1,4,6,4096]{4,3,2,1,0:T(8,128)S(1)} %copy.12.fine, s32[1,4,2]{2,1,0:T(4,128)S(1)} %copy.13.owners, bf16[384,256]{1,0:T(8,128)(2,1)S(1)} %copy-done.3), custom_call_target="tpu_custom_call" | custom-call | flops 1000000 | bytes 4000000 | tf_op jit(solution)/shard_map/pallas_call | solution.py:474
  24.9 1.0 %copy.17 = f32[1,1,4,6,4096]{4,2,3,1,0:T(4,128)} copy(f32[1,1,4,6,4096]{4,3,2,1,0:T(8,128)S(1)} %shard_map.119) | data formatting | bytes 786432
  25.9 5.6 %all-gather.1 = f32[384,128]{1,0:T(8,128)S(1)} all-gather(f32[96,128]{1,0:T(8,128)S(1)} %get-tuple-element.18), channel_id=3, replica_groups=mesh['groups'=2,'gx'=4,'gy'=2,'gz'=2] {'gy','gz'}, dimensions={0}, use_global_device_ids=true | all-gather | bytes 245760 | tf_op jit(solution)/shard_map/all_gather | solution.py:472
  31.5 1.7 %shard_map.118 = f32[6,12,12,128]{3,2,1,0:T(8,128)} custom-call(f32[6,12,12,128]{3,2,1,0:T(8,128)S(1)} %shard_map.115.new, f32[4,96,128]{2,1,0:T(8,128)S(1)} %bitcast.4, s32[1,1,2,3]{3,2,1,0:T(2,128)S(1)} %copy-done.8, s32[1,4,2]{2,1,0:T(4,128)S(1)} %copy.13.owners), custom_call_target="tpu_custom_call" | custom-call | flops 1000000 | bytes 1000000 | tf_op jit(solution)/shard_map/pallas_call | solution.py:482
  (18 shorter events, 0.1 us)
Async XLA Ops:
  0.6 9.5 %collective-permute-start = (f32[6,12,12,128]{3,2,1,0:T(8,128)}, f32[6,12,12,128]{3,2,1,0:T(8,128)S(1)}, u32[]{:S(2)}, u32[]{:S(2)}) collective-permute-start(f32[6,12,12,128]{3,2,1,0:T(8,128)} %refs_0_.1), channel_id=1, source_target_pairs={{0,1},{1,0},{2,3},{3,2},{4,5},{5,4},{6,7},{7,6},{8,9},{9,8},{10,11... | collective-permute-start | bytes 1327112 | tf_op jit(solution)/shard_map/ppermute | solution.py:421
  1.4 1.1 %copy-start = (f32[6,12,12,128]{3,2,1,0:T(8,128)S(1)}, f32[6,12,12,128]{3,2,1,0:T(8,128)}, u32[]{:S(2)}) copy-start(f32[6,12,12,128]{3,2,1,0:T(8,128)} %refs_0_.1) | copy-start | bytes 1327108
  2.4 6.1 %copy-start.9 = (f32[1,1,4,6,4096]{4,2,3,1,0:T(4,128)S(1)}, f32[1,1,4,6,4096]{4,2,3,1,0:T(4,128)}, u32[]{:S(2)}) copy-start(f32[1,1,4,6,4096]{4,2,3,1,0:T(4,128)} %param.12) | copy-start | bytes 1179652
  2.5 7.6 %collective-permute-start.1 = (f32[5,12,128]{2,1,0:T(8,128)S(1)}, f32[5,12,128]{2,1,0:T(8,128)S(1)}, u32[]{:S(2)}, u32[]{:S(2)}) collective-permute-start(f32[5,12,128]{2,1,0:T(8,128)S(1)} %get-tuple-element.11), channel_id=1, source_target_pairs={{0,4},{4,0},{8,12},{12,8},{1,5},{5,1},{9,13},{13,9},{2,6},{6,2},{1... | collective-permute-start | bytes 92168 | tf_op jit(solution)/shard_map/ppermute | solution.py:430
  2.6 5.9 %copy-start.10 = (s32[1,4,2]{1,2,0:T(2,128)S(1)}, s32[1,4,2]{1,2,0:T(2,128)}, u32[]{:S(2)}) copy-start(s32[1,4,2]{1,2,0:T(2,128)} %param.15) | copy-start | bytes 100
  2.6 7.6 %collective-permute-start.2 = (f32[5,12,128]{2,1,0:T(8,128)S(1)}, f32[5,12,128]{2,1,0:T(8,128)S(1)}, u32[]{:S(2)}, u32[]{:S(2)}) collective-permute-start(f32[5,12,128]{2,1,0:T(8,128)S(1)} %get-tuple-element.12), channel_id=1, source_target_pairs={{4,8},{8,4},{5,9},{9,5},{6,10},{10,6},{7,11},{11,7},{20,24},{24,20... | collective-permute-start | bytes 92168 | tf_op jit(solution)/shard_map/ppermute | solution.py:431
  7.2 3.0 %collective-permute-start.3 = (f32[5,12,128]{2,1,0:T(8,128)S(1)}, f32[5,12,128]{2,1,0:T(8,128)S(1)}, u32[]{:S(2)}, u32[]{:S(2)}) collective-permute-start(f32[5,12,128]{2,1,0:T(8,128)S(1)} %get-tuple-element.13), channel_id=1, source_target_pairs={{0,2},{2,0},{1,3},{3,1},{4,6},{6,4},{5,7},{7,5},{8,10},{10,8},{9,1... | collective-permute-start | bytes 92168 | tf_op jit(solution)/shard_map/ppermute | solution.py:432
  8.6 0.9 %copy-start.5 = (bf16[256,384]{1,0:T(8,128)(2,1)S(1)}, bf16[256,384]{1,0:T(8,128)(2,1)}, u32[]{:S(2)}) copy-start(bf16[256,384]{1,0:T(8,128)(2,1)} %constant.8.clone.table) | copy-start | bytes 589828
  8.6 0.9 %copy-start.7 = (f32[1,1,4,4096]{3,2,1,0:T(4,128)S(1)}, f32[1,1,4,4096]{3,2,1,0:T(4,128)}, u32[]{:S(2)}) copy-start(f32[1,1,4,4096]{3,2,1,0:T(4,128)} %perm.3) | copy-start | bytes 196612
  9.5 1.1 %copy-start.1 = (f32[6,12,12,128]{3,2,1,0:T(8,128)S(1)}, f32[6,12,12,128]{3,2,1,0:T(8,128)}, u32[]{:S(2)}) copy-start(f32[6,12,12,128]{3,2,1,0:T(8,128)} %refs_0_.1) | copy-start | bytes 1327108
  9.5 1.1 %copy-start.2 = (f32[12,12,128]{2,1,0:T(8,128)S(1)}, f32[12,12,128]{2,1,0:T(8,128)}, u32[]{:S(2)}) copy-start(f32[12,12,128]{2,1,0:T(8,128)} %perm.2) | copy-start | bytes 221188
  9.5 1.1 %copy-start.8 = (s32[1,1,2,3]{3,2,1,0:T(2,128)S(1)}, s32[1,1,2,3]{3,2,1,0:T(2,128)}, u32[]{:S(2)}) copy-start(s32[1,1,2,3]{3,2,1,0:T(2,128)} %corner.1) | copy-start | bytes 76
  20.8 0.9 %copy-start.4 = (bf16[768,128]{1,0:T(8,128)(2,1)S(1)}, bf16[768,128]{1,0:T(8,128)(2,1)}, u32[]{:S(2)}) copy-start(bf16[768,128]{1,0:T(8,128)(2,1)} %constant.10.clone.means) | copy-start | bytes 589828
  20.8 1.0 %copy-start.6 = (bf16[128,384]{1,0:T(8,128)(2,1)S(1)}, bf16[128,384]{1,0:T(8,128)(2,1)}, u32[]{:S(2)}) copy-start(bf16[128,384]{1,0:T(8,128)(2,1)} %constant.9.clone.ghosts) | copy-start | bytes 294916
  21.8 1.9 %copy-start.3 = (bf16[384,256]{1,0:T(8,128)(2,1)S(1)}, bf16[384,256]{1,0:T(8,128)(2,1)}, u32[]{:S(2)}) copy-start(bf16[384,256]{1,0:T(8,128)(2,1)} %constant.11.clone.table) | copy-start | bytes 589828
where the time goes:
time: 33.4 us; the launch traced here: 33.1 us
  blocking collectives  14.3 us (43%)
  Pallas kernels  7 us (21%)
  starting transfers between devices  6.69 us (20%)
  local copies, waits for them, and re-layouts  4.38 us (13%)
  between operations  0.75 us (2%)
    all_gather x1, blocking collectives, local(): regions = lax.all_gather(packed, ('gy', 'gz'))  8.75 us
    all_gather x1, blocking collectives, local(): means = lax.all_gather(small, ('gy', 'gz'))  5.58 us
    ppermute x1, starting transfers between devices, local(): lax.ppermute(faces[1], 'gx', swap_pairs(count_x, 1))  4.6 us
    unnamed x25, local copies, waits for them, and re-layouts  4.38 us
    pallas_call x1, Pallas kernels, local(): call(fine_kernel, [shape((groups, 18, ROWS_BOX, LANES), F32), shape((grou...  1.85 us
    pallas_call x1, Pallas kernels, local(): call(place_kernel, shape(coarse_fields.shape, F32), [vmem, vmem, smem, sm...  1.66 us
    pallas_call x1, Pallas kernels, local(): call(functools.partial(leap_kernel, two_y), [shape(coarse_fields.shape, F...  1.49 us
    ppermute x1, starting transfers between devices, local(): lax.ppermute(faces[2], 'gy', swap_pairs(count_y, 0))  1.28 us
  transfers between devices with their start and end apart: 4, of which 0 were waited for; matrix products, arithmetic and copies ran while one was open for 1% of the time, Pallas kernels for 2%

commit v1 on v0

--- a/solution.py
+++ b/solution.py
@@ -17,8 +17,9 @@
 WIDE = 384
 BATCH = 4
 ROWS_BOX = PLANES * 8
-ROWS_REGION = 64
-EDGE_ROWS = 40
+ROWS_REGION = 60
+ROWS_PATCH = 128
+ROWS_BESIDE = 160
 X_COMPS = (0, 1, 2, 4, 5)
 Y_COMPS = (0, 1, 2, 3, 5)
 VMEM_BYTES = 48 * 1024 * 1024
@@ -67,12 +68,12 @@
     return pl.BlockSpec(memory_space=memory_space)
 
 
-def call(kernel, outs, in_specs, scratch=(), flops=1_000_000, size=1_000_000, **extra):
+def call(kernel, outs, in_specs, scratch=(), flops=1_000_000, size=1_000_000, out_specs=None, **extra):
     return pl.pallas_call(
         kernel,
         out_shape=outs,
         in_specs=in_specs,
-        out_specs=jax.tree.map(lambda _: whole(), outs),
+        out_specs=jax.tree.map(lambda _: whole(), outs) if out_specs is None else out_specs,
         scratch_shapes=list(scratch),
         compiler_params=pltpu.CompilerParams(vmem_limit_bytes=VMEM_BYTES),
         cost_estimate=pl.CostEstimate(flops=flops, bytes_accessed=size, transcendentals=0),
@@ -87,28 +88,33 @@
     return pairs
 
 
-def faces_kernel(block, x_even, x_odd, y_even, y_odd):
+def faces_kernel(two_y, block, *refs):
+    outs, sems = refs[:-1], refs[-1]
     deep, tall = block.shape[1], block.shape[2]
     gx_odd = lax.rem(lax.axis_index("gx"), 2)
     gy_odd = lax.rem(lax.axis_index("gy"), 2)
-    for k, c in enumerate(X_COMPS):
-        x_even[k] = block[c, (1 - gx_odd) * (deep - 1)]
-        x_odd[k] = block[c, gx_odd * (deep - 1)]
-    for k, c in enumerate(Y_COMPS):
-        for x in range(deep):
-            first = block[c, x, 0:1, :]
-            last = block[c, x, tall - 1 : tall, :]
-            y_even[k, x : x + 1, :] = jnp.where(gy_odd == 0, last, first)
-            if y_odd is not None:
-                y_odd[k, x : x + 1, :] = jnp.where(gy_odd == 0, first, last)
-
-
-def leap_kernel(two_y, *refs):
-    if two_y:
-        block, beside, perm, corner, x_even, x_odd, y_even, y_odd, new, packed, pad, side, mag, rate, fresh = refs
-    else:
-        block, beside, perm, corner, x_even, x_odd, y_even, new, packed, pad, side, mag, rate, fresh = refs
-        y_odd = None
+    copies = []
+    for n, place in enumerate(((1 - gx_odd) * (deep - 1), gx_odd * (deep - 1))):
+        for low, high, k in ((0, 3, 0), (4, 6, 3)):
+            source = block.at[low:high, place]
+            copies.append((source, outs[n].at[k : k + high - low]))
+    for n, place in enumerate(((1 - gy_odd) * (tall - 1), gy_odd * (tall - 1))[: 1 + two_y]):
+        for low, high, k in ((0, 4, 0), (5, 6, 4)):
+            source = block.at[low:high, :, place]
+            copies.append((source, outs[2 + n].at[k : k + high - low]))
+    copies = [pltpu.make_async_copy(a, b, sems.at[i]) for i, (a, b) in enumerate(copies)]
+    for copy in copies:
+        copy.start()
+    for copy in copies:
+        copy.wait()
+
+
+def leap_kernel(two_y, ranks, *refs):
+    block, beside, perm, corner, owners, x_even, x_odd, y_even = refs[:8]
+    y_odd = refs[8] if two_y else None
+    refs = refs[8 + two_y :]
+    new, sends = refs[0], refs[1 : 1 + ranks]
+    pad, side, mag, rate, fresh, packed = refs[1 + ranks :]
     deep, tall = block.shape[1], block.shape[2]
     full = deep + 2
     gx_odd = lax.rem(lax.axis_index("gx"), 2)
@@ -184,7 +190,7 @@
     for q in range(PAR):
         cx, cy, cz = corner[0, 0, q, 0], corner[0, 0, q, 1], corner[0, 0, q, 2]
         for t in range(2):
-            base = (q * 2 + t) * ROWS_REGION
+            base = t * ROWS_REGION
             for c in range(6):
                 total = jnp.zeros((RIM, LANES), F32)
                 for j in range(RIM):
@@ -196,18 +202,22 @@
                     rows = pltpu.roll(rows, shift, 1)
                     inside = (region_lane >= j * RIM) & (region_lane < (j + 1) * RIM)
                     total = jnp.where(inside, rows, total)
-                packed[pl.ds(base + c * RIM, RIM), :] = total
-            packed[pl.ds(base + 6 * RIM, ROWS_REGION - 6 * RIM), :] = jnp.zeros((ROWS_REGION - 6 * RIM, LANES), F32)
-    base = PAR * 2 * ROWS_REGION
+                packed[q, pl.ds(base + c * RIM, RIM), :] = total
+    rank = lax.axis_index("gy") * lax.axis_size("gz") + gz
+    for q in range(PAR):
+        packed[q, 2 * ROWS_REGION : ROWS_PATCH, :] = jnp.zeros((ROWS_PATCH - 2 * ROWS_REGION, LANES), F32)
+        packed[q, 2 * ROWS_REGION : 2 * ROWS_REGION + 1, :] = pad[pl.ds(at(1, full - 1) + tall, 1), :]
+        packed[q, 2 * ROWS_REGION + 1 : 2 * ROWS_REGION + 2, :] = pad[pl.ds(at(0, 0) + 1, 1), :]
+    for k, send in enumerate(sends):
+        q = jnp.where(owners[0, rank, 0] == lax.bitwise_xor(rank, k), 0, 1)
+        send[0:ROWS_PATCH, :] = packed[q]
     half = lane_iota((16, LANES)) < LANES // 2
-    packed[pl.ds(base, 16), :] = jnp.where(half, plane(0, 0)[:, 0:LANES], plane(2, full - 1)[:, 0:LANES])
+    send = sends[1]
+    send[ROWS_PATCH : ROWS_PATCH + 16, :] = jnp.where(half, plane(0, 0)[:, 0:LANES], plane(2, full - 1)[:, 0:LANES])
     low = jnp.where(gy_odd == 0, jnp.zeros_like(y_even[1]) if y_odd is None else y_odd[1], y_even[1])
     high = jnp.where(gy_odd == 0, y_even[2], jnp.zeros_like(y_even[2]) if y_odd is None else y_odd[2])
-    packed[pl.ds(base + 16, 16), :] = jnp.zeros((16, LANES), F32)
-    packed[pl.ds(base + 16, deep), :] = jnp.where(lane_iota((deep, LANES)) < LANES // 2, low, high)
-    packed[pl.ds(base + 32, 8), :] = jnp.zeros((8, LANES), F32)
-    packed[pl.ds(base + 32, 1), :] = pad[pl.ds(at(1, full - 1) + tall, 1), :]
-    packed[pl.ds(base + 33, 1), :] = pad[pl.ds(at(0, 0) + 1, 1), :]
+    send[ROWS_PATCH + 16 : ROWS_PATCH + 32, :] = jnp.zeros((16, LANES), F32)
+    send[ROWS_PATCH + 16 : ROWS_PATCH + 16 + deep, :] = jnp.where(lane_iota((deep, LANES)) < LANES // 2, low, high)
 
 
 def put(ref, g, c, m, value):
@@ -248,7 +258,10 @@
         rate[g] = move(coefs[...], table[...])
 
 
-def fine_kernel(regions, box, rate, owners, ghosts, means, out, small, lhs, now, mag, halves):
+def fine_kernel(ranks, *refs):
+    regions, (box, rate, ghosts, means, out) = refs[:ranks], refs[ranks : ranks + 5]
+    smalls = refs[ranks + 5 : 2 * ranks + 5]
+    lhs, now, mag, halves, small = refs[2 * ranks + 5 :]
     groups = box.shape[0]
     rank = lax.axis_index("gy") * lax.axis_size("gz") + lax.axis_index("gz")
     flat = lane_iota((8, WIDE))
@@ -279,24 +292,23 @@
     def rows_of(m):
         return pl.ds(m * 8, 8)
 
+    for k, region in enumerate(regions):
+        slot = lax.bitwise_xor(rank, k)
+        start = (slot // BATCH) * 6 * ROWS_BOX + lax.rem(slot, BATCH)
+        for c in range(6):
+            old = region[c * RIM : (c + 1) * RIM, :]
+            fresh = region[ROWS_REGION + c * RIM : ROWS_REGION + (c + 1) * RIM, :]
+            for sub, value in enumerate((old, old + 0.5 * (fresh - old))):
+                row = start + c * ROWS_BOX
+                lhs[sub, pl.ds(row, 5, stride=16), :] = value[0:5]
+                lhs[sub, pl.ds(row + 8, 4, stride=16), :] = value[1:5]
+                lhs[sub, pl.ds(row + BATCH, 5, stride=16), :] = value[5:10]
+                lhs[sub, pl.ds(row + BATCH + 8, 4, stride=16), :] = value[5:9]
     for g in range(groups):
         for sub in range(2):
-            for s in range(BATCH):
-                r = g * BATCH + s
-                q = jnp.where(owners[0, r, 0] == rank, 0, 1)
-                for c in range(6):
-                    old = regions[r, pl.ds(q * 2 * ROWS_REGION + c * RIM, RIM), :]
-                    if sub == 1:
-                        fresh = regions[r, pl.ds((q * 2 + 1) * ROWS_REGION + c * RIM, RIM), :]
-                        old = old + 0.5 * (fresh - old)
-                    row = c * ROWS_BOX + s
-                    lhs[pl.ds(row, 5, stride=16), :] = old[0:5]
-                    lhs[pl.ds(row + 8, 4, stride=16), :] = old[1:5]
-                    lhs[pl.ds(row + BATCH, 5, stride=16), :] = old[5:10]
-                    lhs[pl.ds(row + BATCH + 8, 4, stride=16), :] = old[5:9]
             source = box if sub == 0 else out
             for c in range(6):
-                ghost = move(lhs[pl.ds(c * ROWS_BOX, ROWS_BOX), :], ghosts[...])
+                ghost = move(lhs[sub, pl.ds((g * 6 + c) * ROWS_BOX, ROWS_BOX), :], ghosts[...])
                 for m in range(PLANES):
                     now[c, rows_of(m), :] = jnp.where(
                         inner_of(m), get(source, g, c, m), ghost[m * 8 : (m + 1) * 8]
@@ -333,6 +345,11 @@
                 pair = get(out, g, c, 2 * k + 1) + other
                 halves[pl.ds((c * 2 + k // 2) * 8, 8), (k % 2) * WIDE : (k % 2 + 1) * WIDE] = pair
         small[pl.ds(g * 96, 96), :] = move(halves[...], means[...])
+    for k, send in enumerate(smalls):
+        slot = lax.bitwise_xor(rank, k)
+        start = (slot // BATCH) * 96 + lax.rem(slot, BATCH)
+        for xh in range(2):
+            send[xh * 12 : (xh + 1) * 12, :] = small[pl.ds(start + xh * BATCH, 12, stride=8), :]
 
 
 def store_kernel(box, fine, owners, table, out, cells):
@@ -355,27 +372,29 @@
                     out[0, 0, slot, :, cut] = jnp.where(live, value, fine[0, 0, slot, :, cut])
 
 
-def fix_kernel(new, perm, edges, out):
+def fix_kernel(new, perm, *refs):
+    edges, out = refs[:-1], refs[-1]
     deep, tall = new.shape[1], new.shape[2]
-    ranks_y, gy, gz = lax.axis_size("gy"), lax.axis_index("gy"), lax.axis_index("gz")
-    rank = gy * 2 + gz
-    base = PAR * 2 * ROWS_REGION
+    gz = lax.axis_index("gz")
+    rank = lax.axis_index("gy") * 2 + gz
     out[...] = new[...]
 
     def add(c, x, rows, amount):
         out[c, x, rows, :] = out[c, x, rows, :] + 0.25 / perm[x, rows, :] * amount
 
-    lower = edges[jnp.maximum(rank - 2, gz), pl.ds(base + 32, 1), :]
-    higher = edges[jnp.minimum(rank + 2, (ranks_y - 1) * 2 + gz), pl.ds(base + 33, 1), :]
-    add(0, deep - 1, slice(0, 1), jnp.where(gy > 0, lower, 0.0))
-    add(1, 0, slice(tall - 1, tall), jnp.where(gy < ranks_y - 1, higher, 0.0))
-    side = gy * 2 + 1 - gz
+    lower = higher = jnp.zeros((1, LANES), F32)
+    for k, edge in enumerate(edges, 1):
+        row = 2 * ROWS_REGION
+        lower = jnp.where(lax.bitwise_xor(rank, k) == rank - 2, edge[row : row + 1, :], lower)
+        higher = jnp.where(lax.bitwise_xor(rank, k) == rank + 2, edge[row + 1 : row + 2, :], higher)
+    add(0, deep - 1, slice(0, 1), lower)
+    add(1, 0, slice(tall - 1, tall), higher)
     lane = lane_iota((tall, LANES))
-    tile = edges[side, pl.ds(base + 1, tall), :]
+    tile = edges[0][ROWS_PATCH + 1 : ROWS_PATCH + 1 + tall, :]
     add(0, deep - 1, slice(0, tall), jnp.where((lane == 0) & (gz == 1), pltpu.roll(tile, 1, 1), 0.0))
     add(2, 0, slice(0, tall), jnp.where((lane == LANES - 1) & (gz == 0), pltpu.roll(tile, LANES - 1, 1), 0.0))
     lane = lane_iota((deep, LANES))
-    tile = edges[side, pl.ds(base + 16, deep), :]
+    tile = edges[0][ROWS_PATCH + 16 : ROWS_PATCH + 16 + deep, :]
     first = jnp.where((lane == LANES - 1) & (gz == 0), pltpu.roll(tile, LANES - 1, 1), 0.0)
     last = jnp.where((lane == 0) & (gz == 1), pltpu.roll(tile, 1, 1), 0.0)
     for x in range(deep):
@@ -383,28 +402,35 @@
         add(1, x, slice(tall - 1, tall), last[x : x + 1])
 
 
-def place_kernel(new, means, corner, owners, out, spread):
-    stretch = means.shape[1]
+def place_kernel(ranks, new, corner, owners, *refs):
+    means, (out, spread, stage, gathered, sems) = refs[:ranks], refs[ranks:]
     rank = lax.axis_index("gy") * lax.axis_size("gz") + lax.axis_index("gz")
-    out[...] = new[...]
+    for k, mean in enumerate(means):
+        gathered[k] = mean[...]
     lane = lane_iota((HALF, LANES))
-    for q in range(PAR):
-        cx, cy, cz = corner[0, 0, q, 0], corner[0, 0, q, 1], corner[0, 0, q, 2]
-        owner = owners[0, rank, q]
-        start = (rank // BATCH) * 96 + lax.rem(rank, BATCH)
+    spots = [tuple(corner[0, 0, q, d] for d in range(3)) for q in range(PAR)]
+    for q, (cx, cy, cz) in enumerate(spots):
+        k = lax.bitwise_xor(owners[0, rank, q], rank)
         for xh in range(2):
-            rows = means[owner, pl.ds(start + xh * BATCH, 12, stride=8), :]
+            rows = gathered[k, xh * 12 : (xh + 1) * 12, :]
             for odd in range(2):
                 for y in range(HALF):
                     shift = lax.rem(cz - y * HALF - odd * HALF * HALF + 2 * LANES, LANES)
-                    spread[pl.ds((xh * 2 + odd) * 96 + y, 12, stride=8), :] = pltpu.roll(rows, shift, 1)
-        inside = (lane >= cz) & (lane < cz + HALF)
-        for c in range(6):
+                    spread[q, pl.ds((xh * 2 + odd) * 96 + y, 12, stride=8), :] = pltpu.roll(rows, shift, 1)
+    copies = []
+    for c in range(6):
+        stage[c] = new[c]
+        for q, (cx, cy, cz) in enumerate(spots):
+            inside = (lane >= cz) & (lane < cz + HALF)
             for x in range(HALF):
                 xh, k = x // 4, x % 4
-                tile = spread[pl.ds((xh * 2 + k % 2) * 96 + (c * 2 + k // 2) * 8, 8), :]
-                spot = out[c, cx + x, pl.ds(cy, HALF), :]
-                out[c, cx + x, pl.ds(cy, HALF), :] = jnp.where(inside, tile, spot)
+                tile = spread[q, pl.ds((xh * 2 + k % 2) * 96 + (c * 2 + k // 2) * 8, 8), :]
+                spot = stage[c, cx + x, pl.ds(cy, HALF), :]
+                stage[c, cx + x, pl.ds(cy, HALF), :] = jnp.where(inside, tile, spot)
+        copies.append(pltpu.make_async_copy(stage.at[c], out.at[c], sems.at[c]))
+        copies[-1].start()
+    for copy in copies:
+        copy.wait()
 
 
 def local(coarse_fields, permittivity, fine_fields, fine_permittivity, patch_corner, patch_owner):
@@ -421,11 +447,12 @@
     beside = lax.ppermute(coarse_fields, "gz", swap_pairs(2, 0))
     x_face = shape((5, tall, cols), F32)
     y_face = shape((5, deep, cols), F32)
-    if two_y:
-        body = faces_kernel
-    else:
-        body = functools.partial(faces_kernel, y_odd=None)
-    faces = call(body, [x_face, x_face, y_face] + [y_face] * two_y, [vmem])(coarse_fields)
+    faces = call(
+        functools.partial(faces_kernel, two_y),
+        [x_face, x_face, y_face] + [y_face] * two_y,
+        [whole(pl.ANY)],
+        [pltpu.SemaphoreType.DMA((6 + 2 * two_y,))],
+    )(coarse_fields)
     got = [
         lax.ppermute(faces[0], "gx", swap_pairs(count_x, 0)),
         lax.ppermute(faces[1], "gx", swap_pairs(count_x, 1)),
@@ -443,33 +470,41 @@
     )(fine_fields, fine_permittivity, jnp.asarray(grow, BF16))
 
     full = deep + 2
-    payload = PAR * 2 * ROWS_REGION + EDGE_ROWS
-    new, packed = call(
-        functools.partial(leap_kernel, two_y),
-        [shape(coarse_fields.shape, F32), shape((payload, LANES), F32)],
-        [vmem] * 3 + [smem] + [vmem] * len(got),
+    ranks = count_y * lax.axis_size("gz")
+
+    def exchange(parts):
+        swaps = [[(r, r ^ k) for r in range(ranks)] for k in range(ranks)]
+        return [parts[0]] + [lax.ppermute(parts[k], ("gy", "gz"), swaps[k]) for k in range(1, ranks)]
+
+    patches = [shape((ROWS_BESIDE if k == 1 else ROWS_PATCH, LANES), F32) for k in range(ranks)]
+    new, *sends = call(
+        functools.partial(leap_kernel, two_y, ranks),
+        [shape(coarse_fields.shape, F32)] + patches,
+        [vmem] * 3 + [smem] * 2 + [vmem] * len(got),
         [
             pltpu.VMEM((6 * full * 16, LANES), F32),
             pltpu.VMEM((6 * full * 16, LANES), F32),
             pltpu.VMEM((3 * (full - 1) * 16, 2 * LANES), F32),
             pltpu.VMEM((deep * 16, LANES), F32),
             pltpu.VMEM((6 * deep * 16, LANES), F32),
+            pltpu.VMEM((PAR, ROWS_PATCH, LANES), F32),
         ],
-    )(coarse_fields, beside, permittivity, patch_corner, *got)
-    regions = lax.all_gather(packed, ("gy", "gz"))
-
-    box, small = call(
-        fine_kernel,
-        [shape((groups, 18, ROWS_BOX, LANES), F32), shape((groups * 96, LANES), F32)],
-        [vmem] * 3 + [smem] + [vmem] * 2,
+    )(coarse_fields, beside, permittivity, patch_corner, patch_owner, *got)
+    regions = exchange(sends)
+
+    box, *smalls = call(
+        functools.partial(fine_kernel, ranks),
+        [shape((groups, 18, ROWS_BOX, LANES), F32)] + [shape((24, LANES), F32)] * ranks,
+        [vmem] * (ranks + 4),
         [
-            pltpu.VMEM((6 * ROWS_BOX, LANES), F32),
+            pltpu.VMEM((2, groups * 6 * ROWS_BOX, LANES), F32),
             pltpu.VMEM((6, ROWS_BOX, WIDE), F32),
             pltpu.VMEM((3, ROWS_BOX, WIDE), F32),
             pltpu.VMEM((96, 2 * WIDE), F32),
+            pltpu.VMEM((groups * 96, LANES), F32),
         ],
-    )(regions, box, rate, patch_owner, jnp.asarray(ghost_table(), BF16), jnp.asarray(mean_table(), BF16))
-    means = lax.all_gather(small, ("gy", "gz"))
+    )(*regions, box, rate, jnp.asarray(ghost_table(), BF16), jnp.asarray(mean_table(), BF16))
+    means = exchange(smalls)
 
     fine = call(
         store_kernel,
@@ -478,13 +513,19 @@
         [pltpu.VMEM((2, 6 * ROWS_BOX, LANES), F32)],
         size=4_000_000,
     )(box, fine_fields, patch_owner, jnp.asarray(grow.T, BF16))
-    new = call(fix_kernel, shape(coarse_fields.shape, F32), [vmem] * 3)(new, permittivity, regions)
+    new = call(fix_kernel, shape(coarse_fields.shape, F32), [vmem] * (1 + ranks))(new, permittivity, *regions[1:])
     coarse = call(
-        place_kernel,
+        functools.partial(place_kernel, ranks),
         shape(coarse_fields.shape, F32),
-        [vmem, vmem, smem, smem],
-        [pltpu.VMEM((4 * 96, LANES), F32)],
-    )(new, means, patch_corner, patch_owner)
+        [vmem, smem, smem] + [vmem] * ranks,
+        [
+            pltpu.VMEM((PAR, 4 * 96, LANES), F32),
+            pltpu.VMEM(coarse_fields.shape, F32),
+            pltpu.VMEM((ranks, 24, LANES), F32),
+            pltpu.SemaphoreType.DMA((6,)),
+        ],
+        out_specs=whole(pl.ANY),
+    )(new, patch_corner, patch_owner, *means)
     return coarse, fine
 
 

time: 33.4 us -> 27.7 us (0.83)
  the two profiles are of different devices: /device:TPU:9 before, /device:TPU:13 now
where the time goes in v1:
time: 27.7 us; the launch traced here: 27.4 us
  starting transfers between devices  12.4 us (45%)
  Pallas kernels  6.56 us (24%)
  waiting for transfers between devices  4.19 us (15%)
  local copies, waits for them, and re-layouts  3.53 us (13%)
  between operations  0.75 us (3%)
    ppermute x6, starting transfers between devices, exchange(): lax.ppermute(parts[k], ('gy', 'gz'), swaps[k])  5.7 us
    ppermute x1, starting transfers between devices, local(): lax.ppermute(faces[1], 'gx', swap_pairs(count_x, 1))  4.45 us
    unnamed x27, local copies, waits for them, and re-layouts  3.53 us
    ppermute x6, waiting for transfers between devices, exchange(): lax.ppermute(parts[k], ('gy', 'gz'), swaps[k])  2.64 us
    pallas_call x1, Pallas kernels, local(): call(functools.partial(place_kernel, ranks), shape(coarse_fields.shape, F...  1.57 us
    pallas_call x1, Pallas kernels, local(): call(functools.partial(leap_kernel, two_y, ranks), [shape(coarse_fields.s...  1.54 us
    ppermute x1, waiting for transfers between devices, local(): lax.ppermute(faces[2], 'gy', swap_pairs(count_y, 0))  1.54 us
    pallas_call x1, Pallas kernels, local(): call(functools.partial(fine_kernel, ranks), [shape((groups, 18, ROWS_BOX,...  1.39 us
  transfers between devices with their start and end apart: 10, of which 4 were waited for; matrix products, arithmetic and copies ran while one was open for 5% of the time, Pallas kernels for 8%

profile of v1, /device:TPU:13, one launch (start us, length us, event | category | flops | bytes accessed | tf_op | source)
XLA Modules:
  0.0 27.4 jit_solution(12137514132050367459)
XLA Ops:
  0.6 0.7 %collective-permute-start = (f32[6,12,12,128]{3,2,1,0:T(8,128)}, f32[6,12,12,128]{3,2,1,0:T(8,128)S(1)}, u32[]{:S(2)}, u32[]{:S(2)}) collective-permute-start(f32[6,12,12,128]{3,2,1,0:T(8,128)} %refs_0_.1), channel_id=1, source_target_pairs={{0,1},{1,0},{2,3},{3,2},{4,5},{5,4},{6,7},{7,6},{8,9},{9,8},{10,11... | collective-permute-start | bytes 1327112 | tf_op jit(solution)/shard_map/ppermute | solution.py:447
  1.4 1.1 %copy-done = f32[6,12,12,128]{3,2,1,0:T(8,128)S(1)} copy-done((f32[6,12,12,128]{3,2,1,0:T(8,128)S(1)}, f32[6,12,12,128]{3,2,1,0:T(8,128)}, u32[]{:S(2)}) %copy-start) | copy-done | bytes 442392
  2.5 0.2 collective-permute-start.1
  2.8 4.5 %collective-permute-start.2 = (f32[5,12,128]{2,1,0:T(8,128)S(1)}, f32[5,12,128]{2,1,0:T(8,128)S(1)}, u32[]{:S(2)}, u32[]{:S(2)}) collective-permute-start(f32[5,12,128]{2,1,0:T(8,128)S(1)} %get-tuple-element.18), channel_id=1, source_target_pairs={{4,8},{8,4},{5,9},{9,5},{6,10},{10,6},{7,11},{11,7},{20,24},{24,20... | collective-permute-start | bytes 92168 | tf_op jit(solution)/shard_map/ppermute | solution.py:458
  7.3 1.3 %collective-permute-start.3 = (f32[5,12,128]{2,1,0:T(8,128)S(1)}, f32[5,12,128]{2,1,0:T(8,128)S(1)}, u32[]{:S(2)}, u32[]{:S(2)}) collective-permute-start(f32[5,12,128]{2,1,0:T(8,128)S(1)} %get-tuple-element.19), channel_id=1, source_target_pairs={{0,2},{2,0},{1,3},{3,1},{4,6},{6,4},{5,7},{7,5},{8,10},{10,8},{9,1... | collective-permute-start | bytes 92168 | tf_op jit(solution)/shard_map/ppermute | solution.py:459
  8.6 1.5 %collective-permute-done.3.refs_7_ = f32[5,12,128]{2,1,0:T(8,128)S(1)} collective-permute-done((f32[5,12,128]{2,1,0:T(8,128)S(1)}, f32[5,12,128]{2,1,0:T(8,128)S(1)}, u32[]{:S(2)}, u32[]{:S(2)}) %collective-permute-start.3) | collective-permute-done | bytes 30752 | tf_op jit(solution)/shard_map/ppermute | solution.py:459
  10.2 0.9 %copy-done.2 = f32[12,12,128]{2,1,0:T(8,128)S(1)} copy-done((f32[12,12,128]{2,1,0:T(8,128)S(1)}, f32[12,12,128]{2,1,0:T(8,128)}, u32[]{:S(2)}) %copy-start.2) | copy-done | bytes 73752
  11.1 1.5 %shard_map.114 = (f32[6,12,12,128]{3,2,1,0:T(8,128)S(1)}, f32[128,128]{1,0:T(8,128)S(1)}, f32[160,128]{1,0:T(8,128)S(1)}, f32[128,128]{1,0:T(8,128)S(1)}, f32[128,128]{1,0:T(8,128)S(1)}) custom-call(f32[6,12,12,128]{3,2,1,0:T(8,128)S(1)} %copy-done.1, f32[6,12,12,128]{3,2,1,0:T(8,128)S(1)} %collective-permute-done.refs_1_, f32[12,12,128]{2,1,0:T(8,128)S(1)} %copy-done.2, ...), custom_call_target="tpu_custom_call" | custom-call | flops 1000000 | bytes 1000000 | tf_op jit(solution)/shard_map/pallas_call | solution.py:480
  12.6 1.8 %collective-permute-start.4 = (f32[160,128]{1,0:T(8,128)S(1)}, f32[160,128]{1,0:T(8,128)S(1)}, u32[]{:S(2)}, u32[]{:S(2)}) collective-permute-start(f32[160,128]{1,0:T(8,128)S(1)} %get-tuple-element.21), channel_id=1, source_target_pairs={{0,1},{1,0},{2,3},{3,2},{4,5},{5,4},{6,7},{7,6},{8,9},{9,8},{10,11... | collective-permute-start | bytes 245768 | tf_op jit(solution)/shard_map/ppermute | solution.py:477
  14.4 1.2 %collective-permute-start.5 = (f32[128,128]{1,0:T(8,128)S(1)}, f32[128,128]{1,0:T(8,128)S(1)}, u32[]{:S(2)}, u32[]{:S(2)}) collective-permute-start(f32[128,128]{1,0:T(8,128)S(1)} %get-tuple-element.22), channel_id=1, source_target_pairs={{0,2},{1,3},{2,0},{3,1},{4,6},{5,7},{6,4},{7,5},{8,10},{9,11},{10,... | collective-permute-start | bytes 196616 | tf_op jit(solution)/shard_map/ppermute | solution.py:477
  15.7 0.5 %collective-permute-start.6 = (f32[128,128]{1,0:T(8,128)S(1)}, f32[128,128]{1,0:T(8,128)S(1)}, u32[]{:S(2)}, u32[]{:S(2)}) collective-permute-start(f32[128,128]{1,0:T(8,128)S(1)} %get-tuple-element.23), channel_id=1, source_target_pairs={{0,3},{1,2},{2,1},{3,0},{4,7},{5,6},{6,5},{7,4},{8,11},{9,10},{10,... | collective-permute-start | bytes 196616 | tf_op jit(solution)/shard_map/ppermute | solution.py:477
  16.1 0.2 copy.13.fine
  16.4 0.2 copy-done.5
  16.6 0.6 %shard_map.116 = (f32[1,18,72,128]{3,2,1,0:T(8,128)S(1)}, f32[1,72,384]{2,1,0:T(8,128)S(1)}) custom-call(f32[1,1,4,6,4096]{4,3,2,1,0:T(8,128)S(1)} %copy.13.fine, f32[1,1,4,4096]{3,2,1,0:T(4,128)S(1)} %copy-done.8, bf16[256,384]{1,0:T(8,128)(2,1)S(1)} %copy-done.5), custom_call_target="tpu_custom_call" | custom-call | flops 1000000 | bytes 4000000 | tf_op jit(solution)/shard_map/pallas_call | solution.py:464
  17.2 0.9 %collective-permute-done.5.refs_1_.refs_2_ = f32[128,128]{1,0:T(8,128)S(1)} collective-permute-done((f32[128,128]{1,0:T(8,128)S(1)}, f32[128,128]{1,0:T(8,128)S(1)}, u32[]{:S(2)}, u32[]{:S(2)}) %collective-permute-start.5) | collective-permute-done | bytes 65568 | tf_op jit(solution)/shard_map/ppermute | solution.py:477
  18.1 1.6 %collective-permute-done.6.refs_2_.refs_3_ = f32[128,128]{1,0:T(8,128)S(1)} collective-permute-done((f32[128,128]{1,0:T(8,128)S(1)}, f32[128,128]{1,0:T(8,128)S(1)}, u32[]{:S(2)}, u32[]{:S(2)}) %collective-permute-start.6) | collective-permute-done | bytes 65568 | tf_op jit(solution)/shard_map/ppermute | solution.py:477
  19.7 1.4 %shard_map.117 = (f32[1,18,72,128]{3,2,1,0:T(8,128)S(1)}, f32[24,128]{1,0:T(8,128)S(1)}, f32[24,128]{1,0:T(8,128)S(1)}, f32[24,128]{1,0:T(8,128)S(1)}, f32[24,128]{1,0:T(8,128)S(1)}) custom-call(f32[128,128]{1,0:T(8,128)S(1)} %get-tuple-element.24.refs_0_, f32[160,128]{1,0:T(8,128)S(1)} %collective-permute-done.4.refs_0_.refs_1_, ...), custom_call_target="tpu_custom_call" | custom-call | flops 1000000 | bytes 1000000 | tf_op jit(solution)/shard_map/pallas_call | solution.py:495
  21.1 0.4 %collective-permute-start.7 = (f32[24,128]{1,0:T(8,128)S(1)}, f32[24,128]{1,0:T(8,128)S(1)}, u32[]{:S(2)}, u32[]{:S(2)}) collective-permute-start(f32[24,128]{1,0:T(8,128)S(1)} %get-tuple-element.28), channel_id=1, source_target_pairs={{0,1},{1,0},{2,3},{3,2},{4,5},{5,4},{6,7},{7,6},{8,9},{9,8},{10,11... | collective-permute-start | bytes 36872 | tf_op jit(solution)/shard_map/ppermute | solution.py:477
  21.5 1.1 %collective-permute-start.8 = (f32[24,128]{1,0:T(8,128)S(1)}, f32[24,128]{1,0:T(8,128)S(1)}, u32[]{:S(2)}, u32[]{:S(2)}) collective-permute-start(f32[24,128]{1,0:T(8,128)S(1)} %get-tuple-element.29), channel_id=1, source_target_pairs={{0,2},{1,3},{2,0},{3,1},{4,6},{5,7},{6,4},{7,5},{8,10},{9,11},{10,... | collective-permute-start | bytes 36872 | tf_op jit(solution)/shard_map/ppermute | solution.py:477
  22.6 0.7 %collective-permute-start.9 = (f32[24,128]{1,0:T(8,128)S(1)}, f32[24,128]{1,0:T(8,128)S(1)}, u32[]{:S(2)}, u32[]{:S(2)}) collective-permute-start(f32[24,128]{1,0:T(8,128)S(1)} %get-tuple-element.30), channel_id=1, source_target_pairs={{0,3},{1,2},{2,1},{3,0},{4,7},{5,6},{6,5},{7,4},{8,11},{9,10},{10,... | collective-permute-start | bytes 36872 | tf_op jit(solution)/shard_map/ppermute | solution.py:477
  23.3 1.2 %shard_map.119 = f32[1,1,4,6,4096]{4,3,2,1,0:T(8,128)S(1)} custom-call(f32[1,18,72,128]{3,2,1,0:T(8,128)S(1)} %get-tuple-element.31.box, f32[1,1,4,6,4096]{4,3,2,1,0:T(8,128)S(1)} %copy.13.fine, s32[1,4,2]{2,1,0:T(4,128)S(1)} %copy.12.refs_4_.owners, bf16[384,256]{1,0:T(8,128)(2,1)S(1)} %copy-done.4), custom_call_target="tpu_custom_call" | custom-call | flops 1000000 | bytes 4000000 | tf_op jit(solution)/shard_map/pallas_call | solution.py:509
  24.6 1.0 %copy.17 = f32[1,1,4,6,4096]{4,2,3,1,0:T(4,128)} copy(f32[1,1,4,6,4096]{4,3,2,1,0:T(8,128)S(1)} %shard_map.119) | data formatting | bytes 786432
  25.7 0.2 collective-permute-done.9.refs_3_
  25.9 1.6 %shard_map.118 = f32[6,12,12,128]{3,2,1,0:T(8,128)} custom-call(f32[6,12,12,128]{3,2,1,0:T(8,128)S(1)} %shard_map.115.new, s32[1,1,2,3]{3,2,1,0:T(2,128)S(1)} %copy-done.9, s32[1,4,2]{2,1,0:T(4,128)S(1)} %copy.12.refs_4_.owners, f32[24,128]{1,0:T(8,128)S(1)} %get-tuple-element.27.refs_0_, f32[24,128]{1,0:T(8,128)S(1)} %collective-permute-done.7.refs_1_, ...), custom_call_target="tpu_custom_call" | custom-call | flops 1000000 | bytes 1000000 | tf_op jit(solution)/shard_map/pallas_call | solution.py:517
  (30 shorter events, 0.3 us)
Async XLA Ops:
  0.6 9.5 %collective-permute-start = (f32[6,12,12,128]{3,2,1,0:T(8,128)}, f32[6,12,12,128]{3,2,1,0:T(8,128)S(1)}, u32[]{:S(2)}, u32[]{:S(2)}) collective-permute-start(f32[6,12,12,128]{3,2,1,0:T(8,128)} %refs_0_.1), channel_id=1, source_target_pairs={{0,1},{1,0},{2,3},{3,2},{4,5},{5,4},{6,7},{7,6},{8,9},{9,8},{10,11... | collective-permute-start | bytes 1327112 | tf_op jit(solution)/shard_map/ppermute | solution.py:447
  1.4 1.1 %copy-start = (f32[6,12,12,128]{3,2,1,0:T(8,128)S(1)}, f32[6,12,12,128]{3,2,1,0:T(8,128)}, u32[]{:S(2)}) copy-start(f32[6,12,12,128]{3,2,1,0:T(8,128)} %refs_0_.1) | copy-start | bytes 1327108
  2.4 7.7 %copy-start.1 = (f32[6,12,12,128]{3,2,1,0:T(8,128)S(1)}, f32[6,12,12,128]{3,2,1,0:T(8,128)}, u32[]{:S(2)}) copy-start(f32[6,12,12,128]{3,2,1,0:T(8,128)} %refs_0_.1) | copy-start | bytes 1327108
  2.5 6.1 %collective-permute-start.1 = (f32[5,12,128]{2,1,0:T(8,128)S(1)}, f32[5,12,128]{2,1,0:T(8,128)S(1)}, u32[]{:S(2)}, u32[]{:S(2)}) collective-permute-start(f32[5,12,128]{2,1,0:T(8,128)S(1)} %get-tuple-element.17), channel_id=1, source_target_pairs={{0,4},{4,0},{8,12},{12,8},{1,5},{5,1},{9,13},{13,9},{2,6},{6,2},{1... | collective-permute-start | bytes 92168 | tf_op jit(solution)/shard_map/ppermute | solution.py:457
  2.8 5.8 %copy-start.11 = (s32[1,4,2]{1,2,0:T(2,128)S(1)}, s32[1,4,2]{1,2,0:T(2,128)}, u32[]{:S(2)}) copy-start(s32[1,4,2]{1,2,0:T(2,128)} %param.15) | copy-start | bytes 100
  2.8 5.8 %collective-permute-start.2 = (f32[5,12,128]{2,1,0:T(8,128)S(1)}, f32[5,12,128]{2,1,0:T(8,128)S(1)}, u32[]{:S(2)}, u32[]{:S(2)}) collective-permute-start(f32[5,12,128]{2,1,0:T(8,128)S(1)} %get-tuple-element.18), channel_id=1, source_target_pairs={{4,8},{8,4},{5,9},{9,5},{6,10},{10,6},{7,11},{11,7},{20,24},{24,20... | collective-permute-start | bytes 92168 | tf_op jit(solution)/shard_map/ppermute | solution.py:458
  7.2 2.9 %copy-start.9 = (s32[1,1,2,3]{3,2,1,0:T(2,128)S(1)}, s32[1,1,2,3]{3,2,1,0:T(2,128)}, u32[]{:S(2)}) copy-start(s32[1,1,2,3]{3,2,1,0:T(2,128)} %corner.1) | copy-start | bytes 76
  7.3 2.9 %collective-permute-start.3 = (f32[5,12,128]{2,1,0:T(8,128)S(1)}, f32[5,12,128]{2,1,0:T(8,128)S(1)}, u32[]{:S(2)}, u32[]{:S(2)}) collective-permute-start(f32[5,12,128]{2,1,0:T(8,128)S(1)} %get-tuple-element.19), channel_id=1, source_target_pairs={{0,2},{2,0},{1,3},{3,1},{4,6},{6,4},{5,7},{7,5},{8,10},{10,8},{9,1... | collective-permute-start | bytes 92168 | tf_op jit(solution)/shard_map/ppermute | solution.py:459
  10.2 0.9 %copy-start.2 = (f32[12,12,128]{2,1,0:T(8,128)S(1)}, f32[12,12,128]{2,1,0:T(8,128)}, u32[]{:S(2)}) copy-start(f32[12,12,128]{2,1,0:T(8,128)} %perm.2) | copy-start | bytes 221188
  11.1 5.1 %copy-start.10 = (f32[1,1,4,6,4096]{4,2,3,1,0:T(4,128)S(1)}, f32[1,1,4,6,4096]{4,2,3,1,0:T(4,128)}, u32[]{:S(2)}) copy-start(f32[1,1,4,6,4096]{4,2,3,1,0:T(4,128)} %param.12) | copy-start | bytes 1179652
  12.6 7.1 %collective-permute-start.4 = (f32[160,128]{1,0:T(8,128)S(1)}, f32[160,128]{1,0:T(8,128)S(1)}, u32[]{:S(2)}, u32[]{:S(2)}) collective-permute-start(f32[160,128]{1,0:T(8,128)S(1)} %get-tuple-element.21), channel_id=1, source_target_pairs={{0,1},{1,0},{2,3},{3,2},{4,5},{5,4},{6,7},{7,6},{8,9},{9,8},{10,11... | collective-permute-start | bytes 245768 | tf_op jit(solution)/shard_map/ppermute | solution.py:477
  14.4 3.7 %collective-permute-start.5 = (f32[128,128]{1,0:T(8,128)S(1)}, f32[128,128]{1,0:T(8,128)S(1)}, u32[]{:S(2)}, u32[]{:S(2)}) collective-permute-start(f32[128,128]{1,0:T(8,128)S(1)} %get-tuple-element.22), channel_id=1, source_target_pairs={{0,2},{1,3},{2,0},{3,1},{4,6},{5,7},{6,4},{7,5},{8,10},{9,11},{10,... | collective-permute-start | bytes 196616 | tf_op jit(solution)/shard_map/ppermute | solution.py:477
  15.6 0.9 %copy-start.5 = (bf16[256,384]{1,0:T(8,128)(2,1)S(1)}, bf16[256,384]{1,0:T(8,128)(2,1)}, u32[]{:S(2)}) copy-start(bf16[256,384]{1,0:T(8,128)(2,1)} %constant.8.clone.table) | copy-start | bytes 589828
  15.7 0.9 %copy-start.8 = (f32[1,1,4,4096]{3,2,1,0:T(4,128)S(1)}, f32[1,1,4,4096]{3,2,1,0:T(4,128)}, u32[]{:S(2)}) copy-start(f32[1,1,4,4096]{3,2,1,0:T(4,128)} %perm.3) | copy-start | bytes 196612
  15.7 4.0 %collective-permute-start.6 = (f32[128,128]{1,0:T(8,128)S(1)}, f32[128,128]{1,0:T(8,128)S(1)}, u32[]{:S(2)}, u32[]{:S(2)}) collective-permute-start(f32[128,128]{1,0:T(8,128)S(1)} %get-tuple-element.23), channel_id=1, source_target_pairs={{0,3},{1,2},{2,1},{3,0},{4,7},{5,6},{6,5},{7,4},{8,11},{9,10},{10,... | collective-permute-start | bytes 196616 | tf_op jit(solution)/shard_map/ppermute | solution.py:477
  16.6 3.1 %copy-start.6 = (bf16[768,128]{1,0:T(8,128)(2,1)S(1)}, bf16[768,128]{1,0:T(8,128)(2,1)}, u32[]{:S(2)}) copy-start(bf16[768,128]{1,0:T(8,128)(2,1)} %constant.10.clone.refs_7_) | copy-start | bytes 589828
  16.6 3.1 %copy-start.7 = (bf16[128,384]{1,0:T(8,128)(2,1)S(1)}, bf16[128,384]{1,0:T(8,128)(2,1)}, u32[]{:S(2)}) copy-start(bf16[128,384]{1,0:T(8,128)(2,1)} %constant.9.clone.refs_6_) | copy-start | bytes 294916
  19.7 3.6 %copy-start.4 = (bf16[384,256]{1,0:T(8,128)(2,1)S(1)}, bf16[384,256]{1,0:T(8,128)(2,1)}, u32[]{:S(2)}) copy-start(bf16[384,256]{1,0:T(8,128)(2,1)} %constant.11.clone.table) | copy-start | bytes 589828
  21.1 4.6 %collective-permute-start.7 = (f32[24,128]{1,0:T(8,128)S(1)}, f32[24,128]{1,0:T(8,128)S(1)}, u32[]{:S(2)}, u32[]{:S(2)}) collective-permute-start(f32[24,128]{1,0:T(8,128)S(1)} %get-tuple-element.28), channel_id=1, source_target_pairs={{0,1},{1,0},{2,3},{3,2},{4,5},{5,4},{6,7},{7,6},{8,9},{9,8},{10,11... | collective-permute-start | bytes 36872 | tf_op jit(solution)/shard_map/ppermute | solution.py:477
  21.5 4.2 %collective-permute-start.8 = (f32[24,128]{1,0:T(8,128)S(1)}, f32[24,128]{1,0:T(8,128)S(1)}, u32[]{:S(2)}, u32[]{:S(2)}) collective-permute-start(f32[24,128]{1,0:T(8,128)S(1)} %get-tuple-element.29), channel_id=1, source_target_pairs={{0,2},{1,3},{2,0},{3,1},{4,6},{5,7},{6,4},{7,5},{8,10},{9,11},{10,... | collective-permute-start | bytes 36872 | tf_op jit(solution)/shard_map/ppermute | solution.py:477
  22.6 3.3 %collective-permute-start.9 = (f32[24,128]{1,0:T(8,128)S(1)}, f32[24,128]{1,0:T(8,128)S(1)}, u32[]{:S(2)}, u32[]{:S(2)}) collective-permute-start(f32[24,128]{1,0:T(8,128)S(1)} %get-tuple-element.30), channel_id=1, source_target_pairs={{0,3},{1,2},{2,1},{3,0},{4,7},{5,6},{6,5},{7,4},{8,11},{9,10},{10,... | collective-permute-start | bytes 36872 | tf_op jit(solution)/shard_map/ppermute | solution.py:477
  24.6 1.0 %copy-start.3 = (f32[12,12,128]{2,1,0:T(8,128)S(1)}, f32[12,12,128]{2,1,0:T(8,128)}, u32[]{:S(2)}) copy-start(f32[12,12,128]{2,1,0:T(8,128)} %perm.2) | copy-start | bytes 221188

commit v2 on v1

v2 whole, which is shorter than its diff:
```python
import functools
import jax
import jax.numpy as jnp
import numpy as np
from jax import lax
from jax.experimental import pallas as pl
from jax.experimental.pallas import tpu as pltpu
from jax.sharding import PartitionSpec as P

PF = 16
PAR = 2
HALF = PF // 2
RIM = HALF + 2
PLANES = 9
LINE = PF + 2
LANES = 128
WIDE = 384
BATCH = 4
ROWS_BOX = PLANES * 8
ROWS_RIM = 48
ROW_EDGE = 64
ROWS_PATCH = 72
ROWS_BESIDE = 104
X_COMPS = (0, 1, 2, 4, 5)
Y_COMPS = (0, 1, 2, 3, 5)
VMEM_BYTES = 48 * 1024 * 1024
F32 = jnp.float32
BF16 = jnp.bfloat16


def rim_lane(time, j, k):
    if 0 < j < RIM - 1:
        return j * RIM + k + 3 * time
    if j == 0 and time == 0:
        return k
    return (RIM - 1) * RIM + 3 + (2 * time + j // (RIM - 1) - 1) * RIM + k


def grow_table():
    table = np.zeros((PF * PF, WIDE), np.float32)
    for y in range(PF):
        for z in range(PF):
            table[y * PF + z, (y + 1) * LINE + z + 1] = 1.0
    return table


def ghost_table():
    table = np.zeros((2, 2 * LANES, WIDE), np.float32)
    for y in range(LINE):
        for z in range(LINE):
            j, k, lane = (y + 1) // 2, (z + 1) // 2, y * LINE + z
            table[:, LANES + j * RIM + k, lane] = 1.0
            if y in (0, LINE - 1) or z in (0, LINE - 1):
                table[0, rim_lane(0, j, k), lane] = 1.0
                table[1, rim_lane(0, j, k), lane] = 0.5
                table[1, rim_lane(1, j, k), lane] = 0.5
    return table


def mean_table():
    table = np.zeros((2, WIDE, LANES), np.float32)
    for odd in range(2):
        for y in range(PF):
            for z in range(PF):
                lane = odd * HALF * HALF + (y // 2) * HALF + z // 2
                table[odd, (y + 1) * LINE + z + 1, lane] = 0.125
    return table.reshape(2 * WIDE, LANES)


def move(rows, table):
    high = rows.astype(BF16)
    low = (rows - high.astype(F32)).astype(BF16)
    out = jnp.dot(high, table, preferred_element_type=F32)
    return out + jnp.dot(low, table, preferred_element_type=F32)


def lane_iota(shape):
    return lax.broadcasted_iota(jnp.int32, shape, len(shape) - 1)


def whole(memory_space=pltpu.VMEM):
    return pl.BlockSpec(memory_space=memory_space)


def call(kernel, outs, in_specs, scratch=(), flops=1_000_000, size=1_000_000, out_specs=None, **extra):
    return pl.pallas_call(
        kernel,
        out_shape=outs,
        in_specs=in_specs,
        out_specs=jax.tree.map(lambda _: whole(), outs) if out_specs is None else out_specs,
        scratch_shapes=list(scratch),
        compiler_params=pltpu.CompilerParams(vmem_limit_bytes=VMEM_BYTES),
        cost_estimate=pl.CostEstimate(flops=flops, bytes_accessed=size, transcendentals=0),
        **extra,
    )


def swap_pairs(count, first):
    pairs = []
    for i in range(first, count - 1, 2):
        pairs += [(i, i + 1), (i + 1, i)]
    return pairs


def faces_kernel(two_y, block, *refs):
    outs, sems = refs[:-1], refs[-1]
    deep, tall = block.shape[1], block.shape[2]
    gx_odd = lax.rem(lax.axis_index("gx"), 2)
    gy_odd = lax.rem(lax.axis_index("gy"), 2)
    copies = []
    for n, place in enumerate(((1 - gx_odd) * (deep - 1), gx_odd * (deep - 1))):
        for low, high, k in ((0, 3, 0), (4, 6, 3)):
            source = block.at[low:high, place]
            copies.append((source, outs[n].at[k : k + high - low]))
    for n, place in enumerate(((1 - gy_odd) * (tall - 1), gy_odd * (tall - 1))[: 1 + two_y]):
        for low, high, k in ((0, 4, 0), (5, 6, 4)):
            source = block.at[low:high, :, place]
            copies.append((source, outs[2 + n].at[k : k + high - low]))
    copies = [pltpu.make_async_copy(a, b, sems.at[i]) for i, (a, b) in enumerate(copies)]
    for copy in copies:
        copy.start()
    for copy in copies:
        copy.wait()


def leap_kernel(two_y, ranks, *refs):
    block, beside, perm, corner, owners, ahead, x_even, x_odd, y_even = refs[:9]
    y_odd = refs[9] if two_y else None
    refs = refs[9 + two_y :]
    new, sends = refs[0], refs[1 : 1 + ranks]
    pad, side, mag, rate, fresh, packed, sem = refs[1 + ranks :]
    deep, tall = block.shape[1], block.shape[2]
    full = deep + 2
    fetch = pltpu.make_async_copy(perm, rate, sem)
    fetch.start()
    gx_odd = lax.rem(lax.axis_index("gx"), 2)
    gy_odd = lax.rem(lax.axis_index("gy"), 2)
    gz = lax.axis_index("gz")
    rank = lax.axis_index("gy") * lax.axis_size("gz") + gz
    lane = lane_iota((tall, LANES))
    keep = ((lane == 0) & (gz == 0)) | ((lane == LANES - 1) & (gz == 1))
    lane = lane_iota((16, LANES))
    none = jnp.zeros((16, LANES), F32)

    def at(c, x):
        return (c * full + x) * 16

    for c in range(6):
        for x in (0, full - 1):
            pad[pl.ds(at(c, x), 16), :] = none
        for x in range(deep):
            pad[pl.ds(at(c, x + 1), tall), :] = block[c, x]
        pad[pl.ds(at(c, 1) + tall, deep, stride=16), :] = none[0:deep]
        pad[pl.ds(at(c, 1) + 15, deep, stride=16), :] = none[0:deep]
    for c in range(5):
        for x in (0, full - 1):
            side[pl.ds(at(c, x), 16), :] = none
        for x in range(deep):
            side[pl.ds(at(c, x + 1), 16), :] = none
            side[pl.ds(at(c, x + 1), tall), :] = jnp.where(keep, beside[c, x], 0.0)
    for k, c in enumerate(X_COMPS):
        even, odd = x_even[k], x_odd[k]
        pad[pl.ds(at(c, 0), tall), :] = jnp.where(gx_odd == 0, odd, even)
        if c in (1, 2):
            pad[pl.ds(at(c, full - 1), tall), :] = jnp.where(gx_odd == 0, even, odd)
    for k, c in enumerate(Y_COMPS):
        even = y_even[k]
        odd = jnp.zeros_like(even) if y_odd is None else y_odd[k]
        pad[pl.ds(at(c, 1) + 15, deep, stride=16), :] = jnp.where(gy_odd == 0, odd, even)
        if c in (0, 2):
            pad[pl.ds(at(c, 1) + tall, deep, stride=16), :] = jnp.where(gy_odd == 0, even, odd)

    def up_y(a):
        return pltpu.roll(a, 15, 0)

    def down_y(a):
        return pltpu.roll(a, 1, 0)

    def plane(c, x):
        return pad[pl.ds(at(c, x), 16), :]

    def edge(c, x):
        return side[pl.ds(at(c, x), 16), :]

    def field(c, x):
        return mag[pl.ds((c * (full - 1) + x) * 16, 16), :]

    for x in range(full - 1):
        e0, e1, e2 = plane(0, x), plane(1, x), plane(2, x)
        s0, s1, s2 = edge(0, x), edge(1, x), edge(2, x)
        r0, r1 = pltpu.roll(e0, LANES - 1, 1), pltpu.roll(e1, LANES - 1, 1)
        u0 = jnp.where(lane == LANES - 1, pltpu.roll(s0, LANES - 1, 1), r0)
        u1 = jnp.where(lane == LANES - 1, pltpu.roll(s1, LANES - 1, 1), r1)
        h0 = plane(3, x) - 0.5 * ((up_y(e2) - e2) - (u1 - e1))
        h1 = plane(4, x) - 0.5 * ((u0 - e0) - (plane(2, x + 1) - e2))
        h2 = plane(5, x) - 0.5 * ((plane(1, x + 1) - e1) - (up_y(e0) - e0))
        t0 = edge(3, x) - 0.5 * ((up_y(s2) - s2) - (r1 - s1))
        t1 = edge(4, x) - 0.5 * ((r0 - s0) - (edge(2, x + 1) - s2))
        d0 = pltpu.roll(jnp.where(lane == LANES - 1, t0, h0), 1, 1)
        d1 = pltpu.roll(jnp.where(lane == LANES - 1, t1, h1), 1, 1)
        for c, value in enumerate((h0, h1, h2, d0, d1)):
            mag[pl.ds((c * (full - 1) + x) * 16, 16), :] = value
    fetch.wait()
    for x in range(deep):
        h0, h1, h2, d0, d1 = (field(c, x + 1) for c in range(5))
        coef = 0.5 / rate[x]
        c0 = (h2 - down_y(h2)) - (h1 - d1)
        c1 = (h0 - d0) - (h2 - field(2, x))
        c2 = (h1 - field(1, x)) - (h0 - down_y(h0))
        for c, curl in enumerate((c0, c1, c2)):
            value = plane(c, x + 1)[0:tall] + coef * curl[0:tall]
            new[c, x] = value
            new[c + 3, x] = (h0, h1, h2)[c][0:tall]
            fresh[pl.ds((c * deep + x) * 16, tall), :] = value
            fresh[pl.ds(((c + 3) * deep + x) * 16, tall), :] = (h0, h1, h2)[c][0:tall]
    lane = lane_iota((8, LANES))
    for q in range(PAR):
        cx, cy, cz = corner[0, 0, q, 0], corner[0, 0, q, 1], corner[0, 0, q, 2]

        def rows_of(time, c, k, j, count, over_c):
            source, depth, start = (pad, full, cx) if time == 0 else (fresh, deep, cx - 1)
            step = depth * 16 if over_c else 16
            return source[pl.ds((c * depth + start + k) * 16 + cy + (j - 1), count, stride=step), :]

        def aim(rows, target):
            return pltpu.roll(rows, lax.rem(target - (cz - 1) + 2 * LANES, LANES), 1)

        for c in range(6):
            total = jnp.zeros((8, LANES), F32)
            for j in range(RIM):
                if (j == 0 and c == 4) or (j == RIM - 1 and c not in (0, 2)) or (0 < j < RIM - 1 and c == 5):
                    continue
                for time in range(2):
                    first = rim_lane(time, j, 0)
                    rows = aim(rows_of(time, c, 1, j, 8, False), first)
                    if j in (0, RIM - 1):
                        inside = (lane >= first) & (lane < first + RIM)
                    else:
                        inside = (lane == first) | (lane == first + RIM - 1)
                    total = jnp.where(inside, rows, total)
            packed[q, c * 8 : c * 8 + 8, :] = total
        for time in range(2):
            low = jnp.zeros((6, LANES), F32)
            high = jnp.zeros((2, LANES), F32)
            for j in range(RIM):
                first = j * RIM
                inside = (lane >= first) & (lane < first + RIM)
                low = jnp.where(inside[0:6], aim(rows_of(time, 0, 0, j, 6, True), first), low)
                high = jnp.where(inside[0:2], aim(rows_of(time, 1, RIM - 1, j, 2, True), first), high)
            base = ROWS_RIM + time * 8
            packed[q, base : base + 6, :] = low
            packed[q, base + 6 : base + 8, :] = high
        packed[q, ROW_EDGE:ROWS_PATCH, :] = jnp.zeros((ROWS_PATCH - ROW_EDGE, LANES), F32)
        packed[q, ROW_EDGE : ROW_EDGE + 1, :] = pad[pl.ds(at(1, full - 1) + tall - 1, 1), :]
        packed[q, ROW_EDGE + 1 : ROW_EDGE + 2, :] = pad[pl.ds(at(0, 0), 1), :]
    for k, send in enumerate(sends):
        q = jnp.where(owners[0, 0, rank] == lax.bitwise_xor(rank, k), 0, 1)
        send[0:ROWS_PATCH, :] = packed[q]
    half = lane_iota((16, LANES)) < LANES // 2
    send = sends[1]
    send[ROWS_PATCH : ROWS_PATCH + 16, :] = jnp.where(half, plane(0, 0), plane(2, full - 1))
    low = jnp.where(gy_odd == 0, jnp.zeros_like(y_even[1]) if y_odd is None else y_odd[1], y_even[1])
    high = jnp.where(gy_odd == 0, y_even[2], jnp.zeros_like(y_even[2]) if y_odd is None else y_odd[2])
    send[ROWS_PATCH + 16 : ROWS_PATCH + 32, :] = jnp.zeros((16, LANES), F32)
    send[ROWS_PATCH + 16 : ROWS_PATCH + 16 + deep, :] = jnp.where(half[0:deep], low, high)


def places():
    for x in range(PF):
        yield x, (x % 8 + 1) * 8 if x < 8 else (x % 8) * 8 + BATCH


def load_kernel(fine, perm, table, box, rate, lhs, coefs):
    groups = fine.shape[3] // BATCH
    blank = jnp.zeros((8, PF * PF), F32)
    for g in range(groups):
        slots = slice(g * BATCH, (g + 1) * BATCH)
        for c in range(6):
            for row in (0, ROWS_BOX - 8):
                lhs[c * ROWS_BOX + row : c * ROWS_BOX + row + 8, :] = blank
            for x, row in places():
                row += c * ROWS_BOX
                lhs[row : row + BATCH, :] = fine[0, 0, c, slots, x * PF * PF : (x + 1) * PF * PF]
            grown = move(lhs[c * ROWS_BOX : (c + 1) * ROWS_BOX, :], table[...])
            box[g, c] = grown
        for row in (0, ROWS_BOX - 8):
            coefs[row : row + 8, :] = blank
        for x, row in places():
            coefs[row : row + BATCH, :] = 0.5 / perm[0, 0, slots, x * PF * PF : (x + 1) * PF * PF]
        rate[g] = move(coefs[...], table[...])


def fine_kernel(ranks, *refs):
    regions, (box, rate, ghosts, means, out) = refs[:ranks], refs[ranks : ranks + 5]
    smalls = refs[ranks + 5 : 2 * ranks + 5]
    rims, walls, now, mag, halves, small = refs[2 * ranks + 5 :]
    groups = box.shape[0]
    rank = lax.axis_index("gy") * lax.axis_size("gz") + lax.axis_index("gz")
    flat = lane_iota((8, WIDE))
    yy = lax.shift_right_logical(flat * 3641, 16)
    zz = flat - yy * LINE
    inner = (yy >= 1) & (yy <= PF) & (zz >= 1) & (zz <= PF)
    upper = lax.broadcasted_iota(jnp.int32, (8, WIDE), 0) >= BATCH

    def inner_of(m):
        if m == 0:
            return inner & upper
        if m == PLANES - 1:
            return inner & jnp.logical_not(upper)
        return inner

    def up_y(a):
        return pltpu.roll(a, WIDE - LINE, 1)

    def up_z(a):
        return pltpu.roll(a, WIDE - 1, 1)

    def down_y(a):
        return pltpu.roll(a, LINE, 1)

    def down_z(a):
        return pltpu.roll(a, 1, 1)

    def rows_of(m):
        return pl.ds(m * 8, 8)

    blank = jnp.zeros((8, LANES), F32)
    for g in range(groups):
        for c in range(6):
            for m in range(PLANES):
                row = ((g * 6 + c) * PLANES + m) * 8
                if m in (0, PLANES - 1):
                    rims[row : row + 8, :] = blank
                walls[0, row : row + 8, :] = blank
                walls[1, row : row + 8, :] = blank
    for k, region in enumerate(regions):
        slot = lax.bitwise_xor(rank, k)
        start = (slot // BATCH) * 6 * ROWS_BOX + lax.rem(slot, BATCH)
        for c in range(6):
            rows = region[c * 8 : c * 8 + 8, :]
            row = start + c * ROWS_BOX
            rims[pl.ds(row + 8, 4, stride=16), :] = rows[0:4]
            rims[pl.ds(row + 16, 4, stride=16), :] = rows[0:4]
            rims[pl.ds(row + BATCH, 4, stride=16), :] = rows[4:8]
            rims[pl.ds(row + BATCH + 8, 4, stride=16), :] = rows[4:8]
        old = region[ROWS_RIM : ROWS_RIM + 8, :]
        fresh = region[ROWS_RIM + 8 : ROWS_RIM + 16, :]
        for sub, value in enumerate((old, old + 0.5 * (fresh - old))):
            walls[sub, pl.ds(start, 6, stride=ROWS_BOX), :] = value[0:6]
            last = start + ROWS_BOX + (PLANES - 1) * 8 + BATCH
            walls[sub, pl.ds(last, 2, stride=ROWS_BOX), :] = value[6:8]
    for g in range(groups):
        for sub in range(2):
            source = box if sub == 0 else out
            for c in range(6):
                rows = pl.ds((g * 6 + c) * ROWS_BOX, ROWS_BOX)
                ghost = move(jnp.concatenate([rims[rows, :], walls[sub, rows, :]], axis=1), ghosts[sub])
                for m in range(PLANES):
                    now[c, rows_of(m), :] = jnp.where(
                        inner_of(m), source[g, c, rows_of(m), :], ghost[m * 8 : (m + 1) * 8]
                    )

            def next_x(c, m):
                if m == PLANES - 1:
                    return pltpu.roll(now[c, rows_of(0), :], BATCH, 0)
                return now[c, rows_of(m + 1), :]

            def last_x(c, m):
                if m == 0:
                    return pltpu.roll(mag[c, rows_of(PLANES - 1), :], BATCH, 0)
                return mag[c, rows_of(m - 1), :]

            for m in range(PLANES):
                e0, e1, e2 = (now[c, rows_of(m), :] for c in range(3))
                h0, h1, h2 = (now[c, rows_of(m), :] for c in range(3, 6))
                mag[0, rows_of(m), :] = h0 - 0.5 * ((up_y(e2) - e2) - (up_z(e1) - e1))
                mag[1, rows_of(m), :] = h1 - 0.5 * ((up_z(e0) - e0) - (next_x(2, m) - e2))
                mag[2, rows_of(m), :] = h2 - 0.5 * ((next_x(1, m) - e1) - (up_y(e0) - e0))
            for m in range(PLANES):
                h0, h1, h2 = (mag[c, rows_of(m), :] for c in range(3))
                coef = rate[g, rows_of(m), :]
                e0, e1, e2 = (now[c, rows_of(m), :] for c in range(3))
                out[g, 0, rows_of(m), :] = e0 + coef * ((h2 - down_y(h2)) - (h1 - down_z(h1)))
                out[g, 1, rows_of(m), :] = e1 + coef * ((h0 - down_z(h0)) - (h2 - last_x(2, m)))
                out[g, 2, rows_of(m), :] = e2 + coef * ((h1 - last_x(1, m)) - (h0 - down_y(h0)))
                for c, value in enumerate((h0, h1, h2)):
                    out[g, c + 3, rows_of(m), :] = value
        for c in range(6):
            for k in range(4):
                other = jnp.where(upper, out[g, c, rows_of(2 * k), :], out[g, c, rows_of(2 * k + 2), :])
                pair = out[g, c, rows_of(2 * k + 1), :] + other
                halves[pl.ds((c * 2 + k // 2) * 8, 8), (k % 2) * WIDE : (k % 2 + 1) * WIDE] = pair
        small[pl.ds(g * 96, 96), :] = move(halves[...], means[...])
    for k, send in enumerate(smalls):
        slot = lax.bitwise_xor(rank, k)
        start = (slot // BATCH) * 96 + lax.rem(slot, BATCH)
        for xh in range(2):
            send[xh * 12 : (xh + 1) * 12, :] = small[pl.ds(start + xh * BATCH, 12, stride=8), :]


def store_kernel(box, fine, owners, table, out, stage, sems):
    groups = box.shape[0]
    slots = groups * BATCH
    rank = lax.axis_index("gy") * lax.axis_size("gz") + lax.axis_index("gz")
    slot = lax.broadcasted_iota(jnp.int32, (slots, PF * PF), 0)
    live = slot < 0
    for s in range(slots):
        live = live | ((slot == s) & ((owners[0, 0, s] == rank) | (owners[0, 1, s] == rank)))
    copies = []
    for c in range(6):
        flats = [move(box[g, c], table[...]) for g in range(groups)]
        for x, row in places():
            cut = slice(x * PF * PF, (x + 1) * PF * PF)
            for g, flat in enumerate(flats):
                some = slice(g * BATCH, (g + 1) * BATCH)
                stage[0, 0, c, some, cut] = jnp.where(live[some], flat[row : row + BATCH], fine[0, 0, c, some, cut])
        copies.append(pltpu.make_async_copy(stage.at[:, :, c], out.at[:, :, c], sems.at[c]))
        copies[-1].start()
    for copy in copies:
        copy.wait()


def fix_kernel(new, perm, *refs):
    edges, out = refs[:-1], refs[-1]
    deep, tall = new.shape[1], new.shape[2]
    gz = lax.axis_index("gz")
    rank = lax.axis_index("gy") * 2 + gz
    out[...] = new[...]

    def add(c, x, rows, amount):
        out[c, x, rows, :] = out[c, x, rows, :] + 0.25 / perm[x, rows, :] * amount

    lower = higher = jnp.zeros((1, LANES), F32)
    for k, edge in enumerate(edges, 1):
        row = ROW_EDGE
        lower = jnp.where(lax.bitwise_xor(rank, k) == rank - 2, edge[row : row + 1, :], lower)
        higher = jnp.where(lax.bitwise_xor(rank, k) == rank + 2, edge[row + 1 : row + 2, :], higher)
    add(0, deep - 1, slice(0, 1), lower)
    add(1, 0, slice(tall - 1, tall), higher)
    lane = lane_iota((tall, LANES))
    tile = edges[0][ROWS_PATCH : ROWS_PATCH + tall, :]
    add(0, deep - 1, slice(0, tall), jnp.where((lane == 0) & (gz == 1), pltpu.roll(tile, 1, 1), 0.0))
    add(2, 0, slice(0, tall), jnp.where((lane == LANES - 1) & (gz == 0), pltpu.roll(tile, LANES - 1, 1), 0.0))
    lane = lane_iota((deep, LANES))
    tile = edges[0][ROWS_PATCH + 16 : ROWS_PATCH + 16 + deep, :]
    first = jnp.where((lane == LANES - 1) & (gz == 0), pltpu.roll(tile, LANES - 1, 1), 0.0)
    last = jnp.where((lane == 0) & (gz == 1), pltpu.roll(tile, 1, 1), 0.0)
    for x in range(deep):
        add(2, x, slice(0, 1), first[x : x + 1])
        add(1, x, slice(tall - 1, tall), last[x : x + 1])


def place_kernel(ranks, new, corner, owners, *refs):
    means, (out, spread, stage, gathered, sems) = refs[:ranks], refs[ranks:]
    rank = lax.axis_index("gy") * lax.axis_size("gz") + lax.axis_index("gz")
    for k, mean in enumerate(means):
        gathered[k] = mean[...]
    lane = lane_iota((HALF, LANES))
    spots = [tuple(corner[0, 0, q, d] for d in range(3)) for q in range(PAR)]
    for q, (cx, cy, cz) in enumerate(spots):
        k = lax.bitwise_xor(owners[0, q, rank], rank)
        rows = gathered[k]
        for odd in range(2):
            for y in range(HALF):
                shift = lax.rem(cz - y * HALF - odd * HALF * HALF + 2 * LANES, LANES)
                spread[q, pl.ds(odd * 192 + y, 24, stride=8), :] = pltpu.roll(rows, shift, 1)
    copies = []
    for c in range(6):
        stage[c] = new[c]
        for q, (cx, cy, cz) in enumerate(spots):
            inside = (lane >= cz) & (lane < cz + HALF)
            for x in range(HALF):
                xh, k = x // 4, x % 4
                tile = spread[q, pl.ds((k % 2) * 192 + (xh * 12 + c * 2 + k // 2) * 8, 8), :]
                spot = stage[c, cx + x, pl.ds(cy, HALF), :]
                stage[c, cx + x, pl.ds(cy, HALF), :] = jnp.where(inside, tile, spot)
        copies.append(pltpu.make_async_copy(stage.at[c], out.at[c], sems.at[c]))
        copies[-1].start()
    for copy in copies:
        copy.wait()


def local(coarse_fields, permittivity, fine_fields, fine_permittivity, patch_corner, patch_owner):
    deep, tall, cols = coarse_fields.shape[1:]
    slots = fine_fields.shape[2]
    groups = slots // BATCH
    count_x, count_y = lax.axis_size("gx"), lax.axis_size("gy")
    two_y = count_y > 2
    smem = whole(pltpu.SMEM)
    vmem = whole()
    shape = jax.ShapeDtypeStruct
    grow = grow_table()

    beside = lax.ppermute(coarse_fields, "gz", swap_pairs(2, 0))
    x_face = shape((5, tall, cols), F32)
    y_face = shape((5, deep, cols), F32)
    faces = call(
        functools.partial(faces_kernel, two_y),
        [x_face, x_face, y_face] + [y_face] * two_y,
        [whole(pltpu.HBM)],
        [pltpu.SemaphoreType.DMA((6 + 2 * two_y,))],
    )(coarse_fields)
    got = [
        lax.ppermute(faces[0], "gx", swap_pairs(count_x, 0)),
        lax.ppermute(faces[1], "gx", swap_pairs(count_x, 1)),
        lax.ppermute(faces[2], "gy", swap_pairs(count_y, 0)),
    ]
    if two_y:
        got.append(lax.ppermute(faces[3], "gy", swap_pairs(count_y, 1)))

    fine = fine_fields.transpose(0, 1, 3, 2, 4)
    owners = patch_owner.transpose(0, 2, 1)
    box, rate = call(
        load_kernel,
        [shape((groups, 6, ROWS_BOX, WIDE), F32), shape((groups, ROWS_BOX, WIDE), F32)],
        [vmem] * 3,
        [pltpu.VMEM((6 * ROWS_BOX, PF * PF), F32), pltpu.VMEM((ROWS_BOX, PF * PF), F32)],
        size=4_000_000,
    )(fine, fine_permittivity, jnp.asarray(grow, BF16))

    full = deep + 2
    ranks = count_y * lax.axis_size("gz")

    def exchange(parts):
        swaps = [[(r, r ^ k) for r in range(ranks)] for k in range(ranks)]
        return [parts[0]] + [lax.ppermute(parts[k], ("gy", "gz"), swaps[k]) for k in range(1, ranks)]

    patches = [shape((ROWS_BESIDE if k == 1 else ROWS_PATCH, LANES), F32) for k in range(ranks)]
    new, *sends = call(
        functools.partial(leap_kernel, two_y, ranks),
        [shape(coarse_fields.shape, F32)] + patches,
        [vmem, vmem, whole(pltpu.HBM), smem, smem, whole(pl.ANY)] + [vmem] * len(got),
        [
            pltpu.VMEM((6 * full * 16, LANES), F32),
            pltpu.VMEM((6 * full * 16, LANES), F32),
            pltpu.VMEM((5 * (full - 1) * 16, LANES), F32),
            pltpu.VMEM(permittivity.shape, F32),
            pltpu.VMEM((6 * deep * 16, LANES), F32),
            pltpu.VMEM((PAR, ROWS_PATCH, LANES), F32),
            pltpu.SemaphoreType.DMA,
        ],
    )(coarse_fields, beside, permittivity, patch_corner, owners, rate, *got)
    regions = exchange(sends)

    box, *smalls = call(
        functools.partial(fine_kernel, ranks),
        [shape((groups, 6, ROWS_BOX, WIDE), F32)] + [shape((24, LANES), F32)] * ranks,
        [vmem] * (ranks + 4),
        [
            pltpu.VMEM((groups * 6 * ROWS_BOX, LANES), F32),
            pltpu.VMEM((2, groups * 6 * ROWS_BOX, LANES), F32),
            pltpu.VMEM((6, ROWS_BOX, WIDE), F32),
            pltpu.VMEM((3, ROWS_BOX, WIDE), F32),
            pltpu.VMEM((96, 2 * WIDE), F32),
            pltpu.VMEM((groups * 96, LANES), F32),
        ],
    )(*regions, box, rate, jnp.asarray(ghost_table(), BF16), jnp.asarray(mean_table(), BF16))
    means = exchange(smalls)

    fine = call(
        store_kernel,
        shape(fine.shape, F32),
        [vmem, vmem, smem, vmem],
        [pltpu.VMEM(fine.shape, F32), pltpu.SemaphoreType.DMA((6,))],
        size=4_000_000,
        out_specs=whole(pltpu.HBM),
    )(box, fine, owners, jnp.asarray(grow.T, BF16))
    new = call(fix_kernel, shape(coarse_fields.shape, F32), [vmem] * (1 + ranks))(new, permittivity, *regions[1:])
    coarse = call(
        functools.partial(place_kernel, ranks),
        shape(coarse_fields.shape, F32),
        [vmem, smem, smem] + [vmem] * ranks,
        [
            pltpu.VMEM((PAR, 4 * 96, LANES), F32),
            pltpu.VMEM(coarse_fields.shape, F32),
            pltpu.VMEM((ranks, 24, LANES), F32),
            pltpu.SemaphoreType.DMA((6,)),
        ],
        out_specs=whole(pltpu.HBM),
    )(new, patch_corner, owners, *means)
    return coarse, fine.transpose(0, 1, 3, 2, 4)


def solution(mesh):
    in_specs = (
        P(None, ("groups", "gx"), "gy", "gz"),
        P(("groups", "gx"), "gy", "gz"),
        P(("groups", "gx"), "gy", "gz", None, None),
        P(("groups", "gx"), "gy", "gz", None),
        P(("groups", "gx"), "gy", "gz", None),
        P(("groups", "gx"), None, None),
    )
    out_specs = (P(None, ("groups", "gx"), "gy", "gz"), P(("groups", "gx"), "gy", "gz", None, None))
    return jax.shard_map(local, mesh=mesh, in_specs=in_specs, out_specs=out_specs, check_vma=False)
```

time: 27.7 us -> 26.8 us (0.968)
  the two profiles are of different devices: /device:TPU:13 before, /device:TPU:9 now
where the time goes in v2:
time: 26.8 us; the launch traced here: 26.5 us
  starting transfers between devices  11.4 us (43%)
  Pallas kernels  7.12 us (27%)
  local copies, waits for them, and re-layouts  4.53 us (17%)
  waiting for transfers between devices  2.65 us (10%)
  between operations  0.78 us (3%)
    ppermute x6, starting transfers between devices, exchange(): lax.ppermute(parts[k], ('gy', 'gz'), swaps[k])  4.83 us
    unnamed x24, local copies, waits for them, and re-layouts  4.53 us
    ppermute x1, starting transfers between devices, local(): lax.ppermute(faces[1], 'gx', swap_pairs(count_x, 1))  4.48 us
    ppermute x6, waiting for transfers between devices, exchange(): lax.ppermute(parts[k], ('gy', 'gz'), swaps[k])  2.64 us
    pallas_call x1, Pallas kernels, local(): call(store_kernel, shape(fine.shape, F32), [vmem, vmem, smem, vmem], [plt...  1.82 us
    pallas_call x1, Pallas kernels, local(): call(functools.partial(place_kernel, ranks), shape(coarse_fields.shape, F...  1.54 us
    pallas_call x1, Pallas kernels, local(): call(functools.partial(leap_kernel, two_y, ranks), [shape(coarse_fields.s...  1.52 us
    pallas_call x1, Pallas kernels, local(): call(functools.partial(fine_kernel, ranks), [shape((groups, 6, ROWS_BOX,...  1.46 us
  transfers between devices with their start and end apart: 10, of which 3 were waited for; matrix products, arithmetic and copies ran while one was open for 0% of the time, Pallas kernels for 10%

profile of v2, /device:TPU:9, one launch (start us, length us, event | category | flops | bytes accessed | tf_op | source)
XLA Modules:
  0.0 26.5 jit_solution(8183896525864062947)
XLA Ops:
  0.6 0.7 %collective-permute-start = (f32[6,12,12,128]{3,2,1,0:T(8,128)}, f32[6,12,12,128]{3,2,1,0:T(8,128)S(1)}, u32[]{:S(2)}, u32[]{:S(2)}) collective-permute-start(f32[6,12,12,128]{3,2,1,0:T(8,128)} %refs_0_.1), channel_id=1, source_target_pairs={{0,1},{1,0},{2,3},{3,2},{4,5},{5,4},{6,7},{7,6},{8,9},{9,8},{10,11... | collective-permute-start | bytes 1327112 | tf_op jit(solution)/shard_map/ppermute | solution.py:494
  1.4 1.1 %copy-done = f32[6,12,12,128]{3,2,1,0:T(8,128)S(1)} copy-done((f32[6,12,12,128]{3,2,1,0:T(8,128)S(1)}, f32[6,12,12,128]{3,2,1,0:T(8,128)}, u32[]{:S(2)}) %copy-start) | copy-done | bytes 442392
  2.4 0.1 shard_map.114
  2.6 4.5 %collective-permute-start.2 = (f32[5,12,128]{2,1,0:T(8,128)S(1)}, f32[5,12,128]{2,1,0:T(8,128)S(1)}, u32[]{:S(2)}, u32[]{:S(2)}) collective-permute-start(f32[5,12,128]{2,1,0:T(8,128)S(1)} %get-tuple-element.19), channel_id=1, source_target_pairs={{4,8},{8,4},{5,9},{9,5},{6,10},{10,6},{7,11},{11,7},{20,24},{24,20... | collective-permute-start | bytes 92168 | tf_op jit(solution)/shard_map/ppermute | solution.py:505
  7.1 1.3 %collective-permute-start.3 = (f32[5,12,128]{2,1,0:T(8,128)S(1)}, f32[5,12,128]{2,1,0:T(8,128)S(1)}, u32[]{:S(2)}, u32[]{:S(2)}) collective-permute-start(f32[5,12,128]{2,1,0:T(8,128)S(1)} %get-tuple-element.20), channel_id=1, source_target_pairs={{0,2},{2,0},{1,3},{3,1},{4,6},{6,4},{5,7},{7,5},{8,10},{10,8},{9,1... | collective-permute-start | bytes 92168 | tf_op jit(solution)/shard_map/ppermute | solution.py:506
  8.4 1.0 %copy-done.2 = f32[1,1,4,6,4096]{4,2,3,1,0:T(4,128)S(1)} copy-done((f32[1,1,4,6,4096]{4,2,3,1,0:T(4,128)S(1)}, f32[1,1,4,6,4096]{4,2,3,1,0:T(4,128)}, u32[]{:S(2)}) %copy-start.2) | copy-done | bytes 393240
  9.4 0.9 %copy-done.7 = bf16[256,384]{1,0:T(8,128)(2,1)S(1)} copy-done((bf16[256,384]{1,0:T(8,128)(2,1)S(1)}, bf16[256,384]{1,0:T(8,128)(2,1)}, u32[]{:S(2)}) %copy-start.7) | copy-done | bytes 196632
  10.3 0.8 %copy-done.9 = f32[1,1,4,4096]{3,2,1,0:T(4,128)S(1)} copy-done((f32[1,1,4,4096]{3,2,1,0:T(4,128)S(1)}, f32[1,1,4,4096]{3,2,1,0:T(4,128)}, u32[]{:S(2)}) %copy-start.9) | copy-done | bytes 65560
  11.2 0.6 %shard_map.113 = (f32[1,6,72,384]{3,2,1,0:T(8,128)S(1)}, f32[1,72,384]{2,1,0:T(8,128)S(1)}) custom-call(f32[1,1,6,4,4096]{4,3,2,1,0:T(4,128)S(1)} %bitcast.3, f32[1,1,4,4096]{3,2,1,0:T(4,128)S(1)} %copy-done.9, bf16[256,384]{1,0:T(8,128)(2,1)S(1)} %copy-done.7), custom_call_target="tpu_custom_call" | custom-call | flops 1000000 | bytes 4000000 | tf_op jit(solution)/shard_map/pallas_call | solution.py:513
  11.8 0.2 copy-done.5
  12.0 0.4 %copy-done.10 = s32[1,4,2]{1,2,0:T(2,128)S(1)} copy-done((s32[1,4,2]{1,2,0:T(2,128)S(1)}, s32[1,4,2]{1,2,0:T(2,128)}, u32[]{:S(2)}) %copy-start.10) | copy-done | bytes 56
  12.5 1.5 %shard_map.115 = (f32[6,12,12,128]{3,2,1,0:T(8,128)S(1)}, f32[72,128]{1,0:T(8,128)S(1)}, f32[104,128]{1,0:T(8,128)S(1)}, f32[72,128]{1,0:T(8,128)S(1)}, f32[72,128]{1,0:T(8,128)S(1)}) custom-call(f32[6,12,12,128]{3,2,1,0:T(8,128)S(1)} %copy-done.1, f32[6,12,12,128]{3,2,1,0:T(8,128)S(1)} %collective-permute-done.refs_1_, f32[12,12,128]{2,1,0:T(8,128)S(1)} %copy-done.5, ...), custom_call_target="tpu_custom_call" | custom-call | flops 1000000 | bytes 1000000 | tf_op jit(solution)/shard_map/pallas_call | solution.py:529
  14.0 0.9 %collective-permute-start.4 = (f32[104,128]{1,0:T(8,128)S(1)}, f32[104,128]{1,0:T(8,128)S(1)}, u32[]{:S(2)}, u32[]{:S(2)}) collective-permute-start(f32[104,128]{1,0:T(8,128)S(1)} %get-tuple-element.22), channel_id=1, source_target_pairs={{0,1},{1,0},{2,3},{3,2},{4,5},{5,4},{6,7},{7,6},{8,9},{9,8},{10,11... | collective-permute-start | bytes 159752 | tf_op jit(solution)/shard_map/ppermute | solution.py:526
  14.9 0.3 %collective-permute-start.5 = (f32[72,128]{1,0:T(8,128)S(1)}, f32[72,128]{1,0:T(8,128)S(1)}, u32[]{:S(2)}, u32[]{:S(2)}) collective-permute-start(f32[72,128]{1,0:T(8,128)S(1)} %get-tuple-element.23), channel_id=1, source_target_pairs={{0,2},{1,3},{2,0},{3,1},{4,6},{5,7},{6,4},{7,5},{8,10},{9,11},{10,... | collective-permute-start | bytes 110600 | tf_op jit(solution)/shard_map/ppermute | solution.py:526
  15.3 1.4 %collective-permute-start.6 = (f32[72,128]{1,0:T(8,128)S(1)}, f32[72,128]{1,0:T(8,128)S(1)}, u32[]{:S(2)}, u32[]{:S(2)}) collective-permute-start(f32[72,128]{1,0:T(8,128)S(1)} %get-tuple-element.24), channel_id=1, source_target_pairs={{0,3},{1,2},{2,1},{3,0},{4,7},{5,6},{6,5},{7,4},{8,11},{9,10},{10,... | collective-permute-start | bytes 110600 | tf_op jit(solution)/shard_map/ppermute | solution.py:526
  16.7 1.1 %collective-permute-done.5.refs_1_.refs_2_ = f32[72,128]{1,0:T(8,128)S(1)} collective-permute-done((f32[72,128]{1,0:T(8,128)S(1)}, f32[72,128]{1,0:T(8,128)S(1)}, u32[]{:S(2)}, u32[]{:S(2)}) %collective-permute-start.5) | collective-permute-done | bytes 36896 | tf_op jit(solution)/shard_map/ppermute | solution.py:526
  17.8 1.3 %collective-permute-done.6.refs_2_.refs_3_ = f32[72,128]{1,0:T(8,128)S(1)} collective-permute-done((f32[72,128]{1,0:T(8,128)S(1)}, f32[72,128]{1,0:T(8,128)S(1)}, u32[]{:S(2)}, u32[]{:S(2)}) %collective-permute-start.6) | collective-permute-done | bytes 36896 | tf_op jit(solution)/shard_map/ppermute | solution.py:526
  19.1 1.5 %shard_map.117 = (f32[1,6,72,384]{3,2,1,0:T(8,128)S(1)}, f32[24,128]{1,0:T(8,128)S(1)}, f32[24,128]{1,0:T(8,128)S(1)}, f32[24,128]{1,0:T(8,128)S(1)}, f32[24,128]{1,0:T(8,128)S(1)}) custom-call(f32[72,128]{1,0:T(8,128)S(1)} %get-tuple-element.25.refs_0_, f32[104,128]{1,0:T(8,128)S(1)} %collective-permute-done.4.refs_0_.refs_1_, ...), custom_call_target="tpu_custom_call" | custom-call | flops 1000000 | bytes 1000000 | tf_op jit(solution)/shard_map/pallas_call | solution.py:545
  20.6 0.4 %collective-permute-start.7 = (f32[24,128]{1,0:T(8,128)S(1)}, f32[24,128]{1,0:T(8,128)S(1)}, u32[]{:S(2)}, u32[]{:S(2)}) collective-permute-start(f32[24,128]{1,0:T(8,128)S(1)} %get-tuple-element.28), channel_id=1, source_target_pairs={{0,1},{1,0},{2,3},{3,2},{4,5},{5,4},{6,7},{7,6},{8,9},{9,8},{10,11... | collective-permute-start | bytes 36872 | tf_op jit(solution)/shard_map/ppermute | solution.py:526
  21.0 0.8 %collective-permute-start.8 = (f32[24,128]{1,0:T(8,128)S(1)}, f32[24,128]{1,0:T(8,128)S(1)}, u32[]{:S(2)}, u32[]{:S(2)}) collective-permute-start(f32[24,128]{1,0:T(8,128)S(1)} %get-tuple-element.29), channel_id=1, source_target_pairs={{0,2},{1,3},{2,0},{3,1},{4,6},{5,7},{6,4},{7,5},{8,10},{9,11},{10,... | collective-permute-start | bytes 36872 | tf_op jit(solution)/shard_map/ppermute | solution.py:526
  21.8 1.0 %collective-permute-start.9 = (f32[24,128]{1,0:T(8,128)S(1)}, f32[24,128]{1,0:T(8,128)S(1)}, u32[]{:S(2)}, u32[]{:S(2)}) collective-permute-start(f32[24,128]{1,0:T(8,128)S(1)} %get-tuple-element.30), channel_id=1, source_target_pairs={{0,3},{1,2},{2,1},{3,0},{4,7},{5,6},{6,5},{7,4},{8,11},{9,10},{10,... | collective-permute-start | bytes 36872 | tf_op jit(solution)/shard_map/ppermute | solution.py:526
  22.8 1.8 %shard_map.119 = f32[1,1,6,4,4096]{4,3,2,1,0:T(4,128)} custom-call(f32[1,6,72,384]{3,2,1,0:T(8,128)S(1)} %get-tuple-element.31.box, f32[1,1,6,4,4096]{4,3,2,1,0:T(4,128)S(1)} %bitcast.4, s32[1,2,4]{2,1,0:T(2,128)S(1)} %bitcast.6, bf16[384,256]{1,0:T(8,128)(2,1)S(1)} %copy-done.8), custom_call_target="tpu_custom_call" | custom-call | flops 1000000 | bytes 4000000 | tf_op jit(solution)/shard_map/pallas_call | solution.py:560
  24.7 0.2 collective-permute-done.9.refs_3_
  24.9 1.5 %shard_map.118 = f32[6,12,12,128]{3,2,1,0:T(8,128)} custom-call(f32[6,12,12,128]{3,2,1,0:T(8,128)S(1)} %shard_map.116.new, s32[1,1,2,3]{3,2,1,0:T(2,128)S(1)} %copy-done.11, s32[1,2,4]{2,1,0:T(2,128)S(1)} %bitcast.7, f32[24,128]{1,0:T(8,128)S(1)} %get-tuple-element.27.refs_0_, f32[24,128]{1,0:T(8,128)S(1)} %collective-permute-done.7.refs_1_, ...), custom_call_target="tpu_custom_call" | custom-call | flops 1000000 | bytes 1000000 | tf_op jit(solution)/shard_map/pallas_call | solution.py:569
  (27 shorter events, 0.2 us)
Async XLA Ops:
  0.6 11.2 %collective-permute-start = (f32[6,12,12,128]{3,2,1,0:T(8,128)}, f32[6,12,12,128]{3,2,1,0:T(8,128)S(1)}, u32[]{:S(2)}, u32[]{:S(2)}) collective-permute-start(f32[6,12,12,128]{3,2,1,0:T(8,128)} %refs_0_.1), channel_id=1, source_target_pairs={{0,1},{1,0},{2,3},{3,2},{4,5},{5,4},{6,7},{7,6},{8,9},{9,8},{10,11... | collective-permute-start | bytes 1327112 | tf_op jit(solution)/shard_map/ppermute | solution.py:494
  1.4 1.1 %copy-start = (f32[6,12,12,128]{3,2,1,0:T(8,128)S(1)}, f32[6,12,12,128]{3,2,1,0:T(8,128)}, u32[]{:S(2)}) copy-start(f32[6,12,12,128]{3,2,1,0:T(8,128)} %refs_0_.1) | copy-start | bytes 1327108
  2.4 9.4 %copy-start.1 = (f32[6,12,12,128]{3,2,1,0:T(8,128)S(1)}, f32[6,12,12,128]{3,2,1,0:T(8,128)}, u32[]{:S(2)}) copy-start(f32[6,12,12,128]{3,2,1,0:T(8,128)} %refs_0_.1) | copy-start | bytes 1327108
  2.5 9.2 %collective-permute-start.1 = (f32[5,12,128]{2,1,0:T(8,128)S(1)}, f32[5,12,128]{2,1,0:T(8,128)S(1)}, u32[]{:S(2)}, u32[]{:S(2)}) collective-permute-start(f32[5,12,128]{2,1,0:T(8,128)S(1)} %get-tuple-element.18), channel_id=1, source_target_pairs={{0,4},{4,0},{8,12},{12,8},{1,5},{5,1},{9,13},{13,9},{2,6},{6,2},{1... | collective-permute-start | bytes 92168 | tf_op jit(solution)/shard_map/ppermute | solution.py:504
  2.6 9.1 %collective-permute-start.2 = (f32[5,12,128]{2,1,0:T(8,128)S(1)}, f32[5,12,128]{2,1,0:T(8,128)S(1)}, u32[]{:S(2)}, u32[]{:S(2)}) collective-permute-start(f32[5,12,128]{2,1,0:T(8,128)S(1)} %get-tuple-element.19), channel_id=1, source_target_pairs={{4,8},{8,4},{5,9},{9,5},{6,10},{10,6},{7,11},{11,7},{20,24},{24,20... | collective-permute-start | bytes 92168 | tf_op jit(solution)/shard_map/ppermute | solution.py:505
  7.1 4.7 %collective-permute-start.3 = (f32[5,12,128]{2,1,0:T(8,128)S(1)}, f32[5,12,128]{2,1,0:T(8,128)S(1)}, u32[]{:S(2)}, u32[]{:S(2)}) collective-permute-start(f32[5,12,128]{2,1,0:T(8,128)S(1)} %get-tuple-element.20), channel_id=1, source_target_pairs={{0,2},{2,0},{1,3},{3,1},{4,6},{6,4},{5,7},{7,5},{8,10},{10,8},{9,1... | collective-permute-start | bytes 92168 | tf_op jit(solution)/shard_map/ppermute | solution.py:506
  8.4 1.0 %copy-start.2 = (f32[1,1,4,6,4096]{4,2,3,1,0:T(4,128)S(1)}, f32[1,1,4,6,4096]{4,2,3,1,0:T(4,128)}, u32[]{:S(2)}) copy-start(f32[1,1,4,6,4096]{4,2,3,1,0:T(4,128)} %param.12) | copy-start | bytes 1179652
  9.4 0.9 %copy-start.7 = (bf16[256,384]{1,0:T(8,128)(2,1)S(1)}, bf16[256,384]{1,0:T(8,128)(2,1)}, u32[]{:S(2)}) copy-start(bf16[256,384]{1,0:T(8,128)(2,1)} %constant.8.clone.table) | copy-start | bytes 589828
  10.3 0.8 %copy-start.9 = (f32[1,1,4,4096]{3,2,1,0:T(4,128)S(1)}, f32[1,1,4,4096]{3,2,1,0:T(4,128)}, u32[]{:S(2)}) copy-start(f32[1,1,4,4096]{3,2,1,0:T(4,128)} %perm.2) | copy-start | bytes 196612
  11.2 0.9 %copy-start.5 = (f32[12,12,128]{2,1,0:T(8,128)S(1)}, f32[12,12,128]{2,1,0:T(8,128)}, u32[]{:S(2)}) copy-start(f32[12,12,128]{2,1,0:T(8,128)} %perm.3) | copy-start | bytes 221188
  11.2 0.9 %copy-start.11 = (s32[1,1,2,3]{3,2,1,0:T(2,128)S(1)}, s32[1,1,2,3]{3,2,1,0:T(2,128)}, u32[]{:S(2)}) copy-start(s32[1,1,2,3]{3,2,1,0:T(2,128)} %corner.1) | copy-start | bytes 76
  11.8 0.7 %copy-start.10 = (s32[1,4,2]{1,2,0:T(2,128)S(1)}, s32[1,4,2]{1,2,0:T(2,128)}, u32[]{:S(2)}) copy-start(s32[1,4,2]{1,2,0:T(2,128)} %param.15) | copy-start | bytes 100
  12.5 6.6 %copy-start.4 = (bf16[2,256,384]{2,1,0:T(8,128)(2,1)S(1)}, bf16[2,256,384]{2,1,0:T(8,128)(2,1)}, u32[]{:S(2)}) copy-start(bf16[2,256,384]{2,1,0:T(8,128)(2,1)} %constant.9.clone.refs_6_) | copy-start | bytes 1179652
  12.5 6.6 %copy-start.6 = (bf16[768,128]{1,0:T(8,128)(2,1)S(1)}, bf16[768,128]{1,0:T(8,128)(2,1)}, u32[]{:S(2)}) copy-start(bf16[768,128]{1,0:T(8,128)(2,1)} %constant.10.clone.refs_7_) | copy-start | bytes 589828
  14.0 5.1 %collective-permute-start.4 = (f32[104,128]{1,0:T(8,128)S(1)}, f32[104,128]{1,0:T(8,128)S(1)}, u32[]{:S(2)}, u32[]{:S(2)}) collective-permute-start(f32[104,128]{1,0:T(8,128)S(1)} %get-tuple-element.22), channel_id=1, source_target_pairs={{0,1},{1,0},{2,3},{3,2},{4,5},{5,4},{6,7},{7,6},{8,9},{9,8},{10,11... | collective-permute-start | bytes 159752 | tf_op jit(solution)/shard_map/ppermute | solution.py:526
  14.9 2.8 %collective-permute-start.5 = (f32[72,128]{1,0:T(8,128)S(1)}, f32[72,128]{1,0:T(8,128)S(1)}, u32[]{:S(2)}, u32[]{:S(2)}) collective-permute-start(f32[72,128]{1,0:T(8,128)S(1)} %get-tuple-element.23), channel_id=1, source_target_pairs={{0,2},{1,3},{2,0},{3,1},{4,6},{5,7},{6,4},{7,5},{8,10},{9,11},{10,... | collective-permute-start | bytes 110600 | tf_op jit(solution)/shard_map/ppermute | solution.py:526
  15.3 3.8 %collective-permute-start.6 = (f32[72,128]{1,0:T(8,128)S(1)}, f32[72,128]{1,0:T(8,128)S(1)}, u32[]{:S(2)}, u32[]{:S(2)}) collective-permute-start(f32[72,128]{1,0:T(8,128)S(1)} %get-tuple-element.24), channel_id=1, source_target_pairs={{0,3},{1,2},{2,1},{3,0},{4,7},{5,6},{6,5},{7,4},{8,11},{9,10},{10,... | collective-permute-start | bytes 110600 | tf_op jit(solution)/shard_map/ppermute | solution.py:526
  19.1 3.7 %copy-start.3 = (f32[1,1,4,6,4096]{4,2,3,1,0:T(4,128)S(1)}, f32[1,1,4,6,4096]{4,2,3,1,0:T(4,128)}, u32[]{:S(2)}) copy-start(f32[1,1,4,6,4096]{4,2,3,1,0:T(4,128)} %param.12) | copy-start | bytes 1179652
  19.1 3.7 %copy-start.8 = (bf16[384,256]{1,0:T(8,128)(2,1)S(1)}, bf16[384,256]{1,0:T(8,128)(2,1)}, u32[]{:S(2)}) copy-start(bf16[384,256]{1,0:T(8,128)(2,1)} %constant.11.clone.table) | copy-start | bytes 589828
  20.6 4.1 %collective-permute-start.7 = (f32[24,128]{1,0:T(8,128)S(1)}, f32[24,128]{1,0:T(8,128)S(1)}, u32[]{:S(2)}, u32[]{:S(2)}) collective-permute-start(f32[24,128]{1,0:T(8,128)S(1)} %get-tuple-element.28), channel_id=1, source_target_pairs={{0,1},{1,0},{2,3},{3,2},{4,5},{5,4},{6,7},{7,6},{8,9},{9,8},{10,11... | collective-permute-start | bytes 36872 | tf_op jit(solution)/shard_map/ppermute | solution.py:526
  21.0 3.8 %collective-permute-start.8 = (f32[24,128]{1,0:T(8,128)S(1)}, f32[24,128]{1,0:T(8,128)S(1)}, u32[]{:S(2)}, u32[]{:S(2)}) collective-permute-start(f32[24,128]{1,0:T(8,128)S(1)} %get-tuple-element.29), channel_id=1, source_target_pairs={{0,2},{1,3},{2,0},{3,1},{4,6},{5,7},{6,4},{7,5},{8,10},{9,11},{10,... | collective-permute-start | bytes 36872 | tf_op jit(solution)/shard_map/ppermute | solution.py:526
  21.8 3.2 %collective-permute-start.9 = (f32[24,128]{1,0:T(8,128)S(1)}, f32[24,128]{1,0:T(8,128)S(1)}, u32[]{:S(2)}, u32[]{:S(2)}) collective-permute-start(f32[24,128]{1,0:T(8,128)S(1)} %get-tuple-element.30), channel_id=1, source_target_pairs={{0,3},{1,2},{2,1},{3,0},{4,7},{5,6},{6,5},{7,4},{8,11},{9,10},{10,... | collective-permute-start | bytes 36872 | tf_op jit(solution)/shard_map/ppermute | solution.py:526

commit v3 on v2

--- a/solution.py
+++ b/solution.py
@@ -102,41 +102,53 @@
     return pairs
 
 
-def faces_kernel(two_y, block, *refs):
-    outs, sems = refs[:-1], refs[-1]
+def faces_kernel(two_y, block, perm, kept, coef, x_even, x_odd, y_even, *y_odd):
     deep, tall = block.shape[1], block.shape[2]
     gx_odd = lax.rem(lax.axis_index("gx"), 2)
     gy_odd = lax.rem(lax.axis_index("gy"), 2)
-    copies = []
-    for n, place in enumerate(((1 - gx_odd) * (deep - 1), gx_odd * (deep - 1))):
-        for low, high, k in ((0, 3, 0), (4, 6, 3)):
-            source = block.at[low:high, place]
-            copies.append((source, outs[n].at[k : k + high - low]))
-    for n, place in enumerate(((1 - gy_odd) * (tall - 1), gy_odd * (tall - 1))[: 1 + two_y]):
-        for low, high, k in ((0, 4, 0), (5, 6, 4)):
-            source = block.at[low:high, :, place]
-            copies.append((source, outs[2 + n].at[k : k + high - low]))
-    copies = [pltpu.make_async_copy(a, b, sems.at[i]) for i, (a, b) in enumerate(copies)]
-    for copy in copies:
-        copy.start()
-    for copy in copies:
-        copy.wait()
+    for k, c in enumerate(X_COMPS):
+        x_even[k] = block[c, (1 - gx_odd) * (deep - 1)]
+        x_odd[k] = block[c, gx_odd * (deep - 1)]
+    for k, c in enumerate(Y_COMPS):
+        for x in range(deep):
+            first = block[c, x, 0:1, :]
+            last = block[c, x, tall - 1 : tall, :]
+            y_even[k, x : x + 1, :] = jnp.where(gy_odd == 0, last, first)
+            if two_y:
+                y_odd[0][k, x : x + 1, :] = jnp.where(gy_odd == 0, first, last)
+    kept[...] = block[...]
+    coef[...] = 0.5 / perm[...]
+
+
+def notes_kernel(corner, owners, notes):
+    rank = lax.axis_index("gy") * lax.axis_size("gz") + lax.axis_index("gz")
+
+    def note(row, value):
+        notes[row : row + 1, :] = jnp.full((1, LANES), value, jnp.int32)
+
+    for q in range(PAR):
+        for d in range(3):
+            note(q * 4 + d, corner[0, 0, q, d])
+        note(q * 4 + 3, lax.bitwise_xor(owners[0, q, rank], rank))
+    for slot in range(notes.shape[0] - 8):
+        live = (owners[0, 0, slot] == rank) | (owners[0, 1, slot] == rank)
+        note(8 + slot, live.astype(jnp.int32))
 
 
 def leap_kernel(two_y, ranks, *refs):
-    block, beside, perm, corner, owners, ahead, x_even, x_odd, y_even = refs[:9]
-    y_odd = refs[9] if two_y else None
-    refs = refs[9 + two_y :]
+    block, beside, rate, notes, x_even, x_odd, y_even = refs[:7]
+    y_odd = refs[7] if two_y else None
+    refs = refs[7 + two_y :]
     new, sends = refs[0], refs[1 : 1 + ranks]
-    pad, side, mag, rate, fresh, packed, sem = refs[1 + ranks :]
+    pad, side, mag, fresh, packed = refs[1 + ranks :]
     deep, tall = block.shape[1], block.shape[2]
     full = deep + 2
-    fetch = pltpu.make_async_copy(perm, rate, sem)
-    fetch.start()
     gx_odd = lax.rem(lax.axis_index("gx"), 2)
     gy_odd = lax.rem(lax.axis_index("gy"), 2)
     gz = lax.axis_index("gz")
-    rank = lax.axis_index("gy") * lax.axis_size("gz") + gz
+    noted = notes[0:8, :]
+    spots = [[noted[q * 4 + d, 0] for d in range(3)] for q in range(PAR)]
+    chosen = noted[3, 0]
     lane = lane_iota((tall, LANES))
     keep = ((lane == 0) & (gz == 0)) | ((lane == LANES - 1) & (gz == 1))
     lane = lane_iota((16, LANES))
@@ -200,10 +212,9 @@
         d1 = pltpu.roll(jnp.where(lane == LANES - 1, t1, h1), 1, 1)
         for c, value in enumerate((h0, h1, h2, d0, d1)):
             mag[pl.ds((c * (full - 1) + x) * 16, 16), :] = value
-    fetch.wait()
     for x in range(deep):
         h0, h1, h2, d0, d1 = (field(c, x + 1) for c in range(5))
-        coef = 0.5 / rate[x]
+        coef = rate[x]
         c0 = (h2 - down_y(h2)) - (h1 - d1)
         c1 = (h0 - d0) - (h2 - field(2, x))
         c2 = (h1 - field(1, x)) - (h0 - down_y(h0))
@@ -215,7 +226,7 @@
             fresh[pl.ds(((c + 3) * deep + x) * 16, tall), :] = (h0, h1, h2)[c][0:tall]
     lane = lane_iota((8, LANES))
     for q in range(PAR):
-        cx, cy, cz = corner[0, 0, q, 0], corner[0, 0, q, 1], corner[0, 0, q, 2]
+        cx, cy, cz = spots[q]
 
         def rows_of(time, c, k, j, count, over_c):
             source, depth, start = (pad, full, cx) if time == 0 else (fresh, deep, cx - 1)
@@ -254,7 +265,7 @@
         packed[q, ROW_EDGE : ROW_EDGE + 1, :] = pad[pl.ds(at(1, full - 1) + tall - 1, 1), :]
         packed[q, ROW_EDGE + 1 : ROW_EDGE + 2, :] = pad[pl.ds(at(0, 0), 1), :]
     for k, send in enumerate(sends):
-        q = jnp.where(owners[0, 0, rank] == lax.bitwise_xor(rank, k), 0, 1)
+        q = jnp.where(chosen == k, 0, 1)
         send[0:ROWS_PATCH, :] = packed[q]
     half = lane_iota((16, LANES)) < LANES // 2
     send = sends[1]
@@ -398,14 +409,10 @@
             send[xh * 12 : (xh + 1) * 12, :] = small[pl.ds(start + xh * BATCH, 12, stride=8), :]
 
 
-def store_kernel(box, fine, owners, table, out, stage, sems):
+def store_kernel(box, fine, notes, table, out, stage, sems):
     groups = box.shape[0]
     slots = groups * BATCH
-    rank = lax.axis_index("gy") * lax.axis_size("gz") + lax.axis_index("gz")
-    slot = lax.broadcasted_iota(jnp.int32, (slots, PF * PF), 0)
-    live = slot < 0
-    for s in range(slots):
-        live = live | ((slot == s) & ((owners[0, 0, s] == rank) | (owners[0, 1, s] == rank)))
+    live = jnp.concatenate([notes[8 : 8 + slots, :]] * (PF * PF // LANES), axis=1) > 0
     copies = []
     for c in range(6):
         flats = [move(box[g, c], table[...]) for g in range(groups)]
@@ -420,7 +427,7 @@
         copy.wait()
 
 
-def fix_kernel(new, perm, *refs):
+def fix_kernel(new, rate, *refs):
     edges, out = refs[:-1], refs[-1]
     deep, tall = new.shape[1], new.shape[2]
     gz = lax.axis_index("gz")
@@ -428,7 +435,7 @@
     out[...] = new[...]
 
     def add(c, x, rows, amount):
-        out[c, x, rows, :] = out[c, x, rows, :] + 0.25 / perm[x, rows, :] * amount
+        out[c, x, rows, :] = out[c, x, rows, :] + 0.5 * rate[x, rows, :] * amount
 
     lower = higher = jnp.zeros((1, LANES), F32)
     for k, edge in enumerate(edges, 1):
@@ -450,15 +457,15 @@
         add(1, x, slice(tall - 1, tall), last[x : x + 1])
 
 
-def place_kernel(ranks, new, corner, owners, *refs):
+def place_kernel(ranks, new, notes, *refs):
     means, (out, spread, stage, gathered, sems) = refs[:ranks], refs[ranks:]
-    rank = lax.axis_index("gy") * lax.axis_size("gz") + lax.axis_index("gz")
+    noted = notes[0:8, :]
     for k, mean in enumerate(means):
         gathered[k] = mean[...]
     lane = lane_iota((HALF, LANES))
-    spots = [tuple(corner[0, 0, q, d] for d in range(3)) for q in range(PAR)]
+    spots = [tuple(noted[q * 4 + d, 0] for d in range(3)) for q in range(PAR)]
     for q, (cx, cy, cz) in enumerate(spots):
-        k = lax.bitwise_xor(owners[0, q, rank], rank)
+        k = noted[q * 4 + 3, 0]
         rows = gathered[k]
         for odd in range(2):
             for y in range(HALF):
@@ -486,20 +493,17 @@
     groups = slots // BATCH
     count_x, count_y = lax.axis_size("gx"), lax.axis_size("gy")
     two_y = count_y > 2
-    smem = whole(pltpu.SMEM)
     vmem = whole()
     shape = jax.ShapeDtypeStruct
     grow = grow_table()
 
-    beside = lax.ppermute(coarse_fields, "gz", swap_pairs(2, 0))
     x_face = shape((5, tall, cols), F32)
     y_face = shape((5, deep, cols), F32)
-    faces = call(
+    kept, rate, *faces = call(
         functools.partial(faces_kernel, two_y),
-        [x_face, x_face, y_face] + [y_face] * two_y,
-        [whole(pltpu.HBM)],
-        [pltpu.SemaphoreType.DMA((6 + 2 * two_y,))],
-    )(coarse_fields)
+        [shape(coarse_fields.shape, F32), shape(permittivity.shape, F32), x_face, x_face, y_face] + [y_face] * two_y,
+        [vmem, vmem],
+    )(coarse_fields, permittivity)
     got = [
         lax.ppermute(faces[0], "gx", swap_pairs(count_x, 0)),
         lax.ppermute(faces[1], "gx", swap_pairs(count_x, 1)),
@@ -507,10 +511,15 @@
     ]
     if two_y:
         got.append(lax.ppermute(faces[3], "gy", swap_pairs(count_y, 1)))
+    beside = lax.ppermute(kept, "gz", swap_pairs(2, 0))
 
     fine = fine_fields.transpose(0, 1, 3, 2, 4)
-    owners = patch_owner.transpose(0, 2, 1)
-    box, rate = call(
+    notes = call(
+        notes_kernel,
+        shape((8 + slots, LANES), jnp.int32),
+        [whole(pltpu.SMEM)] * 2,
+    )(patch_corner, patch_owner.transpose(0, 2, 1))
+    box, fine_rate = call(
         load_kernel,
         [shape((groups, 6, ROWS_BOX, WIDE), F32), shape((groups, ROWS_BOX, WIDE), F32)],
         [vmem] * 3,
@@ -529,17 +538,15 @@
     new, *sends = call(
         functools.partial(leap_kernel, two_y, ranks),
         [shape(coarse_fields.shape, F32)] + patches,
-        [vmem, vmem, whole(pltpu.HBM), smem, smem, whole(pl.ANY)] + [vmem] * len(got),
+        [vmem] * (4 + len(got)),
         [
             pltpu.VMEM((6 * full * 16, LANES), F32),
             pltpu.VMEM((6 * full * 16, LANES), F32),
             pltpu.VMEM((5 * (full - 1) * 16, LANES), F32),
-            pltpu.VMEM(permittivity.shape, F32),
             pltpu.VMEM((6 * deep * 16, LANES), F32),
             pltpu.VMEM((PAR, ROWS_PATCH, LANES), F32),
-            pltpu.SemaphoreType.DMA,
         ],
-    )(coarse_fields, beside, permittivity, patch_corner, owners, rate, *got)
+    )(kept, beside, rate, notes, *got)
     regions = exchange(sends)
 
     box, *smalls = call(
@@ -554,22 +561,22 @@
             pltpu.VMEM((96, 2 * WIDE), F32),
             pltpu.VMEM((groups * 96, LANES), F32),
         ],
-    )(*regions, box, rate, jnp.asarray(ghost_table(), BF16), jnp.asarray(mean_table(), BF16))
+    )(*regions, box, fine_rate, jnp.asarray(ghost_table(), BF16), jnp.asarray(mean_table(), BF16))
     means = exchange(smalls)
 
     fine = call(
         store_kernel,
         shape(fine.shape, F32),
-        [vmem, vmem, smem, vmem],
+        [vmem] * 4,
         [pltpu.VMEM(fine.shape, F32), pltpu.SemaphoreType.DMA((6,))],
         size=4_000_000,
         out_specs=whole(pltpu.HBM),
-    )(box, fine, owners, jnp.asarray(grow.T, BF16))
-    new = call(fix_kernel, shape(coarse_fields.shape, F32), [vmem] * (1 + ranks))(new, permittivity, *regions[1:])
+    )(box, fine, notes, jnp.asarray(grow.T, BF16))
+    new = call(fix_kernel, shape(coarse_fields.shape, F32), [vmem] * (1 + ranks))(new, rate, *regions[1:])
     coarse = call(
         functools.partial(place_kernel, ranks),
         shape(coarse_fields.shape, F32),
-        [vmem, smem, smem] + [vmem] * ranks,
+        [vmem] * (2 + ranks),
         [
             pltpu.VMEM((PAR, 4 * 96, LANES), F32),
             pltpu.VMEM(coarse_fields.shape, F32),
@@ -577,7 +584,7 @@
             pltpu.SemaphoreType.DMA((6,)),
         ],
         out_specs=whole(pltpu.HBM),
-    )(new, patch_corner, owners, *means)
+    )(new, notes, *means)
     return coarse, fine.transpose(0, 1, 3, 2, 4)
 
 

time: 26.8 us -> 25.5 us (0.951)
  the two profiles are of different devices: /device:TPU:9 before, /device:TPU:13 now
where the time goes in v3:
time: 25.5 us; the launch traced here: 25.3 us
  starting transfers between devices  12.3 us (48%)
  Pallas kernels  6.25 us (25%)
  waiting for transfers between devices  4 us (16%)
  local copies, waits for them, and re-layouts  1.99 us (8%)
  between operations  0.77 us (3%)
    ppermute x6, starting transfers between devices, exchange(): lax.ppermute(parts[k], ('gy', 'gz'), swaps[k])  5.76 us
    ppermute x1, starting transfers between devices, local(): lax.ppermute(faces[1], 'gx', swap_pairs(count_x, 1))  4.32 us
    ppermute x6, waiting for transfers between devices, exchange(): lax.ppermute(parts[k], ('gy', 'gz'), swaps[k])  2.97 us
    unnamed x20, local copies, waits for them, and re-layouts  1.99 us
    pallas_call x1, Pallas kernels, local(): call(functools.partial(fine_kernel, ranks), [shape((groups, 6, ROWS_BOX,...  1.48 us
    pallas_call x1, Pallas kernels, local(): call(store_kernel, shape(fine.shape, F32), [vmem] * 4, [pltpu.VMEM(fine.s...  1.28 us
    ppermute x1, starting transfers between devices, local(): lax.ppermute(faces[2], 'gy', swap_pairs(count_y, 0))  1.28 us
    pallas_call x1, Pallas kernels, local(): call(functools.partial(leap_kernel, two_y, ranks), [shape(coarse_fields.s...  1.13 us
  transfers between devices with their start and end apart: 10, of which 4 were waited for; matrix products, arithmetic and copies ran while one was open for 0% of the time, Pallas kernels for 10%

profile of v3, /device:TPU:13, one launch (start us, length us, event | category | flops | bytes accessed | tf_op | source)
XLA Modules:
  0.0 25.3 jit_solution(15869984679629852493)
XLA Ops:
  0.6 1.1 %copy-done.1 = f32[6,12,12,128]{3,2,1,0:T(8,128)S(1)} copy-done((f32[6,12,12,128]{3,2,1,0:T(8,128)S(1)}, f32[6,12,12,128]{3,2,1,0:T(8,128)}, u32[]{:S(2)}) %copy-start.1) | copy-done | bytes 442392
  1.7 0.9 %copy-done.6 = f32[12,12,128]{2,1,0:T(8,128)S(1)} copy-done((f32[12,12,128]{2,1,0:T(8,128)S(1)}, f32[12,12,128]{2,1,0:T(8,128)}, u32[]{:S(2)}) %copy-start.6) | copy-done | bytes 73752
  2.6 0.1 shard_map.113
  2.7 0.7 %collective-permute-start = (f32[6,12,12,128]{3,2,1,0:T(8,128)S(1)}, f32[6,12,12,128]{3,2,1,0:T(8,128)S(1)}, u32[]{:S(2)}, u32[]{:S(2)}) collective-permute-start(f32[6,12,12,128]{3,2,1,0:T(8,128)S(1)} %get-tuple-element.19.refs_0_), channel_id=1, source_target_pairs={{0,1},{1,0},{2,3},{3,2},{4,5},{5,4},{6,7},{7,6},{8,9},{9,8},{10,11... | collective-permute-start | bytes 1327112 | tf_op jit(solution)/shard_map/ppermute | solution.py:514
  3.4 0.2 collective-permute-start.1
  3.6 4.3 %collective-permute-start.2 = (f32[5,12,128]{2,1,0:T(8,128)S(1)}, f32[5,12,128]{2,1,0:T(8,128)S(1)}, u32[]{:S(2)}, u32[]{:S(2)}) collective-permute-start(f32[5,12,128]{2,1,0:T(8,128)S(1)} %get-tuple-element.22), channel_id=1, source_target_pairs={{4,8},{8,4},{5,9},{9,5},{6,10},{10,6},{7,11},{11,7},{20,24},{24,20... | collective-permute-start | bytes 92168 | tf_op jit(solution)/shard_map/ppermute | solution.py:509
  8.0 1.3 %collective-permute-start.3 = (f32[5,12,128]{2,1,0:T(8,128)S(1)}, f32[5,12,128]{2,1,0:T(8,128)S(1)}, u32[]{:S(2)}, u32[]{:S(2)}) collective-permute-start(f32[5,12,128]{2,1,0:T(8,128)S(1)} %get-tuple-element.23), channel_id=1, source_target_pairs={{0,2},{2,0},{1,3},{3,1},{4,6},{6,4},{5,7},{7,5},{8,10},{10,8},{9,1... | collective-permute-start | bytes 92168 | tf_op jit(solution)/shard_map/ppermute | solution.py:510
  9.2 0.6 %shard_map.114.refs_3_.notes = s32[12,128]{1,0:T(8,128)S(1)} custom-call(s32[1,1,2,3]{3,2,1,0:T(2,128)S(1)} %copy-done.8, s32[1,2,4]{2,1,0:T(2,128)S(1)} %bitcast.5), custom_call_target="tpu_custom_call" | custom-call | flops 1000000 | bytes 1000000 | tf_op jit(solution)/shard_map/pallas_call | solution.py:517
  9.9 1.0 %collective-permute-done.3.refs_6_ = f32[5,12,128]{2,1,0:T(8,128)S(1)} collective-permute-done((f32[5,12,128]{2,1,0:T(8,128)S(1)}, f32[5,12,128]{2,1,0:T(8,128)S(1)}, u32[]{:S(2)}, u32[]{:S(2)}) %collective-permute-start.3) | collective-permute-done | bytes 30752 | tf_op jit(solution)/shard_map/ppermute | solution.py:510
  10.9 1.1 %shard_map.115 = (f32[6,12,12,128]{3,2,1,0:T(8,128)S(1)}, f32[72,128]{1,0:T(8,128)S(1)}, f32[104,128]{1,0:T(8,128)S(1)}, f32[72,128]{1,0:T(8,128)S(1)}, f32[72,128]{1,0:T(8,128)S(1)}) custom-call(f32[6,12,12,128]{3,2,1,0:T(8,128)S(1)} %get-tuple-element.19.refs_0_, f32[6,12,12,128]{3,2,1,0:T(8,128)S(1)} %collective-permute-done.refs_1_, ...), custom_call_target="tpu_custom_call" | custom-call | flops 1000000 | bytes 1000000 | tf_op jit(solution)/shard_map/pallas_call | solution.py:538
  12.0 1.8 %collective-permute-start.4 = (f32[104,128]{1,0:T(8,128)S(1)}, f32[104,128]{1,0:T(8,128)S(1)}, u32[]{:S(2)}, u32[]{:S(2)}) collective-permute-start(f32[104,128]{1,0:T(8,128)S(1)} %get-tuple-element.25), channel_id=1, source_target_pairs={{0,1},{1,0},{2,3},{3,2},{4,5},{5,4},{6,7},{7,6},{8,9},{9,8},{10,11... | collective-permute-start | bytes 159752 | tf_op jit(solution)/shard_map/ppermute | solution.py:535
  13.9 1.2 %collective-permute-start.5 = (f32[72,128]{1,0:T(8,128)S(1)}, f32[72,128]{1,0:T(8,128)S(1)}, u32[]{:S(2)}, u32[]{:S(2)}) collective-permute-start(f32[72,128]{1,0:T(8,128)S(1)} %get-tuple-element.26), channel_id=1, source_target_pairs={{0,2},{1,3},{2,0},{3,1},{4,6},{5,7},{6,4},{7,5},{8,10},{9,11},{10,... | collective-permute-start | bytes 110600 | tf_op jit(solution)/shard_map/ppermute | solution.py:535
  15.1 0.5 %collective-permute-start.6 = (f32[72,128]{1,0:T(8,128)S(1)}, f32[72,128]{1,0:T(8,128)S(1)}, u32[]{:S(2)}, u32[]{:S(2)}) collective-permute-start(f32[72,128]{1,0:T(8,128)S(1)} %get-tuple-element.27), channel_id=1, source_target_pairs={{0,3},{1,2},{2,1},{3,0},{4,7},{5,6},{6,5},{7,4},{8,11},{9,10},{10,... | collective-permute-start | bytes 110600 | tf_op jit(solution)/shard_map/ppermute | solution.py:535
  15.6 0.6 %shard_map.117 = (f32[1,6,72,384]{3,2,1,0:T(8,128)S(1)}, f32[1,72,384]{2,1,0:T(8,128)S(1)}) custom-call(f32[1,1,6,4,4096]{4,3,2,1,0:T(4,128)S(1)} %bitcast.3, f32[1,1,4,4096]{3,2,1,0:T(4,128)S(1)} %copy-done.7, bf16[256,384]{1,0:T(8,128)(2,1)S(1)} %copy-done.5), custom_call_target="tpu_custom_call" | custom-call | flops 1000000 | bytes 4000000 | tf_op jit(solution)/shard_map/pallas_call | solution.py:522
  16.2 0.5 %collective-permute-done.5.refs_1_.refs_2_ = f32[72,128]{1,0:T(8,128)S(1)} collective-permute-done((f32[72,128]{1,0:T(8,128)S(1)}, f32[72,128]{1,0:T(8,128)S(1)}, u32[]{:S(2)}, u32[]{:S(2)}) %collective-permute-start.5) | collective-permute-done | bytes 36896 | tf_op jit(solution)/shard_map/ppermute | solution.py:535
  16.7 1.8 %collective-permute-done.6.refs_2_.refs_3_ = f32[72,128]{1,0:T(8,128)S(1)} collective-permute-done((f32[72,128]{1,0:T(8,128)S(1)}, f32[72,128]{1,0:T(8,128)S(1)}, u32[]{:S(2)}, u32[]{:S(2)}) %collective-permute-start.6) | collective-permute-done | bytes 36896 | tf_op jit(solution)/shard_map/ppermute | solution.py:535
  18.6 1.5 %shard_map.118 = (f32[1,6,72,384]{3,2,1,0:T(8,128)S(1)}, f32[24,128]{1,0:T(8,128)S(1)}, f32[24,128]{1,0:T(8,128)S(1)}, f32[24,128]{1,0:T(8,128)S(1)}, f32[24,128]{1,0:T(8,128)S(1)}) custom-call(f32[72,128]{1,0:T(8,128)S(1)} %get-tuple-element.28.refs_0_, f32[104,128]{1,0:T(8,128)S(1)} %collective-permute-done.4.refs_0_.refs_1_, ...), custom_call_target="tpu_custom_call" | custom-call | flops 1000000 | bytes 1000000 | tf_op jit(solution)/shard_map/pallas_call | solution.py:552
  20.1 0.4 %collective-permute-start.7 = (f32[24,128]{1,0:T(8,128)S(1)}, f32[24,128]{1,0:T(8,128)S(1)}, u32[]{:S(2)}, u32[]{:S(2)}) collective-permute-start(f32[24,128]{1,0:T(8,128)S(1)} %get-tuple-element.32), channel_id=1, source_target_pairs={{0,1},{1,0},{2,3},{3,2},{4,5},{5,4},{6,7},{7,6},{8,9},{9,8},{10,11... | collective-permute-start | bytes 36872 | tf_op jit(solution)/shard_map/ppermute | solution.py:535
  20.5 0.6 %collective-permute-start.8 = (f32[24,128]{1,0:T(8,128)S(1)}, f32[24,128]{1,0:T(8,128)S(1)}, u32[]{:S(2)}, u32[]{:S(2)}) collective-permute-start(f32[24,128]{1,0:T(8,128)S(1)} %get-tuple-element.33), channel_id=1, source_target_pairs={{0,2},{1,3},{2,0},{3,1},{4,6},{5,7},{6,4},{7,5},{8,10},{9,11},{10,... | collective-permute-start | bytes 36872 | tf_op jit(solution)/shard_map/ppermute | solution.py:535
  21.1 1.2 %collective-permute-start.9 = (f32[24,128]{1,0:T(8,128)S(1)}, f32[24,128]{1,0:T(8,128)S(1)}, u32[]{:S(2)}, u32[]{:S(2)}) collective-permute-start(f32[24,128]{1,0:T(8,128)S(1)} %get-tuple-element.34), channel_id=1, source_target_pairs={{0,3},{1,2},{2,1},{3,0},{4,7},{5,6},{6,5},{7,4},{8,11},{9,10},{10,... | collective-permute-start | bytes 36872 | tf_op jit(solution)/shard_map/ppermute | solution.py:535
  22.3 1.3 %shard_map.120 = f32[1,1,6,4,4096]{4,3,2,1,0:T(4,128)} custom-call(f32[1,6,72,384]{3,2,1,0:T(8,128)S(1)} %get-tuple-element.35.box, f32[1,1,6,4,4096]{4,3,2,1,0:T(4,128)S(1)} %bitcast.4, s32[12,128]{1,0:T(8,128)S(1)} %shard_map.114.refs_3_.notes, bf16[384,256]{1,0:T(8,128)(2,1)S(1)} %copy-done.3), custom_call_target="tpu_custom_call" | custom-call | flops 1000000 | bytes 4000000 | tf_op jit(solution)/shard_map/pallas_call | solution.py:567
  23.6 0.1 shard_map.116.new
  23.7 0.6 %collective-permute-done.9.refs_3_ = f32[24,128]{1,0:T(8,128)S(1)} collective-permute-done((f32[24,128]{1,0:T(8,128)S(1)}, f32[24,128]{1,0:T(8,128)S(1)}, u32[]{:S(2)}, u32[]{:S(2)}) %collective-permute-start.9) | collective-permute-done | bytes 12320 | tf_op jit(solution)/shard_map/ppermute | solution.py:535
  24.3 1.0 %shard_map.119 = f32[6,12,12,128]{3,2,1,0:T(8,128)} custom-call(f32[6,12,12,128]{3,2,1,0:T(8,128)S(1)} %shard_map.116.new, s32[12,128]{1,0:T(8,128)S(1)} %shard_map.114.refs_3_.notes, f32[24,128]{1,0:T(8,128)S(1)} %get-tuple-element.31.refs_0_, f32[24,128]{1,0:T(8,128)S(1)} %collective-permute-done.7.refs_1_, f32[24,128]{1,0:T(8,128)S(1)} %collective-permute-done.8.refs_2_, ...), custom_call_target="tpu_custom_call" | custom-call | flops 1000000 | bytes 1000000 | tf_op jit(solution)/shard_map/pallas_call | solution.py:576
  (24 shorter events, 0.1 us)
Async XLA Ops:
  0.6 1.1 %copy-start.1 = (f32[6,12,12,128]{3,2,1,0:T(8,128)S(1)}, f32[6,12,12,128]{3,2,1,0:T(8,128)}, u32[]{:S(2)}) copy-start(f32[6,12,12,128]{3,2,1,0:T(8,128)} %block.1) | copy-start | bytes 1327108
  1.7 0.9 %copy-start.6 = (f32[12,12,128]{2,1,0:T(8,128)S(1)}, f32[12,12,128]{2,1,0:T(8,128)}, u32[]{:S(2)}) copy-start(f32[12,12,128]{2,1,0:T(8,128)} %perm.2) | copy-start | bytes 221188
  2.7 8.2 %collective-permute-start = (f32[6,12,12,128]{3,2,1,0:T(8,128)S(1)}, f32[6,12,12,128]{3,2,1,0:T(8,128)S(1)}, u32[]{:S(2)}, u32[]{:S(2)}) collective-permute-start(f32[6,12,12,128]{3,2,1,0:T(8,128)S(1)} %get-tuple-element.19.refs_0_), channel_id=1, source_target_pairs={{0,1},{1,0},{2,3},{3,2},{4,5},{5,4},{6,7},{7,6},{8,9},{9,8},{10,11... | collective-permute-start | bytes 1327112 | tf_op jit(solution)/shard_map/ppermute | solution.py:514
  3.4 6.4 %collective-permute-start.1 = (f32[5,12,128]{2,1,0:T(8,128)S(1)}, f32[5,12,128]{2,1,0:T(8,128)S(1)}, u32[]{:S(2)}, u32[]{:S(2)}) collective-permute-start(f32[5,12,128]{2,1,0:T(8,128)S(1)} %get-tuple-element.21), channel_id=1, source_target_pairs={{0,4},{4,0},{8,12},{12,8},{1,5},{5,1},{9,13},{13,9},{2,6},{6,2},{1... | collective-permute-start | bytes 92168 | tf_op jit(solution)/shard_map/ppermute | solution.py:508
  3.6 6.2 %collective-permute-start.2 = (f32[5,12,128]{2,1,0:T(8,128)S(1)}, f32[5,12,128]{2,1,0:T(8,128)S(1)}, u32[]{:S(2)}, u32[]{:S(2)}) collective-permute-start(f32[5,12,128]{2,1,0:T(8,128)S(1)} %get-tuple-element.22), channel_id=1, source_target_pairs={{4,8},{8,4},{5,9},{9,5},{6,10},{10,6},{7,11},{11,7},{20,24},{24,20... | collective-permute-start | bytes 92168 | tf_op jit(solution)/shard_map/ppermute | solution.py:509
  7.9 1.3 %copy-start.9 = (s32[1,4,2]{1,2,0:T(2,128)S(1)}, s32[1,4,2]{1,2,0:T(2,128)}, u32[]{:S(2)}) copy-start(s32[1,4,2]{1,2,0:T(2,128)} %param.15) | copy-start | bytes 100
  8.0 1.3 %copy-start.8 = (s32[1,1,2,3]{3,2,1,0:T(2,128)S(1)}, s32[1,1,2,3]{3,2,1,0:T(2,128)}, u32[]{:S(2)}) copy-start(s32[1,1,2,3]{3,2,1,0:T(2,128)} %corner.1) | copy-start | bytes 76
  8.0 2.9 %collective-permute-start.3 = (f32[5,12,128]{2,1,0:T(8,128)S(1)}, f32[5,12,128]{2,1,0:T(8,128)S(1)}, u32[]{:S(2)}, u32[]{:S(2)}) collective-permute-start(f32[5,12,128]{2,1,0:T(8,128)S(1)} %get-tuple-element.23), channel_id=1, source_target_pairs={{0,2},{2,0},{1,3},{3,1},{4,6},{6,4},{5,7},{7,5},{8,10},{10,8},{9,1... | collective-permute-start | bytes 92168 | tf_op jit(solution)/shard_map/ppermute | solution.py:510
  10.9 4.7 %copy-start = (f32[1,1,4,6,4096]{4,2,3,1,0:T(4,128)S(1)}, f32[1,1,4,6,4096]{4,2,3,1,0:T(4,128)}, u32[]{:S(2)}) copy-start(f32[1,1,4,6,4096]{4,2,3,1,0:T(4,128)} %param.12) | copy-start | bytes 1179652
  10.9 4.7 %copy-start.5 = (bf16[256,384]{1,0:T(8,128)(2,1)S(1)}, bf16[256,384]{1,0:T(8,128)(2,1)}, u32[]{:S(2)}) copy-start(bf16[256,384]{1,0:T(8,128)(2,1)} %constant.8.clone.table) | copy-start | bytes 589828
  10.9 4.7 %copy-start.7 = (f32[1,1,4,4096]{3,2,1,0:T(4,128)S(1)}, f32[1,1,4,4096]{3,2,1,0:T(4,128)}, u32[]{:S(2)}) copy-start(f32[1,1,4,4096]{3,2,1,0:T(4,128)} %perm.3) | copy-start | bytes 196612
  12.0 6.5 %copy-start.2 = (bf16[2,256,384]{2,1,0:T(8,128)(2,1)S(1)}, bf16[2,256,384]{2,1,0:T(8,128)(2,1)}, u32[]{:S(2)}) copy-start(bf16[2,256,384]{2,1,0:T(8,128)(2,1)} %constant.9.clone.refs_6_) | copy-start | bytes 1179652
  12.0 6.5 %collective-permute-start.4 = (f32[104,128]{1,0:T(8,128)S(1)}, f32[104,128]{1,0:T(8,128)S(1)}, u32[]{:S(2)}, u32[]{:S(2)}) collective-permute-start(f32[104,128]{1,0:T(8,128)S(1)} %get-tuple-element.25), channel_id=1, source_target_pairs={{0,1},{1,0},{2,3},{3,2},{4,5},{5,4},{6,7},{7,6},{8,9},{9,8},{10,11... | collective-permute-start | bytes 159752 | tf_op jit(solution)/shard_map/ppermute | solution.py:535
  13.9 2.8 %collective-permute-start.5 = (f32[72,128]{1,0:T(8,128)S(1)}, f32[72,128]{1,0:T(8,128)S(1)}, u32[]{:S(2)}, u32[]{:S(2)}) collective-permute-start(f32[72,128]{1,0:T(8,128)S(1)} %get-tuple-element.26), channel_id=1, source_target_pairs={{0,2},{1,3},{2,0},{3,1},{4,6},{5,7},{6,4},{7,5},{8,10},{9,11},{10,... | collective-permute-start | bytes 110600 | tf_op jit(solution)/shard_map/ppermute | solution.py:535
  15.1 3.4 %collective-permute-start.6 = (f32[72,128]{1,0:T(8,128)S(1)}, f32[72,128]{1,0:T(8,128)S(1)}, u32[]{:S(2)}, u32[]{:S(2)}) collective-permute-start(f32[72,128]{1,0:T(8,128)S(1)} %get-tuple-element.27), channel_id=1, source_target_pairs={{0,3},{1,2},{2,1},{3,0},{4,7},{5,6},{6,5},{7,4},{8,11},{9,10},{10,... | collective-permute-start | bytes 110600 | tf_op jit(solution)/shard_map/ppermute | solution.py:535
  15.6 2.9 %copy-start.4 = (bf16[768,128]{1,0:T(8,128)(2,1)S(1)}, bf16[768,128]{1,0:T(8,128)(2,1)}, u32[]{:S(2)}) copy-start(bf16[768,128]{1,0:T(8,128)(2,1)} %constant.10.clone.refs_7_) | copy-start | bytes 589828
  18.6 3.7 %copy-start.3 = (bf16[384,256]{1,0:T(8,128)(2,1)S(1)}, bf16[384,256]{1,0:T(8,128)(2,1)}, u32[]{:S(2)}) copy-start(bf16[384,256]{1,0:T(8,128)(2,1)} %constant.11.clone.table) | copy-start | bytes 589828
  20.1 3.6 %collective-permute-start.7 = (f32[24,128]{1,0:T(8,128)S(1)}, f32[24,128]{1,0:T(8,128)S(1)}, u32[]{:S(2)}, u32[]{:S(2)}) collective-permute-start(f32[24,128]{1,0:T(8,128)S(1)} %get-tuple-element.32), channel_id=1, source_target_pairs={{0,1},{1,0},{2,3},{3,2},{4,5},{5,4},{6,7},{7,6},{8,9},{9,8},{10,11... | collective-permute-start | bytes 36872 | tf_op jit(solution)/shard_map/ppermute | solution.py:535
  20.5 3.2 %collective-permute-start.8 = (f32[24,128]{1,0:T(8,128)S(1)}, f32[24,128]{1,0:T(8,128)S(1)}, u32[]{:S(2)}, u32[]{:S(2)}) collective-permute-start(f32[24,128]{1,0:T(8,128)S(1)} %get-tuple-element.33), channel_id=1, source_target_pairs={{0,2},{1,3},{2,0},{3,1},{4,6},{5,7},{6,4},{7,5},{8,10},{9,11},{10,... | collective-permute-start | bytes 36872 | tf_op jit(solution)/shard_map/ppermute | solution.py:535
  21.1 3.2 %collective-permute-start.9 = (f32[24,128]{1,0:T(8,128)S(1)}, f32[24,128]{1,0:T(8,128)S(1)}, u32[]{:S(2)}, u32[]{:S(2)}) collective-permute-start(f32[24,128]{1,0:T(8,128)S(1)} %get-tuple-element.34), channel_id=1, source_target_pairs={{0,3},{1,2},{2,1},{3,0},{4,7},{5,6},{6,5},{7,4},{8,11},{9,10},{10,... | collective-permute-start | bytes 36872 | tf_op jit(solution)/shard_map/ppermute | solution.py:535

commit v4 on v3

--- a/solution.py
+++ b/solution.py
@@ -102,7 +102,7 @@
     return pairs
 
 
-def faces_kernel(two_y, block, perm, kept, coef, x_even, x_odd, y_even, *y_odd):
+def faces_kernel(two_y, block, kept, x_even, x_odd, y_even, *y_odd):
     deep, tall = block.shape[1], block.shape[2]
     gx_odd = lax.rem(lax.axis_index("gx"), 2)
     gy_odd = lax.rem(lax.axis_index("gy"), 2)
@@ -117,10 +117,9 @@
             if two_y:
                 y_odd[0][k, x : x + 1, :] = jnp.where(gy_odd == 0, first, last)
     kept[...] = block[...]
-    coef[...] = 0.5 / perm[...]
-
-
-def notes_kernel(corner, owners, notes):
+
+
+def notes_kernel(corner, owners, perm, notes, rate):
     rank = lax.axis_index("gy") * lax.axis_size("gz") + lax.axis_index("gz")
 
     def note(row, value):
@@ -133,6 +132,7 @@
     for slot in range(notes.shape[0] - 8):
         live = (owners[0, 0, slot] == rank) | (owners[0, 1, slot] == rank)
         note(8 + slot, live.astype(jnp.int32))
+    rate[...] = 0.5 / perm[...]
 
 
 def leap_kernel(two_y, ranks, *refs):
@@ -499,11 +499,11 @@
 
     x_face = shape((5, tall, cols), F32)
     y_face = shape((5, deep, cols), F32)
-    kept, rate, *faces = call(
+    kept, *faces = call(
         functools.partial(faces_kernel, two_y),
-        [shape(coarse_fields.shape, F32), shape(permittivity.shape, F32), x_face, x_face, y_face] + [y_face] * two_y,
-        [vmem, vmem],
-    )(coarse_fields, permittivity)
+        [shape(coarse_fields.shape, F32), x_face, x_face, y_face] + [y_face] * two_y,
+        [vmem],
+    )(coarse_fields)
     got = [
         lax.ppermute(faces[0], "gx", swap_pairs(count_x, 0)),
         lax.ppermute(faces[1], "gx", swap_pairs(count_x, 1)),
@@ -514,11 +514,11 @@
     beside = lax.ppermute(kept, "gz", swap_pairs(2, 0))
 
     fine = fine_fields.transpose(0, 1, 3, 2, 4)
-    notes = call(
+    notes, rate = call(
         notes_kernel,
-        shape((8 + slots, LANES), jnp.int32),
-        [whole(pltpu.SMEM)] * 2,
-    )(patch_corner, patch_owner.transpose(0, 2, 1))
+        [shape((8 + slots, LANES), jnp.int32), shape(permittivity.shape, F32)],
+        [whole(pltpu.SMEM)] * 2 + [vmem],
+    )(patch_corner, patch_owner.transpose(0, 2, 1), permittivity)
     box, fine_rate = call(
         load_kernel,
         [shape((groups, 6, ROWS_BOX, WIDE), F32), shape((groups, ROWS_BOX, WIDE), F32)],
@@ -532,7 +532,10 @@
 
     def exchange(parts):
         swaps = [[(r, r ^ k) for r in range(ranks)] for k in range(ranks)]
-        return [parts[0]] + [lax.ppermute(parts[k], ("gy", "gz"), swaps[k]) for k in range(1, ranks)]
+        got = list(parts)
+        for k in [*range(2, ranks), 1]:
+            got[k] = lax.ppermute(parts[k], ("gy", "gz"), swaps[k])
+        return got
 
     patches = [shape((ROWS_BESIDE if k == 1 else ROWS_PATCH, LANES), F32) for k in range(ranks)]
     new, *sends = call(

time: 25.5 us -> 24.6 us (0.965)
  the two profiles are of different devices: /device:TPU:13 before, /device:TPU:9 now
where the time goes in v4:
time: 24.6 us; the launch traced here: 24.4 us
  starting transfers between devices  12.3 us (50%)
  Pallas kernels  6.24 us (25%)
  waiting for transfers between devices  4 us (16%)
  local copies, waits for them, and re-layouts  1.1 us (4%)
  between operations  0.77 us (3%)
    ppermute x6, starting transfers between devices, exchange(): got[k] = lax.ppermute(parts[k], ('gy', 'gz'), swaps[k])  5.76 us
    ppermute x1, starting transfers between devices, local(): lax.ppermute(faces[1], 'gx', swap_pairs(count_x, 1))  4.5 us
    ppermute x6, waiting for transfers between devices, exchange(): got[k] = lax.ppermute(parts[k], ('gy', 'gz'), swaps[k])  2.96 us
    pallas_call x1, Pallas kernels, local(): call(functools.partial(fine_kernel, ranks), [shape((groups, 6, ROWS_BOX,...  1.48 us
    pallas_call x1, Pallas kernels, local(): call(store_kernel, shape(fine.shape, F32), [vmem] * 4, [pltpu.VMEM(fine.s...  1.28 us
    ppermute x1, starting transfers between devices, local(): lax.ppermute(faces[2], 'gy', swap_pairs(count_y, 0))  1.28 us
    pallas_call x1, Pallas kernels, local(): call(functools.partial(leap_kernel, two_y, ranks), [shape(coarse_fields.s...  1.14 us
    unnamed x20, local copies, waits for them, and re-layouts  1.1 us
  transfers between devices with their start and end apart: 10, of which 4 were waited for; matrix products, arithmetic and copies ran while one was open for 0% of the time, Pallas kernels for 10%

profile of v4, /device:TPU:9, one launch (start us, length us, event | category | flops | bytes accessed | tf_op | source)
XLA Modules:
  0.0 24.4 jit_solution(17793918534645492925)
XLA Ops:
  0.6 1.1 %copy-done.1 = f32[6,12,12,128]{3,2,1,0:T(8,128)S(1)} copy-done((f32[6,12,12,128]{3,2,1,0:T(8,128)S(1)}, f32[6,12,12,128]{3,2,1,0:T(8,128)}, u32[]{:S(2)}) %copy-start.1) | copy-done | bytes 442392
  1.7 0.1 shard_map.113
  1.8 0.7 %collective-permute-start = (f32[6,12,12,128]{3,2,1,0:T(8,128)S(1)}, f32[6,12,12,128]{3,2,1,0:T(8,128)S(1)}, u32[]{:S(2)}, u32[]{:S(2)}) collective-permute-start(f32[6,12,12,128]{3,2,1,0:T(8,128)S(1)} %get-tuple-element.20.refs_0_), channel_id=1, source_target_pairs={{0,1},{1,0},{2,3},{3,2},{4,5},{5,4},{6,7},{7,6},{8,9},{9,8},{10,11... | collective-permute-start | bytes 1327112 | tf_op jit(solution)/shard_map/ppermute | solution.py:514
  2.5 4.5 %collective-permute-start.2 = (f32[5,12,128]{2,1,0:T(8,128)S(1)}, f32[5,12,128]{2,1,0:T(8,128)S(1)}, u32[]{:S(2)}, u32[]{:S(2)}) collective-permute-start(f32[5,12,128]{2,1,0:T(8,128)S(1)} %get-tuple-element.24), channel_id=1, source_target_pairs={{4,8},{8,4},{5,9},{9,5},{6,10},{10,6},{7,11},{11,7},{20,24},{24,20... | collective-permute-start | bytes 92168 | tf_op jit(solution)/shard_map/ppermute | solution.py:509
  7.0 0.0 copy-start.8
  7.1 1.3 %collective-permute-start.3 = (f32[5,12,128]{2,1,0:T(8,128)S(1)}, f32[5,12,128]{2,1,0:T(8,128)S(1)}, u32[]{:S(2)}, u32[]{:S(2)}) collective-permute-start(f32[5,12,128]{2,1,0:T(8,128)S(1)} %get-tuple-element.25), channel_id=1, source_target_pairs={{0,2},{2,0},{1,3},{3,1},{4,6},{6,4},{5,7},{7,5},{8,10},{10,8},{9,1... | collective-permute-start | bytes 92168 | tf_op jit(solution)/shard_map/ppermute | solution.py:510
  8.3 0.6 %shard_map.114 = (s32[12,128]{1,0:T(8,128)S(1)}, f32[12,12,128]{2,1,0:T(8,128)S(1)}) custom-call(s32[1,1,2,3]{3,2,1,0:T(2,128)S(1)} %copy-done.8, s32[1,2,4]{2,1,0:T(2,128)S(1)} %bitcast.5, f32[12,12,128]{2,1,0:T(8,128)S(1)} %copy-done.6), custom_call_target="tpu_custom_call" | custom-call | flops 1000000 | bytes 1000000 | tf_op jit(solution)/shard_map/pallas_call | solution.py:517
  9.0 1.0 %collective-permute-done.3.refs_6_ = f32[5,12,128]{2,1,0:T(8,128)S(1)} collective-permute-done((f32[5,12,128]{2,1,0:T(8,128)S(1)}, f32[5,12,128]{2,1,0:T(8,128)S(1)}, u32[]{:S(2)}, u32[]{:S(2)}) %collective-permute-start.3) | collective-permute-done | bytes 30752 | tf_op jit(solution)/shard_map/ppermute | solution.py:510
  10.0 1.1 %shard_map.115 = (f32[6,12,12,128]{3,2,1,0:T(8,128)S(1)}, f32[72,128]{1,0:T(8,128)S(1)}, f32[104,128]{1,0:T(8,128)S(1)}, f32[72,128]{1,0:T(8,128)S(1)}, f32[72,128]{1,0:T(8,128)S(1)}) custom-call(f32[6,12,12,128]{3,2,1,0:T(8,128)S(1)} %get-tuple-element.20.refs_0_, f32[6,12,12,128]{3,2,1,0:T(8,128)S(1)} %collective-permute-done.refs_1_, ...), custom_call_target="tpu_custom_call" | custom-call | flops 1000000 | bytes 1000000 | tf_op jit(solution)/shard_map/pallas_call | solution.py:541
  11.1 1.8 %collective-permute-start.4 = (f32[104,128]{1,0:T(8,128)S(1)}, f32[104,128]{1,0:T(8,128)S(1)}, u32[]{:S(2)}, u32[]{:S(2)}) collective-permute-start(f32[104,128]{1,0:T(8,128)S(1)} %get-tuple-element.27), channel_id=1, source_target_pairs={{0,1},{1,0},{2,3},{3,2},{4,5},{5,4},{6,7},{7,6},{8,9},{9,8},{10,11... | collective-permute-start | bytes 159752 | tf_op jit(solution)/shard_map/ppermute | solution.py:537
  13.0 1.2 %collective-permute-start.5 = (f32[72,128]{1,0:T(8,128)S(1)}, f32[72,128]{1,0:T(8,128)S(1)}, u32[]{:S(2)}, u32[]{:S(2)}) collective-permute-start(f32[72,128]{1,0:T(8,128)S(1)} %get-tuple-element.28), channel_id=1, source_target_pairs={{0,2},{1,3},{2,0},{3,1},{4,6},{5,7},{6,4},{7,5},{8,10},{9,11},{10,... | collective-permute-start | bytes 110600 | tf_op jit(solution)/shard_map/ppermute | solution.py:537
  14.2 0.5 %collective-permute-start.6 = (f32[72,128]{1,0:T(8,128)S(1)}, f32[72,128]{1,0:T(8,128)S(1)}, u32[]{:S(2)}, u32[]{:S(2)}) collective-permute-start(f32[72,128]{1,0:T(8,128)S(1)} %get-tuple-element.29), channel_id=1, source_target_pairs={{0,3},{1,2},{2,1},{3,0},{4,7},{5,6},{6,5},{7,4},{8,11},{9,10},{10,... | collective-permute-start | bytes 110600 | tf_op jit(solution)/shard_map/ppermute | solution.py:537
  14.7 0.6 %shard_map.117 = (f32[1,6,72,384]{3,2,1,0:T(8,128)S(1)}, f32[1,72,384]{2,1,0:T(8,128)S(1)}) custom-call(f32[1,1,6,4,4096]{4,3,2,1,0:T(4,128)S(1)} %bitcast.3, f32[1,1,4,4096]{3,2,1,0:T(4,128)S(1)} %copy-done.7, bf16[256,384]{1,0:T(8,128)(2,1)S(1)} %copy-done.5), custom_call_target="tpu_custom_call" | custom-call | flops 1000000 | bytes 4000000 | tf_op jit(solution)/shard_map/pallas_call | solution.py:522
  15.3 0.5 %collective-permute-done.5.refs_1_.refs_2_ = f32[72,128]{1,0:T(8,128)S(1)} collective-permute-done((f32[72,128]{1,0:T(8,128)S(1)}, f32[72,128]{1,0:T(8,128)S(1)}, u32[]{:S(2)}, u32[]{:S(2)}) %collective-permute-start.5) | collective-permute-done | bytes 36896 | tf_op jit(solution)/shard_map/ppermute | solution.py:537
  15.8 1.8 %collective-permute-done.6.refs_2_.refs_3_ = f32[72,128]{1,0:T(8,128)S(1)} collective-permute-done((f32[72,128]{1,0:T(8,128)S(1)}, f32[72,128]{1,0:T(8,128)S(1)}, u32[]{:S(2)}, u32[]{:S(2)}) %collective-permute-start.6) | collective-permute-done | bytes 36896 | tf_op jit(solution)/shard_map/ppermute | solution.py:537
  17.6 0.0 copy-start.3
  17.7 1.5 %shard_map.118 = (f32[1,6,72,384]{3,2,1,0:T(8,128)S(1)}, f32[24,128]{1,0:T(8,128)S(1)}, f32[24,128]{1,0:T(8,128)S(1)}, f32[24,128]{1,0:T(8,128)S(1)}, f32[24,128]{1,0:T(8,128)S(1)}) custom-call(f32[72,128]{1,0:T(8,128)S(1)} %get-tuple-element.30.refs_0_, f32[104,128]{1,0:T(8,128)S(1)} %collective-permute-done.4.refs_0_.refs_1_, ...), custom_call_target="tpu_custom_call" | custom-call | flops 1000000 | bytes 1000000 | tf_op jit(solution)/shard_map/pallas_call | solution.py:555
  19.1 0.4 %collective-permute-start.7 = (f32[24,128]{1,0:T(8,128)S(1)}, f32[24,128]{1,0:T(8,128)S(1)}, u32[]{:S(2)}, u32[]{:S(2)}) collective-permute-start(f32[24,128]{1,0:T(8,128)S(1)} %get-tuple-element.34), channel_id=1, source_target_pairs={{0,1},{1,0},{2,3},{3,2},{4,5},{5,4},{6,7},{7,6},{8,9},{9,8},{10,11... | collective-permute-start | bytes 36872 | tf_op jit(solution)/shard_map/ppermute | solution.py:537
  19.6 0.6 %collective-permute-start.8 = (f32[24,128]{1,0:T(8,128)S(1)}, f32[24,128]{1,0:T(8,128)S(1)}, u32[]{:S(2)}, u32[]{:S(2)}) collective-permute-start(f32[24,128]{1,0:T(8,128)S(1)} %get-tuple-element.35), channel_id=1, source_target_pairs={{0,2},{1,3},{2,0},{3,1},{4,6},{5,7},{6,4},{7,5},{8,10},{9,11},{10,... | collective-permute-start | bytes 36872 | tf_op jit(solution)/shard_map/ppermute | solution.py:537
  20.2 1.2 %collective-permute-start.9 = (f32[24,128]{1,0:T(8,128)S(1)}, f32[24,128]{1,0:T(8,128)S(1)}, u32[]{:S(2)}, u32[]{:S(2)}) collective-permute-start(f32[24,128]{1,0:T(8,128)S(1)} %get-tuple-element.36), channel_id=1, source_target_pairs={{0,3},{1,2},{2,1},{3,0},{4,7},{5,6},{6,5},{7,4},{8,11},{9,10},{10,... | collective-permute-start | bytes 36872 | tf_op jit(solution)/shard_map/ppermute | solution.py:537
  21.4 1.3 %shard_map.120 = f32[1,1,6,4,4096]{4,3,2,1,0:T(4,128)} custom-call(f32[1,6,72,384]{3,2,1,0:T(8,128)S(1)} %get-tuple-element.37.box, f32[1,1,6,4,4096]{4,3,2,1,0:T(4,128)S(1)} %bitcast.4, s32[12,128]{1,0:T(8,128)S(1)} %get-tuple-element.22.refs_3_.notes, bf16[384,256]{1,0:T(8,128)(2,1)S(1)} %copy-done.3), custom_call_target="tpu_custom_call" | custom-call | flops 1000000 | bytes 4000000 | tf_op jit(solution)/shard_map/pallas_call | solution.py:570
  22.6 0.1 shard_map.116.new
  22.8 0.6 %collective-permute-done.9.refs_3_ = f32[24,128]{1,0:T(8,128)S(1)} collective-permute-done((f32[24,128]{1,0:T(8,128)S(1)}, f32[24,128]{1,0:T(8,128)S(1)}, u32[]{:S(2)}, u32[]{:S(2)}) %collective-permute-start.9) | collective-permute-done | bytes 12320 | tf_op jit(solution)/shard_map/ppermute | solution.py:537
  23.4 1.0 %shard_map.119 = f32[6,12,12,128]{3,2,1,0:T(8,128)} custom-call(f32[6,12,12,128]{3,2,1,0:T(8,128)S(1)} %shard_map.116.new, s32[12,128]{1,0:T(8,128)S(1)} %get-tuple-element.22.refs_3_.notes, f32[24,128]{1,0:T(8,128)S(1)} %get-tuple-element.33.refs_0_, f32[24,128]{1,0:T(8,128)S(1)} %collective-permute-done.7.refs_1_, ...), custom_call_target="tpu_custom_call" | custom-call | flops 1000000 | bytes 1000000 | tf_op jit(solution)/shard_map/pallas_call | solution.py:579
  (24 shorter events, 0.1 us)
Async XLA Ops:
  0.6 1.1 %copy-start.1 = (f32[6,12,12,128]{3,2,1,0:T(8,128)S(1)}, f32[6,12,12,128]{3,2,1,0:T(8,128)}, u32[]{:S(2)}) copy-start(f32[6,12,12,128]{3,2,1,0:T(8,128)} %block.1) | copy-start | bytes 1327108
  1.7 6.6 %copy-start.6 = (f32[12,12,128]{2,1,0:T(8,128)S(1)}, f32[12,12,128]{2,1,0:T(8,128)}, u32[]{:S(2)}) copy-start(f32[12,12,128]{2,1,0:T(8,128)} %perm.2) | copy-start | bytes 221188
  1.8 8.2 %collective-permute-start = (f32[6,12,12,128]{3,2,1,0:T(8,128)S(1)}, f32[6,12,12,128]{3,2,1,0:T(8,128)S(1)}, u32[]{:S(2)}, u32[]{:S(2)}) collective-permute-start(f32[6,12,12,128]{3,2,1,0:T(8,128)S(1)} %get-tuple-element.20.refs_0_), channel_id=1, source_target_pairs={{0,1},{1,0},{2,3},{3,2},{4,5},{5,4},{6,7},{7,6},{8,9},{9,8},{10,11... | collective-permute-start | bytes 1327112 | tf_op jit(solution)/shard_map/ppermute | solution.py:514
  2.5 6.4 %collective-permute-start.1 = (f32[5,12,128]{2,1,0:T(8,128)S(1)}, f32[5,12,128]{2,1,0:T(8,128)S(1)}, u32[]{:S(2)}, u32[]{:S(2)}) collective-permute-start(f32[5,12,128]{2,1,0:T(8,128)S(1)} %get-tuple-element.23), channel_id=1, source_target_pairs={{0,4},{4,0},{8,12},{12,8},{1,5},{5,1},{9,13},{13,9},{2,6},{6,2},{1... | collective-permute-start | bytes 92168 | tf_op jit(solution)/shard_map/ppermute | solution.py:508
  2.5 6.4 %collective-permute-start.2 = (f32[5,12,128]{2,1,0:T(8,128)S(1)}, f32[5,12,128]{2,1,0:T(8,128)S(1)}, u32[]{:S(2)}, u32[]{:S(2)}) collective-permute-start(f32[5,12,128]{2,1,0:T(8,128)S(1)} %get-tuple-element.24), channel_id=1, source_target_pairs={{4,8},{8,4},{5,9},{9,5},{6,10},{10,6},{7,11},{11,7},{20,24},{24,20... | collective-permute-start | bytes 92168 | tf_op jit(solution)/shard_map/ppermute | solution.py:509
  7.0 1.3 %copy-start.9 = (s32[1,4,2]{1,2,0:T(2,128)S(1)}, s32[1,4,2]{1,2,0:T(2,128)}, u32[]{:S(2)}) copy-start(s32[1,4,2]{1,2,0:T(2,128)} %param.15) | copy-start | bytes 100
  7.0 1.3 %copy-start.8 = (s32[1,1,2,3]{3,2,1,0:T(2,128)S(1)}, s32[1,1,2,3]{3,2,1,0:T(2,128)}, u32[]{:S(2)}) copy-start(s32[1,1,2,3]{3,2,1,0:T(2,128)} %corner.1) | copy-start | bytes 76
  7.1 2.9 %collective-permute-start.3 = (f32[5,12,128]{2,1,0:T(8,128)S(1)}, f32[5,12,128]{2,1,0:T(8,128)S(1)}, u32[]{:S(2)}, u32[]{:S(2)}) collective-permute-start(f32[5,12,128]{2,1,0:T(8,128)S(1)} %get-tuple-element.25), channel_id=1, source_target_pairs={{0,2},{2,0},{1,3},{3,1},{4,6},{6,4},{5,7},{7,5},{8,10},{10,8},{9,1... | collective-permute-start | bytes 92168 | tf_op jit(solution)/shard_map/ppermute | solution.py:510
  10.0 4.7 %copy-start = (f32[1,1,4,6,4096]{4,2,3,1,0:T(4,128)S(1)}, f32[1,1,4,6,4096]{4,2,3,1,0:T(4,128)}, u32[]{:S(2)}) copy-start(f32[1,1,4,6,4096]{4,2,3,1,0:T(4,128)} %param.12) | copy-start | bytes 1179652
  10.0 4.7 %copy-start.5 = (bf16[256,384]{1,0:T(8,128)(2,1)S(1)}, bf16[256,384]{1,0:T(8,128)(2,1)}, u32[]{:S(2)}) copy-start(bf16[256,384]{1,0:T(8,128)(2,1)} %constant.8.clone.table) | copy-start | bytes 589828
  10.0 4.7 %copy-start.7 = (f32[1,1,4,4096]{3,2,1,0:T(4,128)S(1)}, f32[1,1,4,4096]{3,2,1,0:T(4,128)}, u32[]{:S(2)}) copy-start(f32[1,1,4,4096]{3,2,1,0:T(4,128)} %perm.3) | copy-start | bytes 196612
  11.1 6.5 %copy-start.2 = (bf16[2,256,384]{2,1,0:T(8,128)(2,1)S(1)}, bf16[2,256,384]{2,1,0:T(8,128)(2,1)}, u32[]{:S(2)}) copy-start(bf16[2,256,384]{2,1,0:T(8,128)(2,1)} %constant.9.clone.refs_6_) | copy-start | bytes 1179652
  11.1 6.5 %collective-permute-start.4 = (f32[104,128]{1,0:T(8,128)S(1)}, f32[104,128]{1,0:T(8,128)S(1)}, u32[]{:S(2)}, u32[]{:S(2)}) collective-permute-start(f32[104,128]{1,0:T(8,128)S(1)} %get-tuple-element.27), channel_id=1, source_target_pairs={{0,1},{1,0},{2,3},{3,2},{4,5},{5,4},{6,7},{7,6},{8,9},{9,8},{10,11... | collective-permute-start | bytes 159752 | tf_op jit(solution)/shard_map/ppermute | solution.py:537
  13.0 2.8 %collective-permute-start.5 = (f32[72,128]{1,0:T(8,128)S(1)}, f32[72,128]{1,0:T(8,128)S(1)}, u32[]{:S(2)}, u32[]{:S(2)}) collective-permute-start(f32[72,128]{1,0:T(8,128)S(1)} %get-tuple-element.28), channel_id=1, source_target_pairs={{0,2},{1,3},{2,0},{3,1},{4,6},{5,7},{6,4},{7,5},{8,10},{9,11},{10,... | collective-permute-start | bytes 110600 | tf_op jit(solution)/shard_map/ppermute | solution.py:537
  14.2 3.4 %collective-permute-start.6 = (f32[72,128]{1,0:T(8,128)S(1)}, f32[72,128]{1,0:T(8,128)S(1)}, u32[]{:S(2)}, u32[]{:S(2)}) collective-permute-start(f32[72,128]{1,0:T(8,128)S(1)} %get-tuple-element.29), channel_id=1, source_target_pairs={{0,3},{1,2},{2,1},{3,0},{4,7},{5,6},{6,5},{7,4},{8,11},{9,10},{10,... | collective-permute-start | bytes 110600 | tf_op jit(solution)/shard_map/ppermute | solution.py:537
  14.7 2.9 %copy-start.4 = (bf16[768,128]{1,0:T(8,128)(2,1)S(1)}, bf16[768,128]{1,0:T(8,128)(2,1)}, u32[]{:S(2)}) copy-start(bf16[768,128]{1,0:T(8,128)(2,1)} %constant.10.clone.refs_7_) | copy-start | bytes 589828
  17.6 3.7 %copy-start.3 = (bf16[384,256]{1,0:T(8,128)(2,1)S(1)}, bf16[384,256]{1,0:T(8,128)(2,1)}, u32[]{:S(2)}) copy-start(bf16[384,256]{1,0:T(8,128)(2,1)} %constant.11.clone.table) | copy-start | bytes 589828
  19.1 3.6 %collective-permute-start.7 = (f32[24,128]{1,0:T(8,128)S(1)}, f32[24,128]{1,0:T(8,128)S(1)}, u32[]{:S(2)}, u32[]{:S(2)}) collective-permute-start(f32[24,128]{1,0:T(8,128)S(1)} %get-tuple-element.34), channel_id=1, source_target_pairs={{0,1},{1,0},{2,3},{3,2},{4,5},{5,4},{6,7},{7,6},{8,9},{9,8},{10,11... | collective-permute-start | bytes 36872 | tf_op jit(solution)/shard_map/ppermute | solution.py:537
  19.6 3.2 %collective-permute-start.8 = (f32[24,128]{1,0:T(8,128)S(1)}, f32[24,128]{1,0:T(8,128)S(1)}, u32[]{:S(2)}, u32[]{:S(2)}) collective-permute-start(f32[24,128]{1,0:T(8,128)S(1)} %get-tuple-element.35), channel_id=1, source_target_pairs={{0,2},{1,3},{2,0},{3,1},{4,6},{5,7},{6,4},{7,5},{8,10},{9,11},{10,... | collective-permute-start | bytes 36872 | tf_op jit(solution)/shard_map/ppermute | solution.py:537
  20.2 3.2 %collective-permute-start.9 = (f32[24,128]{1,0:T(8,128)S(1)}, f32[24,128]{1,0:T(8,128)S(1)}, u32[]{:S(2)}, u32[]{:S(2)}) collective-permute-start(f32[24,128]{1,0:T(8,128)S(1)} %get-tuple-element.36), channel_id=1, source_target_pairs={{0,3},{1,2},{2,1},{3,0},{4,7},{5,6},{6,5},{7,4},{8,11},{9,10},{10,... | collective-permute-start | bytes 36872 | tf_op jit(solution)/shard_map/ppermute | solution.py:537

commit v5 on v4

--- a/solution.py
+++ b/solution.py
@@ -102,7 +102,15 @@
     return pairs
 
 
-def faces_kernel(two_y, block, kept, x_even, x_odd, y_even, *y_odd):
+def far_first(parts):
+    return [parts[0], *parts[2:], parts[1]]
+
+
+def by_rank(parts):
+    return [parts[0], parts[-1], *parts[1:-1]]
+
+
+def faces_kernel(two_y, block, kept, x_odd, x_even, y_even, *y_odd):
     deep, tall = block.shape[1], block.shape[2]
     gx_odd = lax.rem(lax.axis_index("gx"), 2)
     gy_odd = lax.rem(lax.axis_index("gy"), 2)
@@ -136,10 +144,10 @@
 
 
 def leap_kernel(two_y, ranks, *refs):
-    block, beside, rate, notes, x_even, x_odd, y_even = refs[:7]
+    block, beside, rate, notes, x_odd, x_even, y_even = refs[:7]
     y_odd = refs[7] if two_y else None
     refs = refs[7 + two_y :]
-    new, sends = refs[0], refs[1 : 1 + ranks]
+    new, sends = refs[0], by_rank(refs[1 : 1 + ranks])
     pad, side, mag, fresh, packed = refs[1 + ranks :]
     deep, tall = block.shape[1], block.shape[2]
     full = deep + 2
@@ -303,7 +311,7 @@
 
 def fine_kernel(ranks, *refs):
     regions, (box, rate, ghosts, means, out) = refs[:ranks], refs[ranks : ranks + 5]
-    smalls = refs[ranks + 5 : 2 * ranks + 5]
+    smalls = by_rank(refs[ranks + 5 : 2 * ranks + 5])
     rims, walls, now, mag, halves, small = refs[2 * ranks + 5 :]
     groups = box.shape[0]
     rank = lax.axis_index("gy") * lax.axis_size("gz") + lax.axis_index("gz")
@@ -505,8 +513,8 @@
         [vmem],
     )(coarse_fields)
     got = [
-        lax.ppermute(faces[0], "gx", swap_pairs(count_x, 0)),
-        lax.ppermute(faces[1], "gx", swap_pairs(count_x, 1)),
+        lax.ppermute(faces[0], "gx", swap_pairs(count_x, 1)),
+        lax.ppermute(faces[1], "gx", swap_pairs(count_x, 0)),
         lax.ppermute(faces[2], "gy", swap_pairs(count_y, 0)),
     ]
     if two_y:
@@ -540,7 +548,7 @@
     patches = [shape((ROWS_BESIDE if k == 1 else ROWS_PATCH, LANES), F32) for k in range(ranks)]
     new, *sends = call(
         functools.partial(leap_kernel, two_y, ranks),
-        [shape(coarse_fields.shape, F32)] + patches,
+        [shape(coarse_fields.shape, F32)] + far_first(patches),
         [vmem] * (4 + len(got)),
         [
             pltpu.VMEM((6 * full * 16, LANES), F32),
@@ -550,7 +558,7 @@
             pltpu.VMEM((PAR, ROWS_PATCH, LANES), F32),
         ],
     )(kept, beside, rate, notes, *got)
-    regions = exchange(sends)
+    regions = exchange(by_rank(sends))
 
     box, *smalls = call(
         functools.partial(fine_kernel, ranks),
@@ -565,7 +573,7 @@
             pltpu.VMEM((groups * 96, LANES), F32),
         ],
     )(*regions, box, fine_rate, jnp.asarray(ghost_table(), BF16), jnp.asarray(mean_table(), BF16))
-    means = exchange(smalls)
+    means = exchange(by_rank(smalls))
 
     fine = call(
         store_kernel,

time: 24.6 us -> 25.7 us (1.045)
  the two profiles are of different devices: /device:TPU:9 before, /device:TPU:0 now
where the time goes in v5:
time: 25.7 us; the launch traced here: 25.5 us
  starting transfers between devices  12 us (47%)
  Pallas kernels  6.24 us (24%)
  waiting for transfers between devices  5.38 us (21%)
  local copies, waits for them, and re-layouts  1.09 us (4%)
  between operations  0.76 us (3%)
    ppermute x1, starting transfers between devices, local(): lax.ppermute(faces[1], 'gx', swap_pairs(count_x, 0))  5.48 us
    ppermute x6, starting transfers between devices, exchange(): got[k] = lax.ppermute(parts[k], ('gy', 'gz'), swaps[k])  3.86 us
    ppermute x6, waiting for transfers between devices, exchange(): got[k] = lax.ppermute(parts[k], ('gy', 'gz'), swaps[k])  3.48 us
    ppermute x1, waiting for transfers between devices, local(): lax.ppermute(faces[2], 'gy', swap_pairs(count_y, 0))  1.89 us
    ppermute x1, starting transfers between devices, local(): lax.ppermute(faces[2], 'gy', swap_pairs(count_y, 0))  1.49 us
    pallas_call x1, Pallas kernels, local(): call(functools.partial(fine_kernel, ranks), [shape((groups, 6, ROWS_BOX,...  1.48 us
    pallas_call x1, Pallas kernels, local(): call(store_kernel, shape(fine.shape, F32), [vmem] * 4, [pltpu.VMEM(fine.s...  1.29 us
    pallas_call x1, Pallas kernels, local(): call(functools.partial(leap_kernel, two_y, ranks), [shape(coarse_fields.s...  1.14 us
  transfers between devices with their start and end apart: 10, of which 5 were waited for; matrix products, arithmetic and copies ran while one was open for 0% of the time, Pallas kernels for 10%

profile of v5, /device:TPU:0, one launch (start us, length us, event | category | flops | bytes accessed | tf_op | source)
XLA Modules:
  0.0 25.5 jit_solution(13319879855009153214)
XLA Ops:
  0.6 1.1 %copy-done.1 = f32[6,12,12,128]{3,2,1,0:T(8,128)S(1)} copy-done((f32[6,12,12,128]{3,2,1,0:T(8,128)S(1)}, f32[6,12,12,128]{3,2,1,0:T(8,128)}, u32[]{:S(2)}) %copy-start.1) | copy-done | bytes 442392
  1.7 0.1 shard_map.113
  1.8 0.5 %collective-permute-start = (f32[6,12,12,128]{3,2,1,0:T(8,128)S(1)}, f32[6,12,12,128]{3,2,1,0:T(8,128)S(1)}, u32[]{:S(2)}, u32[]{:S(2)}) collective-permute-start(f32[6,12,12,128]{3,2,1,0:T(8,128)S(1)} %get-tuple-element.20.refs_0_), channel_id=1, source_target_pairs={{0,1},{1,0},{2,3},{3,2},{4,5},{5,4},{6,7},{7,6},{8,9},{9,8},{10,11... | collective-permute-start | bytes 1327112 | tf_op jit(solution)/shard_map/ppermute | solution.py:522
  2.3 0.7 %collective-permute-start.1 = (f32[5,12,128]{2,1,0:T(8,128)S(1)}, f32[5,12,128]{2,1,0:T(8,128)S(1)}, u32[]{:S(2)}, u32[]{:S(2)}) collective-permute-start(f32[5,12,128]{2,1,0:T(8,128)S(1)} %get-tuple-element.23), channel_id=1, source_target_pairs={{4,8},{8,4},{5,9},{9,5},{6,10},{10,6},{7,11},{11,7},{20,24},{24,20... | collective-permute-start | bytes 92168 | tf_op jit(solution)/shard_map/ppermute | solution.py:516
  3.0 5.5 %collective-permute-start.2 = (f32[5,12,128]{2,1,0:T(8,128)S(1)}, f32[5,12,128]{2,1,0:T(8,128)S(1)}, u32[]{:S(2)}, u32[]{:S(2)}) collective-permute-start(f32[5,12,128]{2,1,0:T(8,128)S(1)} %get-tuple-element.24), channel_id=1, source_target_pairs={{0,4},{4,0},{8,12},{12,8},{1,5},{5,1},{9,13},{13,9},{2,6},{6,2},{1... | collective-permute-start | bytes 92168 | tf_op jit(solution)/shard_map/ppermute | solution.py:517
  8.4 1.5 %collective-permute-start.3 = (f32[5,12,128]{2,1,0:T(8,128)S(1)}, f32[5,12,128]{2,1,0:T(8,128)S(1)}, u32[]{:S(2)}, u32[]{:S(2)}) collective-permute-start(f32[5,12,128]{2,1,0:T(8,128)S(1)} %get-tuple-element.25), channel_id=1, source_target_pairs={{0,2},{2,0},{1,3},{3,1},{4,6},{6,4},{5,7},{7,5},{8,10},{10,8},{9,1... | collective-permute-start | bytes 92168 | tf_op jit(solution)/shard_map/ppermute | solution.py:518
  9.9 0.6 %shard_map.114 = (s32[12,128]{1,0:T(8,128)S(1)}, f32[12,12,128]{2,1,0:T(8,128)S(1)}) custom-call(s32[1,1,2,3]{3,2,1,0:T(2,128)S(1)} %copy-done.8, s32[1,2,4]{2,1,0:T(2,128)S(1)} %bitcast.5, f32[12,12,128]{2,1,0:T(8,128)S(1)} %copy-done.6), custom_call_target="tpu_custom_call" | custom-call | flops 1000000 | bytes 1000000 | tf_op jit(solution)/shard_map/pallas_call | solution.py:525
  10.6 1.9 %collective-permute-done.3.refs_6_ = f32[5,12,128]{2,1,0:T(8,128)S(1)} collective-permute-done((f32[5,12,128]{2,1,0:T(8,128)S(1)}, f32[5,12,128]{2,1,0:T(8,128)S(1)}, u32[]{:S(2)}, u32[]{:S(2)}) %collective-permute-start.3) | collective-permute-done | bytes 30752 | tf_op jit(solution)/shard_map/ppermute | solution.py:518
  12.5 1.1 %shard_map.115 = (f32[6,12,12,128]{3,2,1,0:T(8,128)S(1)}, f32[72,128]{1,0:T(8,128)S(1)}, f32[72,128]{1,0:T(8,128)S(1)}, f32[72,128]{1,0:T(8,128)S(1)}, f32[104,128]{1,0:T(8,128)S(1)}) custom-call(f32[6,12,12,128]{3,2,1,0:T(8,128)S(1)} %get-tuple-element.20.refs_0_, f32[6,12,12,128]{3,2,1,0:T(8,128)S(1)} %collective-permute-done.refs_1_, ...), custom_call_target="tpu_custom_call" | custom-call | flops 1000000 | bytes 1000000 | tf_op jit(solution)/shard_map/pallas_call | solution.py:549
  13.6 0.1 collective-permute-start.4
  13.7 1.6 %collective-permute-start.5 = (f32[72,128]{1,0:T(8,128)S(1)}, f32[72,128]{1,0:T(8,128)S(1)}, u32[]{:S(2)}, u32[]{:S(2)}) collective-permute-start(f32[72,128]{1,0:T(8,128)S(1)} %get-tuple-element.28), channel_id=1, source_target_pairs={{0,2},{1,3},{2,0},{3,1},{4,6},{5,7},{6,4},{7,5},{8,10},{9,11},{10,... | collective-permute-start | bytes 110600 | tf_op jit(solution)/shard_map/ppermute | solution.py:545
  15.2 0.3 %collective-permute-start.6 = (f32[72,128]{1,0:T(8,128)S(1)}, f32[72,128]{1,0:T(8,128)S(1)}, u32[]{:S(2)}, u32[]{:S(2)}) collective-permute-start(f32[72,128]{1,0:T(8,128)S(1)} %get-tuple-element.29), channel_id=1, source_target_pairs={{0,3},{1,2},{2,1},{3,0},{4,7},{5,6},{6,5},{7,4},{8,11},{9,10},{10,... | collective-permute-start | bytes 110600 | tf_op jit(solution)/shard_map/ppermute | solution.py:545
  15.6 0.6 %shard_map.117 = (f32[1,6,72,384]{3,2,1,0:T(8,128)S(1)}, f32[1,72,384]{2,1,0:T(8,128)S(1)}) custom-call(f32[1,1,6,4,4096]{4,3,2,1,0:T(4,128)S(1)} %bitcast.3, f32[1,1,4,4096]{3,2,1,0:T(4,128)S(1)} %copy-done.7, bf16[256,384]{1,0:T(8,128)(2,1)S(1)} %copy-done.5), custom_call_target="tpu_custom_call" | custom-call | flops 1000000 | bytes 4000000 | tf_op jit(solution)/shard_map/pallas_call | solution.py:530
  16.2 1.5 %collective-permute-done.5.refs_1_.refs_2_ = f32[72,128]{1,0:T(8,128)S(1)} collective-permute-done((f32[72,128]{1,0:T(8,128)S(1)}, f32[72,128]{1,0:T(8,128)S(1)}, u32[]{:S(2)}, u32[]{:S(2)}) %collective-permute-start.5) | collective-permute-done | bytes 36896 | tf_op jit(solution)/shard_map/ppermute | solution.py:545
  17.7 1.0 %collective-permute-done.6.refs_2_.refs_3_ = f32[72,128]{1,0:T(8,128)S(1)} collective-permute-done((f32[72,128]{1,0:T(8,128)S(1)}, f32[72,128]{1,0:T(8,128)S(1)}, u32[]{:S(2)}, u32[]{:S(2)}) %collective-permute-start.6) | collective-permute-done | bytes 36896 | tf_op jit(solution)/shard_map/ppermute | solution.py:545
  18.7 1.5 %shard_map.118 = (f32[1,6,72,384]{3,2,1,0:T(8,128)S(1)}, f32[24,128]{1,0:T(8,128)S(1)}, f32[24,128]{1,0:T(8,128)S(1)}, f32[24,128]{1,0:T(8,128)S(1)}, f32[24,128]{1,0:T(8,128)S(1)}) custom-call(f32[72,128]{1,0:T(8,128)S(1)} %get-tuple-element.30.refs_0_, f32[104,128]{1,0:T(8,128)S(1)} %collective-permute-done.4.refs_0_.refs_1_, ...), custom_call_target="tpu_custom_call" | custom-call | flops 1000000 | bytes 1000000 | tf_op jit(solution)/shard_map/pallas_call | solution.py:563
  20.2 0.2 collective-permute-start.7
  20.4 0.9 %collective-permute-start.8 = (f32[24,128]{1,0:T(8,128)S(1)}, f32[24,128]{1,0:T(8,128)S(1)}, u32[]{:S(2)}, u32[]{:S(2)}) collective-permute-start(f32[24,128]{1,0:T(8,128)S(1)} %get-tuple-element.35), channel_id=1, source_target_pairs={{0,2},{1,3},{2,0},{3,1},{4,6},{5,7},{6,4},{7,5},{8,10},{9,11},{10,... | collective-permute-start | bytes 36872 | tf_op jit(solution)/shard_map/ppermute | solution.py:545
  21.3 0.8 %collective-permute-start.9 = (f32[24,128]{1,0:T(8,128)S(1)}, f32[24,128]{1,0:T(8,128)S(1)}, u32[]{:S(2)}, u32[]{:S(2)}) collective-permute-start(f32[24,128]{1,0:T(8,128)S(1)} %get-tuple-element.36), channel_id=1, source_target_pairs={{0,3},{1,2},{2,1},{3,0},{4,7},{5,6},{6,5},{7,4},{8,11},{9,10},{10,... | collective-permute-start | bytes 36872 | tf_op jit(solution)/shard_map/ppermute | solution.py:545
  22.1 1.3 %shard_map.120 = f32[1,1,6,4,4096]{4,3,2,1,0:T(4,128)} custom-call(f32[1,6,72,384]{3,2,1,0:T(8,128)S(1)} %get-tuple-element.37.box, f32[1,1,6,4,4096]{4,3,2,1,0:T(4,128)S(1)} %bitcast.4, s32[12,128]{1,0:T(8,128)S(1)} %get-tuple-element.22.refs_3_.notes, bf16[384,256]{1,0:T(8,128)(2,1)S(1)} %copy-done.3), custom_call_target="tpu_custom_call" | custom-call | flops 1000000 | bytes 4000000 | tf_op jit(solution)/shard_map/pallas_call | solution.py:578
  23.4 0.1 shard_map.116.new
  23.5 0.6 %collective-permute-done.8.refs_2_ = f32[24,128]{1,0:T(8,128)S(1)} collective-permute-done((f32[24,128]{1,0:T(8,128)S(1)}, f32[24,128]{1,0:T(8,128)S(1)}, u32[]{:S(2)}, u32[]{:S(2)}) %collective-permute-start.8) | collective-permute-done | bytes 12320 | tf_op jit(solution)/shard_map/ppermute | solution.py:545
  24.1 0.4 %collective-permute-done.9.refs_3_ = f32[24,128]{1,0:T(8,128)S(1)} collective-permute-done((f32[24,128]{1,0:T(8,128)S(1)}, f32[24,128]{1,0:T(8,128)S(1)}, u32[]{:S(2)}, u32[]{:S(2)}) %collective-permute-start.9) | collective-permute-done | bytes 12320 | tf_op jit(solution)/shard_map/ppermute | solution.py:545
  24.5 1.0 %shard_map.119 = f32[6,12,12,128]{3,2,1,0:T(8,128)} custom-call(f32[6,12,12,128]{3,2,1,0:T(8,128)S(1)} %shard_map.116.new, s32[12,128]{1,0:T(8,128)S(1)} %get-tuple-element.22.refs_3_.notes, f32[24,128]{1,0:T(8,128)S(1)} %get-tuple-element.33.refs_0_, f32[24,128]{1,0:T(8,128)S(1)} %collective-permute-done.7.refs_1_, ...), custom_call_target="tpu_custom_call" | custom-call | flops 1000000 | bytes 1000000 | tf_op jit(solution)/shard_map/pallas_call | solution.py:587
  (24 shorter events, 0.1 us)
Async XLA Ops:
  0.6 1.1 %copy-start.1 = (f32[6,12,12,128]{3,2,1,0:T(8,128)S(1)}, f32[6,12,12,128]{3,2,1,0:T(8,128)}, u32[]{:S(2)}) copy-start(f32[6,12,12,128]{3,2,1,0:T(8,128)} %block.1) | copy-start | bytes 1327108
  1.7 8.2 %copy-start.6 = (f32[12,12,128]{2,1,0:T(8,128)S(1)}, f32[12,12,128]{2,1,0:T(8,128)}, u32[]{:S(2)}) copy-start(f32[12,12,128]{2,1,0:T(8,128)} %perm.2) | copy-start | bytes 221188
  1.8 10.7 %collective-permute-start = (f32[6,12,12,128]{3,2,1,0:T(8,128)S(1)}, f32[6,12,12,128]{3,2,1,0:T(8,128)S(1)}, u32[]{:S(2)}, u32[]{:S(2)}) collective-permute-start(f32[6,12,12,128]{3,2,1,0:T(8,128)S(1)} %get-tuple-element.20.refs_0_), channel_id=1, source_target_pairs={{0,1},{1,0},{2,3},{3,2},{4,5},{5,4},{6,7},{7,6},{8,9},{9,8},{10,11... | collective-permute-start | bytes 1327112 | tf_op jit(solution)/shard_map/ppermute | solution.py:522
  2.3 8.2 %collective-permute-start.1 = (f32[5,12,128]{2,1,0:T(8,128)S(1)}, f32[5,12,128]{2,1,0:T(8,128)S(1)}, u32[]{:S(2)}, u32[]{:S(2)}) collective-permute-start(f32[5,12,128]{2,1,0:T(8,128)S(1)} %get-tuple-element.23), channel_id=1, source_target_pairs={{4,8},{8,4},{5,9},{9,5},{6,10},{10,6},{7,11},{11,7},{20,24},{24,20... | collective-permute-start | bytes 92168 | tf_op jit(solution)/shard_map/ppermute | solution.py:516
  3.0 7.6 %collective-permute-start.2 = (f32[5,12,128]{2,1,0:T(8,128)S(1)}, f32[5,12,128]{2,1,0:T(8,128)S(1)}, u32[]{:S(2)}, u32[]{:S(2)}) collective-permute-start(f32[5,12,128]{2,1,0:T(8,128)S(1)} %get-tuple-element.24), channel_id=1, source_target_pairs={{0,4},{4,0},{8,12},{12,8},{1,5},{5,1},{9,13},{13,9},{2,6},{6,2},{1... | collective-permute-start | bytes 92168 | tf_op jit(solution)/shard_map/ppermute | solution.py:517
  8.4 1.5 %copy-start.9 = (s32[1,4,2]{1,2,0:T(2,128)S(1)}, s32[1,4,2]{1,2,0:T(2,128)}, u32[]{:S(2)}) copy-start(s32[1,4,2]{1,2,0:T(2,128)} %param.15) | copy-start | bytes 100
  8.4 1.5 %copy-start.8 = (s32[1,1,2,3]{3,2,1,0:T(2,128)S(1)}, s32[1,1,2,3]{3,2,1,0:T(2,128)}, u32[]{:S(2)}) copy-start(s32[1,1,2,3]{3,2,1,0:T(2,128)} %corner.1) | copy-start | bytes 76
  8.4 4.0 %collective-permute-start.3 = (f32[5,12,128]{2,1,0:T(8,128)S(1)}, f32[5,12,128]{2,1,0:T(8,128)S(1)}, u32[]{:S(2)}, u32[]{:S(2)}) collective-permute-start(f32[5,12,128]{2,1,0:T(8,128)S(1)} %get-tuple-element.25), channel_id=1, source_target_pairs={{0,2},{2,0},{1,3},{3,1},{4,6},{6,4},{5,7},{7,5},{8,10},{10,8},{9,1... | collective-permute-start | bytes 92168 | tf_op jit(solution)/shard_map/ppermute | solution.py:518
  12.5 3.1 %copy-start = (f32[1,1,4,6,4096]{4,2,3,1,0:T(4,128)S(1)}, f32[1,1,4,6,4096]{4,2,3,1,0:T(4,128)}, u32[]{:S(2)}) copy-start(f32[1,1,4,6,4096]{4,2,3,1,0:T(4,128)} %param.12) | copy-start | bytes 1179652
  12.5 3.1 %copy-start.5 = (bf16[256,384]{1,0:T(8,128)(2,1)S(1)}, bf16[256,384]{1,0:T(8,128)(2,1)}, u32[]{:S(2)}) copy-start(bf16[256,384]{1,0:T(8,128)(2,1)} %constant.8.clone.table) | copy-start | bytes 589828
  12.5 3.1 %copy-start.7 = (f32[1,1,4,4096]{3,2,1,0:T(4,128)S(1)}, f32[1,1,4,4096]{3,2,1,0:T(4,128)}, u32[]{:S(2)}) copy-start(f32[1,1,4,4096]{3,2,1,0:T(4,128)} %perm.3) | copy-start | bytes 196612
  13.6 5.1 %copy-start.2 = (bf16[2,256,384]{2,1,0:T(8,128)(2,1)S(1)}, bf16[2,256,384]{2,1,0:T(8,128)(2,1)}, u32[]{:S(2)}) copy-start(bf16[2,256,384]{2,1,0:T(8,128)(2,1)} %constant.9.clone.refs_6_) | copy-start | bytes 1179652
  13.6 5.1 %collective-permute-start.4 = (f32[104,128]{1,0:T(8,128)S(1)}, f32[104,128]{1,0:T(8,128)S(1)}, u32[]{:S(2)}, u32[]{:S(2)}) collective-permute-start(f32[104,128]{1,0:T(8,128)S(1)} %get-tuple-element.27), channel_id=1, source_target_pairs={{0,1},{1,0},{2,3},{3,2},{4,5},{5,4},{6,7},{7,6},{8,9},{9,8},{10,11... | collective-permute-start | bytes 159752 | tf_op jit(solution)/shard_map/ppermute | solution.py:545
  13.7 4.0 %collective-permute-start.5 = (f32[72,128]{1,0:T(8,128)S(1)}, f32[72,128]{1,0:T(8,128)S(1)}, u32[]{:S(2)}, u32[]{:S(2)}) collective-permute-start(f32[72,128]{1,0:T(8,128)S(1)} %get-tuple-element.28), channel_id=1, source_target_pairs={{0,2},{1,3},{2,0},{3,1},{4,6},{5,7},{6,4},{7,5},{8,10},{9,11},{10,... | collective-permute-start | bytes 110600 | tf_op jit(solution)/shard_map/ppermute | solution.py:545
  15.2 3.4 %collective-permute-start.6 = (f32[72,128]{1,0:T(8,128)S(1)}, f32[72,128]{1,0:T(8,128)S(1)}, u32[]{:S(2)}, u32[]{:S(2)}) collective-permute-start(f32[72,128]{1,0:T(8,128)S(1)} %get-tuple-element.29), channel_id=1, source_target_pairs={{0,3},{1,2},{2,1},{3,0},{4,7},{5,6},{6,5},{7,4},{8,11},{9,10},{10,... | collective-permute-start | bytes 110600 | tf_op jit(solution)/shard_map/ppermute | solution.py:545
  15.6 3.1 %copy-start.4 = (bf16[768,128]{1,0:T(8,128)(2,1)S(1)}, bf16[768,128]{1,0:T(8,128)(2,1)}, u32[]{:S(2)}) copy-start(bf16[768,128]{1,0:T(8,128)(2,1)} %constant.10.clone.refs_7_) | copy-start | bytes 589828
  18.7 3.4 %copy-start.3 = (bf16[384,256]{1,0:T(8,128)(2,1)S(1)}, bf16[384,256]{1,0:T(8,128)(2,1)}, u32[]{:S(2)}) copy-start(bf16[384,256]{1,0:T(8,128)(2,1)} %constant.11.clone.table) | copy-start | bytes 589828
  20.2 3.3 %collective-permute-start.7 = (f32[24,128]{1,0:T(8,128)S(1)}, f32[24,128]{1,0:T(8,128)S(1)}, u32[]{:S(2)}, u32[]{:S(2)}) collective-permute-start(f32[24,128]{1,0:T(8,128)S(1)} %get-tuple-element.34), channel_id=1, source_target_pairs={{0,1},{1,0},{2,3},{3,2},{4,5},{5,4},{6,7},{7,6},{8,9},{9,8},{10,11... | collective-permute-start | bytes 36872 | tf_op jit(solution)/shard_map/ppermute | solution.py:545
  20.4 3.7 %collective-permute-start.8 = (f32[24,128]{1,0:T(8,128)S(1)}, f32[24,128]{1,0:T(8,128)S(1)}, u32[]{:S(2)}, u32[]{:S(2)}) collective-permute-start(f32[24,128]{1,0:T(8,128)S(1)} %get-tuple-element.35), channel_id=1, source_target_pairs={{0,2},{1,3},{2,0},{3,1},{4,6},{5,7},{6,4},{7,5},{8,10},{9,11},{10,... | collective-permute-start | bytes 36872 | tf_op jit(solution)/shard_map/ppermute | solution.py:545
  21.3 3.1 %collective-permute-start.9 = (f32[24,128]{1,0:T(8,128)S(1)}, f32[24,128]{1,0:T(8,128)S(1)}, u32[]{:S(2)}, u32[]{:S(2)}) collective-permute-start(f32[24,128]{1,0:T(8,128)S(1)} %get-tuple-element.36), channel_id=1, source_target_pairs={{0,3},{1,2},{2,1},{3,0},{4,7},{5,6},{6,5},{7,4},{8,11},{9,10},{10,... | collective-permute-start | bytes 36872 | tf_op jit(solution)/shard_map/ppermute | solution.py:545

commit v6 on v5

--- a/solution.py
+++ b/solution.py
@@ -110,7 +110,8 @@
     return [parts[0], parts[-1], *parts[1:-1]]
 
 
-def faces_kernel(two_y, block, kept, x_odd, x_even, y_even, *y_odd):
+def faces_kernel(two_y, block, kept, x_even, x_odd, y_even, *more):
+    y_odd, z_face = more[:-1], more[-1]
     deep, tall = block.shape[1], block.shape[2]
     gx_odd = lax.rem(lax.axis_index("gx"), 2)
     gy_odd = lax.rem(lax.axis_index("gy"), 2)
@@ -124,6 +125,13 @@
             y_even[k, x : x + 1, :] = jnp.where(gy_odd == 0, last, first)
             if two_y:
                 y_odd[0][k, x : x + 1, :] = jnp.where(gy_odd == 0, first, last)
+    gz = lax.axis_index("gz")
+    lane = lane_iota((tall, LANES))
+    for c in range(5):
+        total = jnp.zeros((tall, LANES), F32)
+        for x in range(deep):
+            total = jnp.where(lane == x, pltpu.roll(block[c, x], x + 1 - gz, 1), total)
+        z_face[c] = total
     kept[...] = block[...]
 
 
@@ -144,7 +152,7 @@
 
 
 def leap_kernel(two_y, ranks, *refs):
-    block, beside, rate, notes, x_odd, x_even, y_even = refs[:7]
+    block, beside, rate, notes, x_even, x_odd, y_even = refs[:7]
     y_odd = refs[7] if two_y else None
     refs = refs[7 + two_y :]
     new, sends = refs[0], by_rank(refs[1 : 1 + ranks])
@@ -177,7 +185,8 @@
             side[pl.ds(at(c, x), 16), :] = none
         for x in range(deep):
             side[pl.ds(at(c, x + 1), 16), :] = none
-            side[pl.ds(at(c, x + 1), tall), :] = jnp.where(keep, beside[c, x], 0.0)
+            turned = pltpu.roll(beside[c], lax.rem(LANES - x + (LANES - 1) * gz, LANES), 1)
+            side[pl.ds(at(c, x + 1), tall), :] = jnp.where(keep, turned, 0.0)
     for k, c in enumerate(X_COMPS):
         even, odd = x_even[k], x_odd[k]
         pad[pl.ds(at(c, 0), tall), :] = jnp.where(gx_odd == 0, odd, even)
@@ -509,17 +518,17 @@
     y_face = shape((5, deep, cols), F32)
     kept, *faces = call(
         functools.partial(faces_kernel, two_y),
-        [shape(coarse_fields.shape, F32), x_face, x_face, y_face] + [y_face] * two_y,
+        [shape(coarse_fields.shape, F32), x_face, x_face, y_face] + [y_face] * two_y + [shape((5, tall, cols), F32)],
         [vmem],
     )(coarse_fields)
     got = [
-        lax.ppermute(faces[0], "gx", swap_pairs(count_x, 1)),
-        lax.ppermute(faces[1], "gx", swap_pairs(count_x, 0)),
+        lax.ppermute(faces[0], "gx", swap_pairs(count_x, 0)),
+        lax.ppermute(faces[1], "gx", swap_pairs(count_x, 1)),
         lax.ppermute(faces[2], "gy", swap_pairs(count_y, 0)),
     ]
     if two_y:
         got.append(lax.ppermute(faces[3], "gy", swap_pairs(count_y, 1)))
-    beside = lax.ppermute(kept, "gz", swap_pairs(2, 0))
+    beside = lax.ppermute(faces[-1], "gz", swap_pairs(2, 0))
 
     fine = fine_fields.transpose(0, 1, 3, 2, 4)
     notes, rate = call(

time: 25.7 us -> 25.2 us (0.981)
  the two profiles are of different devices: /device:TPU:0 before, /device:TPU:9 now
where the time goes in v6:
time: 25.2 us; the launch traced here: 25 us
  starting transfers between devices  12.3 us (49%)
  Pallas kernels  6.88 us (27%)
  waiting for transfers between devices  3.99 us (16%)
  local copies, waits for them, and re-layouts  1.1 us (4%)
  between operations  0.78 us (3%)
    ppermute x6, starting transfers between devices, exchange(): got[k] = lax.ppermute(parts[k], ('gy', 'gz'), swaps[k])  5.75 us
    ppermute x1, starting transfers between devices, local(): lax.ppermute(faces[1], 'gx', swap_pairs(count_x, 1))  4.5 us
    ppermute x6, waiting for transfers between devices, exchange(): got[k] = lax.ppermute(parts[k], ('gy', 'gz'), swaps[k])  2.97 us
    pallas_call x1, Pallas kernels, local(): call(functools.partial(leap_kernel, two_y, ranks), [shape(coarse_fields.s...  1.62 us
    pallas_call x1, Pallas kernels, local(): call(functools.partial(fine_kernel, ranks), [shape((groups, 6, ROWS_BOX,...  1.47 us
    pallas_call x1, Pallas kernels, local(): call(store_kernel, shape(fine.shape, F32), [vmem] * 4, [pltpu.VMEM(fine.s...  1.29 us
    ppermute x1, starting transfers between devices, local(): lax.ppermute(faces[2], 'gy', swap_pairs(count_y, 0))  1.28 us
    unnamed x20, local copies, waits for them, and re-layouts  1.1 us
  transfers between devices with their start and end apart: 10, of which 4 were waited for; matrix products, arithmetic and copies ran while one was open for 0% of the time, Pallas kernels for 10%

profile of v6, /device:TPU:9, one launch (start us, length us, event | category | flops | bytes accessed | tf_op | source)
XLA Modules:
  0.0 25.0 jit_solution(6617452814292434517)
XLA Ops:
  0.6 1.1 %copy-done.1 = f32[6,12,12,128]{3,2,1,0:T(8,128)S(1)} copy-done((f32[6,12,12,128]{3,2,1,0:T(8,128)S(1)}, f32[6,12,12,128]{3,2,1,0:T(8,128)}, u32[]{:S(2)}) %copy-start.1) | copy-done | bytes 442392
  1.7 0.2 shard_map.113
  1.9 0.7 %collective-permute-start = (f32[5,12,128]{2,1,0:T(8,128)S(1)}, f32[5,12,128]{2,1,0:T(8,128)S(1)}, u32[]{:S(2)}, u32[]{:S(2)}) collective-permute-start(f32[5,12,128]{2,1,0:T(8,128)S(1)} %get-tuple-element.22), channel_id=1, source_target_pairs={{0,1},{1,0},{2,3},{3,2},{4,5},{5,4},{6,7},{7,6},{8,9},{9,8},{10,11... | collective-permute-start | bytes 92168 | tf_op jit(solution)/shard_map/ppermute | solution.py:531
  2.7 4.5 %collective-permute-start.2 = (f32[5,12,128]{2,1,0:T(8,128)S(1)}, f32[5,12,128]{2,1,0:T(8,128)S(1)}, u32[]{:S(2)}, u32[]{:S(2)}) collective-permute-start(f32[5,12,128]{2,1,0:T(8,128)S(1)} %get-tuple-element.26), channel_id=1, source_target_pairs={{4,8},{8,4},{5,9},{9,5},{6,10},{10,6},{7,11},{11,7},{20,24},{24,20... | collective-permute-start | bytes 92168 | tf_op jit(solution)/shard_map/ppermute | solution.py:526
  7.2 0.0 copy-start.9
  7.2 1.3 %collective-permute-start.3 = (f32[5,12,128]{2,1,0:T(8,128)S(1)}, f32[5,12,128]{2,1,0:T(8,128)S(1)}, u32[]{:S(2)}, u32[]{:S(2)}) collective-permute-start(f32[5,12,128]{2,1,0:T(8,128)S(1)} %get-tuple-element.27), channel_id=1, source_target_pairs={{0,2},{2,0},{1,3},{3,1},{4,6},{6,4},{5,7},{7,5},{8,10},{10,8},{9,1... | collective-permute-start | bytes 92168 | tf_op jit(solution)/shard_map/ppermute | solution.py:527
  8.5 0.6 %shard_map.114 = (s32[12,128]{1,0:T(8,128)S(1)}, f32[12,12,128]{2,1,0:T(8,128)S(1)}) custom-call(s32[1,1,2,3]{3,2,1,0:T(2,128)S(1)} %copy-done.8, s32[1,2,4]{2,1,0:T(2,128)S(1)} %bitcast.5, f32[12,12,128]{2,1,0:T(8,128)S(1)} %copy-done.6), custom_call_target="tpu_custom_call" | custom-call | flops 1000000 | bytes 1000000 | tf_op jit(solution)/shard_map/pallas_call | solution.py:534
  9.1 1.0 %collective-permute-done.3.refs_6_ = f32[5,12,128]{2,1,0:T(8,128)S(1)} collective-permute-done((f32[5,12,128]{2,1,0:T(8,128)S(1)}, f32[5,12,128]{2,1,0:T(8,128)S(1)}, u32[]{:S(2)}, u32[]{:S(2)}) %collective-permute-start.3) | collective-permute-done | bytes 30752 | tf_op jit(solution)/shard_map/ppermute | solution.py:527
  10.1 1.6 %shard_map.115 = (f32[6,12,12,128]{3,2,1,0:T(8,128)S(1)}, f32[72,128]{1,0:T(8,128)S(1)}, f32[72,128]{1,0:T(8,128)S(1)}, f32[72,128]{1,0:T(8,128)S(1)}, f32[104,128]{1,0:T(8,128)S(1)}) custom-call(f32[6,12,12,128]{3,2,1,0:T(8,128)S(1)} %get-tuple-element.21.refs_0_, f32[5,12,128]{2,1,0:T(8,128)S(1)} %collective-permute-done.refs_1_, ...), custom_call_target="tpu_custom_call" | custom-call | flops 1000000 | bytes 1000000 | tf_op jit(solution)/shard_map/pallas_call | solution.py:558
  11.8 1.8 %collective-permute-start.4 = (f32[104,128]{1,0:T(8,128)S(1)}, f32[104,128]{1,0:T(8,128)S(1)}, u32[]{:S(2)}, u32[]{:S(2)}) collective-permute-start(f32[104,128]{1,0:T(8,128)S(1)} %get-tuple-element.29), channel_id=1, source_target_pairs={{0,1},{1,0},{2,3},{3,2},{4,5},{5,4},{6,7},{7,6},{8,9},{9,8},{10,11... | collective-permute-start | bytes 159752 | tf_op jit(solution)/shard_map/ppermute | solution.py:554
  13.6 1.2 %collective-permute-start.5 = (f32[72,128]{1,0:T(8,128)S(1)}, f32[72,128]{1,0:T(8,128)S(1)}, u32[]{:S(2)}, u32[]{:S(2)}) collective-permute-start(f32[72,128]{1,0:T(8,128)S(1)} %get-tuple-element.30), channel_id=1, source_target_pairs={{0,2},{1,3},{2,0},{3,1},{4,6},{5,7},{6,4},{7,5},{8,10},{9,11},{10,... | collective-permute-start | bytes 110600 | tf_op jit(solution)/shard_map/ppermute | solution.py:554
  14.8 0.5 %collective-permute-start.6 = (f32[72,128]{1,0:T(8,128)S(1)}, f32[72,128]{1,0:T(8,128)S(1)}, u32[]{:S(2)}, u32[]{:S(2)}) collective-permute-start(f32[72,128]{1,0:T(8,128)S(1)} %get-tuple-element.31), channel_id=1, source_target_pairs={{0,3},{1,2},{2,1},{3,0},{4,7},{5,6},{6,5},{7,4},{8,11},{9,10},{10,... | collective-permute-start | bytes 110600 | tf_op jit(solution)/shard_map/ppermute | solution.py:554
  15.3 0.6 %shard_map.117 = (f32[1,6,72,384]{3,2,1,0:T(8,128)S(1)}, f32[1,72,384]{2,1,0:T(8,128)S(1)}) custom-call(f32[1,1,6,4,4096]{4,3,2,1,0:T(4,128)S(1)} %bitcast.3, f32[1,1,4,4096]{3,2,1,0:T(4,128)S(1)} %copy-done.7, bf16[256,384]{1,0:T(8,128)(2,1)S(1)} %copy-done.5), custom_call_target="tpu_custom_call" | custom-call | flops 1000000 | bytes 4000000 | tf_op jit(solution)/shard_map/pallas_call | solution.py:539
  15.9 0.5 %collective-permute-done.5.refs_1_.refs_2_ = f32[72,128]{1,0:T(8,128)S(1)} collective-permute-done((f32[72,128]{1,0:T(8,128)S(1)}, f32[72,128]{1,0:T(8,128)S(1)}, u32[]{:S(2)}, u32[]{:S(2)}) %collective-permute-start.5) | collective-permute-done | bytes 36896 | tf_op jit(solution)/shard_map/ppermute | solution.py:554
  16.4 1.8 %collective-permute-done.6.refs_2_.refs_3_ = f32[72,128]{1,0:T(8,128)S(1)} collective-permute-done((f32[72,128]{1,0:T(8,128)S(1)}, f32[72,128]{1,0:T(8,128)S(1)}, u32[]{:S(2)}, u32[]{:S(2)}) %collective-permute-start.6) | collective-permute-done | bytes 36896 | tf_op jit(solution)/shard_map/ppermute | solution.py:554
  18.3 0.0 copy-start.3
  18.3 1.5 %shard_map.118 = (f32[1,6,72,384]{3,2,1,0:T(8,128)S(1)}, f32[24,128]{1,0:T(8,128)S(1)}, f32[24,128]{1,0:T(8,128)S(1)}, f32[24,128]{1,0:T(8,128)S(1)}, f32[24,128]{1,0:T(8,128)S(1)}) custom-call(f32[72,128]{1,0:T(8,128)S(1)} %get-tuple-element.32.refs_0_, f32[104,128]{1,0:T(8,128)S(1)} %collective-permute-done.4.refs_0_.refs_1_, ...), custom_call_target="tpu_custom_call" | custom-call | flops 1000000 | bytes 1000000 | tf_op jit(solution)/shard_map/pallas_call | solution.py:572
  19.8 0.4 %collective-permute-start.7 = (f32[24,128]{1,0:T(8,128)S(1)}, f32[24,128]{1,0:T(8,128)S(1)}, u32[]{:S(2)}, u32[]{:S(2)}) collective-permute-start(f32[24,128]{1,0:T(8,128)S(1)} %get-tuple-element.36), channel_id=1, source_target_pairs={{0,1},{1,0},{2,3},{3,2},{4,5},{5,4},{6,7},{7,6},{8,9},{9,8},{10,11... | collective-permute-start | bytes 36872 | tf_op jit(solution)/shard_map/ppermute | solution.py:554
  20.2 0.6 %collective-permute-start.8 = (f32[24,128]{1,0:T(8,128)S(1)}, f32[24,128]{1,0:T(8,128)S(1)}, u32[]{:S(2)}, u32[]{:S(2)}) collective-permute-start(f32[24,128]{1,0:T(8,128)S(1)} %get-tuple-element.37), channel_id=1, source_target_pairs={{0,2},{1,3},{2,0},{3,1},{4,6},{5,7},{6,4},{7,5},{8,10},{9,11},{10,... | collective-permute-start | bytes 36872 | tf_op jit(solution)/shard_map/ppermute | solution.py:554
  20.8 1.2 %collective-permute-start.9 = (f32[24,128]{1,0:T(8,128)S(1)}, f32[24,128]{1,0:T(8,128)S(1)}, u32[]{:S(2)}, u32[]{:S(2)}) collective-permute-start(f32[24,128]{1,0:T(8,128)S(1)} %get-tuple-element.38), channel_id=1, source_target_pairs={{0,3},{1,2},{2,1},{3,0},{4,7},{5,6},{6,5},{7,4},{8,11},{9,10},{10,... | collective-permute-start | bytes 36872 | tf_op jit(solution)/shard_map/ppermute | solution.py:554
  22.0 1.3 %shard_map.120 = f32[1,1,6,4,4096]{4,3,2,1,0:T(4,128)} custom-call(f32[1,6,72,384]{3,2,1,0:T(8,128)S(1)} %get-tuple-element.39.box, f32[1,1,6,4,4096]{4,3,2,1,0:T(4,128)S(1)} %bitcast.4, s32[12,128]{1,0:T(8,128)S(1)} %get-tuple-element.24.refs_3_.notes, bf16[384,256]{1,0:T(8,128)(2,1)S(1)} %copy-done.3), custom_call_target="tpu_custom_call" | custom-call | flops 1000000 | bytes 4000000 | tf_op jit(solution)/shard_map/pallas_call | solution.py:587
  23.3 0.1 shard_map.116.new
  23.4 0.6 %collective-permute-done.9.refs_3_ = f32[24,128]{1,0:T(8,128)S(1)} collective-permute-done((f32[24,128]{1,0:T(8,128)S(1)}, f32[24,128]{1,0:T(8,128)S(1)}, u32[]{:S(2)}, u32[]{:S(2)}) %collective-permute-start.9) | collective-permute-done | bytes 12320 | tf_op jit(solution)/shard_map/ppermute | solution.py:554
  24.0 1.0 %shard_map.119 = f32[6,12,12,128]{3,2,1,0:T(8,128)} custom-call(f32[6,12,12,128]{3,2,1,0:T(8,128)S(1)} %shard_map.116.new, s32[12,128]{1,0:T(8,128)S(1)} %get-tuple-element.24.refs_3_.notes, f32[24,128]{1,0:T(8,128)S(1)} %get-tuple-element.35.refs_0_, f32[24,128]{1,0:T(8,128)S(1)} %collective-permute-done.7.refs_1_, ...), custom_call_target="tpu_custom_call" | custom-call | flops 1000000 | bytes 1000000 | tf_op jit(solution)/shard_map/pallas_call | solution.py:596
  (24 shorter events, 0.1 us)
Async XLA Ops:
  0.6 1.1 %copy-start.1 = (f32[6,12,12,128]{3,2,1,0:T(8,128)S(1)}, f32[6,12,12,128]{3,2,1,0:T(8,128)}, u32[]{:S(2)}) copy-start(f32[6,12,12,128]{3,2,1,0:T(8,128)} %block.1) | copy-start | bytes 1327108
  1.7 6.8 %copy-start.6 = (f32[12,12,128]{2,1,0:T(8,128)S(1)}, f32[12,12,128]{2,1,0:T(8,128)}, u32[]{:S(2)}) copy-start(f32[12,12,128]{2,1,0:T(8,128)} %perm.2) | copy-start | bytes 221188
  1.9 7.2 %collective-permute-start = (f32[5,12,128]{2,1,0:T(8,128)S(1)}, f32[5,12,128]{2,1,0:T(8,128)S(1)}, u32[]{:S(2)}, u32[]{:S(2)}) collective-permute-start(f32[5,12,128]{2,1,0:T(8,128)S(1)} %get-tuple-element.22), channel_id=1, source_target_pairs={{0,1},{1,0},{2,3},{3,2},{4,5},{5,4},{6,7},{7,6},{8,9},{9,8},{10,11... | collective-permute-start | bytes 92168 | tf_op jit(solution)/shard_map/ppermute | solution.py:531
  2.7 6.4 %collective-permute-start.1 = (f32[5,12,128]{2,1,0:T(8,128)S(1)}, f32[5,12,128]{2,1,0:T(8,128)S(1)}, u32[]{:S(2)}, u32[]{:S(2)}) collective-permute-start(f32[5,12,128]{2,1,0:T(8,128)S(1)} %get-tuple-element.25), channel_id=1, source_target_pairs={{0,4},{4,0},{8,12},{12,8},{1,5},{5,1},{9,13},{13,9},{2,6},{6,2},{1... | collective-permute-start | bytes 92168 | tf_op jit(solution)/shard_map/ppermute | solution.py:525
  2.7 6.4 %collective-permute-start.2 = (f32[5,12,128]{2,1,0:T(8,128)S(1)}, f32[5,12,128]{2,1,0:T(8,128)S(1)}, u32[]{:S(2)}, u32[]{:S(2)}) collective-permute-start(f32[5,12,128]{2,1,0:T(8,128)S(1)} %get-tuple-element.26), channel_id=1, source_target_pairs={{4,8},{8,4},{5,9},{9,5},{6,10},{10,6},{7,11},{11,7},{20,24},{24,20... | collective-permute-start | bytes 92168 | tf_op jit(solution)/shard_map/ppermute | solution.py:526
  7.2 1.3 %copy-start.9 = (s32[1,4,2]{1,2,0:T(2,128)S(1)}, s32[1,4,2]{1,2,0:T(2,128)}, u32[]{:S(2)}) copy-start(s32[1,4,2]{1,2,0:T(2,128)} %param.15) | copy-start | bytes 100
  7.2 1.3 %copy-start.8 = (s32[1,1,2,3]{3,2,1,0:T(2,128)S(1)}, s32[1,1,2,3]{3,2,1,0:T(2,128)}, u32[]{:S(2)}) copy-start(s32[1,1,2,3]{3,2,1,0:T(2,128)} %corner.1) | copy-start | bytes 76
  7.2 2.9 %collective-permute-start.3 = (f32[5,12,128]{2,1,0:T(8,128)S(1)}, f32[5,12,128]{2,1,0:T(8,128)S(1)}, u32[]{:S(2)}, u32[]{:S(2)}) collective-permute-start(f32[5,12,128]{2,1,0:T(8,128)S(1)} %get-tuple-element.27), channel_id=1, source_target_pairs={{0,2},{2,0},{1,3},{3,1},{4,6},{6,4},{5,7},{7,5},{8,10},{10,8},{9,1... | collective-permute-start | bytes 92168 | tf_op jit(solution)/shard_map/ppermute | solution.py:527
  10.1 5.2 %copy-start = (f32[1,1,4,6,4096]{4,2,3,1,0:T(4,128)S(1)}, f32[1,1,4,6,4096]{4,2,3,1,0:T(4,128)}, u32[]{:S(2)}) copy-start(f32[1,1,4,6,4096]{4,2,3,1,0:T(4,128)} %param.12) | copy-start | bytes 1179652
  10.1 5.2 %copy-start.5 = (bf16[256,384]{1,0:T(8,128)(2,1)S(1)}, bf16[256,384]{1,0:T(8,128)(2,1)}, u32[]{:S(2)}) copy-start(bf16[256,384]{1,0:T(8,128)(2,1)} %constant.8.clone.table) | copy-start | bytes 589828
  10.1 5.2 %copy-start.7 = (f32[1,1,4,4096]{3,2,1,0:T(4,128)S(1)}, f32[1,1,4,4096]{3,2,1,0:T(4,128)}, u32[]{:S(2)}) copy-start(f32[1,1,4,4096]{3,2,1,0:T(4,128)} %perm.3) | copy-start | bytes 196612
  11.8 6.5 %copy-start.2 = (bf16[2,256,384]{2,1,0:T(8,128)(2,1)S(1)}, bf16[2,256,384]{2,1,0:T(8,128)(2,1)}, u32[]{:S(2)}) copy-start(bf16[2,256,384]{2,1,0:T(8,128)(2,1)} %constant.9.clone.refs_6_) | copy-start | bytes 1179652
  11.8 6.5 %collective-permute-start.4 = (f32[104,128]{1,0:T(8,128)S(1)}, f32[104,128]{1,0:T(8,128)S(1)}, u32[]{:S(2)}, u32[]{:S(2)}) collective-permute-start(f32[104,128]{1,0:T(8,128)S(1)} %get-tuple-element.29), channel_id=1, source_target_pairs={{0,1},{1,0},{2,3},{3,2},{4,5},{5,4},{6,7},{7,6},{8,9},{9,8},{10,11... | collective-permute-start | bytes 159752 | tf_op jit(solution)/shard_map/ppermute | solution.py:554
  13.6 2.8 %collective-permute-start.5 = (f32[72,128]{1,0:T(8,128)S(1)}, f32[72,128]{1,0:T(8,128)S(1)}, u32[]{:S(2)}, u32[]{:S(2)}) collective-permute-start(f32[72,128]{1,0:T(8,128)S(1)} %get-tuple-element.30), channel_id=1, source_target_pairs={{0,2},{1,3},{2,0},{3,1},{4,6},{5,7},{6,4},{7,5},{8,10},{9,11},{10,... | collective-permute-start | bytes 110600 | tf_op jit(solution)/shard_map/ppermute | solution.py:554
  14.8 3.4 %collective-permute-start.6 = (f32[72,128]{1,0:T(8,128)S(1)}, f32[72,128]{1,0:T(8,128)S(1)}, u32[]{:S(2)}, u32[]{:S(2)}) collective-permute-start(f32[72,128]{1,0:T(8,128)S(1)} %get-tuple-element.31), channel_id=1, source_target_pairs={{0,3},{1,2},{2,1},{3,0},{4,7},{5,6},{6,5},{7,4},{8,11},{9,10},{10,... | collective-permute-start | bytes 110600 | tf_op jit(solution)/shard_map/ppermute | solution.py:554
  15.3 3.0 %copy-start.4 = (bf16[768,128]{1,0:T(8,128)(2,1)S(1)}, bf16[768,128]{1,0:T(8,128)(2,1)}, u32[]{:S(2)}) copy-start(bf16[768,128]{1,0:T(8,128)(2,1)} %constant.10.clone.refs_7_) | copy-start | bytes 589828
  18.3 3.7 %copy-start.3 = (bf16[384,256]{1,0:T(8,128)(2,1)S(1)}, bf16[384,256]{1,0:T(8,128)(2,1)}, u32[]{:S(2)}) copy-start(bf16[384,256]{1,0:T(8,128)(2,1)} %constant.11.clone.table) | copy-start | bytes 589828
  19.8 3.6 %collective-permute-start.7 = (f32[24,128]{1,0:T(8,128)S(1)}, f32[24,128]{1,0:T(8,128)S(1)}, u32[]{:S(2)}, u32[]{:S(2)}) collective-permute-start(f32[24,128]{1,0:T(8,128)S(1)} %get-tuple-element.36), channel_id=1, source_target_pairs={{0,1},{1,0},{2,3},{3,2},{4,5},{5,4},{6,7},{7,6},{8,9},{9,8},{10,11... | collective-permute-start | bytes 36872 | tf_op jit(solution)/shard_map/ppermute | solution.py:554
  20.2 3.2 %collective-permute-start.8 = (f32[24,128]{1,0:T(8,128)S(1)}, f32[24,128]{1,0:T(8,128)S(1)}, u32[]{:S(2)}, u32[]{:S(2)}) collective-permute-start(f32[24,128]{1,0:T(8,128)S(1)} %get-tuple-element.37), channel_id=1, source_target_pairs={{0,2},{1,3},{2,0},{3,1},{4,6},{5,7},{6,4},{7,5},{8,10},{9,11},{10,... | collective-permute-start | bytes 36872 | tf_op jit(solution)/shard_map/ppermute | solution.py:554
  20.8 3.2 %collective-permute-start.9 = (f32[24,128]{1,0:T(8,128)S(1)}, f32[24,128]{1,0:T(8,128)S(1)}, u32[]{:S(2)}, u32[]{:S(2)}) collective-permute-start(f32[24,128]{1,0:T(8,128)S(1)} %get-tuple-element.38), channel_id=1, source_target_pairs={{0,3},{1,2},{2,1},{3,0},{4,7},{5,6},{6,5},{7,4},{8,11},{9,10},{10,... | collective-permute-start | bytes 36872 | tf_op jit(solution)/shard_map/ppermute | solution.py:554

commit v7 on v4

--- a/solution.py
+++ b/solution.py
@@ -102,6 +102,18 @@
     return pairs
 
 
+def full_pairs(count_x, count_y):
+    pairs = []
+    for i in range(count_x):
+        for j in range(count_y):
+            if 0 < i < count_x - 1:
+                target = (i + 1 if i % 2 else i - 1) * count_y + j
+            else:
+                target = i * count_y + (j ^ 1)
+            pairs.append((i * count_y + j, target))
+    return pairs
+
+
 def faces_kernel(two_y, block, kept, x_even, x_odd, y_even, *y_odd):
     deep, tall = block.shape[1], block.shape[2]
     gx_odd = lax.rem(lax.axis_index("gx"), 2)
@@ -143,7 +155,8 @@
     pad, side, mag, fresh, packed = refs[1 + ranks :]
     deep, tall = block.shape[1], block.shape[2]
     full = deep + 2
-    gx_odd = lax.rem(lax.axis_index("gx"), 2)
+    gx = lax.axis_index("gx")
+    gx_odd = lax.rem(gx, 2)
     gy_odd = lax.rem(lax.axis_index("gy"), 2)
     gz = lax.axis_index("gz")
     noted = notes[0:8, :]
@@ -172,9 +185,10 @@
             side[pl.ds(at(c, x + 1), tall), :] = jnp.where(keep, beside[c, x], 0.0)
     for k, c in enumerate(X_COMPS):
         even, odd = x_even[k], x_odd[k]
-        pad[pl.ds(at(c, 0), tall), :] = jnp.where(gx_odd == 0, odd, even)
+        low, high = jnp.where(gx_odd == 0, odd, even), jnp.where(gx_odd == 0, even, odd)
+        pad[pl.ds(at(c, 0), tall), :] = jnp.where(gx == 0, 0.0, low)
         if c in (1, 2):
-            pad[pl.ds(at(c, full - 1), tall), :] = jnp.where(gx_odd == 0, even, odd)
+            pad[pl.ds(at(c, full - 1), tall), :] = jnp.where(gx == lax.axis_size("gx") - 1, 0.0, high)
     for k, c in enumerate(Y_COMPS):
         even = y_even[k]
         odd = jnp.zeros_like(even) if y_odd is None else y_odd[k]
@@ -506,7 +520,7 @@
     )(coarse_fields)
     got = [
         lax.ppermute(faces[0], "gx", swap_pairs(count_x, 0)),
-        lax.ppermute(faces[1], "gx", swap_pairs(count_x, 1)),
+        lax.ppermute(faces[1], ("gx", "gy"), full_pairs(count_x, count_y)),
         lax.ppermute(faces[2], "gy", swap_pairs(count_y, 0)),
     ]
     if two_y:

time: 24.6 us -> 23.3 us (0.947)
  the two profiles are of different devices: /device:TPU:9 before, /device:TPU:0 now
where the time goes in v7:
time: 23.3 us; the launch traced here: 23.1 us
  starting transfers between devices  9.05 us (39%)
  Pallas kernels  6.24 us (27%)
  waiting for transfers between devices  5.79 us (25%)
  local copies, waits for them, and re-layouts  1.24 us (5%)
  between operations  0.75 us (3%)
    ppermute x6, starting transfers between devices, exchange(): got[k] = lax.ppermute(parts[k], ('gy', 'gz'), swaps[k])  3.86 us
    ppermute x6, waiting for transfers between devices, exchange(): got[k] = lax.ppermute(parts[k], ('gy', 'gz'), swaps[k])  3.07 us
    ppermute x1, starting transfers between devices, local(): lax.ppermute(faces[0], 'gx', swap_pairs(count_x, 0))  2.65 us
    ppermute x1, starting transfers between devices, local(): lax.ppermute(faces[1], ('gx', 'gy'), full_pairs(count_x, count_y))  1.49 us
    pallas_call x1, Pallas kernels, local(): call(functools.partial(fine_kernel, ranks), [shape((groups, 6, ROWS_BOX,...  1.48 us
    ppermute x1, waiting for transfers between devices, local(): lax.ppermute(faces[2], 'gy', swap_pairs(count_y, 0))  1.39 us
    ppermute x1, waiting for transfers between devices, local(): lax.ppermute(faces[1], ('gx', 'gy'), full_pairs(count_x, count_y))  1.32 us
    pallas_call x1, Pallas kernels, local(): call(store_kernel, shape(fine.shape, F32), [vmem] * 4, [pltpu.VMEM(fine.s...  1.29 us
  transfers between devices with their start and end apart: 10, of which 5 were waited for; matrix products, arithmetic and copies ran while one was open for 0% of the time, Pallas kernels for 11%

profile of v7, /device:TPU:0, one launch (start us, length us, event | category | flops | bytes accessed | tf_op | source)
XLA Modules:
  0.0 23.1 jit_solution(15242795745624194199)
XLA Ops:
  0.6 1.1 %copy-done.1 = f32[6,12,12,128]{3,2,1,0:T(8,128)S(1)} copy-done((f32[6,12,12,128]{3,2,1,0:T(8,128)S(1)}, f32[6,12,12,128]{3,2,1,0:T(8,128)}, u32[]{:S(2)}) %copy-start.1) | copy-done | bytes 442392
  1.7 0.1 shard_map.113
  1.8 0.5 %collective-permute-start = (f32[6,12,12,128]{3,2,1,0:T(8,128)S(1)}, f32[6,12,12,128]{3,2,1,0:T(8,128)S(1)}, u32[]{:S(2)}, u32[]{:S(2)}) collective-permute-start(f32[6,12,12,128]{3,2,1,0:T(8,128)S(1)} %get-tuple-element.20.refs_0_), channel_id=1, source_target_pairs={{0,1},{1,0},{2,3},{3,2},{4,5},{5,4},{6,7},{7,6},{8,9},{9,8},{10,11... | collective-permute-start | bytes 1327112 | tf_op jit(solution)/shard_map/ppermute | solution.py:528
  2.3 2.6 %collective-permute-start.1 = (f32[5,12,128]{2,1,0:T(8,128)S(1)}, f32[5,12,128]{2,1,0:T(8,128)S(1)}, u32[]{:S(2)}, u32[]{:S(2)}) collective-permute-start(f32[5,12,128]{2,1,0:T(8,128)S(1)} %get-tuple-element.23), channel_id=1, source_target_pairs={{0,4},{4,0},{8,12},{12,8},{1,5},{5,1},{9,13},{13,9},{2,6},{6,2},{1... | collective-permute-start | bytes 92168 | tf_op jit(solution)/shard_map/ppermute | solution.py:522
  4.9 1.5 %collective-permute-start.2 = (f32[5,12,128]{2,1,0:T(8,128)S(1)}, f32[5,12,128]{2,1,0:T(8,128)S(1)}, u32[]{:S(2)}, u32[]{:S(2)}) collective-permute-start(f32[5,12,128]{2,1,0:T(8,128)S(1)} %get-tuple-element.24), channel_id=1, source_target_pairs={{0,2},{2,0},{4,8},{6,10},{8,4},{10,6},{12,14},{14,12},{1,3},{3,1},... | collective-permute-start | bytes 92168 | tf_op jit(solution)/shard_map/ppermute | solution.py:523
  6.4 0.5 %collective-permute-start.3 = (f32[5,12,128]{2,1,0:T(8,128)S(1)}, f32[5,12,128]{2,1,0:T(8,128)S(1)}, u32[]{:S(2)}, u32[]{:S(2)}) collective-permute-start(f32[5,12,128]{2,1,0:T(8,128)S(1)} %get-tuple-element.25), channel_id=1, source_target_pairs={{0,2},{2,0},{1,3},{3,1},{4,6},{6,4},{5,7},{7,5},{8,10},{10,8},{9,1... | collective-permute-start | bytes 92168 | tf_op jit(solution)/shard_map/ppermute | solution.py:524
  7.0 0.1 copy-done.9
  7.1 0.6 %shard_map.114 = (s32[12,128]{1,0:T(8,128)S(1)}, f32[12,12,128]{2,1,0:T(8,128)S(1)}) custom-call(s32[1,1,2,3]{3,2,1,0:T(2,128)S(1)} %copy-done.8, s32[1,2,4]{2,1,0:T(2,128)S(1)} %bitcast.5, f32[12,12,128]{2,1,0:T(8,128)S(1)} %copy-done.6), custom_call_target="tpu_custom_call" | custom-call | flops 1000000 | bytes 1000000 | tf_op jit(solution)/shard_map/pallas_call | solution.py:531
  7.7 1.3 %collective-permute-done.2.refs_5_ = f32[5,12,128]{2,1,0:T(8,128)S(1)} collective-permute-done((f32[5,12,128]{2,1,0:T(8,128)S(1)}, f32[5,12,128]{2,1,0:T(8,128)S(1)}, u32[]{:S(2)}, u32[]{:S(2)}) %collective-permute-start.2) | collective-permute-done | bytes 30752 | tf_op jit(solution)/shard_map/ppermute | solution.py:523
  9.1 1.4 %collective-permute-done.3.refs_6_ = f32[5,12,128]{2,1,0:T(8,128)S(1)} collective-permute-done((f32[5,12,128]{2,1,0:T(8,128)S(1)}, f32[5,12,128]{2,1,0:T(8,128)S(1)}, u32[]{:S(2)}, u32[]{:S(2)}) %collective-permute-start.3) | collective-permute-done | bytes 30752 | tf_op jit(solution)/shard_map/ppermute | solution.py:524
  10.5 1.1 %shard_map.115 = (f32[6,12,12,128]{3,2,1,0:T(8,128)S(1)}, f32[72,128]{1,0:T(8,128)S(1)}, f32[104,128]{1,0:T(8,128)S(1)}, f32[72,128]{1,0:T(8,128)S(1)}, f32[72,128]{1,0:T(8,128)S(1)}) custom-call(f32[6,12,12,128]{3,2,1,0:T(8,128)S(1)} %get-tuple-element.20.refs_0_, f32[6,12,12,128]{3,2,1,0:T(8,128)S(1)} %collective-permute-done.refs_1_, ...), custom_call_target="tpu_custom_call" | custom-call | flops 1000000 | bytes 1000000 | tf_op jit(solution)/shard_map/pallas_call | solution.py:555
  11.7 0.6 %collective-permute-start.5 = (f32[72,128]{1,0:T(8,128)S(1)}, f32[72,128]{1,0:T(8,128)S(1)}, u32[]{:S(2)}, u32[]{:S(2)}) collective-permute-start(f32[72,128]{1,0:T(8,128)S(1)} %get-tuple-element.28), channel_id=1, source_target_pairs={{0,2},{1,3},{2,0},{3,1},{4,6},{5,7},{6,4},{7,5},{8,10},{9,11},{10,... | collective-permute-start | bytes 110600 | tf_op jit(solution)/shard_map/ppermute | solution.py:551
  12.3 1.3 %collective-permute-start.6 = (f32[72,128]{1,0:T(8,128)S(1)}, f32[72,128]{1,0:T(8,128)S(1)}, u32[]{:S(2)}, u32[]{:S(2)}) collective-permute-start(f32[72,128]{1,0:T(8,128)S(1)} %get-tuple-element.29), channel_id=1, source_target_pairs={{0,3},{1,2},{2,1},{3,0},{4,7},{5,6},{6,5},{7,4},{8,11},{9,10},{10,... | collective-permute-start | bytes 110600 | tf_op jit(solution)/shard_map/ppermute | solution.py:551
  13.6 0.6 %shard_map.117 = (f32[1,6,72,384]{3,2,1,0:T(8,128)S(1)}, f32[1,72,384]{2,1,0:T(8,128)S(1)}) custom-call(f32[1,1,6,4,4096]{4,3,2,1,0:T(4,128)S(1)} %bitcast.3, f32[1,1,4,4096]{3,2,1,0:T(4,128)S(1)} %copy-done.7, bf16[256,384]{1,0:T(8,128)(2,1)S(1)} %copy-done.5), custom_call_target="tpu_custom_call" | custom-call | flops 1000000 | bytes 4000000 | tf_op jit(solution)/shard_map/pallas_call | solution.py:536
  14.2 1.9 %collective-permute-done.5.refs_1_.refs_2_ = f32[72,128]{1,0:T(8,128)S(1)} collective-permute-done((f32[72,128]{1,0:T(8,128)S(1)}, f32[72,128]{1,0:T(8,128)S(1)}, u32[]{:S(2)}, u32[]{:S(2)}) %collective-permute-start.5) | collective-permute-done | bytes 36896 | tf_op jit(solution)/shard_map/ppermute | solution.py:551
  16.1 1.5 %shard_map.118 = (f32[1,6,72,384]{3,2,1,0:T(8,128)S(1)}, f32[24,128]{1,0:T(8,128)S(1)}, f32[24,128]{1,0:T(8,128)S(1)}, f32[24,128]{1,0:T(8,128)S(1)}, f32[24,128]{1,0:T(8,128)S(1)}) custom-call(f32[72,128]{1,0:T(8,128)S(1)} %get-tuple-element.30.refs_0_, f32[104,128]{1,0:T(8,128)S(1)} %collective-permute-done.4.refs_0_.refs_1_, ...), custom_call_target="tpu_custom_call" | custom-call | flops 1000000 | bytes 1000000 | tf_op jit(solution)/shard_map/pallas_call | solution.py:569
  17.6 0.3 %collective-permute-start.7 = (f32[24,128]{1,0:T(8,128)S(1)}, f32[24,128]{1,0:T(8,128)S(1)}, u32[]{:S(2)}, u32[]{:S(2)}) collective-permute-start(f32[24,128]{1,0:T(8,128)S(1)} %get-tuple-element.34), channel_id=1, source_target_pairs={{0,1},{1,0},{2,3},{3,2},{4,5},{5,4},{6,7},{7,6},{8,9},{9,8},{10,11... | collective-permute-start | bytes 36872 | tf_op jit(solution)/shard_map/ppermute | solution.py:551
  17.9 1.1 %collective-permute-start.8 = (f32[24,128]{1,0:T(8,128)S(1)}, f32[24,128]{1,0:T(8,128)S(1)}, u32[]{:S(2)}, u32[]{:S(2)}) collective-permute-start(f32[24,128]{1,0:T(8,128)S(1)} %get-tuple-element.35), channel_id=1, source_target_pairs={{0,2},{1,3},{2,0},{3,1},{4,6},{5,7},{6,4},{7,5},{8,10},{9,11},{10,... | collective-permute-start | bytes 36872 | tf_op jit(solution)/shard_map/ppermute | solution.py:551
  19.0 0.6 %collective-permute-start.9 = (f32[24,128]{1,0:T(8,128)S(1)}, f32[24,128]{1,0:T(8,128)S(1)}, u32[]{:S(2)}, u32[]{:S(2)}) collective-permute-start(f32[24,128]{1,0:T(8,128)S(1)} %get-tuple-element.36), channel_id=1, source_target_pairs={{0,3},{1,2},{2,1},{3,0},{4,7},{5,6},{6,5},{7,4},{8,11},{9,10},{10,... | collective-permute-start | bytes 36872 | tf_op jit(solution)/shard_map/ppermute | solution.py:551
  19.5 1.3 %shard_map.120 = f32[1,1,6,4,4096]{4,3,2,1,0:T(4,128)} custom-call(f32[1,6,72,384]{3,2,1,0:T(8,128)S(1)} %get-tuple-element.37.box, f32[1,1,6,4,4096]{4,3,2,1,0:T(4,128)S(1)} %bitcast.4, s32[12,128]{1,0:T(8,128)S(1)} %get-tuple-element.22.refs_3_.notes, bf16[384,256]{1,0:T(8,128)(2,1)S(1)} %copy-done.3), custom_call_target="tpu_custom_call" | custom-call | flops 1000000 | bytes 4000000 | tf_op jit(solution)/shard_map/pallas_call | solution.py:584
  20.8 0.1 shard_map.116.new
  20.9 0.6 %collective-permute-done.8.refs_2_ = f32[24,128]{1,0:T(8,128)S(1)} collective-permute-done((f32[24,128]{1,0:T(8,128)S(1)}, f32[24,128]{1,0:T(8,128)S(1)}, u32[]{:S(2)}, u32[]{:S(2)}) %collective-permute-start.8) | collective-permute-done | bytes 12320 | tf_op jit(solution)/shard_map/ppermute | solution.py:551
  21.5 0.5 %collective-permute-done.9.refs_3_ = f32[24,128]{1,0:T(8,128)S(1)} collective-permute-done((f32[24,128]{1,0:T(8,128)S(1)}, f32[24,128]{1,0:T(8,128)S(1)}, u32[]{:S(2)}, u32[]{:S(2)}) %collective-permute-start.9) | collective-permute-done | bytes 12320 | tf_op jit(solution)/shard_map/ppermute | solution.py:551
  22.1 1.0 %shard_map.119 = f32[6,12,12,128]{3,2,1,0:T(8,128)} custom-call(f32[6,12,12,128]{3,2,1,0:T(8,128)S(1)} %shard_map.116.new, s32[12,128]{1,0:T(8,128)S(1)} %get-tuple-element.22.refs_3_.notes, f32[24,128]{1,0:T(8,128)S(1)} %get-tuple-element.33.refs_0_, f32[24,128]{1,0:T(8,128)S(1)} %collective-permute-done.7.refs_1_, ...), custom_call_target="tpu_custom_call" | custom-call | flops 1000000 | bytes 1000000 | tf_op jit(solution)/shard_map/pallas_call | solution.py:593
  (24 shorter events, 0.1 us)
Async XLA Ops:
  0.6 1.1 %copy-start.1 = (f32[6,12,12,128]{3,2,1,0:T(8,128)S(1)}, f32[6,12,12,128]{3,2,1,0:T(8,128)}, u32[]{:S(2)}) copy-start(f32[6,12,12,128]{3,2,1,0:T(8,128)} %block.1) | copy-start | bytes 1327108
  1.7 5.3 %copy-start.6 = (f32[12,12,128]{2,1,0:T(8,128)S(1)}, f32[12,12,128]{2,1,0:T(8,128)}, u32[]{:S(2)}) copy-start(f32[12,12,128]{2,1,0:T(8,128)} %perm.2) | copy-start | bytes 221188
  1.8 8.7 %collective-permute-start = (f32[6,12,12,128]{3,2,1,0:T(8,128)S(1)}, f32[6,12,12,128]{3,2,1,0:T(8,128)S(1)}, u32[]{:S(2)}, u32[]{:S(2)}) collective-permute-start(f32[6,12,12,128]{3,2,1,0:T(8,128)S(1)} %get-tuple-element.20.refs_0_), channel_id=1, source_target_pairs={{0,1},{1,0},{2,3},{3,2},{4,5},{5,4},{6,7},{7,6},{8,9},{9,8},{10,11... | collective-permute-start | bytes 1327112 | tf_op jit(solution)/shard_map/ppermute | solution.py:528
  2.3 5.4 %collective-permute-start.1 = (f32[5,12,128]{2,1,0:T(8,128)S(1)}, f32[5,12,128]{2,1,0:T(8,128)S(1)}, u32[]{:S(2)}, u32[]{:S(2)}) collective-permute-start(f32[5,12,128]{2,1,0:T(8,128)S(1)} %get-tuple-element.23), channel_id=1, source_target_pairs={{0,4},{4,0},{8,12},{12,8},{1,5},{5,1},{9,13},{13,9},{2,6},{6,2},{1... | collective-permute-start | bytes 92168 | tf_op jit(solution)/shard_map/ppermute | solution.py:522
  4.9 4.1 %collective-permute-start.2 = (f32[5,12,128]{2,1,0:T(8,128)S(1)}, f32[5,12,128]{2,1,0:T(8,128)S(1)}, u32[]{:S(2)}, u32[]{:S(2)}) collective-permute-start(f32[5,12,128]{2,1,0:T(8,128)S(1)} %get-tuple-element.24), channel_id=1, source_target_pairs={{0,2},{2,0},{4,8},{6,10},{8,4},{10,6},{12,14},{14,12},{1,3},{3,1},... | collective-permute-start | bytes 92168 | tf_op jit(solution)/shard_map/ppermute | solution.py:523
  6.4 0.7 %copy-start.9 = (s32[1,4,2]{1,2,0:T(2,128)S(1)}, s32[1,4,2]{1,2,0:T(2,128)}, u32[]{:S(2)}) copy-start(s32[1,4,2]{1,2,0:T(2,128)} %param.15) | copy-start | bytes 100
  6.4 0.7 %copy-start.8 = (s32[1,1,2,3]{3,2,1,0:T(2,128)S(1)}, s32[1,1,2,3]{3,2,1,0:T(2,128)}, u32[]{:S(2)}) copy-start(s32[1,1,2,3]{3,2,1,0:T(2,128)} %corner.1) | copy-start | bytes 76
  6.4 4.0 %collective-permute-start.3 = (f32[5,12,128]{2,1,0:T(8,128)S(1)}, f32[5,12,128]{2,1,0:T(8,128)S(1)}, u32[]{:S(2)}, u32[]{:S(2)}) collective-permute-start(f32[5,12,128]{2,1,0:T(8,128)S(1)} %get-tuple-element.25), channel_id=1, source_target_pairs={{0,2},{2,0},{1,3},{3,1},{4,6},{6,4},{5,7},{7,5},{8,10},{10,8},{9,1... | collective-permute-start | bytes 92168 | tf_op jit(solution)/shard_map/ppermute | solution.py:524
  10.4 3.1 %copy-start = (f32[1,1,4,6,4096]{4,2,3,1,0:T(4,128)S(1)}, f32[1,1,4,6,4096]{4,2,3,1,0:T(4,128)}, u32[]{:S(2)}) copy-start(f32[1,1,4,6,4096]{4,2,3,1,0:T(4,128)} %param.12) | copy-start | bytes 1179652
  10.5 3.1 %copy-start.5 = (bf16[256,384]{1,0:T(8,128)(2,1)S(1)}, bf16[256,384]{1,0:T(8,128)(2,1)}, u32[]{:S(2)}) copy-start(bf16[256,384]{1,0:T(8,128)(2,1)} %constant.8.clone.table) | copy-start | bytes 589828
  10.5 3.1 %copy-start.7 = (f32[1,1,4,4096]{3,2,1,0:T(4,128)S(1)}, f32[1,1,4,4096]{3,2,1,0:T(4,128)}, u32[]{:S(2)}) copy-start(f32[1,1,4,4096]{3,2,1,0:T(4,128)} %perm.3) | copy-start | bytes 196612
  11.6 4.5 %copy-start.2 = (bf16[2,256,384]{2,1,0:T(8,128)(2,1)S(1)}, bf16[2,256,384]{2,1,0:T(8,128)(2,1)}, u32[]{:S(2)}) copy-start(bf16[2,256,384]{2,1,0:T(8,128)(2,1)} %constant.9.clone.refs_6_) | copy-start | bytes 1179652
  11.6 4.5 %collective-permute-start.4 = (f32[104,128]{1,0:T(8,128)S(1)}, f32[104,128]{1,0:T(8,128)S(1)}, u32[]{:S(2)}, u32[]{:S(2)}) collective-permute-start(f32[104,128]{1,0:T(8,128)S(1)} %get-tuple-element.27), channel_id=1, source_target_pairs={{0,1},{1,0},{2,3},{3,2},{4,5},{5,4},{6,7},{7,6},{8,9},{9,8},{10,11... | collective-permute-start | bytes 159752 | tf_op jit(solution)/shard_map/ppermute | solution.py:551
  11.7 4.4 %collective-permute-start.5 = (f32[72,128]{1,0:T(8,128)S(1)}, f32[72,128]{1,0:T(8,128)S(1)}, u32[]{:S(2)}, u32[]{:S(2)}) collective-permute-start(f32[72,128]{1,0:T(8,128)S(1)} %get-tuple-element.28), channel_id=1, source_target_pairs={{0,2},{1,3},{2,0},{3,1},{4,6},{5,7},{6,4},{7,5},{8,10},{9,11},{10,... | collective-permute-start | bytes 110600 | tf_op jit(solution)/shard_map/ppermute | solution.py:551
  12.3 3.8 %collective-permute-start.6 = (f32[72,128]{1,0:T(8,128)S(1)}, f32[72,128]{1,0:T(8,128)S(1)}, u32[]{:S(2)}, u32[]{:S(2)}) collective-permute-start(f32[72,128]{1,0:T(8,128)S(1)} %get-tuple-element.29), channel_id=1, source_target_pairs={{0,3},{1,2},{2,1},{3,0},{4,7},{5,6},{6,5},{7,4},{8,11},{9,10},{10,... | collective-permute-start | bytes 110600 | tf_op jit(solution)/shard_map/ppermute | solution.py:551
  13.6 2.5 %copy-start.4 = (bf16[768,128]{1,0:T(8,128)(2,1)S(1)}, bf16[768,128]{1,0:T(8,128)(2,1)}, u32[]{:S(2)}) copy-start(bf16[768,128]{1,0:T(8,128)(2,1)} %constant.10.clone.refs_7_) | copy-start | bytes 589828
  16.1 3.4 %copy-start.3 = (bf16[384,256]{1,0:T(8,128)(2,1)S(1)}, bf16[384,256]{1,0:T(8,128)(2,1)}, u32[]{:S(2)}) copy-start(bf16[384,256]{1,0:T(8,128)(2,1)} %constant.11.clone.table) | copy-start | bytes 589828
  17.6 3.3 %collective-permute-start.7 = (f32[24,128]{1,0:T(8,128)S(1)}, f32[24,128]{1,0:T(8,128)S(1)}, u32[]{:S(2)}, u32[]{:S(2)}) collective-permute-start(f32[24,128]{1,0:T(8,128)S(1)} %get-tuple-element.34), channel_id=1, source_target_pairs={{0,1},{1,0},{2,3},{3,2},{4,5},{5,4},{6,7},{7,6},{8,9},{9,8},{10,11... | collective-permute-start | bytes 36872 | tf_op jit(solution)/shard_map/ppermute | solution.py:551
  17.9 3.7 %collective-permute-start.8 = (f32[24,128]{1,0:T(8,128)S(1)}, f32[24,128]{1,0:T(8,128)S(1)}, u32[]{:S(2)}, u32[]{:S(2)}) collective-permute-start(f32[24,128]{1,0:T(8,128)S(1)} %get-tuple-element.35), channel_id=1, source_target_pairs={{0,2},{1,3},{2,0},{3,1},{4,6},{5,7},{6,4},{7,5},{8,10},{9,11},{10,... | collective-permute-start | bytes 36872 | tf_op jit(solution)/shard_map/ppermute | solution.py:551
  19.0 3.1 %collective-permute-start.9 = (f32[24,128]{1,0:T(8,128)S(1)}, f32[24,128]{1,0:T(8,128)S(1)}, u32[]{:S(2)}, u32[]{:S(2)}) collective-permute-start(f32[24,128]{1,0:T(8,128)S(1)} %get-tuple-element.36), channel_id=1, source_target_pairs={{0,3},{1,2},{2,1},{3,0},{4,7},{5,6},{6,5},{7,4},{8,11},{9,10},{10,... | collective-permute-start | bytes 36872 | tf_op jit(solution)/shard_map/ppermute | solution.py:551

commit v8 on v7

--- a/solution.py
+++ b/solution.py
@@ -102,19 +102,19 @@
     return pairs
 
 
-def full_pairs(count_x, count_y):
+def full_pairs(count_x):
     pairs = []
     for i in range(count_x):
-        for j in range(count_y):
+        for j in range(2):
             if 0 < i < count_x - 1:
-                target = (i + 1 if i % 2 else i - 1) * count_y + j
+                target = (i + 1 if i % 2 else i - 1) * 2 + j
             else:
-                target = i * count_y + (j ^ 1)
-            pairs.append((i * count_y + j, target))
+                target = i * 2 + 1 - j
+            pairs.append((i * 2 + j, target))
     return pairs
 
 
-def faces_kernel(two_y, block, kept, x_even, x_odd, y_even, *y_odd):
+def faces_kernel(two_y, block, kept, x_even, y_even, x_odd, *y_odd):
     deep, tall = block.shape[1], block.shape[2]
     gx_odd = lax.rem(lax.axis_index("gx"), 2)
     gy_odd = lax.rem(lax.axis_index("gy"), 2)
@@ -148,7 +148,7 @@
 
 
 def leap_kernel(two_y, ranks, *refs):
-    block, beside, rate, notes, x_even, x_odd, y_even = refs[:7]
+    block, beside, rate, notes, x_even, y_even, x_odd = refs[:7]
     y_odd = refs[7] if two_y else None
     refs = refs[7 + two_y :]
     new, sends = refs[0], refs[1 : 1 + ranks]
@@ -515,13 +515,13 @@
     y_face = shape((5, deep, cols), F32)
     kept, *faces = call(
         functools.partial(faces_kernel, two_y),
-        [shape(coarse_fields.shape, F32), x_face, x_face, y_face] + [y_face] * two_y,
+        [shape(coarse_fields.shape, F32), x_face, y_face, x_face] + [y_face] * two_y,
         [vmem],
     )(coarse_fields)
     got = [
         lax.ppermute(faces[0], "gx", swap_pairs(count_x, 0)),
-        lax.ppermute(faces[1], ("gx", "gy"), full_pairs(count_x, count_y)),
-        lax.ppermute(faces[2], "gy", swap_pairs(count_y, 0)),
+        lax.ppermute(faces[1], "gy", swap_pairs(count_y, 0)),
+        lax.ppermute(faces[2], ("gx", "gz"), full_pairs(count_x)),
     ]
     if two_y:
         got.append(lax.ppermute(faces[3], "gy", swap_pairs(count_y, 1)))

time: 23.3 us -> 22.2 us (0.953)
  waiting for transfers between devices: 5.79 us -> 4.7 us
  local copies, waits for them, and re-layouts: 1.24 us -> 1.78 us
  starting transfers between devices: 9.05 us -> 8.52 us
    ppermute x2, waiting for transfers between devices: 2.71 us -> 1.22 us  [the longest x1 1.22 us: local(): lax.ppermute(faces[1], 'gy', swap_pairs(count_y, 0))]
    unnamed x20, local copies, waits for them, and re-layouts: 1.24 us -> 1.78 us
    ppermute x2, starting transfers between devices: 2.03 us -> 1.49 us  [the longest x1 1.49 us: local(): lax.ppermute(faces[1], 'gy', swap_pairs(count_y, 0))]
    ppermute x6, waiting for transfers between devices: 3.07 us -> 3.47 us  [exchange(): got[k] = lax.ppermute(parts[k], ('gy', 'gz'), swaps[k])]
  transfers between devices with their start and end apart: 10 -> 10, of which waited for: 5 -> 5; matrix products, arithmetic and copies ran while one was open for 0% -> 0% of each run, Pallas kernels for 11% -> 12%
where the time goes in v8:
time: 22.2 us; the launch traced here: 22 us
  starting transfers between devices  8.52 us (38%)
  Pallas kernels  6.24 us (28%)
  waiting for transfers between devices  4.7 us (21%)
  local copies, waits for them, and re-layouts  1.78 us (8%)
  between operations  0.76 us (3%)
    ppermute x6, starting transfers between devices, exchange(): got[k] = lax.ppermute(parts[k], ('gy', 'gz'), swaps[k])  3.86 us
    ppermute x6, waiting for transfers between devices, exchange(): got[k] = lax.ppermute(parts[k], ('gy', 'gz'), swaps[k])  3.47 us
    ppermute x1, starting transfers between devices, local(): lax.ppermute(faces[0], 'gx', swap_pairs(count_x, 0))  2.65 us
    unnamed x20, local copies, waits for them, and re-layouts  1.78 us
    ppermute x1, starting transfers between devices, local(): lax.ppermute(faces[1], 'gy', swap_pairs(count_y, 0))  1.49 us
    pallas_call x1, Pallas kernels, local(): call(functools.partial(fine_kernel, ranks), [shape((groups, 6, ROWS_BOX,...  1.48 us
    pallas_call x1, Pallas kernels, local(): call(store_kernel, shape(fine.shape, F32), [vmem] * 4, [pltpu.VMEM(fine.s...  1.29 us
    ppermute x1, waiting for transfers between devices, local(): lax.ppermute(faces[1], 'gy', swap_pairs(count_y, 0))  1.22 us
  transfers between devices with their start and end apart: 10, of which 5 were waited for; matrix products, arithmetic and copies ran while one was open for 0% of the time, Pallas kernels for 12%

profile of v8, /device:TPU:0, one launch (start us, length us, event | category | flops | bytes accessed | tf_op | source)
XLA Modules:
  0.0 22.0 jit_solution(2201628493486020960)
XLA Ops:
  0.6 1.1 %copy-done.1 = f32[6,12,12,128]{3,2,1,0:T(8,128)S(1)} copy-done((f32[6,12,12,128]{3,2,1,0:T(8,128)S(1)}, f32[6,12,12,128]{3,2,1,0:T(8,128)}, u32[]{:S(2)}) %copy-start.1) | copy-done | bytes 442392
  1.7 0.1 shard_map.113
  1.8 0.5 %collective-permute-start = (f32[6,12,12,128]{3,2,1,0:T(8,128)S(1)}, f32[6,12,12,128]{3,2,1,0:T(8,128)S(1)}, u32[]{:S(2)}, u32[]{:S(2)}) collective-permute-start(f32[6,12,12,128]{3,2,1,0:T(8,128)S(1)} %get-tuple-element.20.refs_0_), channel_id=1, source_target_pairs={{0,1},{1,0},{2,3},{3,2},{4,5},{5,4},{6,7},{7,6},{8,9},{9,8},{10,11... | collective-permute-start | bytes 1327112 | tf_op jit(solution)/shard_map/ppermute | solution.py:528
  2.3 2.6 %collective-permute-start.1 = (f32[5,12,128]{2,1,0:T(8,128)S(1)}, f32[5,12,128]{2,1,0:T(8,128)S(1)}, u32[]{:S(2)}, u32[]{:S(2)}) collective-permute-start(f32[5,12,128]{2,1,0:T(8,128)S(1)} %get-tuple-element.23), channel_id=1, source_target_pairs={{0,4},{4,0},{8,12},{12,8},{1,5},{5,1},{9,13},{13,9},{2,6},{6,2},{1... | collective-permute-start | bytes 92168 | tf_op jit(solution)/shard_map/ppermute | solution.py:522
  4.9 1.5 %collective-permute-start.2 = (f32[5,12,128]{2,1,0:T(8,128)S(1)}, f32[5,12,128]{2,1,0:T(8,128)S(1)}, u32[]{:S(2)}, u32[]{:S(2)}) collective-permute-start(f32[5,12,128]{2,1,0:T(8,128)S(1)} %get-tuple-element.24), channel_id=1, source_target_pairs={{0,2},{2,0},{1,3},{3,1},{4,6},{6,4},{5,7},{7,5},{8,10},{10,8},{9,1... | collective-permute-start | bytes 92168 | tf_op jit(solution)/shard_map/ppermute | solution.py:523
  6.5 0.7 %copy-done.9 = s32[1,4,2]{1,2,0:T(2,128)S(1)} copy-done((s32[1,4,2]{1,2,0:T(2,128)S(1)}, s32[1,4,2]{1,2,0:T(2,128)}, u32[]{:S(2)}) %copy-start.9) | copy-done | bytes 56
  7.1 0.6 %shard_map.114 = (s32[12,128]{1,0:T(8,128)S(1)}, f32[12,12,128]{2,1,0:T(8,128)S(1)}) custom-call(s32[1,1,2,3]{3,2,1,0:T(2,128)S(1)} %copy-done.8, s32[1,2,4]{2,1,0:T(2,128)S(1)} %bitcast.5, f32[12,12,128]{2,1,0:T(8,128)S(1)} %copy-done.6), custom_call_target="tpu_custom_call" | custom-call | flops 1000000 | bytes 1000000 | tf_op jit(solution)/shard_map/pallas_call | solution.py:531
  7.7 1.2 %collective-permute-done.2.refs_5_ = f32[5,12,128]{2,1,0:T(8,128)S(1)} collective-permute-done((f32[5,12,128]{2,1,0:T(8,128)S(1)}, f32[5,12,128]{2,1,0:T(8,128)S(1)}, u32[]{:S(2)}, u32[]{:S(2)}) %collective-permute-start.2) | collective-permute-done | bytes 30752 | tf_op jit(solution)/shard_map/ppermute | solution.py:523
  9.0 1.1 %shard_map.115 = (f32[6,12,12,128]{3,2,1,0:T(8,128)S(1)}, f32[72,128]{1,0:T(8,128)S(1)}, f32[104,128]{1,0:T(8,128)S(1)}, f32[72,128]{1,0:T(8,128)S(1)}, f32[72,128]{1,0:T(8,128)S(1)}) custom-call(f32[6,12,12,128]{3,2,1,0:T(8,128)S(1)} %get-tuple-element.20.refs_0_, f32[6,12,12,128]{3,2,1,0:T(8,128)S(1)} %collective-permute-done.refs_1_, ...), custom_call_target="tpu_custom_call" | custom-call | flops 1000000 | bytes 1000000 | tf_op jit(solution)/shard_map/pallas_call | solution.py:555
  10.1 0.1 collective-permute-start.4
  10.2 1.6 %collective-permute-start.5 = (f32[72,128]{1,0:T(8,128)S(1)}, f32[72,128]{1,0:T(8,128)S(1)}, u32[]{:S(2)}, u32[]{:S(2)}) collective-permute-start(f32[72,128]{1,0:T(8,128)S(1)} %get-tuple-element.28), channel_id=1, source_target_pairs={{0,2},{1,3},{2,0},{3,1},{4,6},{5,7},{6,4},{7,5},{8,10},{9,11},{10,... | collective-permute-start | bytes 110600 | tf_op jit(solution)/shard_map/ppermute | solution.py:551
  11.8 0.3 %collective-permute-start.6 = (f32[72,128]{1,0:T(8,128)S(1)}, f32[72,128]{1,0:T(8,128)S(1)}, u32[]{:S(2)}, u32[]{:S(2)}) collective-permute-start(f32[72,128]{1,0:T(8,128)S(1)} %get-tuple-element.29), channel_id=1, source_target_pairs={{0,3},{1,2},{2,1},{3,0},{4,7},{5,6},{6,5},{7,4},{8,11},{9,10},{10,... | collective-permute-start | bytes 110600 | tf_op jit(solution)/shard_map/ppermute | solution.py:551
  12.1 0.6 %shard_map.117 = (f32[1,6,72,384]{3,2,1,0:T(8,128)S(1)}, f32[1,72,384]{2,1,0:T(8,128)S(1)}) custom-call(f32[1,1,6,4,4096]{4,3,2,1,0:T(4,128)S(1)} %bitcast.3, f32[1,1,4,4096]{3,2,1,0:T(4,128)S(1)} %copy-done.7, bf16[256,384]{1,0:T(8,128)(2,1)S(1)} %copy-done.5), custom_call_target="tpu_custom_call" | custom-call | flops 1000000 | bytes 4000000 | tf_op jit(solution)/shard_map/pallas_call | solution.py:536
  12.7 1.5 %collective-permute-done.5.refs_1_.refs_2_ = f32[72,128]{1,0:T(8,128)S(1)} collective-permute-done((f32[72,128]{1,0:T(8,128)S(1)}, f32[72,128]{1,0:T(8,128)S(1)}, u32[]{:S(2)}, u32[]{:S(2)}) %collective-permute-start.5) | collective-permute-done | bytes 36896 | tf_op jit(solution)/shard_map/ppermute | solution.py:551
  14.2 1.0 %collective-permute-done.6.refs_2_.refs_3_ = f32[72,128]{1,0:T(8,128)S(1)} collective-permute-done((f32[72,128]{1,0:T(8,128)S(1)}, f32[72,128]{1,0:T(8,128)S(1)}, u32[]{:S(2)}, u32[]{:S(2)}) %collective-permute-start.6) | collective-permute-done | bytes 36896 | tf_op jit(solution)/shard_map/ppermute | solution.py:551
  15.2 1.5 %shard_map.118 = (f32[1,6,72,384]{3,2,1,0:T(8,128)S(1)}, f32[24,128]{1,0:T(8,128)S(1)}, f32[24,128]{1,0:T(8,128)S(1)}, f32[24,128]{1,0:T(8,128)S(1)}, f32[24,128]{1,0:T(8,128)S(1)}) custom-call(f32[72,128]{1,0:T(8,128)S(1)} %get-tuple-element.30.refs_0_, f32[104,128]{1,0:T(8,128)S(1)} %collective-permute-done.4.refs_0_.refs_1_, ...), custom_call_target="tpu_custom_call" | custom-call | flops 1000000 | bytes 1000000 | tf_op jit(solution)/shard_map/pallas_call | solution.py:569
  16.7 0.2 %collective-permute-start.7 = (f32[24,128]{1,0:T(8,128)S(1)}, f32[24,128]{1,0:T(8,128)S(1)}, u32[]{:S(2)}, u32[]{:S(2)}) collective-permute-start(f32[24,128]{1,0:T(8,128)S(1)} %get-tuple-element.34), channel_id=1, source_target_pairs={{0,1},{1,0},{2,3},{3,2},{4,5},{5,4},{6,7},{7,6},{8,9},{9,8},{10,11... | collective-permute-start | bytes 36872 | tf_op jit(solution)/shard_map/ppermute | solution.py:551
  16.9 0.9 %collective-permute-start.8 = (f32[24,128]{1,0:T(8,128)S(1)}, f32[24,128]{1,0:T(8,128)S(1)}, u32[]{:S(2)}, u32[]{:S(2)}) collective-permute-start(f32[24,128]{1,0:T(8,128)S(1)} %get-tuple-element.35), channel_id=1, source_target_pairs={{0,2},{1,3},{2,0},{3,1},{4,6},{5,7},{6,4},{7,5},{8,10},{9,11},{10,... | collective-permute-start | bytes 36872 | tf_op jit(solution)/shard_map/ppermute | solution.py:551
  17.9 0.8 %collective-permute-start.9 = (f32[24,128]{1,0:T(8,128)S(1)}, f32[24,128]{1,0:T(8,128)S(1)}, u32[]{:S(2)}, u32[]{:S(2)}) collective-permute-start(f32[24,128]{1,0:T(8,128)S(1)} %get-tuple-element.36), channel_id=1, source_target_pairs={{0,3},{1,2},{2,1},{3,0},{4,7},{5,6},{6,5},{7,4},{8,11},{9,10},{10,... | collective-permute-start | bytes 36872 | tf_op jit(solution)/shard_map/ppermute | solution.py:551
  18.6 1.3 %shard_map.120 = f32[1,1,6,4,4096]{4,3,2,1,0:T(4,128)} custom-call(f32[1,6,72,384]{3,2,1,0:T(8,128)S(1)} %get-tuple-element.37.box, f32[1,1,6,4,4096]{4,3,2,1,0:T(4,128)S(1)} %bitcast.4, s32[12,128]{1,0:T(8,128)S(1)} %get-tuple-element.22.refs_3_.notes, bf16[384,256]{1,0:T(8,128)(2,1)S(1)} %copy-done.3), custom_call_target="tpu_custom_call" | custom-call | flops 1000000 | bytes 4000000 | tf_op jit(solution)/shard_map/pallas_call | solution.py:584
  19.9 0.1 shard_map.116.new
  20.0 0.6 %collective-permute-done.8.refs_2_ = f32[24,128]{1,0:T(8,128)S(1)} collective-permute-done((f32[24,128]{1,0:T(8,128)S(1)}, f32[24,128]{1,0:T(8,128)S(1)}, u32[]{:S(2)}, u32[]{:S(2)}) %collective-permute-start.8) | collective-permute-done | bytes 12320 | tf_op jit(solution)/shard_map/ppermute | solution.py:551
  20.6 0.4 %collective-permute-done.9.refs_3_ = f32[24,128]{1,0:T(8,128)S(1)} collective-permute-done((f32[24,128]{1,0:T(8,128)S(1)}, f32[24,128]{1,0:T(8,128)S(1)}, u32[]{:S(2)}, u32[]{:S(2)}) %collective-permute-start.9) | collective-permute-done | bytes 12320 | tf_op jit(solution)/shard_map/ppermute | solution.py:551
  21.0 1.0 %shard_map.119 = f32[6,12,12,128]{3,2,1,0:T(8,128)} custom-call(f32[6,12,12,128]{3,2,1,0:T(8,128)S(1)} %shard_map.116.new, s32[12,128]{1,0:T(8,128)S(1)} %get-tuple-element.22.refs_3_.notes, f32[24,128]{1,0:T(8,128)S(1)} %get-tuple-element.33.refs_0_, f32[24,128]{1,0:T(8,128)S(1)} %collective-permute-done.7.refs_1_, ...), custom_call_target="tpu_custom_call" | custom-call | flops 1000000 | bytes 1000000 | tf_op jit(solution)/shard_map/pallas_call | solution.py:593
  (24 shorter events, 0.1 us)
Async XLA Ops:
  0.6 1.1 %copy-start.1 = (f32[6,12,12,128]{3,2,1,0:T(8,128)S(1)}, f32[6,12,12,128]{3,2,1,0:T(8,128)}, u32[]{:S(2)}) copy-start(f32[6,12,12,128]{3,2,1,0:T(8,128)} %block.1) | copy-start | bytes 1327108
  1.7 4.8 %copy-start.6 = (f32[12,12,128]{2,1,0:T(8,128)S(1)}, f32[12,12,128]{2,1,0:T(8,128)}, u32[]{:S(2)}) copy-start(f32[12,12,128]{2,1,0:T(8,128)} %perm.2) | copy-start | bytes 221188
  1.8 7.2 %collective-permute-start = (f32[6,12,12,128]{3,2,1,0:T(8,128)S(1)}, f32[6,12,12,128]{3,2,1,0:T(8,128)S(1)}, u32[]{:S(2)}, u32[]{:S(2)}) collective-permute-start(f32[6,12,12,128]{3,2,1,0:T(8,128)S(1)} %get-tuple-element.20.refs_0_), channel_id=1, source_target_pairs={{0,1},{1,0},{2,3},{3,2},{4,5},{5,4},{6,7},{7,6},{8,9},{9,8},{10,11... | collective-permute-start | bytes 1327112 | tf_op jit(solution)/shard_map/ppermute | solution.py:528
  2.3 5.4 %collective-permute-start.1 = (f32[5,12,128]{2,1,0:T(8,128)S(1)}, f32[5,12,128]{2,1,0:T(8,128)S(1)}, u32[]{:S(2)}, u32[]{:S(2)}) collective-permute-start(f32[5,12,128]{2,1,0:T(8,128)S(1)} %get-tuple-element.23), channel_id=1, source_target_pairs={{0,4},{4,0},{8,12},{12,8},{1,5},{5,1},{9,13},{13,9},{2,6},{6,2},{1... | collective-permute-start | bytes 92168 | tf_op jit(solution)/shard_map/ppermute | solution.py:522
  4.9 4.0 %collective-permute-start.2 = (f32[5,12,128]{2,1,0:T(8,128)S(1)}, f32[5,12,128]{2,1,0:T(8,128)S(1)}, u32[]{:S(2)}, u32[]{:S(2)}) collective-permute-start(f32[5,12,128]{2,1,0:T(8,128)S(1)} %get-tuple-element.24), channel_id=1, source_target_pairs={{0,2},{2,0},{1,3},{3,1},{4,6},{6,4},{5,7},{7,5},{8,10},{10,8},{9,1... | collective-permute-start | bytes 92168 | tf_op jit(solution)/shard_map/ppermute | solution.py:523
  6.4 0.7 %copy-start.9 = (s32[1,4,2]{1,2,0:T(2,128)S(1)}, s32[1,4,2]{1,2,0:T(2,128)}, u32[]{:S(2)}) copy-start(s32[1,4,2]{1,2,0:T(2,128)} %param.15) | copy-start | bytes 100
  6.4 0.7 %copy-start.8 = (s32[1,1,2,3]{3,2,1,0:T(2,128)S(1)}, s32[1,1,2,3]{3,2,1,0:T(2,128)}, u32[]{:S(2)}) copy-start(s32[1,1,2,3]{3,2,1,0:T(2,128)} %corner.1) | copy-start | bytes 76
  6.4 2.5 %collective-permute-start.3 = (f32[5,12,128]{2,1,0:T(8,128)S(1)}, f32[5,12,128]{2,1,0:T(8,128)S(1)}, u32[]{:S(2)}, u32[]{:S(2)}) collective-permute-start(f32[5,12,128]{2,1,0:T(8,128)S(1)} %get-tuple-element.25), channel_id=1, source_target_pairs={{0,1},{1,0},{4,8},{5,9},{8,4},{9,5},{12,13},{13,12},{2,3},{3,2},{6... | collective-permute-start | bytes 92168 | tf_op jit(solution)/shard_map/ppermute | solution.py:524
  9.0 3.1 %copy-start = (f32[1,1,4,6,4096]{4,2,3,1,0:T(4,128)S(1)}, f32[1,1,4,6,4096]{4,2,3,1,0:T(4,128)}, u32[]{:S(2)}) copy-start(f32[1,1,4,6,4096]{4,2,3,1,0:T(4,128)} %param.12) | copy-start | bytes 1179652
  9.0 3.1 %copy-start.5 = (bf16[256,384]{1,0:T(8,128)(2,1)S(1)}, bf16[256,384]{1,0:T(8,128)(2,1)}, u32[]{:S(2)}) copy-start(bf16[256,384]{1,0:T(8,128)(2,1)} %constant.8.clone.table) | copy-start | bytes 589828
  9.0 3.1 %copy-start.7 = (f32[1,1,4,4096]{3,2,1,0:T(4,128)S(1)}, f32[1,1,4,4096]{3,2,1,0:T(4,128)}, u32[]{:S(2)}) copy-start(f32[1,1,4,4096]{3,2,1,0:T(4,128)} %perm.3) | copy-start | bytes 196612
  10.1 5.1 %copy-start.2 = (bf16[2,256,384]{2,1,0:T(8,128)(2,1)S(1)}, bf16[2,256,384]{2,1,0:T(8,128)(2,1)}, u32[]{:S(2)}) copy-start(bf16[2,256,384]{2,1,0:T(8,128)(2,1)} %constant.9.clone.refs_6_) | copy-start | bytes 1179652
  10.1 5.1 %collective-permute-start.4 = (f32[104,128]{1,0:T(8,128)S(1)}, f32[104,128]{1,0:T(8,128)S(1)}, u32[]{:S(2)}, u32[]{:S(2)}) collective-permute-start(f32[104,128]{1,0:T(8,128)S(1)} %get-tuple-element.27), channel_id=1, source_target_pairs={{0,1},{1,0},{2,3},{3,2},{4,5},{5,4},{6,7},{7,6},{8,9},{9,8},{10,11... | collective-permute-start | bytes 159752 | tf_op jit(solution)/shard_map/ppermute | solution.py:551
  10.2 4.0 %collective-permute-start.5 = (f32[72,128]{1,0:T(8,128)S(1)}, f32[72,128]{1,0:T(8,128)S(1)}, u32[]{:S(2)}, u32[]{:S(2)}) collective-permute-start(f32[72,128]{1,0:T(8,128)S(1)} %get-tuple-element.28), channel_id=1, source_target_pairs={{0,2},{1,3},{2,0},{3,1},{4,6},{5,7},{6,4},{7,5},{8,10},{9,11},{10,... | collective-permute-start | bytes 110600 | tf_op jit(solution)/shard_map/ppermute | solution.py:551
  11.8 3.4 %collective-permute-start.6 = (f32[72,128]{1,0:T(8,128)S(1)}, f32[72,128]{1,0:T(8,128)S(1)}, u32[]{:S(2)}, u32[]{:S(2)}) collective-permute-start(f32[72,128]{1,0:T(8,128)S(1)} %get-tuple-element.29), channel_id=1, source_target_pairs={{0,3},{1,2},{2,1},{3,0},{4,7},{5,6},{6,5},{7,4},{8,11},{9,10},{10,... | collective-permute-start | bytes 110600 | tf_op jit(solution)/shard_map/ppermute | solution.py:551
  12.1 3.1 %copy-start.4 = (bf16[768,128]{1,0:T(8,128)(2,1)S(1)}, bf16[768,128]{1,0:T(8,128)(2,1)}, u32[]{:S(2)}) copy-start(bf16[768,128]{1,0:T(8,128)(2,1)} %constant.10.clone.refs_7_) | copy-start | bytes 589828
  15.2 3.4 %copy-start.3 = (bf16[384,256]{1,0:T(8,128)(2,1)S(1)}, bf16[384,256]{1,0:T(8,128)(2,1)}, u32[]{:S(2)}) copy-start(bf16[384,256]{1,0:T(8,128)(2,1)} %constant.11.clone.table) | copy-start | bytes 589828
  16.7 3.3 %collective-permute-start.7 = (f32[24,128]{1,0:T(8,128)S(1)}, f32[24,128]{1,0:T(8,128)S(1)}, u32[]{:S(2)}, u32[]{:S(2)}) collective-permute-start(f32[24,128]{1,0:T(8,128)S(1)} %get-tuple-element.34), channel_id=1, source_target_pairs={{0,1},{1,0},{2,3},{3,2},{4,5},{5,4},{6,7},{7,6},{8,9},{9,8},{10,11... | collective-permute-start | bytes 36872 | tf_op jit(solution)/shard_map/ppermute | solution.py:551
  16.9 3.7 %collective-permute-start.8 = (f32[24,128]{1,0:T(8,128)S(1)}, f32[24,128]{1,0:T(8,128)S(1)}, u32[]{:S(2)}, u32[]{:S(2)}) collective-permute-start(f32[24,128]{1,0:T(8,128)S(1)} %get-tuple-element.35), channel_id=1, source_target_pairs={{0,2},{1,3},{2,0},{3,1},{4,6},{5,7},{6,4},{7,5},{8,10},{9,11},{10,... | collective-permute-start | bytes 36872 | tf_op jit(solution)/shard_map/ppermute | solution.py:551
  17.9 3.1 %collective-permute-start.9 = (f32[24,128]{1,0:T(8,128)S(1)}, f32[24,128]{1,0:T(8,128)S(1)}, u32[]{:S(2)}, u32[]{:S(2)}) collective-permute-start(f32[24,128]{1,0:T(8,128)S(1)} %get-tuple-element.36), channel_id=1, source_target_pairs={{0,3},{1,2},{2,1},{3,0},{4,7},{5,6},{6,5},{7,4},{8,11},{9,10},{10,... | collective-permute-start | bytes 36872 | tf_op jit(solution)/shard_map/ppermute | solution.py:551

commit v9 on v8

--- a/solution.py
+++ b/solution.py
@@ -70,8 +70,8 @@
 def move(rows, table):
     high = rows.astype(BF16)
     low = (rows - high.astype(F32)).astype(BF16)
-    out = jnp.dot(high, table, preferred_element_type=F32)
-    return out + jnp.dot(low, table, preferred_element_type=F32)
+    out = jnp.dot(jnp.concatenate([high, low], axis=0), table, preferred_element_type=F32)
+    return out[: rows.shape[0]] + out[rows.shape[0] :]
 
 
 def lane_iota(shape):
@@ -318,7 +318,7 @@
 def fine_kernel(ranks, *refs):
     regions, (box, rate, ghosts, means, out) = refs[:ranks], refs[ranks : ranks + 5]
     smalls = refs[ranks + 5 : 2 * ranks + 5]
-    rims, walls, now, mag, halves, small = refs[2 * ranks + 5 :]
+    rims, walls, now, halves, small = refs[2 * ranks + 5 :]
     groups = box.shape[0]
     rank = lax.axis_index("gy") * lax.axis_size("gz") + lax.axis_index("gz")
     flat = lane_iota((8, WIDE))
@@ -377,12 +377,13 @@
     for g in range(groups):
         for sub in range(2):
             source = box if sub == 0 else out
+            rows = pl.ds(g * 6 * ROWS_BOX, 6 * ROWS_BOX)
+            ghost = move(jnp.concatenate([rims[rows, :], walls[sub, rows, :]], axis=1), ghosts[sub])
             for c in range(6):
-                rows = pl.ds((g * 6 + c) * ROWS_BOX, ROWS_BOX)
-                ghost = move(jnp.concatenate([rims[rows, :], walls[sub, rows, :]], axis=1), ghosts[sub])
                 for m in range(PLANES):
+                    row = c * ROWS_BOX + m * 8
                     now[c, rows_of(m), :] = jnp.where(
-                        inner_of(m), source[g, c, rows_of(m), :], ghost[m * 8 : (m + 1) * 8]
+                        inner_of(m), source[g, c, rows_of(m), :], ghost[row : row + 8]
                     )
 
             def next_x(c, m):
@@ -392,24 +393,22 @@
 
             def last_x(c, m):
                 if m == 0:
-                    return pltpu.roll(mag[c, rows_of(PLANES - 1), :], BATCH, 0)
-                return mag[c, rows_of(m - 1), :]
+                    return pltpu.roll(out[g, c + 3, rows_of(PLANES - 1), :], BATCH, 0)
+                return out[g, c + 3, rows_of(m - 1), :]
 
             for m in range(PLANES):
                 e0, e1, e2 = (now[c, rows_of(m), :] for c in range(3))
                 h0, h1, h2 = (now[c, rows_of(m), :] for c in range(3, 6))
-                mag[0, rows_of(m), :] = h0 - 0.5 * ((up_y(e2) - e2) - (up_z(e1) - e1))
-                mag[1, rows_of(m), :] = h1 - 0.5 * ((up_z(e0) - e0) - (next_x(2, m) - e2))
-                mag[2, rows_of(m), :] = h2 - 0.5 * ((next_x(1, m) - e1) - (up_y(e0) - e0))
+                out[g, 3, rows_of(m), :] = h0 - 0.5 * ((up_y(e2) - e2) - (up_z(e1) - e1))
+                out[g, 4, rows_of(m), :] = h1 - 0.5 * ((up_z(e0) - e0) - (next_x(2, m) - e2))
+                out[g, 5, rows_of(m), :] = h2 - 0.5 * ((next_x(1, m) - e1) - (up_y(e0) - e0))
             for m in range(PLANES):
-                h0, h1, h2 = (mag[c, rows_of(m), :] for c in range(3))
+                h0, h1, h2 = (out[g, c, rows_of(m), :] for c in range(3, 6))
                 coef = rate[g, rows_of(m), :]
                 e0, e1, e2 = (now[c, rows_of(m), :] for c in range(3))
                 out[g, 0, rows_of(m), :] = e0 + coef * ((h2 - down_y(h2)) - (h1 - down_z(h1)))
                 out[g, 1, rows_of(m), :] = e1 + coef * ((h0 - down_z(h0)) - (h2 - last_x(2, m)))
                 out[g, 2, rows_of(m), :] = e2 + coef * ((h1 - last_x(1, m)) - (h0 - down_y(h0)))
-                for c, value in enumerate((h0, h1, h2)):
-                    out[g, c + 3, rows_of(m), :] = value
         for c in range(6):
             for k in range(4):
                 other = jnp.where(upper, out[g, c, rows_of(2 * k), :], out[g, c, rows_of(2 * k + 2), :])
@@ -574,7 +573,6 @@
             pltpu.VMEM((groups * 6 * ROWS_BOX, LANES), F32),
             pltpu.VMEM((2, groups * 6 * ROWS_BOX, LANES), F32),
             pltpu.VMEM((6, ROWS_BOX, WIDE), F32),
-            pltpu.VMEM((3, ROWS_BOX, WIDE), F32),
             pltpu.VMEM((96, 2 * WIDE), F32),
             pltpu.VMEM((groups * 96, LANES), F32),
         ],

time: 22.2 us -> 21.9 us (0.986)
  Pallas kernels: 6.24 us -> 5.6 us
  waiting for transfers between devices: 4.7 us -> 5.03 us
    ppermute x6, waiting for transfers between devices: 3.47 us -> 3.81 us  [exchange(): got[k] = lax.ppermute(parts[k], ('gy', 'gz'), swaps[k])]
    pallas_call x1, Pallas kernels: 1.48 us -> 1.17 us  [local(): call(functools.partial(fine_kernel, ranks), [shape((groups, 6, ROWS_BOX,...]
  transfers between devices with their start and end apart: 10 -> 10, of which waited for: 5 -> 5; matrix products, arithmetic and copies ran while one was open for 0% -> 0% of each run, Pallas kernels for 12% -> 10%
where the time goes in v9:
time: 21.9 us; the launch traced here: 21.7 us
  starting transfers between devices  8.52 us (39%)
  Pallas kernels  5.6 us (26%)
  waiting for transfers between devices  5.03 us (23%)
  local copies, waits for them, and re-layouts  1.78 us (8%)
  between operations  0.76 us (3%)
    ppermute x6, starting transfers between devices, exchange(): got[k] = lax.ppermute(parts[k], ('gy', 'gz'), swaps[k])  3.86 us
    ppermute x6, waiting for transfers between devices, exchange(): got[k] = lax.ppermute(parts[k], ('gy', 'gz'), swaps[k])  3.81 us
    ppermute x1, starting transfers between devices, local(): lax.ppermute(faces[0], 'gx', swap_pairs(count_x, 0))  2.65 us
    unnamed x20, local copies, waits for them, and re-layouts  1.78 us
    ppermute x1, starting transfers between devices, local(): lax.ppermute(faces[1], 'gy', swap_pairs(count_y, 0))  1.49 us
    ppermute x1, waiting for transfers between devices, local(): lax.ppermute(faces[1], 'gy', swap_pairs(count_y, 0))  1.22 us
    pallas_call x1, Pallas kernels, local(): call(functools.partial(fine_kernel, ranks), [shape((groups, 6, ROWS_BOX,...  1.17 us
    pallas_call x1, Pallas kernels, local(): call(functools.partial(leap_kernel, two_y, ranks), [shape(coarse_fields.s...  1.14 us
  transfers between devices with their start and end apart: 10, of which 5 were waited for; matrix products, arithmetic and copies ran while one was open for 0% of the time, Pallas kernels for 10%

profile of v9, /device:TPU:0, one launch (start us, length us, event | category | flops | bytes accessed | tf_op | source)
XLA Modules:
  0.0 21.7 jit_solution(2960489539635753358)
XLA Ops:
  0.6 1.1 %copy-done.1 = f32[6,12,12,128]{3,2,1,0:T(8,128)S(1)} copy-done((f32[6,12,12,128]{3,2,1,0:T(8,128)S(1)}, f32[6,12,12,128]{3,2,1,0:T(8,128)}, u32[]{:S(2)}) %copy-start.1) | copy-done | bytes 442392
  1.7 0.1 shard_map.113
  1.8 0.5 %collective-permute-start = (f32[6,12,12,128]{3,2,1,0:T(8,128)S(1)}, f32[6,12,12,128]{3,2,1,0:T(8,128)S(1)}, u32[]{:S(2)}, u32[]{:S(2)}) collective-permute-start(f32[6,12,12,128]{3,2,1,0:T(8,128)S(1)} %get-tuple-element.20.refs_0_), channel_id=1, source_target_pairs={{0,1},{1,0},{2,3},{3,2},{4,5},{5,4},{6,7},{7,6},{8,9},{9,8},{10,11... | collective-permute-start | bytes 1327112 | tf_op jit(solution)/shard_map/ppermute | solution.py:527
  2.3 2.6 %collective-permute-start.1 = (f32[5,12,128]{2,1,0:T(8,128)S(1)}, f32[5,12,128]{2,1,0:T(8,128)S(1)}, u32[]{:S(2)}, u32[]{:S(2)}) collective-permute-start(f32[5,12,128]{2,1,0:T(8,128)S(1)} %get-tuple-element.23), channel_id=1, source_target_pairs={{0,4},{4,0},{8,12},{12,8},{1,5},{5,1},{9,13},{13,9},{2,6},{6,2},{1... | collective-permute-start | bytes 92168 | tf_op jit(solution)/shard_map/ppermute | solution.py:521
  4.9 1.5 %collective-permute-start.2 = (f32[5,12,128]{2,1,0:T(8,128)S(1)}, f32[5,12,128]{2,1,0:T(8,128)S(1)}, u32[]{:S(2)}, u32[]{:S(2)}) collective-permute-start(f32[5,12,128]{2,1,0:T(8,128)S(1)} %get-tuple-element.24), channel_id=1, source_target_pairs={{0,2},{2,0},{1,3},{3,1},{4,6},{6,4},{5,7},{7,5},{8,10},{10,8},{9,1... | collective-permute-start | bytes 92168 | tf_op jit(solution)/shard_map/ppermute | solution.py:522
  6.5 0.7 %copy-done.9 = s32[1,4,2]{1,2,0:T(2,128)S(1)} copy-done((s32[1,4,2]{1,2,0:T(2,128)S(1)}, s32[1,4,2]{1,2,0:T(2,128)}, u32[]{:S(2)}) %copy-start.9) | copy-done | bytes 56
  7.1 0.6 %shard_map.114 = (s32[12,128]{1,0:T(8,128)S(1)}, f32[12,12,128]{2,1,0:T(8,128)S(1)}) custom-call(s32[1,1,2,3]{3,2,1,0:T(2,128)S(1)} %copy-done.8, s32[1,2,4]{2,1,0:T(2,128)S(1)} %bitcast.5, f32[12,12,128]{2,1,0:T(8,128)S(1)} %copy-done.6), custom_call_target="tpu_custom_call" | custom-call | flops 1000000 | bytes 1000000 | tf_op jit(solution)/shard_map/pallas_call | solution.py:530
  7.7 1.2 %collective-permute-done.2.refs_5_ = f32[5,12,128]{2,1,0:T(8,128)S(1)} collective-permute-done((f32[5,12,128]{2,1,0:T(8,128)S(1)}, f32[5,12,128]{2,1,0:T(8,128)S(1)}, u32[]{:S(2)}, u32[]{:S(2)}) %collective-permute-start.2) | collective-permute-done | bytes 30752 | tf_op jit(solution)/shard_map/ppermute | solution.py:522
  9.0 1.1 %shard_map.115 = (f32[6,12,12,128]{3,2,1,0:T(8,128)S(1)}, f32[72,128]{1,0:T(8,128)S(1)}, f32[104,128]{1,0:T(8,128)S(1)}, f32[72,128]{1,0:T(8,128)S(1)}, f32[72,128]{1,0:T(8,128)S(1)}) custom-call(f32[6,12,12,128]{3,2,1,0:T(8,128)S(1)} %get-tuple-element.20.refs_0_, f32[6,12,12,128]{3,2,1,0:T(8,128)S(1)} %collective-permute-done.refs_1_, ...), custom_call_target="tpu_custom_call" | custom-call | flops 1000000 | bytes 1000000 | tf_op jit(solution)/shard_map/pallas_call | solution.py:554
  10.1 0.1 collective-permute-start.4
  10.2 1.6 %collective-permute-start.5 = (f32[72,128]{1,0:T(8,128)S(1)}, f32[72,128]{1,0:T(8,128)S(1)}, u32[]{:S(2)}, u32[]{:S(2)}) collective-permute-start(f32[72,128]{1,0:T(8,128)S(1)} %get-tuple-element.28), channel_id=1, source_target_pairs={{0,2},{1,3},{2,0},{3,1},{4,6},{5,7},{6,4},{7,5},{8,10},{9,11},{10,... | collective-permute-start | bytes 110600 | tf_op jit(solution)/shard_map/ppermute | solution.py:550
  11.8 0.3 %collective-permute-start.6 = (f32[72,128]{1,0:T(8,128)S(1)}, f32[72,128]{1,0:T(8,128)S(1)}, u32[]{:S(2)}, u32[]{:S(2)}) collective-permute-start(f32[72,128]{1,0:T(8,128)S(1)} %get-tuple-element.29), channel_id=1, source_target_pairs={{0,3},{1,2},{2,1},{3,0},{4,7},{5,6},{6,5},{7,4},{8,11},{9,10},{10,... | collective-permute-start | bytes 110600 | tf_op jit(solution)/shard_map/ppermute | solution.py:550
  12.1 0.4 %shard_map.117 = (f32[1,6,72,384]{3,2,1,0:T(8,128)S(1)}, f32[1,72,384]{2,1,0:T(8,128)S(1)}) custom-call(f32[1,1,6,4,4096]{4,3,2,1,0:T(4,128)S(1)} %bitcast.3, f32[1,1,4,4096]{3,2,1,0:T(4,128)S(1)} %copy-done.7, bf16[256,384]{1,0:T(8,128)(2,1)S(1)} %copy-done.5), custom_call_target="tpu_custom_call" | custom-call | flops 1000000 | bytes 4000000 | tf_op jit(solution)/shard_map/pallas_call | solution.py:535
  12.5 1.7 %collective-permute-done.5.refs_1_.refs_2_ = f32[72,128]{1,0:T(8,128)S(1)} collective-permute-done((f32[72,128]{1,0:T(8,128)S(1)}, f32[72,128]{1,0:T(8,128)S(1)}, u32[]{:S(2)}, u32[]{:S(2)}) %collective-permute-start.5) | collective-permute-done | bytes 36896 | tf_op jit(solution)/shard_map/ppermute | solution.py:550
  14.2 1.0 %collective-permute-done.6.refs_2_.refs_3_ = f32[72,128]{1,0:T(8,128)S(1)} collective-permute-done((f32[72,128]{1,0:T(8,128)S(1)}, f32[72,128]{1,0:T(8,128)S(1)}, u32[]{:S(2)}, u32[]{:S(2)}) %collective-permute-start.6) | collective-permute-done | bytes 36896 | tf_op jit(solution)/shard_map/ppermute | solution.py:550
  15.2 1.2 %shard_map.118 = (f32[1,6,72,384]{3,2,1,0:T(8,128)S(1)}, f32[24,128]{1,0:T(8,128)S(1)}, f32[24,128]{1,0:T(8,128)S(1)}, f32[24,128]{1,0:T(8,128)S(1)}, f32[24,128]{1,0:T(8,128)S(1)}) custom-call(f32[72,128]{1,0:T(8,128)S(1)} %get-tuple-element.30.refs_0_, f32[104,128]{1,0:T(8,128)S(1)} %collective-permute-done.4.refs_0_.refs_1_, ...), custom_call_target="tpu_custom_call" | custom-call | flops 1000000 | bytes 1000000 | tf_op jit(solution)/shard_map/pallas_call | solution.py:568
  16.4 0.2 %collective-permute-start.7 = (f32[24,128]{1,0:T(8,128)S(1)}, f32[24,128]{1,0:T(8,128)S(1)}, u32[]{:S(2)}, u32[]{:S(2)}) collective-permute-start(f32[24,128]{1,0:T(8,128)S(1)} %get-tuple-element.34), channel_id=1, source_target_pairs={{0,1},{1,0},{2,3},{3,2},{4,5},{5,4},{6,7},{7,6},{8,9},{9,8},{10,11... | collective-permute-start | bytes 36872 | tf_op jit(solution)/shard_map/ppermute | solution.py:550
  16.6 0.9 %collective-permute-start.8 = (f32[24,128]{1,0:T(8,128)S(1)}, f32[24,128]{1,0:T(8,128)S(1)}, u32[]{:S(2)}, u32[]{:S(2)}) collective-permute-start(f32[24,128]{1,0:T(8,128)S(1)} %get-tuple-element.35), channel_id=1, source_target_pairs={{0,2},{1,3},{2,0},{3,1},{4,6},{5,7},{6,4},{7,5},{8,10},{9,11},{10,... | collective-permute-start | bytes 36872 | tf_op jit(solution)/shard_map/ppermute | solution.py:550
  17.6 0.8 %collective-permute-start.9 = (f32[24,128]{1,0:T(8,128)S(1)}, f32[24,128]{1,0:T(8,128)S(1)}, u32[]{:S(2)}, u32[]{:S(2)}) collective-permute-start(f32[24,128]{1,0:T(8,128)S(1)} %get-tuple-element.36), channel_id=1, source_target_pairs={{0,3},{1,2},{2,1},{3,0},{4,7},{5,6},{6,5},{7,4},{8,11},{9,10},{10,... | collective-permute-start | bytes 36872 | tf_op jit(solution)/shard_map/ppermute | solution.py:550
  18.3 1.1 %shard_map.120 = f32[1,1,6,4,4096]{4,3,2,1,0:T(4,128)} custom-call(f32[1,6,72,384]{3,2,1,0:T(8,128)S(1)} %get-tuple-element.37.box, f32[1,1,6,4,4096]{4,3,2,1,0:T(4,128)S(1)} %bitcast.4, s32[12,128]{1,0:T(8,128)S(1)} %get-tuple-element.22.refs_3_.notes, bf16[384,256]{1,0:T(8,128)(2,1)S(1)} %copy-done.3), custom_call_target="tpu_custom_call" | custom-call | flops 1000000 | bytes 4000000 | tf_op jit(solution)/shard_map/pallas_call | solution.py:582
  19.5 0.1 shard_map.116.new
  19.6 0.8 %collective-permute-done.8.refs_2_ = f32[24,128]{1,0:T(8,128)S(1)} collective-permute-done((f32[24,128]{1,0:T(8,128)S(1)}, f32[24,128]{1,0:T(8,128)S(1)}, u32[]{:S(2)}, u32[]{:S(2)}) %collective-permute-start.8) | collective-permute-done | bytes 12320 | tf_op jit(solution)/shard_map/ppermute | solution.py:550
  20.3 0.4 %collective-permute-done.9.refs_3_ = f32[24,128]{1,0:T(8,128)S(1)} collective-permute-done((f32[24,128]{1,0:T(8,128)S(1)}, f32[24,128]{1,0:T(8,128)S(1)}, u32[]{:S(2)}, u32[]{:S(2)}) %collective-permute-start.9) | collective-permute-done | bytes 12320 | tf_op jit(solution)/shard_map/ppermute | solution.py:550
  20.7 1.0 %shard_map.119 = f32[6,12,12,128]{3,2,1,0:T(8,128)} custom-call(f32[6,12,12,128]{3,2,1,0:T(8,128)S(1)} %shard_map.116.new, s32[12,128]{1,0:T(8,128)S(1)} %get-tuple-element.22.refs_3_.notes, f32[24,128]{1,0:T(8,128)S(1)} %get-tuple-element.33.refs_0_, f32[24,128]{1,0:T(8,128)S(1)} %collective-permute-done.7.refs_1_, ...), custom_call_target="tpu_custom_call" | custom-call | flops 1000000 | bytes 1000000 | tf_op jit(solution)/shard_map/pallas_call | solution.py:591
  (24 shorter events, 0.1 us)
Async XLA Ops:
  0.6 1.1 %copy-start.1 = (f32[6,12,12,128]{3,2,1,0:T(8,128)S(1)}, f32[6,12,12,128]{3,2,1,0:T(8,128)}, u32[]{:S(2)}) copy-start(f32[6,12,12,128]{3,2,1,0:T(8,128)} %block.1) | copy-start | bytes 1327108
  1.7 4.8 %copy-start.6 = (f32[12,12,128]{2,1,0:T(8,128)S(1)}, f32[12,12,128]{2,1,0:T(8,128)}, u32[]{:S(2)}) copy-start(f32[12,12,128]{2,1,0:T(8,128)} %perm.2) | copy-start | bytes 221188
  1.8 7.2 %collective-permute-start = (f32[6,12,12,128]{3,2,1,0:T(8,128)S(1)}, f32[6,12,12,128]{3,2,1,0:T(8,128)S(1)}, u32[]{:S(2)}, u32[]{:S(2)}) collective-permute-start(f32[6,12,12,128]{3,2,1,0:T(8,128)S(1)} %get-tuple-element.20.refs_0_), channel_id=1, source_target_pairs={{0,1},{1,0},{2,3},{3,2},{4,5},{5,4},{6,7},{7,6},{8,9},{9,8},{10,11... | collective-permute-start | bytes 1327112 | tf_op jit(solution)/shard_map/ppermute | solution.py:527
  2.3 5.4 %collective-permute-start.1 = (f32[5,12,128]{2,1,0:T(8,128)S(1)}, f32[5,12,128]{2,1,0:T(8,128)S(1)}, u32[]{:S(2)}, u32[]{:S(2)}) collective-permute-start(f32[5,12,128]{2,1,0:T(8,128)S(1)} %get-tuple-element.23), channel_id=1, source_target_pairs={{0,4},{4,0},{8,12},{12,8},{1,5},{5,1},{9,13},{13,9},{2,6},{6,2},{1... | collective-permute-start | bytes 92168 | tf_op jit(solution)/shard_map/ppermute | solution.py:521
  4.9 4.0 %collective-permute-start.2 = (f32[5,12,128]{2,1,0:T(8,128)S(1)}, f32[5,12,128]{2,1,0:T(8,128)S(1)}, u32[]{:S(2)}, u32[]{:S(2)}) collective-permute-start(f32[5,12,128]{2,1,0:T(8,128)S(1)} %get-tuple-element.24), channel_id=1, source_target_pairs={{0,2},{2,0},{1,3},{3,1},{4,6},{6,4},{5,7},{7,5},{8,10},{10,8},{9,1... | collective-permute-start | bytes 92168 | tf_op jit(solution)/shard_map/ppermute | solution.py:522
  6.4 0.7 %copy-start.9 = (s32[1,4,2]{1,2,0:T(2,128)S(1)}, s32[1,4,2]{1,2,0:T(2,128)}, u32[]{:S(2)}) copy-start(s32[1,4,2]{1,2,0:T(2,128)} %param.15) | copy-start | bytes 100
  6.4 0.7 %copy-start.8 = (s32[1,1,2,3]{3,2,1,0:T(2,128)S(1)}, s32[1,1,2,3]{3,2,1,0:T(2,128)}, u32[]{:S(2)}) copy-start(s32[1,1,2,3]{3,2,1,0:T(2,128)} %corner.1) | copy-start | bytes 76
  6.4 2.5 %collective-permute-start.3 = (f32[5,12,128]{2,1,0:T(8,128)S(1)}, f32[5,12,128]{2,1,0:T(8,128)S(1)}, u32[]{:S(2)}, u32[]{:S(2)}) collective-permute-start(f32[5,12,128]{2,1,0:T(8,128)S(1)} %get-tuple-element.25), channel_id=1, source_target_pairs={{0,1},{1,0},{4,8},{5,9},{8,4},{9,5},{12,13},{13,12},{2,3},{3,2},{6... | collective-permute-start | bytes 92168 | tf_op jit(solution)/shard_map/ppermute | solution.py:523
  9.0 3.1 %copy-start = (f32[1,1,4,6,4096]{4,2,3,1,0:T(4,128)S(1)}, f32[1,1,4,6,4096]{4,2,3,1,0:T(4,128)}, u32[]{:S(2)}) copy-start(f32[1,1,4,6,4096]{4,2,3,1,0:T(4,128)} %param.12) | copy-start | bytes 1179652
  9.0 3.1 %copy-start.5 = (bf16[256,384]{1,0:T(8,128)(2,1)S(1)}, bf16[256,384]{1,0:T(8,128)(2,1)}, u32[]{:S(2)}) copy-start(bf16[256,384]{1,0:T(8,128)(2,1)} %constant.8.clone.table) | copy-start | bytes 589828
  9.0 3.1 %copy-start.7 = (f32[1,1,4,4096]{3,2,1,0:T(4,128)S(1)}, f32[1,1,4,4096]{3,2,1,0:T(4,128)}, u32[]{:S(2)}) copy-start(f32[1,1,4,4096]{3,2,1,0:T(4,128)} %perm.3) | copy-start | bytes 196612
  10.1 5.1 %copy-start.2 = (bf16[2,256,384]{2,1,0:T(8,128)(2,1)S(1)}, bf16[2,256,384]{2,1,0:T(8,128)(2,1)}, u32[]{:S(2)}) copy-start(bf16[2,256,384]{2,1,0:T(8,128)(2,1)} %constant.9.clone.refs_6_) | copy-start | bytes 1179652
  10.1 5.1 %collective-permute-start.4 = (f32[104,128]{1,0:T(8,128)S(1)}, f32[104,128]{1,0:T(8,128)S(1)}, u32[]{:S(2)}, u32[]{:S(2)}) collective-permute-start(f32[104,128]{1,0:T(8,128)S(1)} %get-tuple-element.27), channel_id=1, source_target_pairs={{0,1},{1,0},{2,3},{3,2},{4,5},{5,4},{6,7},{7,6},{8,9},{9,8},{10,11... | collective-permute-start | bytes 159752 | tf_op jit(solution)/shard_map/ppermute | solution.py:550
  10.2 4.0 %collective-permute-start.5 = (f32[72,128]{1,0:T(8,128)S(1)}, f32[72,128]{1,0:T(8,128)S(1)}, u32[]{:S(2)}, u32[]{:S(2)}) collective-permute-start(f32[72,128]{1,0:T(8,128)S(1)} %get-tuple-element.28), channel_id=1, source_target_pairs={{0,2},{1,3},{2,0},{3,1},{4,6},{5,7},{6,4},{7,5},{8,10},{9,11},{10,... | collective-permute-start | bytes 110600 | tf_op jit(solution)/shard_map/ppermute | solution.py:550
  11.8 3.4 %collective-permute-start.6 = (f32[72,128]{1,0:T(8,128)S(1)}, f32[72,128]{1,0:T(8,128)S(1)}, u32[]{:S(2)}, u32[]{:S(2)}) collective-permute-start(f32[72,128]{1,0:T(8,128)S(1)} %get-tuple-element.29), channel_id=1, source_target_pairs={{0,3},{1,2},{2,1},{3,0},{4,7},{5,6},{6,5},{7,4},{8,11},{9,10},{10,... | collective-permute-start | bytes 110600 | tf_op jit(solution)/shard_map/ppermute | solution.py:550
  12.1 3.1 %copy-start.4 = (bf16[768,128]{1,0:T(8,128)(2,1)S(1)}, bf16[768,128]{1,0:T(8,128)(2,1)}, u32[]{:S(2)}) copy-start(bf16[768,128]{1,0:T(8,128)(2,1)} %constant.10.clone.refs_7_) | copy-start | bytes 589828
  15.2 3.1 %copy-start.3 = (bf16[384,256]{1,0:T(8,128)(2,1)S(1)}, bf16[384,256]{1,0:T(8,128)(2,1)}, u32[]{:S(2)}) copy-start(bf16[384,256]{1,0:T(8,128)(2,1)} %constant.11.clone.table) | copy-start | bytes 589828
  16.4 3.1 %collective-permute-start.7 = (f32[24,128]{1,0:T(8,128)S(1)}, f32[24,128]{1,0:T(8,128)S(1)}, u32[]{:S(2)}, u32[]{:S(2)}) collective-permute-start(f32[24,128]{1,0:T(8,128)S(1)} %get-tuple-element.34), channel_id=1, source_target_pairs={{0,1},{1,0},{2,3},{3,2},{4,5},{5,4},{6,7},{7,6},{8,9},{9,8},{10,11... | collective-permute-start | bytes 36872 | tf_op jit(solution)/shard_map/ppermute | solution.py:550
  16.6 3.7 %collective-permute-start.8 = (f32[24,128]{1,0:T(8,128)S(1)}, f32[24,128]{1,0:T(8,128)S(1)}, u32[]{:S(2)}, u32[]{:S(2)}) collective-permute-start(f32[24,128]{1,0:T(8,128)S(1)} %get-tuple-element.35), channel_id=1, source_target_pairs={{0,2},{1,3},{2,0},{3,1},{4,6},{5,7},{6,4},{7,5},{8,10},{9,11},{10,... | collective-permute-start | bytes 36872 | tf_op jit(solution)/shard_map/ppermute | solution.py:550
  17.6 3.1 %collective-permute-start.9 = (f32[24,128]{1,0:T(8,128)S(1)}, f32[24,128]{1,0:T(8,128)S(1)}, u32[]{:S(2)}, u32[]{:S(2)}) collective-permute-start(f32[24,128]{1,0:T(8,128)S(1)} %get-tuple-element.36), channel_id=1, source_target_pairs={{0,3},{1,2},{2,1},{3,0},{4,7},{5,6},{6,5},{7,4},{8,11},{9,10},{10,... | collective-permute-start | bytes 36872 | tf_op jit(solution)/shard_map/ppermute | solution.py:550

commit v10 on v9

--- a/solution.py
+++ b/solution.py
@@ -131,7 +131,44 @@
     kept[...] = block[...]
 
 
-def notes_kernel(corner, owners, perm, notes, rate):
+def pack(source, deep, spot, time, packed, q, early):
+    lane = lane_iota((8, LANES))
+    cx, cy, cz = spot
+
+    def rows_of(c, k, j, count, over_c):
+        step = deep * 16 if over_c else 16
+        return source[pl.ds((c * deep + cx - 1 + k) * 16 + cy + (j - 1), count, stride=step), :]
+
+    def aim(rows, target):
+        return pltpu.roll(rows, lax.rem(target - (cz - 1) + 2 * LANES, LANES), 1)
+
+    for c in range(6):
+        total = jnp.zeros((8, LANES), F32) if early is None else early[q, c * 8 : c * 8 + 8, :]
+        for j in range(RIM):
+            if (j == 0 and c == 4) or (j == RIM - 1 and c not in (0, 2)) or (0 < j < RIM - 1 and c == 5):
+                continue
+            first = rim_lane(time, j, 0)
+            if j in (0, RIM - 1):
+                inside = (lane >= first) & (lane < first + RIM)
+            else:
+                inside = (lane == first) | (lane == first + RIM - 1)
+            total = jnp.where(inside, aim(rows_of(c, 1, j, 8, False), first), total)
+        packed[q, c * 8 : c * 8 + 8, :] = total
+    low = jnp.zeros((6, LANES), F32)
+    high = jnp.zeros((2, LANES), F32)
+    for j in range(RIM):
+        first = j * RIM
+        inside = (lane >= first) & (lane < first + RIM)
+        low = jnp.where(inside[0:6], aim(rows_of(0, 0, j, 6, True), first), low)
+        high = jnp.where(inside[0:2], aim(rows_of(1, RIM - 1, j, 2, True), first), high)
+    base = ROWS_RIM + time * 8
+    packed[q, base : base + 6, :] = low
+    packed[q, base + 6 : base + 8, :] = high
+    if early is not None:
+        packed[q, ROWS_RIM:base, :] = early[q, ROWS_RIM:base, :]
+
+
+def notes_kernel(corner, owners, perm, block, notes, rate, early, flat):
     rank = lax.axis_index("gy") * lax.axis_size("gz") + lax.axis_index("gz")
 
     def note(row, value):
@@ -145,12 +182,19 @@
         live = (owners[0, 0, slot] == rank) | (owners[0, 1, slot] == rank)
         note(8 + slot, live.astype(jnp.int32))
     rate[...] = 0.5 / perm[...]
+    deep, tall = block.shape[1], block.shape[2]
+    for c in range(6):
+        for x in range(deep):
+            flat[pl.ds((c * deep + x) * 16, tall), :] = block[c, x]
+    for q in range(PAR):
+        spot = [corner[0, 0, q, d] for d in range(3)]
+        pack(flat, deep, spot, 0, early, q, None)
 
 
 def leap_kernel(two_y, ranks, *refs):
-    block, beside, rate, notes, x_even, y_even, x_odd = refs[:7]
-    y_odd = refs[7] if two_y else None
-    refs = refs[7 + two_y :]
+    block, beside, rate, notes, early, x_even, y_even, x_odd = refs[:8]
+    y_odd = refs[8] if two_y else None
+    refs = refs[8 + two_y :]
     new, sends = refs[0], refs[1 : 1 + ranks]
     pad, side, mag, fresh, packed = refs[1 + ranks :]
     deep, tall = block.shape[1], block.shape[2]
@@ -238,43 +282,8 @@
             new[c + 3, x] = (h0, h1, h2)[c][0:tall]
             fresh[pl.ds((c * deep + x) * 16, tall), :] = value
             fresh[pl.ds(((c + 3) * deep + x) * 16, tall), :] = (h0, h1, h2)[c][0:tall]
-    lane = lane_iota((8, LANES))
     for q in range(PAR):
-        cx, cy, cz = spots[q]
-
-        def rows_of(time, c, k, j, count, over_c):
-            source, depth, start = (pad, full, cx) if time == 0 else (fresh, deep, cx - 1)
-            step = depth * 16 if over_c else 16
-            return source[pl.ds((c * depth + start + k) * 16 + cy + (j - 1), count, stride=step), :]
-
-        def aim(rows, target):
-            return pltpu.roll(rows, lax.rem(target - (cz - 1) + 2 * LANES, LANES), 1)
-
-        for c in range(6):
-            total = jnp.zeros((8, LANES), F32)
-            for j in range(RIM):
-                if (j == 0 and c == 4) or (j == RIM - 1 and c not in (0, 2)) or (0 < j < RIM - 1 and c == 5):
-                    continue
-                for time in range(2):
-                    first = rim_lane(time, j, 0)
-                    rows = aim(rows_of(time, c, 1, j, 8, False), first)
-                    if j in (0, RIM - 1):
-                        inside = (lane >= first) & (lane < first + RIM)
-                    else:
-                        inside = (lane == first) | (lane == first + RIM - 1)
-                    total = jnp.where(inside, rows, total)
-            packed[q, c * 8 : c * 8 + 8, :] = total
-        for time in range(2):
-            low = jnp.zeros((6, LANES), F32)
-            high = jnp.zeros((2, LANES), F32)
-            for j in range(RIM):
-                first = j * RIM
-                inside = (lane >= first) & (lane < first + RIM)
-                low = jnp.where(inside[0:6], aim(rows_of(time, 0, 0, j, 6, True), first), low)
-                high = jnp.where(inside[0:2], aim(rows_of(time, 1, RIM - 1, j, 2, True), first), high)
-            base = ROWS_RIM + time * 8
-            packed[q, base : base + 6, :] = low
-            packed[q, base + 6 : base + 8, :] = high
+        pack(fresh, deep, spots[q], 1, packed, q, early)
         packed[q, ROW_EDGE:ROWS_PATCH, :] = jnp.zeros((ROWS_PATCH - ROW_EDGE, LANES), F32)
         packed[q, ROW_EDGE : ROW_EDGE + 1, :] = pad[pl.ds(at(1, full - 1) + tall - 1, 1), :]
         packed[q, ROW_EDGE + 1 : ROW_EDGE + 2, :] = pad[pl.ds(at(0, 0), 1), :]
@@ -527,11 +536,16 @@
     beside = lax.ppermute(kept, "gz", swap_pairs(2, 0))
 
     fine = fine_fields.transpose(0, 1, 3, 2, 4)
-    notes, rate = call(
+    notes, rate, early = call(
         notes_kernel,
-        [shape((8 + slots, LANES), jnp.int32), shape(permittivity.shape, F32)],
-        [whole(pltpu.SMEM)] * 2 + [vmem],
-    )(patch_corner, patch_owner.transpose(0, 2, 1), permittivity)
+        [
+            shape((8 + slots, LANES), jnp.int32),
+            shape(permittivity.shape, F32),
+            shape((PAR, ROWS_RIM + 8, LANES), F32),
+        ],
+        [whole(pltpu.SMEM)] * 2 + [vmem] * 2,
+        [pltpu.VMEM((6 * deep * 16, LANES), F32)],
+    )(patch_corner, patch_owner.transpose(0, 2, 1), permittivity, kept)
     box, fine_rate = call(
         load_kernel,
         [shape((groups, 6, ROWS_BOX, WIDE), F32), shape((groups, ROWS_BOX, WIDE), F32)],
@@ -554,7 +568,7 @@
     new, *sends = call(
         functools.partial(leap_kernel, two_y, ranks),
         [shape(coarse_fields.shape, F32)] + patches,
-        [vmem] * (4 + len(got)),
+        [vmem] * (5 + len(got)),
         [
             pltpu.VMEM((6 * full * 16, LANES), F32),
             pltpu.VMEM((6 * full * 16, LANES), F32),
@@ -562,7 +576,7 @@
             pltpu.VMEM((6 * deep * 16, LANES), F32),
             pltpu.VMEM((PAR, ROWS_PATCH, LANES), F32),
         ],
-    )(kept, beside, rate, notes, *got)
+    )(kept, beside, rate, notes, early, *got)
     regions = exchange(sends)
 
     box, *smalls = call(

time: 21.9 us -> 21.7 us (level)
  waiting for transfers between devices: 5.03 us -> 4.79 us
    pallas_call x1, Pallas kernels: 0.58 us -> 0.84 us  [local(): call(notes_kernel, [shape((8 + slots, LANES), jnp.int32), shape(permittiv...]
    ppermute x1, waiting for transfers between devices: 1.22 us -> 0.97 us  [local(): lax.ppermute(faces[1], 'gy', swap_pairs(count_y, 0))]
  transfers between devices with their start and end apart: 10 -> 10, of which waited for: 5 -> 5; matrix products, arithmetic and copies ran while one was open for 0% -> 0% of each run, Pallas kernels for 10% -> 11%
where the time goes in v10:
time: 21.7 us; the launch traced here: 21.5 us
  starting transfers between devices  8.52 us (39%)
  Pallas kernels  5.68 us (26%)
  waiting for transfers between devices  4.79 us (22%)
  local copies, waits for them, and re-layouts  1.78 us (8%)
  between operations  0.75 us (3%)
    ppermute x6, starting transfers between devices, exchange(): got[k] = lax.ppermute(parts[k], ('gy', 'gz'), swaps[k])  3.86 us
    ppermute x6, waiting for transfers between devices, exchange(): got[k] = lax.ppermute(parts[k], ('gy', 'gz'), swaps[k])  3.82 us
    ppermute x1, starting transfers between devices, local(): lax.ppermute(faces[0], 'gx', swap_pairs(count_x, 0))  2.65 us
    unnamed x20, local copies, waits for them, and re-layouts  1.78 us
    ppermute x1, starting transfers between devices, local(): lax.ppermute(faces[1], 'gy', swap_pairs(count_y, 0))  1.49 us
    pallas_call x1, Pallas kernels, local(): call(functools.partial(fine_kernel, ranks), [shape((groups, 6, ROWS_BOX,...  1.16 us
    pallas_call x1, Pallas kernels, local(): call(store_kernel, shape(fine.shape, F32), [vmem] * 4, [pltpu.VMEM(fine.s...  1.11 us
    pallas_call x1, Pallas kernels, local(): call(functools.partial(place_kernel, ranks), shape(coarse_fields.shape, F...  1 us
  transfers between devices with their start and end apart: 10, of which 5 were waited for; matrix products, arithmetic and copies ran while one was open for 0% of the time, Pallas kernels for 11%

profile of v10, /device:TPU:0, one launch (start us, length us, event | category | flops | bytes accessed | tf_op | source)
XLA Modules:
  0.0 21.5 jit_solution(8120747890847823448)
XLA Ops:
  0.6 1.1 %copy-done.1 = f32[6,12,12,128]{3,2,1,0:T(8,128)S(1)} copy-done((f32[6,12,12,128]{3,2,1,0:T(8,128)S(1)}, f32[6,12,12,128]{3,2,1,0:T(8,128)}, u32[]{:S(2)}) %copy-start.1) | copy-done | bytes 442392
  1.7 0.1 shard_map.113
  1.8 0.5 %collective-permute-start = (f32[6,12,12,128]{3,2,1,0:T(8,128)S(1)}, f32[6,12,12,128]{3,2,1,0:T(8,128)S(1)}, u32[]{:S(2)}, u32[]{:S(2)}) collective-permute-start(f32[6,12,12,128]{3,2,1,0:T(8,128)S(1)} %get-tuple-element.21.block.refs_0_), channel_id=1, source_target_pairs={{0,1},{1,0},{2,3},{3,2},{4,5},{5,4},{6,7},{7,6},{8,9},{9,8},{10,11... | collective-permute-start | bytes 1327112 | tf_op jit(solution)/shard_map/ppermute | solution.py:536
  2.3 2.6 %collective-permute-start.1 = (f32[5,12,128]{2,1,0:T(8,128)S(1)}, f32[5,12,128]{2,1,0:T(8,128)S(1)}, u32[]{:S(2)}, u32[]{:S(2)}) collective-permute-start(f32[5,12,128]{2,1,0:T(8,128)S(1)} %get-tuple-element.25), channel_id=1, source_target_pairs={{0,4},{4,0},{8,12},{12,8},{1,5},{5,1},{9,13},{13,9},{2,6},{6,2},{1... | collective-permute-start | bytes 92168 | tf_op jit(solution)/shard_map/ppermute | solution.py:530
  4.9 1.5 %collective-permute-start.2 = (f32[5,12,128]{2,1,0:T(8,128)S(1)}, f32[5,12,128]{2,1,0:T(8,128)S(1)}, u32[]{:S(2)}, u32[]{:S(2)}) collective-permute-start(f32[5,12,128]{2,1,0:T(8,128)S(1)} %get-tuple-element.26), channel_id=1, source_target_pairs={{0,2},{2,0},{1,3},{3,1},{4,6},{6,4},{5,7},{7,5},{8,10},{10,8},{9,1... | collective-permute-start | bytes 92168 | tf_op jit(solution)/shard_map/ppermute | solution.py:531
  6.5 0.7 %copy-done.9 = s32[1,4,2]{1,2,0:T(2,128)S(1)} copy-done((s32[1,4,2]{1,2,0:T(2,128)S(1)}, s32[1,4,2]{1,2,0:T(2,128)}, u32[]{:S(2)}) %copy-start.9) | copy-done | bytes 56
  7.1 0.8 %shard_map.114 = (s32[12,128]{1,0:T(8,128)S(1)}, f32[12,12,128]{2,1,0:T(8,128)S(1)}, f32[2,56,128]{2,1,0:T(8,128)S(1)}) custom-call(s32[1,1,2,3]{3,2,1,0:T(2,128)S(1)} %copy-done.8, s32[1,2,4]{2,1,0:T(2,128)S(1)} %bitcast.5, f32[12,12,128]{2,1,0:T(8,128)S(1)} %copy-done.6, f32[6,12,12,128]{3,2,1,0:T(8,128)S(1)} %get-tuple-element.21.block.refs_0_), custom_call_target="tpu_custom_call" | custom-call | flops 1000000 | bytes 1000000 | tf_op jit(solution)/shard_map/pallas_call | solution.py:539
  8.0 1.0 %collective-permute-done.2.refs_6_ = f32[5,12,128]{2,1,0:T(8,128)S(1)} collective-permute-done((f32[5,12,128]{2,1,0:T(8,128)S(1)}, f32[5,12,128]{2,1,0:T(8,128)S(1)}, u32[]{:S(2)}, u32[]{:S(2)}) %collective-permute-start.2) | collective-permute-done | bytes 30752 | tf_op jit(solution)/shard_map/ppermute | solution.py:531
  9.0 1.0 %shard_map.115 = (f32[6,12,12,128]{3,2,1,0:T(8,128)S(1)}, f32[72,128]{1,0:T(8,128)S(1)}, f32[104,128]{1,0:T(8,128)S(1)}, f32[72,128]{1,0:T(8,128)S(1)}, f32[72,128]{1,0:T(8,128)S(1)}) custom-call(f32[6,12,12,128]{3,2,1,0:T(8,128)S(1)} %get-tuple-element.21.block.refs_0_, f32[6,12,12,128]{3,2,1,0:T(8,128)S(1)} %collective-permute-done.refs_1_, ...), custom_call_target="tpu_custom_call" | custom-call | flops 1000000 | bytes 1000000 | tf_op jit(solution)/shard_map/pallas_call | solution.py:568
  10.0 0.1 collective-permute-start.4
  10.1 1.6 %collective-permute-start.5 = (f32[72,128]{1,0:T(8,128)S(1)}, f32[72,128]{1,0:T(8,128)S(1)}, u32[]{:S(2)}, u32[]{:S(2)}) collective-permute-start(f32[72,128]{1,0:T(8,128)S(1)} %get-tuple-element.30), channel_id=1, source_target_pairs={{0,2},{1,3},{2,0},{3,1},{4,6},{5,7},{6,4},{7,5},{8,10},{9,11},{10,... | collective-permute-start | bytes 110600 | tf_op jit(solution)/shard_map/ppermute | solution.py:564
  11.6 0.3 %collective-permute-start.6 = (f32[72,128]{1,0:T(8,128)S(1)}, f32[72,128]{1,0:T(8,128)S(1)}, u32[]{:S(2)}, u32[]{:S(2)}) collective-permute-start(f32[72,128]{1,0:T(8,128)S(1)} %get-tuple-element.31), channel_id=1, source_target_pairs={{0,3},{1,2},{2,1},{3,0},{4,7},{5,6},{6,5},{7,4},{8,11},{9,10},{10,... | collective-permute-start | bytes 110600 | tf_op jit(solution)/shard_map/ppermute | solution.py:564
  11.9 0.4 %shard_map.117 = (f32[1,6,72,384]{3,2,1,0:T(8,128)S(1)}, f32[1,72,384]{2,1,0:T(8,128)S(1)}) custom-call(f32[1,1,6,4,4096]{4,3,2,1,0:T(4,128)S(1)} %bitcast.3, f32[1,1,4,4096]{3,2,1,0:T(4,128)S(1)} %copy-done.7, bf16[256,384]{1,0:T(8,128)(2,1)S(1)} %copy-done.5), custom_call_target="tpu_custom_call" | custom-call | flops 1000000 | bytes 4000000 | tf_op jit(solution)/shard_map/pallas_call | solution.py:549
  12.4 1.7 %collective-permute-done.5.refs_1_.refs_2_ = f32[72,128]{1,0:T(8,128)S(1)} collective-permute-done((f32[72,128]{1,0:T(8,128)S(1)}, f32[72,128]{1,0:T(8,128)S(1)}, u32[]{:S(2)}, u32[]{:S(2)}) %collective-permute-start.5) | collective-permute-done | bytes 36896 | tf_op jit(solution)/shard_map/ppermute | solution.py:564
  14.1 1.0 %collective-permute-done.6.refs_2_.refs_3_ = f32[72,128]{1,0:T(8,128)S(1)} collective-permute-done((f32[72,128]{1,0:T(8,128)S(1)}, f32[72,128]{1,0:T(8,128)S(1)}, u32[]{:S(2)}, u32[]{:S(2)}) %collective-permute-start.6) | collective-permute-done | bytes 36896 | tf_op jit(solution)/shard_map/ppermute | solution.py:564
  15.1 1.2 %shard_map.118 = (f32[1,6,72,384]{3,2,1,0:T(8,128)S(1)}, f32[24,128]{1,0:T(8,128)S(1)}, f32[24,128]{1,0:T(8,128)S(1)}, f32[24,128]{1,0:T(8,128)S(1)}, f32[24,128]{1,0:T(8,128)S(1)}) custom-call(f32[72,128]{1,0:T(8,128)S(1)} %get-tuple-element.32.refs_0_, f32[104,128]{1,0:T(8,128)S(1)} %collective-permute-done.4.refs_0_.refs_1_, ...), custom_call_target="tpu_custom_call" | custom-call | flops 1000000 | bytes 1000000 | tf_op jit(solution)/shard_map/pallas_call | solution.py:582
  16.2 0.2 %collective-permute-start.7 = (f32[24,128]{1,0:T(8,128)S(1)}, f32[24,128]{1,0:T(8,128)S(1)}, u32[]{:S(2)}, u32[]{:S(2)}) collective-permute-start(f32[24,128]{1,0:T(8,128)S(1)} %get-tuple-element.36), channel_id=1, source_target_pairs={{0,1},{1,0},{2,3},{3,2},{4,5},{5,4},{6,7},{7,6},{8,9},{9,8},{10,11... | collective-permute-start | bytes 36872 | tf_op jit(solution)/shard_map/ppermute | solution.py:564
  16.5 0.9 %collective-permute-start.8 = (f32[24,128]{1,0:T(8,128)S(1)}, f32[24,128]{1,0:T(8,128)S(1)}, u32[]{:S(2)}, u32[]{:S(2)}) collective-permute-start(f32[24,128]{1,0:T(8,128)S(1)} %get-tuple-element.37), channel_id=1, source_target_pairs={{0,2},{1,3},{2,0},{3,1},{4,6},{5,7},{6,4},{7,5},{8,10},{9,11},{10,... | collective-permute-start | bytes 36872 | tf_op jit(solution)/shard_map/ppermute | solution.py:564
  17.4 0.8 %collective-permute-start.9 = (f32[24,128]{1,0:T(8,128)S(1)}, f32[24,128]{1,0:T(8,128)S(1)}, u32[]{:S(2)}, u32[]{:S(2)}) collective-permute-start(f32[24,128]{1,0:T(8,128)S(1)} %get-tuple-element.38), channel_id=1, source_target_pairs={{0,3},{1,2},{2,1},{3,0},{4,7},{5,6},{6,5},{7,4},{8,11},{9,10},{10,... | collective-permute-start | bytes 36872 | tf_op jit(solution)/shard_map/ppermute | solution.py:564
  18.2 1.1 %shard_map.120 = f32[1,1,6,4,4096]{4,3,2,1,0:T(4,128)} custom-call(f32[1,6,72,384]{3,2,1,0:T(8,128)S(1)} %get-tuple-element.39.box, f32[1,1,6,4,4096]{4,3,2,1,0:T(4,128)S(1)} %bitcast.4, s32[12,128]{1,0:T(8,128)S(1)} %get-tuple-element.23.refs_3_.notes, bf16[384,256]{1,0:T(8,128)(2,1)S(1)} %copy-done.3), custom_call_target="tpu_custom_call" | custom-call | flops 1000000 | bytes 4000000 | tf_op jit(solution)/shard_map/pallas_call | solution.py:596
  19.3 0.1 shard_map.116.new
  19.4 0.8 %collective-permute-done.8.refs_2_ = f32[24,128]{1,0:T(8,128)S(1)} collective-permute-done((f32[24,128]{1,0:T(8,128)S(1)}, f32[24,128]{1,0:T(8,128)S(1)}, u32[]{:S(2)}, u32[]{:S(2)}) %collective-permute-start.8) | collective-permute-done | bytes 12320 | tf_op jit(solution)/shard_map/ppermute | solution.py:564
  20.2 0.4 %collective-permute-done.9.refs_3_ = f32[24,128]{1,0:T(8,128)S(1)} collective-permute-done((f32[24,128]{1,0:T(8,128)S(1)}, f32[24,128]{1,0:T(8,128)S(1)}, u32[]{:S(2)}, u32[]{:S(2)}) %collective-permute-start.9) | collective-permute-done | bytes 12320 | tf_op jit(solution)/shard_map/ppermute | solution.py:564
  20.5 1.0 %shard_map.119 = f32[6,12,12,128]{3,2,1,0:T(8,128)} custom-call(f32[6,12,12,128]{3,2,1,0:T(8,128)S(1)} %shard_map.116.new, s32[12,128]{1,0:T(8,128)S(1)} %get-tuple-element.23.refs_3_.notes, f32[24,128]{1,0:T(8,128)S(1)} %get-tuple-element.35.refs_0_, f32[24,128]{1,0:T(8,128)S(1)} %collective-permute-done.7.refs_1_, ...), custom_call_target="tpu_custom_call" | custom-call | flops 1000000 | bytes 1000000 | tf_op jit(solution)/shard_map/pallas_call | solution.py:605
  (24 shorter events, 0.1 us)
Async XLA Ops:
  0.6 1.1 %copy-start.1 = (f32[6,12,12,128]{3,2,1,0:T(8,128)S(1)}, f32[6,12,12,128]{3,2,1,0:T(8,128)}, u32[]{:S(2)}) copy-start(f32[6,12,12,128]{3,2,1,0:T(8,128)} %block.1) | copy-start | bytes 1327108
  1.7 4.8 %copy-start.6 = (f32[12,12,128]{2,1,0:T(8,128)S(1)}, f32[12,12,128]{2,1,0:T(8,128)}, u32[]{:S(2)}) copy-start(f32[12,12,128]{2,1,0:T(8,128)} %perm.2) | copy-start | bytes 221188
  1.8 7.2 %collective-permute-start = (f32[6,12,12,128]{3,2,1,0:T(8,128)S(1)}, f32[6,12,12,128]{3,2,1,0:T(8,128)S(1)}, u32[]{:S(2)}, u32[]{:S(2)}) collective-permute-start(f32[6,12,12,128]{3,2,1,0:T(8,128)S(1)} %get-tuple-element.21.block.refs_0_), channel_id=1, source_target_pairs={{0,1},{1,0},{2,3},{3,2},{4,5},{5,4},{6,7},{7,6},{8,9},{9,8},{10,11... | collective-permute-start | bytes 1327112 | tf_op jit(solution)/shard_map/ppermute | solution.py:536
  2.3 5.7 %collective-permute-start.1 = (f32[5,12,128]{2,1,0:T(8,128)S(1)}, f32[5,12,128]{2,1,0:T(8,128)S(1)}, u32[]{:S(2)}, u32[]{:S(2)}) collective-permute-start(f32[5,12,128]{2,1,0:T(8,128)S(1)} %get-tuple-element.25), channel_id=1, source_target_pairs={{0,4},{4,0},{8,12},{12,8},{1,5},{5,1},{9,13},{13,9},{2,6},{6,2},{1... | collective-permute-start | bytes 92168 | tf_op jit(solution)/shard_map/ppermute | solution.py:530
  4.9 4.0 %collective-permute-start.2 = (f32[5,12,128]{2,1,0:T(8,128)S(1)}, f32[5,12,128]{2,1,0:T(8,128)S(1)}, u32[]{:S(2)}, u32[]{:S(2)}) collective-permute-start(f32[5,12,128]{2,1,0:T(8,128)S(1)} %get-tuple-element.26), channel_id=1, source_target_pairs={{0,2},{2,0},{1,3},{3,1},{4,6},{6,4},{5,7},{7,5},{8,10},{10,8},{9,1... | collective-permute-start | bytes 92168 | tf_op jit(solution)/shard_map/ppermute | solution.py:531
  6.4 0.7 %copy-start.9 = (s32[1,4,2]{1,2,0:T(2,128)S(1)}, s32[1,4,2]{1,2,0:T(2,128)}, u32[]{:S(2)}) copy-start(s32[1,4,2]{1,2,0:T(2,128)} %param.15) | copy-start | bytes 100
  6.4 0.7 %copy-start.8 = (s32[1,1,2,3]{3,2,1,0:T(2,128)S(1)}, s32[1,1,2,3]{3,2,1,0:T(2,128)}, u32[]{:S(2)}) copy-start(s32[1,1,2,3]{3,2,1,0:T(2,128)} %corner.1) | copy-start | bytes 76
  6.4 2.5 %collective-permute-start.3 = (f32[5,12,128]{2,1,0:T(8,128)S(1)}, f32[5,12,128]{2,1,0:T(8,128)S(1)}, u32[]{:S(2)}, u32[]{:S(2)}) collective-permute-start(f32[5,12,128]{2,1,0:T(8,128)S(1)} %get-tuple-element.27), channel_id=1, source_target_pairs={{0,1},{1,0},{4,8},{5,9},{8,4},{9,5},{12,13},{13,12},{2,3},{3,2},{6... | collective-permute-start | bytes 92168 | tf_op jit(solution)/shard_map/ppermute | solution.py:532
  9.0 3.0 %copy-start = (f32[1,1,4,6,4096]{4,2,3,1,0:T(4,128)S(1)}, f32[1,1,4,6,4096]{4,2,3,1,0:T(4,128)}, u32[]{:S(2)}) copy-start(f32[1,1,4,6,4096]{4,2,3,1,0:T(4,128)} %param.12) | copy-start | bytes 1179652
  9.0 3.0 %copy-start.5 = (bf16[256,384]{1,0:T(8,128)(2,1)S(1)}, bf16[256,384]{1,0:T(8,128)(2,1)}, u32[]{:S(2)}) copy-start(bf16[256,384]{1,0:T(8,128)(2,1)} %constant.8.clone.table) | copy-start | bytes 589828
  9.0 2.9 %copy-start.7 = (f32[1,1,4,4096]{3,2,1,0:T(4,128)S(1)}, f32[1,1,4,4096]{3,2,1,0:T(4,128)}, u32[]{:S(2)}) copy-start(f32[1,1,4,4096]{3,2,1,0:T(4,128)} %perm.3) | copy-start | bytes 196612
  10.0 5.1 %copy-start.2 = (bf16[2,256,384]{2,1,0:T(8,128)(2,1)S(1)}, bf16[2,256,384]{2,1,0:T(8,128)(2,1)}, u32[]{:S(2)}) copy-start(bf16[2,256,384]{2,1,0:T(8,128)(2,1)} %constant.9.clone.refs_6_) | copy-start | bytes 1179652
  10.0 5.1 %collective-permute-start.4 = (f32[104,128]{1,0:T(8,128)S(1)}, f32[104,128]{1,0:T(8,128)S(1)}, u32[]{:S(2)}, u32[]{:S(2)}) collective-permute-start(f32[104,128]{1,0:T(8,128)S(1)} %get-tuple-element.29), channel_id=1, source_target_pairs={{0,1},{1,0},{2,3},{3,2},{4,5},{5,4},{6,7},{7,6},{8,9},{9,8},{10,11... | collective-permute-start | bytes 159752 | tf_op jit(solution)/shard_map/ppermute | solution.py:564
  10.1 4.0 %collective-permute-start.5 = (f32[72,128]{1,0:T(8,128)S(1)}, f32[72,128]{1,0:T(8,128)S(1)}, u32[]{:S(2)}, u32[]{:S(2)}) collective-permute-start(f32[72,128]{1,0:T(8,128)S(1)} %get-tuple-element.30), channel_id=1, source_target_pairs={{0,2},{1,3},{2,0},{3,1},{4,6},{5,7},{6,4},{7,5},{8,10},{9,11},{10,... | collective-permute-start | bytes 110600 | tf_op jit(solution)/shard_map/ppermute | solution.py:564
  11.6 3.4 %collective-permute-start.6 = (f32[72,128]{1,0:T(8,128)S(1)}, f32[72,128]{1,0:T(8,128)S(1)}, u32[]{:S(2)}, u32[]{:S(2)}) collective-permute-start(f32[72,128]{1,0:T(8,128)S(1)} %get-tuple-element.31), channel_id=1, source_target_pairs={{0,3},{1,2},{2,1},{3,0},{4,7},{5,6},{6,5},{7,4},{8,11},{9,10},{10,... | collective-permute-start | bytes 110600 | tf_op jit(solution)/shard_map/ppermute | solution.py:564
  11.9 3.1 %copy-start.4 = (bf16[768,128]{1,0:T(8,128)(2,1)S(1)}, bf16[768,128]{1,0:T(8,128)(2,1)}, u32[]{:S(2)}) copy-start(bf16[768,128]{1,0:T(8,128)(2,1)} %constant.10.clone.refs_7_) | copy-start | bytes 589828
  15.1 3.1 %copy-start.3 = (bf16[384,256]{1,0:T(8,128)(2,1)S(1)}, bf16[384,256]{1,0:T(8,128)(2,1)}, u32[]{:S(2)}) copy-start(bf16[384,256]{1,0:T(8,128)(2,1)} %constant.11.clone.table) | copy-start | bytes 589828
  16.2 3.1 %collective-permute-start.7 = (f32[24,128]{1,0:T(8,128)S(1)}, f32[24,128]{1,0:T(8,128)S(1)}, u32[]{:S(2)}, u32[]{:S(2)}) collective-permute-start(f32[24,128]{1,0:T(8,128)S(1)} %get-tuple-element.36), channel_id=1, source_target_pairs={{0,1},{1,0},{2,3},{3,2},{4,5},{5,4},{6,7},{7,6},{8,9},{9,8},{10,11... | collective-permute-start | bytes 36872 | tf_op jit(solution)/shard_map/ppermute | solution.py:564
  16.5 3.7 %collective-permute-start.8 = (f32[24,128]{1,0:T(8,128)S(1)}, f32[24,128]{1,0:T(8,128)S(1)}, u32[]{:S(2)}, u32[]{:S(2)}) collective-permute-start(f32[24,128]{1,0:T(8,128)S(1)} %get-tuple-element.37), channel_id=1, source_target_pairs={{0,2},{1,3},{2,0},{3,1},{4,6},{5,7},{6,4},{7,5},{8,10},{9,11},{10,... | collective-permute-start | bytes 36872 | tf_op jit(solution)/shard_map/ppermute | solution.py:564
  17.4 3.1 %collective-permute-start.9 = (f32[24,128]{1,0:T(8,128)S(1)}, f32[24,128]{1,0:T(8,128)S(1)}, u32[]{:S(2)}, u32[]{:S(2)}) collective-permute-start(f32[24,128]{1,0:T(8,128)S(1)} %get-tuple-element.38), channel_id=1, source_target_pairs={{0,3},{1,2},{2,1},{3,0},{4,7},{5,6},{6,5},{7,4},{8,11},{9,10},{10,... | collective-permute-start | bytes 36872 | tf_op jit(solution)/shard_map/ppermute | solution.py:564

commit v11 on v10

--- a/solution.py
+++ b/solution.py
@@ -112,6 +112,14 @@
                 target = i * 2 + 1 - j
             pairs.append((i * 2 + j, target))
     return pairs
+
+
+def far_first(parts):
+    return [parts[0], *parts[2:], parts[1]]
+
+
+def by_rank(parts):
+    return [parts[0], parts[-1], *parts[1:-1]]
 
 
 def faces_kernel(two_y, block, kept, x_even, y_even, x_odd, *y_odd):
@@ -192,10 +200,10 @@
 
 
 def leap_kernel(two_y, ranks, *refs):
-    block, beside, rate, notes, early, x_even, y_even, x_odd = refs[:8]
-    y_odd = refs[8] if two_y else None
-    refs = refs[8 + two_y :]
-    new, sends = refs[0], refs[1 : 1 + ranks]
+    block, rate, notes, early, x_even, y_even, x_odd = refs[:7]
+    y_odd = refs[7] if two_y else None
+    beside, refs = refs[7 + two_y], refs[8 + two_y :]
+    new, sends = refs[0], by_rank(refs[1 : 1 + ranks])
     pad, side, mag, fresh, packed = refs[1 + ranks :]
     deep, tall = block.shape[1], block.shape[2]
     full = deep + 2
@@ -325,8 +333,8 @@
 
 
 def fine_kernel(ranks, *refs):
-    regions, (box, rate, ghosts, means, out) = refs[:ranks], refs[ranks : ranks + 5]
-    smalls = refs[ranks + 5 : 2 * ranks + 5]
+    regions, (box, rate, ghosts, means, out) = by_rank(refs[:ranks]), refs[ranks : ranks + 5]
+    smalls = by_rank(refs[ranks + 5 : 2 * ranks + 5])
     rims, walls, now, halves, small = refs[2 * ranks + 5 :]
     groups = box.shape[0]
     rank = lax.axis_index("gy") * lax.axis_size("gz") + lax.axis_index("gz")
@@ -480,7 +488,7 @@
 
 
 def place_kernel(ranks, new, notes, *refs):
-    means, (out, spread, stage, gathered, sems) = refs[:ranks], refs[ranks:]
+    means, (out, spread, stage, gathered, sems) = by_rank(refs[:ranks]), refs[ranks:]
     noted = notes[0:8, :]
     for k, mean in enumerate(means):
         gathered[k] = mean[...]
@@ -567,7 +575,7 @@
     patches = [shape((ROWS_BESIDE if k == 1 else ROWS_PATCH, LANES), F32) for k in range(ranks)]
     new, *sends = call(
         functools.partial(leap_kernel, two_y, ranks),
-        [shape(coarse_fields.shape, F32)] + patches,
+        [shape(coarse_fields.shape, F32)] + far_first(patches),
         [vmem] * (5 + len(got)),
         [
             pltpu.VMEM((6 * full * 16, LANES), F32),
@@ -576,8 +584,8 @@
             pltpu.VMEM((6 * deep * 16, LANES), F32),
             pltpu.VMEM((PAR, ROWS_PATCH, LANES), F32),
         ],
-    )(kept, beside, rate, notes, early, *got)
-    regions = exchange(sends)
+    )(kept, rate, notes, early, *got, beside)
+    regions = exchange(by_rank(sends))
 
     box, *smalls = call(
         functools.partial(fine_kernel, ranks),
@@ -590,8 +598,8 @@
             pltpu.VMEM((96, 2 * WIDE), F32),
             pltpu.VMEM((groups * 96, LANES), F32),
         ],
-    )(*regions, box, fine_rate, jnp.asarray(ghost_table(), BF16), jnp.asarray(mean_table(), BF16))
-    means = exchange(smalls)
+    )(*far_first(regions), box, fine_rate, jnp.asarray(ghost_table(), BF16), jnp.asarray(mean_table(), BF16))
+    means = exchange(by_rank(smalls))
 
     fine = call(
         store_kernel,
@@ -613,7 +621,7 @@
             pltpu.SemaphoreType.DMA((6,)),
         ],
         out_specs=whole(pltpu.HBM),
-    )(new, notes, *means)
+    )(new, notes, *far_first(means))
     return coarse, fine.transpose(0, 1, 3, 2, 4)
 
 

time: 21.7 us -> 21.5 us (level)
  waiting for transfers between devices: 4.79 us -> 4.33 us
  starting transfers between devices: 8.52 us -> 8.8 us
    ppermute x6, waiting for transfers between devices: 3.82 us -> 3.36 us  [exchange(): got[k] = lax.ppermute(parts[k], ('gy', 'gz'), swaps[k])]
    ppermute x6, starting transfers between devices: 3.86 us -> 4.14 us  [exchange(): got[k] = lax.ppermute(parts[k], ('gy', 'gz'), swaps[k])]
  transfers between devices with their start and end apart: 10 -> 10, of which waited for: 5 -> 5; matrix products, arithmetic and copies ran while one was open for 0% -> 0% of each run, Pallas kernels for 11% -> 12%
where the time goes in v11:
time: 21.5 us; the launch traced here: 21.3 us
  starting transfers between devices  8.8 us (41%)
  Pallas kernels  5.69 us (26%)
  waiting for transfers between devices  4.33 us (20%)
  local copies, waits for them, and re-layouts  1.78 us (8%)
  between operations  0.74 us (3%)
    ppermute x6, starting transfers between devices, exchange(): got[k] = lax.ppermute(parts[k], ('gy', 'gz'), swaps[k])  4.14 us
    ppermute x6, waiting for transfers between devices, exchange(): got[k] = lax.ppermute(parts[k], ('gy', 'gz'), swaps[k])  3.36 us
    ppermute x1, starting transfers between devices, local(): lax.ppermute(faces[0], 'gx', swap_pairs(count_x, 0))  2.65 us
    unnamed x20, local copies, waits for them, and re-layouts  1.78 us
    ppermute x1, starting transfers between devices, local(): lax.ppermute(faces[1], 'gy', swap_pairs(count_y, 0))  1.49 us
    pallas_call x1, Pallas kernels, local(): call(functools.partial(fine_kernel, ranks), [shape((groups, 6, ROWS_BOX,...  1.16 us
    pallas_call x1, Pallas kernels, local(): call(store_kernel, shape(fine.shape, F32), [vmem] * 4, [pltpu.VMEM(fine.s...  1.11 us
    pallas_call x1, Pallas kernels, local(): call(functools.partial(place_kernel, ranks), shape(coarse_fields.shape, F...  1.01 us
  transfers between devices with their start and end apart: 10, of which 5 were waited for; matrix products, arithmetic and copies ran while one was open for 0% of the time, Pallas kernels for 12%

profile of v11, /device:TPU:0, one launch (start us, length us, event | category | flops | bytes accessed | tf_op | source)
XLA Modules:
  0.0 21.3 jit_solution(14188733690808017731)
XLA Ops:
  0.6 1.1 %copy-done.1 = f32[6,12,12,128]{3,2,1,0:T(8,128)S(1)} copy-done((f32[6,12,12,128]{3,2,1,0:T(8,128)S(1)}, f32[6,12,12,128]{3,2,1,0:T(8,128)}, u32[]{:S(2)}) %copy-start.1) | copy-done | bytes 442392
  1.7 0.1 shard_map.113
  1.8 0.5 %collective-permute-start.3 = (f32[6,12,12,128]{3,2,1,0:T(8,128)S(1)}, f32[6,12,12,128]{3,2,1,0:T(8,128)S(1)}, u32[]{:S(2)}, u32[]{:S(2)}) collective-permute-start(f32[6,12,12,128]{3,2,1,0:T(8,128)S(1)} %get-tuple-element.21.block.refs_0_), channel_id=1, source_target_pairs={{0,1},{1,0},{2,3},{3,2},{4,5},{5,4},{6,7},{7,6},{8,9},{9,8},{10,11... | collective-permute-start | bytes 1327112 | tf_op jit(solution)/shard_map/ppermute | solution.py:544
  2.3 2.6 %collective-permute-start = (f32[5,12,128]{2,1,0:T(8,128)S(1)}, f32[5,12,128]{2,1,0:T(8,128)S(1)}, u32[]{:S(2)}, u32[]{:S(2)}) collective-permute-start(f32[5,12,128]{2,1,0:T(8,128)S(1)} %get-tuple-element.25), channel_id=1, source_target_pairs={{0,4},{4,0},{8,12},{12,8},{1,5},{5,1},{9,13},{13,9},{2,6},{6,2},{1... | collective-permute-start | bytes 92168 | tf_op jit(solution)/shard_map/ppermute | solution.py:538
  4.9 1.5 %collective-permute-start.1 = (f32[5,12,128]{2,1,0:T(8,128)S(1)}, f32[5,12,128]{2,1,0:T(8,128)S(1)}, u32[]{:S(2)}, u32[]{:S(2)}) collective-permute-start(f32[5,12,128]{2,1,0:T(8,128)S(1)} %get-tuple-element.26), channel_id=1, source_target_pairs={{0,2},{2,0},{1,3},{3,1},{4,6},{6,4},{5,7},{7,5},{8,10},{10,8},{9,1... | collective-permute-start | bytes 92168 | tf_op jit(solution)/shard_map/ppermute | solution.py:539
  6.5 0.7 %copy-done.9 = s32[1,4,2]{1,2,0:T(2,128)S(1)} copy-done((s32[1,4,2]{1,2,0:T(2,128)S(1)}, s32[1,4,2]{1,2,0:T(2,128)}, u32[]{:S(2)}) %copy-start.9) | copy-done | bytes 56
  7.1 0.8 %shard_map.114 = (s32[12,128]{1,0:T(8,128)S(1)}, f32[12,12,128]{2,1,0:T(8,128)S(1)}, f32[2,56,128]{2,1,0:T(8,128)S(1)}) custom-call(s32[1,1,2,3]{3,2,1,0:T(2,128)S(1)} %copy-done.8, s32[1,2,4]{2,1,0:T(2,128)S(1)} %bitcast.5, f32[12,12,128]{2,1,0:T(8,128)S(1)} %copy-done.6, f32[6,12,12,128]{3,2,1,0:T(8,128)S(1)} %get-tuple-element.21.block.refs_0_), custom_call_target="tpu_custom_call" | custom-call | flops 1000000 | bytes 1000000 | tf_op jit(solution)/shard_map/pallas_call | solution.py:547
  8.0 1.0 %collective-permute-done.1.refs_5_ = f32[5,12,128]{2,1,0:T(8,128)S(1)} collective-permute-done((f32[5,12,128]{2,1,0:T(8,128)S(1)}, f32[5,12,128]{2,1,0:T(8,128)S(1)}, u32[]{:S(2)}, u32[]{:S(2)}) %collective-permute-start.1) | collective-permute-done | bytes 30752 | tf_op jit(solution)/shard_map/ppermute | solution.py:539
  9.0 1.0 %shard_map.115 = (f32[6,12,12,128]{3,2,1,0:T(8,128)S(1)}, f32[72,128]{1,0:T(8,128)S(1)}, f32[72,128]{1,0:T(8,128)S(1)}, f32[72,128]{1,0:T(8,128)S(1)}, f32[104,128]{1,0:T(8,128)S(1)}) custom-call(f32[6,12,12,128]{3,2,1,0:T(8,128)S(1)} %get-tuple-element.21.block.refs_0_, f32[12,12,128]{2,1,0:T(8,128)S(1)} %get-tuple-element.22.refs_1_.rate, ...), custom_call_target="tpu_custom_call" | custom-call | flops 1000000 | bytes 1000000 | tf_op jit(solution)/shard_map/pallas_call | solution.py:576
  10.0 0.1 collective-permute-start.4
  10.1 1.6 %collective-permute-start.5 = (f32[72,128]{1,0:T(8,128)S(1)}, f32[72,128]{1,0:T(8,128)S(1)}, u32[]{:S(2)}, u32[]{:S(2)}) collective-permute-start(f32[72,128]{1,0:T(8,128)S(1)} %get-tuple-element.30), channel_id=1, source_target_pairs={{0,2},{1,3},{2,0},{3,1},{4,6},{5,7},{6,4},{7,5},{8,10},{9,11},{10,... | collective-permute-start | bytes 110600 | tf_op jit(solution)/shard_map/ppermute | solution.py:572
  11.6 0.3 %collective-permute-start.6 = (f32[72,128]{1,0:T(8,128)S(1)}, f32[72,128]{1,0:T(8,128)S(1)}, u32[]{:S(2)}, u32[]{:S(2)}) collective-permute-start(f32[72,128]{1,0:T(8,128)S(1)} %get-tuple-element.31), channel_id=1, source_target_pairs={{0,3},{1,2},{2,1},{3,0},{4,7},{5,6},{6,5},{7,4},{8,11},{9,10},{10,... | collective-permute-start | bytes 110600 | tf_op jit(solution)/shard_map/ppermute | solution.py:572
  11.9 0.4 %shard_map.117 = (f32[1,6,72,384]{3,2,1,0:T(8,128)S(1)}, f32[1,72,384]{2,1,0:T(8,128)S(1)}) custom-call(f32[1,1,6,4,4096]{4,3,2,1,0:T(4,128)S(1)} %bitcast.3, f32[1,1,4,4096]{3,2,1,0:T(4,128)S(1)} %copy-done.7, bf16[256,384]{1,0:T(8,128)(2,1)S(1)} %copy-done.5), custom_call_target="tpu_custom_call" | custom-call | flops 1000000 | bytes 4000000 | tf_op jit(solution)/shard_map/pallas_call | solution.py:557
  12.4 1.7 %collective-permute-done.5.refs_1_ = f32[72,128]{1,0:T(8,128)S(1)} collective-permute-done((f32[72,128]{1,0:T(8,128)S(1)}, f32[72,128]{1,0:T(8,128)S(1)}, u32[]{:S(2)}, u32[]{:S(2)}) %collective-permute-start.5) | collective-permute-done | bytes 36896 | tf_op jit(solution)/shard_map/ppermute | solution.py:572
  14.1 1.0 %collective-permute-done.6.refs_2_ = f32[72,128]{1,0:T(8,128)S(1)} collective-permute-done((f32[72,128]{1,0:T(8,128)S(1)}, f32[72,128]{1,0:T(8,128)S(1)}, u32[]{:S(2)}, u32[]{:S(2)}) %collective-permute-start.6) | collective-permute-done | bytes 36896 | tf_op jit(solution)/shard_map/ppermute | solution.py:572
  15.1 1.2 %shard_map.118 = (f32[1,6,72,384]{3,2,1,0:T(8,128)S(1)}, f32[24,128]{1,0:T(8,128)S(1)}, f32[24,128]{1,0:T(8,128)S(1)}, f32[24,128]{1,0:T(8,128)S(1)}, f32[24,128]{1,0:T(8,128)S(1)}) custom-call(f32[72,128]{1,0:T(8,128)S(1)} %get-tuple-element.32.refs_0_, f32[72,128]{1,0:T(8,128)S(1)} %collective-permute-done.5.refs_1_, ...), custom_call_target="tpu_custom_call" | custom-call | flops 1000000 | bytes 1000000 | tf_op jit(solution)/shard_map/pallas_call | solution.py:590
  16.2 1.0 %collective-permute-start.7 = (f32[24,128]{1,0:T(8,128)S(1)}, f32[24,128]{1,0:T(8,128)S(1)}, u32[]{:S(2)}, u32[]{:S(2)}) collective-permute-start(f32[24,128]{1,0:T(8,128)S(1)} %get-tuple-element.36), channel_id=1, source_target_pairs={{0,2},{1,3},{2,0},{3,1},{4,6},{5,7},{6,4},{7,5},{8,10},{9,11},{10,... | collective-permute-start | bytes 36872 | tf_op jit(solution)/shard_map/ppermute | solution.py:572
  17.2 0.6 %collective-permute-start.8 = (f32[24,128]{1,0:T(8,128)S(1)}, f32[24,128]{1,0:T(8,128)S(1)}, u32[]{:S(2)}, u32[]{:S(2)}) collective-permute-start(f32[24,128]{1,0:T(8,128)S(1)} %get-tuple-element.37), channel_id=1, source_target_pairs={{0,3},{1,2},{2,1},{3,0},{4,7},{5,6},{6,5},{7,4},{8,11},{9,10},{10,... | collective-permute-start | bytes 36872 | tf_op jit(solution)/shard_map/ppermute | solution.py:572
  17.8 0.6 %collective-permute-start.9 = (f32[24,128]{1,0:T(8,128)S(1)}, f32[24,128]{1,0:T(8,128)S(1)}, u32[]{:S(2)}, u32[]{:S(2)}) collective-permute-start(f32[24,128]{1,0:T(8,128)S(1)} %get-tuple-element.38), channel_id=1, source_target_pairs={{0,1},{1,0},{2,3},{3,2},{4,5},{5,4},{6,7},{7,6},{8,9},{9,8},{10,11... | collective-permute-start | bytes 36872 | tf_op jit(solution)/shard_map/ppermute | solution.py:572
  18.4 1.1 %shard_map.120 = f32[1,1,6,4,4096]{4,3,2,1,0:T(4,128)} custom-call(f32[1,6,72,384]{3,2,1,0:T(8,128)S(1)} %get-tuple-element.39.box, f32[1,1,6,4,4096]{4,3,2,1,0:T(4,128)S(1)} %bitcast.4, s32[12,128]{1,0:T(8,128)S(1)} %get-tuple-element.23.refs_2_.notes, bf16[384,256]{1,0:T(8,128)(2,1)S(1)} %copy-done.3), custom_call_target="tpu_custom_call" | custom-call | flops 1000000 | bytes 4000000 | tf_op jit(solution)/shard_map/pallas_call | solution.py:604
  19.6 0.1 shard_map.116.new
  19.7 0.3 %collective-permute-done.7.refs_1_ = f32[24,128]{1,0:T(8,128)S(1)} collective-permute-done((f32[24,128]{1,0:T(8,128)S(1)}, f32[24,128]{1,0:T(8,128)S(1)}, u32[]{:S(2)}, u32[]{:S(2)}) %collective-permute-start.7) | collective-permute-done | bytes 12320 | tf_op jit(solution)/shard_map/ppermute | solution.py:572
  20.0 0.3 %collective-permute-done.8.refs_2_ = f32[24,128]{1,0:T(8,128)S(1)} collective-permute-done((f32[24,128]{1,0:T(8,128)S(1)}, f32[24,128]{1,0:T(8,128)S(1)}, u32[]{:S(2)}, u32[]{:S(2)}) %collective-permute-start.8) | collective-permute-done | bytes 12320 | tf_op jit(solution)/shard_map/ppermute | solution.py:572
  20.3 1.0 %shard_map.119 = f32[6,12,12,128]{3,2,1,0:T(8,128)} custom-call(f32[6,12,12,128]{3,2,1,0:T(8,128)S(1)} %shard_map.116.new, s32[12,128]{1,0:T(8,128)S(1)} %get-tuple-element.23.refs_2_.notes, f32[24,128]{1,0:T(8,128)S(1)} %get-tuple-element.35.refs_0_, f32[24,128]{1,0:T(8,128)S(1)} %collective-permute-done.7.refs_1_, ...), custom_call_target="tpu_custom_call" | custom-call | flops 1000000 | bytes 1000000 | tf_op jit(solution)/shard_map/pallas_call | solution.py:613
  (24 shorter events, 0.1 us)
Async XLA Ops:
  0.6 1.1 %copy-start.1 = (f32[6,12,12,128]{3,2,1,0:T(8,128)S(1)}, f32[6,12,12,128]{3,2,1,0:T(8,128)}, u32[]{:S(2)}) copy-start(f32[6,12,12,128]{3,2,1,0:T(8,128)} %block.1) | copy-start | bytes 1327108
  1.7 4.8 %copy-start.6 = (f32[12,12,128]{2,1,0:T(8,128)S(1)}, f32[12,12,128]{2,1,0:T(8,128)}, u32[]{:S(2)}) copy-start(f32[12,12,128]{2,1,0:T(8,128)} %perm.2) | copy-start | bytes 221188
  1.8 7.2 %collective-permute-start.3 = (f32[6,12,12,128]{3,2,1,0:T(8,128)S(1)}, f32[6,12,12,128]{3,2,1,0:T(8,128)S(1)}, u32[]{:S(2)}, u32[]{:S(2)}) collective-permute-start(f32[6,12,12,128]{3,2,1,0:T(8,128)S(1)} %get-tuple-element.21.block.refs_0_), channel_id=1, source_target_pairs={{0,1},{1,0},{2,3},{3,2},{4,5},{5,4},{6,7},{7,6},{8,9},{9,8},{10,11... | collective-permute-start | bytes 1327112 | tf_op jit(solution)/shard_map/ppermute | solution.py:544
  2.3 5.7 %collective-permute-start = (f32[5,12,128]{2,1,0:T(8,128)S(1)}, f32[5,12,128]{2,1,0:T(8,128)S(1)}, u32[]{:S(2)}, u32[]{:S(2)}) collective-permute-start(f32[5,12,128]{2,1,0:T(8,128)S(1)} %get-tuple-element.25), channel_id=1, source_target_pairs={{0,4},{4,0},{8,12},{12,8},{1,5},{5,1},{9,13},{13,9},{2,6},{6,2},{1... | collective-permute-start | bytes 92168 | tf_op jit(solution)/shard_map/ppermute | solution.py:538
  4.9 4.0 %collective-permute-start.1 = (f32[5,12,128]{2,1,0:T(8,128)S(1)}, f32[5,12,128]{2,1,0:T(8,128)S(1)}, u32[]{:S(2)}, u32[]{:S(2)}) collective-permute-start(f32[5,12,128]{2,1,0:T(8,128)S(1)} %get-tuple-element.26), channel_id=1, source_target_pairs={{0,2},{2,0},{1,3},{3,1},{4,6},{6,4},{5,7},{7,5},{8,10},{10,8},{9,1... | collective-permute-start | bytes 92168 | tf_op jit(solution)/shard_map/ppermute | solution.py:539
  6.4 0.7 %copy-start.9 = (s32[1,4,2]{1,2,0:T(2,128)S(1)}, s32[1,4,2]{1,2,0:T(2,128)}, u32[]{:S(2)}) copy-start(s32[1,4,2]{1,2,0:T(2,128)} %param.15) | copy-start | bytes 100
  6.4 0.7 %copy-start.8 = (s32[1,1,2,3]{3,2,1,0:T(2,128)S(1)}, s32[1,1,2,3]{3,2,1,0:T(2,128)}, u32[]{:S(2)}) copy-start(s32[1,1,2,3]{3,2,1,0:T(2,128)} %corner.1) | copy-start | bytes 76
  6.4 2.5 %collective-permute-start.2 = (f32[5,12,128]{2,1,0:T(8,128)S(1)}, f32[5,12,128]{2,1,0:T(8,128)S(1)}, u32[]{:S(2)}, u32[]{:S(2)}) collective-permute-start(f32[5,12,128]{2,1,0:T(8,128)S(1)} %get-tuple-element.27), channel_id=1, source_target_pairs={{0,1},{1,0},{4,8},{5,9},{8,4},{9,5},{12,13},{13,12},{2,3},{3,2},{6... | collective-permute-start | bytes 92168 | tf_op jit(solution)/shard_map/ppermute | solution.py:540
  9.0 3.0 %copy-start = (f32[1,1,4,6,4096]{4,2,3,1,0:T(4,128)S(1)}, f32[1,1,4,6,4096]{4,2,3,1,0:T(4,128)}, u32[]{:S(2)}) copy-start(f32[1,1,4,6,4096]{4,2,3,1,0:T(4,128)} %param.12) | copy-start | bytes 1179652
  9.0 3.0 %copy-start.5 = (bf16[256,384]{1,0:T(8,128)(2,1)S(1)}, bf16[256,384]{1,0:T(8,128)(2,1)}, u32[]{:S(2)}) copy-start(bf16[256,384]{1,0:T(8,128)(2,1)} %constant.8.clone.table) | copy-start | bytes 589828
  9.0 2.9 %copy-start.7 = (f32[1,1,4,4096]{3,2,1,0:T(4,128)S(1)}, f32[1,1,4,4096]{3,2,1,0:T(4,128)}, u32[]{:S(2)}) copy-start(f32[1,1,4,4096]{3,2,1,0:T(4,128)} %perm.3) | copy-start | bytes 196612
  10.0 5.1 %copy-start.2 = (bf16[2,256,384]{2,1,0:T(8,128)(2,1)S(1)}, bf16[2,256,384]{2,1,0:T(8,128)(2,1)}, u32[]{:S(2)}) copy-start(bf16[2,256,384]{2,1,0:T(8,128)(2,1)} %constant.9.clone.refs_6_) | copy-start | bytes 1179652
  10.0 5.1 %collective-permute-start.4 = (f32[104,128]{1,0:T(8,128)S(1)}, f32[104,128]{1,0:T(8,128)S(1)}, u32[]{:S(2)}, u32[]{:S(2)}) collective-permute-start(f32[104,128]{1,0:T(8,128)S(1)} %get-tuple-element.29), channel_id=1, source_target_pairs={{0,1},{1,0},{2,3},{3,2},{4,5},{5,4},{6,7},{7,6},{8,9},{9,8},{10,11... | collective-permute-start | bytes 159752 | tf_op jit(solution)/shard_map/ppermute | solution.py:572
  10.1 4.0 %collective-permute-start.5 = (f32[72,128]{1,0:T(8,128)S(1)}, f32[72,128]{1,0:T(8,128)S(1)}, u32[]{:S(2)}, u32[]{:S(2)}) collective-permute-start(f32[72,128]{1,0:T(8,128)S(1)} %get-tuple-element.30), channel_id=1, source_target_pairs={{0,2},{1,3},{2,0},{3,1},{4,6},{5,7},{6,4},{7,5},{8,10},{9,11},{10,... | collective-permute-start | bytes 110600 | tf_op jit(solution)/shard_map/ppermute | solution.py:572
  11.6 3.4 %collective-permute-start.6 = (f32[72,128]{1,0:T(8,128)S(1)}, f32[72,128]{1,0:T(8,128)S(1)}, u32[]{:S(2)}, u32[]{:S(2)}) collective-permute-start(f32[72,128]{1,0:T(8,128)S(1)} %get-tuple-element.31), channel_id=1, source_target_pairs={{0,3},{1,2},{2,1},{3,0},{4,7},{5,6},{6,5},{7,4},{8,11},{9,10},{10,... | collective-permute-start | bytes 110600 | tf_op jit(solution)/shard_map/ppermute | solution.py:572
  11.9 3.1 %copy-start.4 = (bf16[768,128]{1,0:T(8,128)(2,1)S(1)}, bf16[768,128]{1,0:T(8,128)(2,1)}, u32[]{:S(2)}) copy-start(bf16[768,128]{1,0:T(8,128)(2,1)} %constant.10.clone.refs_7_) | copy-start | bytes 589828
  15.1 3.4 %copy-start.3 = (bf16[384,256]{1,0:T(8,128)(2,1)S(1)}, bf16[384,256]{1,0:T(8,128)(2,1)}, u32[]{:S(2)}) copy-start(bf16[384,256]{1,0:T(8,128)(2,1)} %constant.11.clone.table) | copy-start | bytes 589828
  16.2 3.8 %collective-permute-start.7 = (f32[24,128]{1,0:T(8,128)S(1)}, f32[24,128]{1,0:T(8,128)S(1)}, u32[]{:S(2)}, u32[]{:S(2)}) collective-permute-start(f32[24,128]{1,0:T(8,128)S(1)} %get-tuple-element.36), channel_id=1, source_target_pairs={{0,2},{1,3},{2,0},{3,1},{4,6},{5,7},{6,4},{7,5},{8,10},{9,11},{10,... | collective-permute-start | bytes 36872 | tf_op jit(solution)/shard_map/ppermute | solution.py:572
  17.2 3.1 %collective-permute-start.8 = (f32[24,128]{1,0:T(8,128)S(1)}, f32[24,128]{1,0:T(8,128)S(1)}, u32[]{:S(2)}, u32[]{:S(2)}) collective-permute-start(f32[24,128]{1,0:T(8,128)S(1)} %get-tuple-element.37), channel_id=1, source_target_pairs={{0,3},{1,2},{2,1},{3,0},{4,7},{5,6},{6,5},{7,4},{8,11},{9,10},{10,... | collective-permute-start | bytes 36872 | tf_op jit(solution)/shard_map/ppermute | solution.py:572
  17.8 2.5 %collective-permute-start.9 = (f32[24,128]{1,0:T(8,128)S(1)}, f32[24,128]{1,0:T(8,128)S(1)}, u32[]{:S(2)}, u32[]{:S(2)}) collective-permute-start(f32[24,128]{1,0:T(8,128)S(1)} %get-tuple-element.38), channel_id=1, source_target_pairs={{0,1},{1,0},{2,3},{3,2},{4,5},{5,4},{6,7},{7,6},{8,9},{9,8},{10,11... | collective-permute-start | bytes 36872 | tf_op jit(solution)/shard_map/ppermute | solution.py:572

commit v12 on v10

--- a/solution.py
+++ b/solution.py
@@ -114,7 +114,7 @@
     return pairs
 
 
-def faces_kernel(two_y, block, kept, x_even, y_even, x_odd, *y_odd):
+def faces_kernel(two_y, block, kept, y_even, x_even, x_odd, *y_odd):
     deep, tall = block.shape[1], block.shape[2]
     gx_odd = lax.rem(lax.axis_index("gx"), 2)
     gy_odd = lax.rem(lax.axis_index("gy"), 2)
@@ -192,7 +192,7 @@
 
 
 def leap_kernel(two_y, ranks, *refs):
-    block, beside, rate, notes, early, x_even, y_even, x_odd = refs[:8]
+    block, beside, rate, notes, early, y_even, x_even, x_odd = refs[:8]
     y_odd = refs[8] if two_y else None
     refs = refs[8 + two_y :]
     new, sends = refs[0], refs[1 : 1 + ranks]
@@ -523,12 +523,12 @@
     y_face = shape((5, deep, cols), F32)
     kept, *faces = call(
         functools.partial(faces_kernel, two_y),
-        [shape(coarse_fields.shape, F32), x_face, y_face, x_face] + [y_face] * two_y,
+        [shape(coarse_fields.shape, F32), y_face, x_face, x_face] + [y_face] * two_y,
         [vmem],
     )(coarse_fields)
     got = [
-        lax.ppermute(faces[0], "gx", swap_pairs(count_x, 0)),
-        lax.ppermute(faces[1], "gy", swap_pairs(count_y, 0)),
+        lax.ppermute(faces[0], "gy", swap_pairs(count_y, 0)),
+        lax.ppermute(faces[1], "gx", swap_pairs(count_x, 0)),
         lax.ppermute(faces[2], ("gx", "gz"), full_pairs(count_x)),
     ]
     if two_y:

time: 21.7 us -> 21.6 us (level)
  the two profiles are of different devices: /device:TPU:0 before, /device:TPU:17 now
where the time goes in v12:
time: 21.6 us; the launch traced here: 21.4 us
  starting transfers between devices  9.02 us (42%)
  Pallas kernels  5.69 us (26%)
  waiting for transfers between devices  4.22 us (20%)
  local copies, waits for them, and re-layouts  1.77 us (8%)
  between operations  0.74 us (3%)
    ppermute x6, starting transfers between devices, exchange(): got[k] = lax.ppermute(parts[k], ('gy', 'gz'), swaps[k])  5.75 us
    ppermute x6, waiting for transfers between devices, exchange(): got[k] = lax.ppermute(parts[k], ('gy', 'gz'), swaps[k])  2.9 us
    unnamed x20, local copies, waits for them, and re-layouts  1.77 us
    ppermute x1, waiting for transfers between devices, local(): lax.ppermute(faces[2], ('gx', 'gz'), full_pairs(count_x))  1.3 us
    ppermute x1, starting transfers between devices, local(): lax.ppermute(faces[1], 'gx', swap_pairs(count_x, 0))  1.3 us
    ppermute x1, starting transfers between devices, local(): lax.ppermute(faces[0], 'gy', swap_pairs(count_y, 0))  1.23 us
    pallas_call x1, Pallas kernels, local(): call(functools.partial(fine_kernel, ranks), [shape((groups, 6, ROWS_BOX,...  1.17 us
    pallas_call x1, Pallas kernels, local(): call(store_kernel, shape(fine.shape, F32), [vmem] * 4, [pltpu.VMEM(fine.s...  1.11 us
  transfers between devices with their start and end apart: 10, of which 4 were waited for; matrix products, arithmetic and copies ran while one was open for 0% of the time, Pallas kernels for 12%

profile of v12, /device:TPU:17, one launch (start us, length us, event | category | flops | bytes accessed | tf_op | source)
XLA Modules:
  0.0 21.4 jit_solution(13760403789172181993)
XLA Ops:
  0.6 1.1 %copy-done.1 = f32[6,12,12,128]{3,2,1,0:T(8,128)S(1)} copy-done((f32[6,12,12,128]{3,2,1,0:T(8,128)S(1)}, f32[6,12,12,128]{3,2,1,0:T(8,128)}, u32[]{:S(2)}) %copy-start.1) | copy-done | bytes 442392
  1.7 0.1 shard_map.113
  1.8 0.7 %collective-permute-start = (f32[6,12,12,128]{3,2,1,0:T(8,128)S(1)}, f32[6,12,12,128]{3,2,1,0:T(8,128)S(1)}, u32[]{:S(2)}, u32[]{:S(2)}) collective-permute-start(f32[6,12,12,128]{3,2,1,0:T(8,128)S(1)} %get-tuple-element.21.block.refs_0_), channel_id=1, source_target_pairs={{0,1},{1,0},{2,3},{3,2},{4,5},{5,4},{6,7},{7,6},{8,9},{9,8},{10,11... | collective-permute-start | bytes 1327112 | tf_op jit(solution)/shard_map/ppermute | solution.py:536
  2.5 1.2 %collective-permute-start.1 = (f32[5,12,128]{2,1,0:T(8,128)S(1)}, f32[5,12,128]{2,1,0:T(8,128)S(1)}, u32[]{:S(2)}, u32[]{:S(2)}) collective-permute-start(f32[5,12,128]{2,1,0:T(8,128)S(1)} %get-tuple-element.25), channel_id=1, source_target_pairs={{0,2},{2,0},{1,3},{3,1},{4,6},{6,4},{5,7},{7,5},{8,10},{10,8},{9,1... | collective-permute-start | bytes 92168 | tf_op jit(solution)/shard_map/ppermute | solution.py:530
  3.7 1.3 %collective-permute-start.2 = (f32[5,12,128]{2,1,0:T(8,128)S(1)}, f32[5,12,128]{2,1,0:T(8,128)S(1)}, u32[]{:S(2)}, u32[]{:S(2)}) collective-permute-start(f32[5,12,128]{2,1,0:T(8,128)S(1)} %get-tuple-element.26), channel_id=1, source_target_pairs={{0,4},{4,0},{8,12},{12,8},{1,5},{5,1},{9,13},{13,9},{2,6},{6,2},{1... | collective-permute-start | bytes 92168 | tf_op jit(solution)/shard_map/ppermute | solution.py:531
  5.1 0.7 %copy-done.9 = s32[1,4,2]{1,2,0:T(2,128)S(1)} copy-done((s32[1,4,2]{1,2,0:T(2,128)S(1)}, s32[1,4,2]{1,2,0:T(2,128)}, u32[]{:S(2)}) %copy-start.9) | copy-done | bytes 56
  5.7 0.0 copy-done.8
  5.7 0.8 %shard_map.114 = (s32[12,128]{1,0:T(8,128)S(1)}, f32[12,12,128]{2,1,0:T(8,128)S(1)}, f32[2,56,128]{2,1,0:T(8,128)S(1)}) custom-call(s32[1,1,2,3]{3,2,1,0:T(2,128)S(1)} %copy-done.8, s32[1,2,4]{2,1,0:T(2,128)S(1)} %bitcast.5, f32[12,12,128]{2,1,0:T(8,128)S(1)} %copy-done.6, f32[6,12,12,128]{3,2,1,0:T(8,128)S(1)} %get-tuple-element.21.block.refs_0_), custom_call_target="tpu_custom_call" | custom-call | flops 1000000 | bytes 1000000 | tf_op jit(solution)/shard_map/pallas_call | solution.py:539
  6.6 1.3 %collective-permute-done.3.refs_7_ = f32[5,12,128]{2,1,0:T(8,128)S(1)} collective-permute-done((f32[5,12,128]{2,1,0:T(8,128)S(1)}, f32[5,12,128]{2,1,0:T(8,128)S(1)}, u32[]{:S(2)}, u32[]{:S(2)}) %collective-permute-start.3) | collective-permute-done | bytes 30752 | tf_op jit(solution)/shard_map/ppermute | solution.py:532
  7.9 1.0 %shard_map.115 = (f32[6,12,12,128]{3,2,1,0:T(8,128)S(1)}, f32[72,128]{1,0:T(8,128)S(1)}, f32[104,128]{1,0:T(8,128)S(1)}, f32[72,128]{1,0:T(8,128)S(1)}, f32[72,128]{1,0:T(8,128)S(1)}) custom-call(f32[6,12,12,128]{3,2,1,0:T(8,128)S(1)} %get-tuple-element.21.block.refs_0_, f32[6,12,12,128]{3,2,1,0:T(8,128)S(1)} %collective-permute-done.refs_1_, ...), custom_call_target="tpu_custom_call" | custom-call | flops 1000000 | bytes 1000000 | tf_op jit(solution)/shard_map/pallas_call | solution.py:568
  8.9 1.8 %collective-permute-start.4 = (f32[104,128]{1,0:T(8,128)S(1)}, f32[104,128]{1,0:T(8,128)S(1)}, u32[]{:S(2)}, u32[]{:S(2)}) collective-permute-start(f32[104,128]{1,0:T(8,128)S(1)} %get-tuple-element.29), channel_id=1, source_target_pairs={{0,1},{1,0},{2,3},{3,2},{4,5},{5,4},{6,7},{7,6},{8,9},{9,8},{10,11... | collective-permute-start | bytes 159752 | tf_op jit(solution)/shard_map/ppermute | solution.py:564
  10.7 0.3 %collective-permute-start.5 = (f32[72,128]{1,0:T(8,128)S(1)}, f32[72,128]{1,0:T(8,128)S(1)}, u32[]{:S(2)}, u32[]{:S(2)}) collective-permute-start(f32[72,128]{1,0:T(8,128)S(1)} %get-tuple-element.30), channel_id=1, source_target_pairs={{0,2},{1,3},{2,0},{3,1},{4,6},{5,7},{6,4},{7,5},{8,10},{9,11},{10,... | collective-permute-start | bytes 110600 | tf_op jit(solution)/shard_map/ppermute | solution.py:564
  11.0 1.4 %collective-permute-start.6 = (f32[72,128]{1,0:T(8,128)S(1)}, f32[72,128]{1,0:T(8,128)S(1)}, u32[]{:S(2)}, u32[]{:S(2)}) collective-permute-start(f32[72,128]{1,0:T(8,128)S(1)} %get-tuple-element.31), channel_id=1, source_target_pairs={{0,3},{1,2},{2,1},{3,0},{4,7},{5,6},{6,5},{7,4},{8,11},{9,10},{10,... | collective-permute-start | bytes 110600 | tf_op jit(solution)/shard_map/ppermute | solution.py:564
  12.5 0.4 %shard_map.117 = (f32[1,6,72,384]{3,2,1,0:T(8,128)S(1)}, f32[1,72,384]{2,1,0:T(8,128)S(1)}) custom-call(f32[1,1,6,4,4096]{4,3,2,1,0:T(4,128)S(1)} %bitcast.3, f32[1,1,4,4096]{3,2,1,0:T(4,128)S(1)} %copy-done.7, bf16[256,384]{1,0:T(8,128)(2,1)S(1)} %copy-done.5), custom_call_target="tpu_custom_call" | custom-call | flops 1000000 | bytes 4000000 | tf_op jit(solution)/shard_map/pallas_call | solution.py:549
  12.9 0.7 %collective-permute-done.5.refs_1_.refs_2_ = f32[72,128]{1,0:T(8,128)S(1)} collective-permute-done((f32[72,128]{1,0:T(8,128)S(1)}, f32[72,128]{1,0:T(8,128)S(1)}, u32[]{:S(2)}, u32[]{:S(2)}) %collective-permute-start.5) | collective-permute-done | bytes 36896 | tf_op jit(solution)/shard_map/ppermute | solution.py:564
  13.6 1.3 %collective-permute-done.6.refs_2_.refs_3_ = f32[72,128]{1,0:T(8,128)S(1)} collective-permute-done((f32[72,128]{1,0:T(8,128)S(1)}, f32[72,128]{1,0:T(8,128)S(1)}, u32[]{:S(2)}, u32[]{:S(2)}) %collective-permute-start.6) | collective-permute-done | bytes 36896 | tf_op jit(solution)/shard_map/ppermute | solution.py:564
  14.9 1.2 %shard_map.118 = (f32[1,6,72,384]{3,2,1,0:T(8,128)S(1)}, f32[24,128]{1,0:T(8,128)S(1)}, f32[24,128]{1,0:T(8,128)S(1)}, f32[24,128]{1,0:T(8,128)S(1)}, f32[24,128]{1,0:T(8,128)S(1)}) custom-call(f32[72,128]{1,0:T(8,128)S(1)} %get-tuple-element.32.refs_0_, f32[104,128]{1,0:T(8,128)S(1)} %collective-permute-done.4.refs_0_.refs_1_, ...), custom_call_target="tpu_custom_call" | custom-call | flops 1000000 | bytes 1000000 | tf_op jit(solution)/shard_map/pallas_call | solution.py:582
  16.0 0.4 %collective-permute-start.7 = (f32[24,128]{1,0:T(8,128)S(1)}, f32[24,128]{1,0:T(8,128)S(1)}, u32[]{:S(2)}, u32[]{:S(2)}) collective-permute-start(f32[24,128]{1,0:T(8,128)S(1)} %get-tuple-element.36), channel_id=1, source_target_pairs={{0,1},{1,0},{2,3},{3,2},{4,5},{5,4},{6,7},{7,6},{8,9},{9,8},{10,11... | collective-permute-start | bytes 36872 | tf_op jit(solution)/shard_map/ppermute | solution.py:564
  16.4 0.9 %collective-permute-start.8 = (f32[24,128]{1,0:T(8,128)S(1)}, f32[24,128]{1,0:T(8,128)S(1)}, u32[]{:S(2)}, u32[]{:S(2)}) collective-permute-start(f32[24,128]{1,0:T(8,128)S(1)} %get-tuple-element.37), channel_id=1, source_target_pairs={{0,2},{1,3},{2,0},{3,1},{4,6},{5,7},{6,4},{7,5},{8,10},{9,11},{10,... | collective-permute-start | bytes 36872 | tf_op jit(solution)/shard_map/ppermute | solution.py:564
  17.3 1.0 %collective-permute-start.9 = (f32[24,128]{1,0:T(8,128)S(1)}, f32[24,128]{1,0:T(8,128)S(1)}, u32[]{:S(2)}, u32[]{:S(2)}) collective-permute-start(f32[24,128]{1,0:T(8,128)S(1)} %get-tuple-element.38), channel_id=1, source_target_pairs={{0,3},{1,2},{2,1},{3,0},{4,7},{5,6},{6,5},{7,4},{8,11},{9,10},{10,... | collective-permute-start | bytes 36872 | tf_op jit(solution)/shard_map/ppermute | solution.py:564
  18.2 1.1 %shard_map.120 = f32[1,1,6,4,4096]{4,3,2,1,0:T(4,128)} custom-call(f32[1,6,72,384]{3,2,1,0:T(8,128)S(1)} %get-tuple-element.39.box, f32[1,1,6,4,4096]{4,3,2,1,0:T(4,128)S(1)} %bitcast.4, s32[12,128]{1,0:T(8,128)S(1)} %get-tuple-element.23.refs_3_.notes, bf16[384,256]{1,0:T(8,128)(2,1)S(1)} %copy-done.3), custom_call_target="tpu_custom_call" | custom-call | flops 1000000 | bytes 4000000 | tf_op jit(solution)/shard_map/pallas_call | solution.py:596
  19.4 0.1 shard_map.116.new
  19.5 1.0 %collective-permute-done.9.refs_3_ = f32[24,128]{1,0:T(8,128)S(1)} collective-permute-done((f32[24,128]{1,0:T(8,128)S(1)}, f32[24,128]{1,0:T(8,128)S(1)}, u32[]{:S(2)}, u32[]{:S(2)}) %collective-permute-start.9) | collective-permute-done | bytes 12320 | tf_op jit(solution)/shard_map/ppermute | solution.py:564
  20.4 1.0 %shard_map.119 = f32[6,12,12,128]{3,2,1,0:T(8,128)} custom-call(f32[6,12,12,128]{3,2,1,0:T(8,128)S(1)} %shard_map.116.new, s32[12,128]{1,0:T(8,128)S(1)} %get-tuple-element.23.refs_3_.notes, f32[24,128]{1,0:T(8,128)S(1)} %get-tuple-element.35.refs_0_, f32[24,128]{1,0:T(8,128)S(1)} %collective-permute-done.7.refs_1_, ...), custom_call_target="tpu_custom_call" | custom-call | flops 1000000 | bytes 1000000 | tf_op jit(solution)/shard_map/pallas_call | solution.py:605
  (24 shorter events, 0.1 us)
Async XLA Ops:
  0.6 1.1 %copy-start.1 = (f32[6,12,12,128]{3,2,1,0:T(8,128)S(1)}, f32[6,12,12,128]{3,2,1,0:T(8,128)}, u32[]{:S(2)}) copy-start(f32[6,12,12,128]{3,2,1,0:T(8,128)} %block.1) | copy-start | bytes 1327108
  1.7 3.4 %copy-start.6 = (f32[12,12,128]{2,1,0:T(8,128)S(1)}, f32[12,12,128]{2,1,0:T(8,128)}, u32[]{:S(2)}) copy-start(f32[12,12,128]{2,1,0:T(8,128)} %perm.2) | copy-start | bytes 221188
  1.8 6.1 %collective-permute-start = (f32[6,12,12,128]{3,2,1,0:T(8,128)S(1)}, f32[6,12,12,128]{3,2,1,0:T(8,128)S(1)}, u32[]{:S(2)}, u32[]{:S(2)}) collective-permute-start(f32[6,12,12,128]{3,2,1,0:T(8,128)S(1)} %get-tuple-element.21.block.refs_0_), channel_id=1, source_target_pairs={{0,1},{1,0},{2,3},{3,2},{4,5},{5,4},{6,7},{7,6},{8,9},{9,8},{10,11... | collective-permute-start | bytes 1327112 | tf_op jit(solution)/shard_map/ppermute | solution.py:536
  2.5 4.1 %collective-permute-start.1 = (f32[5,12,128]{2,1,0:T(8,128)S(1)}, f32[5,12,128]{2,1,0:T(8,128)S(1)}, u32[]{:S(2)}, u32[]{:S(2)}) collective-permute-start(f32[5,12,128]{2,1,0:T(8,128)S(1)} %get-tuple-element.25), channel_id=1, source_target_pairs={{0,2},{2,0},{1,3},{3,1},{4,6},{6,4},{5,7},{7,5},{8,10},{10,8},{9,1... | collective-permute-start | bytes 92168 | tf_op jit(solution)/shard_map/ppermute | solution.py:530
  3.7 2.9 %collective-permute-start.2 = (f32[5,12,128]{2,1,0:T(8,128)S(1)}, f32[5,12,128]{2,1,0:T(8,128)S(1)}, u32[]{:S(2)}, u32[]{:S(2)}) collective-permute-start(f32[5,12,128]{2,1,0:T(8,128)S(1)} %get-tuple-element.26), channel_id=1, source_target_pairs={{0,4},{4,0},{8,12},{12,8},{1,5},{5,1},{9,13},{13,9},{2,6},{6,2},{1... | collective-permute-start | bytes 92168 | tf_op jit(solution)/shard_map/ppermute | solution.py:531
  5.0 0.7 %copy-start.9 = (s32[1,4,2]{1,2,0:T(2,128)S(1)}, s32[1,4,2]{1,2,0:T(2,128)}, u32[]{:S(2)}) copy-start(s32[1,4,2]{1,2,0:T(2,128)} %param.15) | copy-start | bytes 100
  5.0 0.7 %copy-start.8 = (s32[1,1,2,3]{3,2,1,0:T(2,128)S(1)}, s32[1,1,2,3]{3,2,1,0:T(2,128)}, u32[]{:S(2)}) copy-start(s32[1,1,2,3]{3,2,1,0:T(2,128)} %corner.1) | copy-start | bytes 76
  5.0 2.9 %collective-permute-start.3 = (f32[5,12,128]{2,1,0:T(8,128)S(1)}, f32[5,12,128]{2,1,0:T(8,128)S(1)}, u32[]{:S(2)}, u32[]{:S(2)}) collective-permute-start(f32[5,12,128]{2,1,0:T(8,128)S(1)} %get-tuple-element.27), channel_id=1, source_target_pairs={{0,1},{1,0},{4,8},{5,9},{8,4},{9,5},{12,13},{13,12},{2,3},{3,2},{6... | collective-permute-start | bytes 92168 | tf_op jit(solution)/shard_map/ppermute | solution.py:532
  7.9 4.6 %copy-start = (f32[1,1,4,6,4096]{4,2,3,1,0:T(4,128)S(1)}, f32[1,1,4,6,4096]{4,2,3,1,0:T(4,128)}, u32[]{:S(2)}) copy-start(f32[1,1,4,6,4096]{4,2,3,1,0:T(4,128)} %param.12) | copy-start | bytes 1179652
  7.9 4.6 %copy-start.5 = (bf16[256,384]{1,0:T(8,128)(2,1)S(1)}, bf16[256,384]{1,0:T(8,128)(2,1)}, u32[]{:S(2)}) copy-start(bf16[256,384]{1,0:T(8,128)(2,1)} %constant.8.clone.table) | copy-start | bytes 589828
  7.9 4.6 %copy-start.7 = (f32[1,1,4,4096]{3,2,1,0:T(4,128)S(1)}, f32[1,1,4,4096]{3,2,1,0:T(4,128)}, u32[]{:S(2)}) copy-start(f32[1,1,4,4096]{3,2,1,0:T(4,128)} %perm.3) | copy-start | bytes 196612
  8.9 6.0 %copy-start.2 = (bf16[2,256,384]{2,1,0:T(8,128)(2,1)S(1)}, bf16[2,256,384]{2,1,0:T(8,128)(2,1)}, u32[]{:S(2)}) copy-start(bf16[2,256,384]{2,1,0:T(8,128)(2,1)} %constant.9.clone.refs_6_) | copy-start | bytes 1179652
  8.9 5.9 %collective-permute-start.4 = (f32[104,128]{1,0:T(8,128)S(1)}, f32[104,128]{1,0:T(8,128)S(1)}, u32[]{:S(2)}, u32[]{:S(2)}) collective-permute-start(f32[104,128]{1,0:T(8,128)S(1)} %get-tuple-element.29), channel_id=1, source_target_pairs={{0,1},{1,0},{2,3},{3,2},{4,5},{5,4},{6,7},{7,6},{8,9},{9,8},{10,11... | collective-permute-start | bytes 159752 | tf_op jit(solution)/shard_map/ppermute | solution.py:564
  10.7 2.8 %collective-permute-start.5 = (f32[72,128]{1,0:T(8,128)S(1)}, f32[72,128]{1,0:T(8,128)S(1)}, u32[]{:S(2)}, u32[]{:S(2)}) collective-permute-start(f32[72,128]{1,0:T(8,128)S(1)} %get-tuple-element.30), channel_id=1, source_target_pairs={{0,2},{1,3},{2,0},{3,1},{4,6},{5,7},{6,4},{7,5},{8,10},{9,11},{10,... | collective-permute-start | bytes 110600 | tf_op jit(solution)/shard_map/ppermute | solution.py:564
  11.0 3.8 %collective-permute-start.6 = (f32[72,128]{1,0:T(8,128)S(1)}, f32[72,128]{1,0:T(8,128)S(1)}, u32[]{:S(2)}, u32[]{:S(2)}) collective-permute-start(f32[72,128]{1,0:T(8,128)S(1)} %get-tuple-element.31), channel_id=1, source_target_pairs={{0,3},{1,2},{2,1},{3,0},{4,7},{5,6},{6,5},{7,4},{8,11},{9,10},{10,... | collective-permute-start | bytes 110600 | tf_op jit(solution)/shard_map/ppermute | solution.py:564
  12.5 2.4 %copy-start.4 = (bf16[768,128]{1,0:T(8,128)(2,1)S(1)}, bf16[768,128]{1,0:T(8,128)(2,1)}, u32[]{:S(2)}) copy-start(bf16[768,128]{1,0:T(8,128)(2,1)} %constant.10.clone.refs_7_) | copy-start | bytes 589828
  14.9 3.4 %copy-start.3 = (bf16[384,256]{1,0:T(8,128)(2,1)S(1)}, bf16[384,256]{1,0:T(8,128)(2,1)}, u32[]{:S(2)}) copy-start(bf16[384,256]{1,0:T(8,128)(2,1)} %constant.11.clone.table) | copy-start | bytes 589828
  16.0 3.4 %collective-permute-start.7 = (f32[24,128]{1,0:T(8,128)S(1)}, f32[24,128]{1,0:T(8,128)S(1)}, u32[]{:S(2)}, u32[]{:S(2)}) collective-permute-start(f32[24,128]{1,0:T(8,128)S(1)} %get-tuple-element.36), channel_id=1, source_target_pairs={{0,1},{1,0},{2,3},{3,2},{4,5},{5,4},{6,7},{7,6},{8,9},{9,8},{10,11... | collective-permute-start | bytes 36872 | tf_op jit(solution)/shard_map/ppermute | solution.py:564
  16.4 3.1 %collective-permute-start.8 = (f32[24,128]{1,0:T(8,128)S(1)}, f32[24,128]{1,0:T(8,128)S(1)}, u32[]{:S(2)}, u32[]{:S(2)}) collective-permute-start(f32[24,128]{1,0:T(8,128)S(1)} %get-tuple-element.37), channel_id=1, source_target_pairs={{0,2},{1,3},{2,0},{3,1},{4,6},{5,7},{6,4},{7,5},{8,10},{9,11},{10,... | collective-permute-start | bytes 36872 | tf_op jit(solution)/shard_map/ppermute | solution.py:564
  17.3 3.2 %collective-permute-start.9 = (f32[24,128]{1,0:T(8,128)S(1)}, f32[24,128]{1,0:T(8,128)S(1)}, u32[]{:S(2)}, u32[]{:S(2)}) collective-permute-start(f32[24,128]{1,0:T(8,128)S(1)} %get-tuple-element.38), channel_id=1, source_target_pairs={{0,3},{1,2},{2,1},{3,0},{4,7},{5,6},{6,5},{7,4},{8,11},{9,10},{10,... | collective-permute-start | bytes 36872 | tf_op jit(solution)/shard_map/ppermute | solution.py:564

commit v13 on v10

--- a/solution.py
+++ b/solution.py
@@ -17,10 +17,10 @@
 WIDE = 384
 BATCH = 4
 ROWS_BOX = PLANES * 8
-ROWS_RIM = 48
-ROW_EDGE = 64
-ROWS_PATCH = 72
-ROWS_BESIDE = 104
+ROWS_RIM = 40
+ROW_EDGE = 43
+ROWS_PATCH = 56
+ROWS_BESIDE = 88
 X_COMPS = (0, 1, 2, 4, 5)
 Y_COMPS = (0, 1, 2, 3, 5)
 VMEM_BYTES = 48 * 1024 * 1024
@@ -142,17 +142,18 @@
     def aim(rows, target):
         return pltpu.roll(rows, lax.rem(target - (cz - 1) + 2 * LANES, LANES), 1)
 
-    for c in range(6):
+    for c in range(5):
         total = jnp.zeros((8, LANES), F32) if early is None else early[q, c * 8 : c * 8 + 8, :]
         for j in range(RIM):
-            if (j == 0 and c == 4) or (j == RIM - 1 and c not in (0, 2)) or (0 < j < RIM - 1 and c == 5):
+            if j == RIM - 1 and c not in (0, 2):
                 continue
+            source_c = 5 if c == 4 and j == 0 else c
             first = rim_lane(time, j, 0)
             if j in (0, RIM - 1):
                 inside = (lane >= first) & (lane < first + RIM)
             else:
                 inside = (lane == first) | (lane == first + RIM - 1)
-            total = jnp.where(inside, aim(rows_of(c, 1, j, 8, False), first), total)
+            total = jnp.where(inside, aim(rows_of(source_c, 1, j, 8, False), first), total)
         packed[q, c * 8 : c * 8 + 8, :] = total
     low = jnp.zeros((6, LANES), F32)
     high = jnp.zeros((2, LANES), F32)
@@ -284,9 +285,8 @@
             fresh[pl.ds(((c + 3) * deep + x) * 16, tall), :] = (h0, h1, h2)[c][0:tall]
     for q in range(PAR):
         pack(fresh, deep, spots[q], 1, packed, q, early)
-        packed[q, ROW_EDGE:ROWS_PATCH, :] = jnp.zeros((ROWS_PATCH - ROW_EDGE, LANES), F32)
         packed[q, ROW_EDGE : ROW_EDGE + 1, :] = pad[pl.ds(at(1, full - 1) + tall - 1, 1), :]
-        packed[q, ROW_EDGE + 1 : ROW_EDGE + 2, :] = pad[pl.ds(at(0, 0), 1), :]
+        packed[q, ROW_EDGE + 8 : ROW_EDGE + 9, :] = pad[pl.ds(at(0, 0), 1), :]
     for k, send in enumerate(sends):
         q = jnp.where(chosen == k, 0, 1)
         send[0:ROWS_PATCH, :] = packed[q]
@@ -371,7 +371,7 @@
         slot = lax.bitwise_xor(rank, k)
         start = (slot // BATCH) * 6 * ROWS_BOX + lax.rem(slot, BATCH)
         for c in range(6):
-            rows = region[c * 8 : c * 8 + 8, :]
+            rows = region[min(c, 4) * 8 : min(c, 4) * 8 + 8, :]
             row = start + c * ROWS_BOX
             rims[pl.ds(row + 8, 4, stride=16), :] = rows[0:4]
             rims[pl.ds(row + 16, 4, stride=16), :] = rows[0:4]
@@ -463,7 +463,7 @@
     for k, edge in enumerate(edges, 1):
         row = ROW_EDGE
         lower = jnp.where(lax.bitwise_xor(rank, k) == rank - 2, edge[row : row + 1, :], lower)
-        higher = jnp.where(lax.bitwise_xor(rank, k) == rank + 2, edge[row + 1 : row + 2, :], higher)
+        higher = jnp.where(lax.bitwise_xor(rank, k) == rank + 2, edge[row + 8 : row + 9, :], higher)
     add(0, deep - 1, slice(0, 1), lower)
     add(1, 0, slice(tall - 1, tall), higher)
     lane = lane_iota((tall, LANES))

time: 21.7 us -> 21.5 us (level)
  waiting for transfers between devices: 4.79 us -> 4.56 us
    ppermute x6, waiting for transfers between devices: 3.82 us -> 3.59 us  [exchange(): got[k] = lax.ppermute(parts[k], ('gy', 'gz'), swaps[k])]
  transfers between devices with their start and end apart: 10 -> 10, of which waited for: 5 -> 5; matrix products, arithmetic and copies ran while one was open for 0% -> 0% of each run, Pallas kernels for 11% -> 12%
where the time goes in v13:
time: 21.5 us; the launch traced here: 21.3 us
  starting transfers between devices  8.52 us (40%)
  Pallas kernels  5.69 us (26%)
  waiting for transfers between devices  4.56 us (21%)
  local copies, waits for them, and re-layouts  1.78 us (8%)
  between operations  0.75 us (3%)
    ppermute x6, starting transfers between devices, exchange(): got[k] = lax.ppermute(parts[k], ('gy', 'gz'), swaps[k])  3.86 us
    ppermute x6, waiting for transfers between devices, exchange(): got[k] = lax.ppermute(parts[k], ('gy', 'gz'), swaps[k])  3.59 us
    ppermute x1, starting transfers between devices, local(): lax.ppermute(faces[0], 'gx', swap_pairs(count_x, 0))  2.65 us
    unnamed x20, local copies, waits for them, and re-layouts  1.78 us
    ppermute x1, starting transfers between devices, local(): lax.ppermute(faces[1], 'gy', swap_pairs(count_y, 0))  1.49 us
    pallas_call x1, Pallas kernels, local(): call(functools.partial(fine_kernel, ranks), [shape((groups, 6, ROWS_BOX,...  1.19 us
    pallas_call x1, Pallas kernels, local(): call(store_kernel, shape(fine.shape, F32), [vmem] * 4, [pltpu.VMEM(fine.s...  1.12 us
    pallas_call x1, Pallas kernels, local(): call(functools.partial(place_kernel, ranks), shape(coarse_fields.shape, F...  1 us
  transfers between devices with their start and end apart: 10, of which 5 were waited for; matrix products, arithmetic and copies ran while one was open for 0% of the time, Pallas kernels for 12%

profile of v13, /device:TPU:0, one launch (start us, length us, event | category | flops | bytes accessed | tf_op | source)
XLA Modules:
  0.0 21.3 jit_solution(28687849405109049)
XLA Ops:
  0.6 1.1 %copy-done.1 = f32[6,12,12,128]{3,2,1,0:T(8,128)S(1)} copy-done((f32[6,12,12,128]{3,2,1,0:T(8,128)S(1)}, f32[6,12,12,128]{3,2,1,0:T(8,128)}, u32[]{:S(2)}) %copy-start.1) | copy-done | bytes 442392
  1.7 0.1 shard_map.113
  1.8 0.5 %collective-permute-start = (f32[6,12,12,128]{3,2,1,0:T(8,128)S(1)}, f32[6,12,12,128]{3,2,1,0:T(8,128)S(1)}, u32[]{:S(2)}, u32[]{:S(2)}) collective-permute-start(f32[6,12,12,128]{3,2,1,0:T(8,128)S(1)} %get-tuple-element.21.block.refs_0_), channel_id=1, source_target_pairs={{0,1},{1,0},{2,3},{3,2},{4,5},{5,4},{6,7},{7,6},{8,9},{9,8},{10,11... | collective-permute-start | bytes 1327112 | tf_op jit(solution)/shard_map/ppermute | solution.py:536
  2.3 2.6 %collective-permute-start.1 = (f32[5,12,128]{2,1,0:T(8,128)S(1)}, f32[5,12,128]{2,1,0:T(8,128)S(1)}, u32[]{:S(2)}, u32[]{:S(2)}) collective-permute-start(f32[5,12,128]{2,1,0:T(8,128)S(1)} %get-tuple-element.25), channel_id=1, source_target_pairs={{0,4},{4,0},{8,12},{12,8},{1,5},{5,1},{9,13},{13,9},{2,6},{6,2},{1... | collective-permute-start | bytes 92168 | tf_op jit(solution)/shard_map/ppermute | solution.py:530
  4.9 1.5 %collective-permute-start.2 = (f32[5,12,128]{2,1,0:T(8,128)S(1)}, f32[5,12,128]{2,1,0:T(8,128)S(1)}, u32[]{:S(2)}, u32[]{:S(2)}) collective-permute-start(f32[5,12,128]{2,1,0:T(8,128)S(1)} %get-tuple-element.26), channel_id=1, source_target_pairs={{0,2},{2,0},{1,3},{3,1},{4,6},{6,4},{5,7},{7,5},{8,10},{10,8},{9,1... | collective-permute-start | bytes 92168 | tf_op jit(solution)/shard_map/ppermute | solution.py:531
  6.5 0.7 %copy-done.9 = s32[1,4,2]{1,2,0:T(2,128)S(1)} copy-done((s32[1,4,2]{1,2,0:T(2,128)S(1)}, s32[1,4,2]{1,2,0:T(2,128)}, u32[]{:S(2)}) %copy-start.9) | copy-done | bytes 56
  7.1 0.8 %shard_map.114 = (s32[12,128]{1,0:T(8,128)S(1)}, f32[12,12,128]{2,1,0:T(8,128)S(1)}, f32[2,48,128]{2,1,0:T(8,128)S(1)}) custom-call(s32[1,1,2,3]{3,2,1,0:T(2,128)S(1)} %copy-done.8, s32[1,2,4]{2,1,0:T(2,128)S(1)} %bitcast.5, f32[12,12,128]{2,1,0:T(8,128)S(1)} %copy-done.6, f32[6,12,12,128]{3,2,1,0:T(8,128)S(1)} %get-tuple-element.21.block.refs_0_), custom_call_target="tpu_custom_call" | custom-call | flops 1000000 | bytes 1000000 | tf_op jit(solution)/shard_map/pallas_call | solution.py:539
  8.0 1.0 %collective-permute-done.2.refs_6_ = f32[5,12,128]{2,1,0:T(8,128)S(1)} collective-permute-done((f32[5,12,128]{2,1,0:T(8,128)S(1)}, f32[5,12,128]{2,1,0:T(8,128)S(1)}, u32[]{:S(2)}, u32[]{:S(2)}) %collective-permute-start.2) | collective-permute-done | bytes 30752 | tf_op jit(solution)/shard_map/ppermute | solution.py:531
  9.0 1.0 %shard_map.115 = (f32[6,12,12,128]{3,2,1,0:T(8,128)S(1)}, f32[56,128]{1,0:T(8,128)S(1)}, f32[88,128]{1,0:T(8,128)S(1)}, f32[56,128]{1,0:T(8,128)S(1)}, f32[56,128]{1,0:T(8,128)S(1)}) custom-call(f32[6,12,12,128]{3,2,1,0:T(8,128)S(1)} %get-tuple-element.21.block.refs_0_, f32[6,12,12,128]{3,2,1,0:T(8,128)S(1)} %collective-permute-done.refs_1_, ...), custom_call_target="tpu_custom_call" | custom-call | flops 1000000 | bytes 1000000 | tf_op jit(solution)/shard_map/pallas_call | solution.py:568
  10.0 0.1 collective-permute-start.4
  10.0 1.6 %collective-permute-start.5 = (f32[56,128]{1,0:T(8,128)S(1)}, f32[56,128]{1,0:T(8,128)S(1)}, u32[]{:S(2)}, u32[]{:S(2)}) collective-permute-start(f32[56,128]{1,0:T(8,128)S(1)} %get-tuple-element.30), channel_id=1, source_target_pairs={{0,2},{1,3},{2,0},{3,1},{4,6},{5,7},{6,4},{7,5},{8,10},{9,11},{10,... | collective-permute-start | bytes 86024 | tf_op jit(solution)/shard_map/ppermute | solution.py:564
  11.6 0.3 %collective-permute-start.6 = (f32[56,128]{1,0:T(8,128)S(1)}, f32[56,128]{1,0:T(8,128)S(1)}, u32[]{:S(2)}, u32[]{:S(2)}) collective-permute-start(f32[56,128]{1,0:T(8,128)S(1)} %get-tuple-element.31), channel_id=1, source_target_pairs={{0,3},{1,2},{2,1},{3,0},{4,7},{5,6},{6,5},{7,4},{8,11},{9,10},{10,... | collective-permute-start | bytes 86024 | tf_op jit(solution)/shard_map/ppermute | solution.py:564
  11.9 0.4 %shard_map.117 = (f32[1,6,72,384]{3,2,1,0:T(8,128)S(1)}, f32[1,72,384]{2,1,0:T(8,128)S(1)}) custom-call(f32[1,1,6,4,4096]{4,3,2,1,0:T(4,128)S(1)} %bitcast.3, f32[1,1,4,4096]{3,2,1,0:T(4,128)S(1)} %copy-done.7, bf16[256,384]{1,0:T(8,128)(2,1)S(1)} %copy-done.4), custom_call_target="tpu_custom_call" | custom-call | flops 1000000 | bytes 4000000 | tf_op jit(solution)/shard_map/pallas_call | solution.py:549
  12.3 1.6 %collective-permute-done.5.refs_1_.refs_2_ = f32[56,128]{1,0:T(8,128)S(1)} collective-permute-done((f32[56,128]{1,0:T(8,128)S(1)}, f32[56,128]{1,0:T(8,128)S(1)}, u32[]{:S(2)}, u32[]{:S(2)}) %collective-permute-start.5) | collective-permute-done | bytes 28704 | tf_op jit(solution)/shard_map/ppermute | solution.py:564
  14.0 0.9 %collective-permute-done.6.refs_2_.refs_3_ = f32[56,128]{1,0:T(8,128)S(1)} collective-permute-done((f32[56,128]{1,0:T(8,128)S(1)}, f32[56,128]{1,0:T(8,128)S(1)}, u32[]{:S(2)}, u32[]{:S(2)}) %collective-permute-start.6) | collective-permute-done | bytes 28704 | tf_op jit(solution)/shard_map/ppermute | solution.py:564
  14.9 1.2 %shard_map.118 = (f32[1,6,72,384]{3,2,1,0:T(8,128)S(1)}, f32[24,128]{1,0:T(8,128)S(1)}, f32[24,128]{1,0:T(8,128)S(1)}, f32[24,128]{1,0:T(8,128)S(1)}, f32[24,128]{1,0:T(8,128)S(1)}) custom-call(f32[56,128]{1,0:T(8,128)S(1)} %get-tuple-element.32.refs_0_, f32[88,128]{1,0:T(8,128)S(1)} %collective-permute-done.4.refs_0_.refs_1_, ...), custom_call_target="tpu_custom_call" | custom-call | flops 1000000 | bytes 1000000 | tf_op jit(solution)/shard_map/pallas_call | solution.py:582
  16.1 0.2 %collective-permute-start.7 = (f32[24,128]{1,0:T(8,128)S(1)}, f32[24,128]{1,0:T(8,128)S(1)}, u32[]{:S(2)}, u32[]{:S(2)}) collective-permute-start(f32[24,128]{1,0:T(8,128)S(1)} %get-tuple-element.36), channel_id=1, source_target_pairs={{0,1},{1,0},{2,3},{3,2},{4,5},{5,4},{6,7},{7,6},{8,9},{9,8},{10,11... | collective-permute-start | bytes 36872 | tf_op jit(solution)/shard_map/ppermute | solution.py:564
  16.3 0.8 %collective-permute-start.8 = (f32[24,128]{1,0:T(8,128)S(1)}, f32[24,128]{1,0:T(8,128)S(1)}, u32[]{:S(2)}, u32[]{:S(2)}) collective-permute-start(f32[24,128]{1,0:T(8,128)S(1)} %get-tuple-element.37), channel_id=1, source_target_pairs={{0,2},{1,3},{2,0},{3,1},{4,6},{5,7},{6,4},{7,5},{8,10},{9,11},{10,... | collective-permute-start | bytes 36872 | tf_op jit(solution)/shard_map/ppermute | solution.py:564
  17.2 0.9 %collective-permute-start.9 = (f32[24,128]{1,0:T(8,128)S(1)}, f32[24,128]{1,0:T(8,128)S(1)}, u32[]{:S(2)}, u32[]{:S(2)}) collective-permute-start(f32[24,128]{1,0:T(8,128)S(1)} %get-tuple-element.38), channel_id=1, source_target_pairs={{0,3},{1,2},{2,1},{3,0},{4,7},{5,6},{6,5},{7,4},{8,11},{9,10},{10,... | collective-permute-start | bytes 36872 | tf_op jit(solution)/shard_map/ppermute | solution.py:564
  18.0 1.1 %shard_map.120 = f32[1,1,6,4,4096]{4,3,2,1,0:T(4,128)} custom-call(f32[1,6,72,384]{3,2,1,0:T(8,128)S(1)} %get-tuple-element.39.box, f32[1,1,6,4,4096]{4,3,2,1,0:T(4,128)S(1)} %bitcast.4, s32[12,128]{1,0:T(8,128)S(1)} %get-tuple-element.23.refs_3_.notes, bf16[384,256]{1,0:T(8,128)(2,1)S(1)} %copy-done.3), custom_call_target="tpu_custom_call" | custom-call | flops 1000000 | bytes 4000000 | tf_op jit(solution)/shard_map/pallas_call | solution.py:596
  19.2 0.1 shard_map.116.new
  19.3 0.8 %collective-permute-done.8.refs_2_ = f32[24,128]{1,0:T(8,128)S(1)} collective-permute-done((f32[24,128]{1,0:T(8,128)S(1)}, f32[24,128]{1,0:T(8,128)S(1)}, u32[]{:S(2)}, u32[]{:S(2)}) %collective-permute-start.8) | collective-permute-done | bytes 12320 | tf_op jit(solution)/shard_map/ppermute | solution.py:564
  20.0 0.3 %collective-permute-done.9.refs_3_ = f32[24,128]{1,0:T(8,128)S(1)} collective-permute-done((f32[24,128]{1,0:T(8,128)S(1)}, f32[24,128]{1,0:T(8,128)S(1)}, u32[]{:S(2)}, u32[]{:S(2)}) %collective-permute-start.9) | collective-permute-done | bytes 12320 | tf_op jit(solution)/shard_map/ppermute | solution.py:564
  20.3 1.0 %shard_map.119 = f32[6,12,12,128]{3,2,1,0:T(8,128)} custom-call(f32[6,12,12,128]{3,2,1,0:T(8,128)S(1)} %shard_map.116.new, s32[12,128]{1,0:T(8,128)S(1)} %get-tuple-element.23.refs_3_.notes, f32[24,128]{1,0:T(8,128)S(1)} %get-tuple-element.35.refs_0_, f32[24,128]{1,0:T(8,128)S(1)} %collective-permute-done.7.refs_1_, ...), custom_call_target="tpu_custom_call" | custom-call | flops 1000000 | bytes 1000000 | tf_op jit(solution)/shard_map/pallas_call | solution.py:605
  (24 shorter events, 0.1 us)
Async XLA Ops:
  0.6 1.1 %copy-start.1 = (f32[6,12,12,128]{3,2,1,0:T(8,128)S(1)}, f32[6,12,12,128]{3,2,1,0:T(8,128)}, u32[]{:S(2)}) copy-start(f32[6,12,12,128]{3,2,1,0:T(8,128)} %block.1) | copy-start | bytes 1327108
  1.7 4.8 %copy-start.6 = (f32[12,12,128]{2,1,0:T(8,128)S(1)}, f32[12,12,128]{2,1,0:T(8,128)}, u32[]{:S(2)}) copy-start(f32[12,12,128]{2,1,0:T(8,128)} %perm.2) | copy-start | bytes 221188
  1.8 7.2 %collective-permute-start = (f32[6,12,12,128]{3,2,1,0:T(8,128)S(1)}, f32[6,12,12,128]{3,2,1,0:T(8,128)S(1)}, u32[]{:S(2)}, u32[]{:S(2)}) collective-permute-start(f32[6,12,12,128]{3,2,1,0:T(8,128)S(1)} %get-tuple-element.21.block.refs_0_), channel_id=1, source_target_pairs={{0,1},{1,0},{2,3},{3,2},{4,5},{5,4},{6,7},{7,6},{8,9},{9,8},{10,11... | collective-permute-start | bytes 1327112 | tf_op jit(solution)/shard_map/ppermute | solution.py:536
  2.3 5.7 %collective-permute-start.1 = (f32[5,12,128]{2,1,0:T(8,128)S(1)}, f32[5,12,128]{2,1,0:T(8,128)S(1)}, u32[]{:S(2)}, u32[]{:S(2)}) collective-permute-start(f32[5,12,128]{2,1,0:T(8,128)S(1)} %get-tuple-element.25), channel_id=1, source_target_pairs={{0,4},{4,0},{8,12},{12,8},{1,5},{5,1},{9,13},{13,9},{2,6},{6,2},{1... | collective-permute-start | bytes 92168 | tf_op jit(solution)/shard_map/ppermute | solution.py:530
  4.9 4.0 %collective-permute-start.2 = (f32[5,12,128]{2,1,0:T(8,128)S(1)}, f32[5,12,128]{2,1,0:T(8,128)S(1)}, u32[]{:S(2)}, u32[]{:S(2)}) collective-permute-start(f32[5,12,128]{2,1,0:T(8,128)S(1)} %get-tuple-element.26), channel_id=1, source_target_pairs={{0,2},{2,0},{1,3},{3,1},{4,6},{6,4},{5,7},{7,5},{8,10},{10,8},{9,1... | collective-permute-start | bytes 92168 | tf_op jit(solution)/shard_map/ppermute | solution.py:531
  6.4 0.7 %copy-start.9 = (s32[1,4,2]{1,2,0:T(2,128)S(1)}, s32[1,4,2]{1,2,0:T(2,128)}, u32[]{:S(2)}) copy-start(s32[1,4,2]{1,2,0:T(2,128)} %param.15) | copy-start | bytes 100
  6.4 0.7 %copy-start.8 = (s32[1,1,2,3]{3,2,1,0:T(2,128)S(1)}, s32[1,1,2,3]{3,2,1,0:T(2,128)}, u32[]{:S(2)}) copy-start(s32[1,1,2,3]{3,2,1,0:T(2,128)} %corner.1) | copy-start | bytes 76
  6.4 2.5 %collective-permute-start.3 = (f32[5,12,128]{2,1,0:T(8,128)S(1)}, f32[5,12,128]{2,1,0:T(8,128)S(1)}, u32[]{:S(2)}, u32[]{:S(2)}) collective-permute-start(f32[5,12,128]{2,1,0:T(8,128)S(1)} %get-tuple-element.27), channel_id=1, source_target_pairs={{0,1},{1,0},{4,8},{5,9},{8,4},{9,5},{12,13},{13,12},{2,3},{3,2},{6... | collective-permute-start | bytes 92168 | tf_op jit(solution)/shard_map/ppermute | solution.py:532
  9.0 2.9 %copy-start = (f32[1,1,4,6,4096]{4,2,3,1,0:T(4,128)S(1)}, f32[1,1,4,6,4096]{4,2,3,1,0:T(4,128)}, u32[]{:S(2)}) copy-start(f32[1,1,4,6,4096]{4,2,3,1,0:T(4,128)} %param.12) | copy-start | bytes 1179652
  9.0 2.9 %copy-start.4 = (bf16[256,384]{1,0:T(8,128)(2,1)S(1)}, bf16[256,384]{1,0:T(8,128)(2,1)}, u32[]{:S(2)}) copy-start(bf16[256,384]{1,0:T(8,128)(2,1)} %constant.8.clone.table) | copy-start | bytes 589828
  9.0 2.9 %copy-start.7 = (f32[1,1,4,4096]{3,2,1,0:T(4,128)S(1)}, f32[1,1,4,4096]{3,2,1,0:T(4,128)}, u32[]{:S(2)}) copy-start(f32[1,1,4,4096]{3,2,1,0:T(4,128)} %perm.3) | copy-start | bytes 196612
  9.9 4.9 %copy-start.2 = (bf16[2,256,384]{2,1,0:T(8,128)(2,1)S(1)}, bf16[2,256,384]{2,1,0:T(8,128)(2,1)}, u32[]{:S(2)}) copy-start(bf16[2,256,384]{2,1,0:T(8,128)(2,1)} %constant.9.clone.refs_6_) | copy-start | bytes 1179652
  10.0 4.9 %collective-permute-start.4 = (f32[88,128]{1,0:T(8,128)S(1)}, f32[88,128]{1,0:T(8,128)S(1)}, u32[]{:S(2)}, u32[]{:S(2)}) collective-permute-start(f32[88,128]{1,0:T(8,128)S(1)} %get-tuple-element.29), channel_id=1, source_target_pairs={{0,1},{1,0},{2,3},{3,2},{4,5},{5,4},{6,7},{7,6},{8,9},{9,8},{10,11... | collective-permute-start | bytes 135176 | tf_op jit(solution)/shard_map/ppermute | solution.py:564
  10.0 3.9 %collective-permute-start.5 = (f32[56,128]{1,0:T(8,128)S(1)}, f32[56,128]{1,0:T(8,128)S(1)}, u32[]{:S(2)}, u32[]{:S(2)}) collective-permute-start(f32[56,128]{1,0:T(8,128)S(1)} %get-tuple-element.30), channel_id=1, source_target_pairs={{0,2},{1,3},{2,0},{3,1},{4,6},{5,7},{6,4},{7,5},{8,10},{9,11},{10,... | collective-permute-start | bytes 86024 | tf_op jit(solution)/shard_map/ppermute | solution.py:564
  11.6 3.3 %collective-permute-start.6 = (f32[56,128]{1,0:T(8,128)S(1)}, f32[56,128]{1,0:T(8,128)S(1)}, u32[]{:S(2)}, u32[]{:S(2)}) collective-permute-start(f32[56,128]{1,0:T(8,128)S(1)} %get-tuple-element.31), channel_id=1, source_target_pairs={{0,3},{1,2},{2,1},{3,0},{4,7},{5,6},{6,5},{7,4},{8,11},{9,10},{10,... | collective-permute-start | bytes 86024 | tf_op jit(solution)/shard_map/ppermute | solution.py:564
  11.9 3.0 %copy-start.5 = (bf16[768,128]{1,0:T(8,128)(2,1)S(1)}, bf16[768,128]{1,0:T(8,128)(2,1)}, u32[]{:S(2)}) copy-start(bf16[768,128]{1,0:T(8,128)(2,1)} %constant.10.clone.refs_7_) | copy-start | bytes 589828
  14.9 3.1 %copy-start.3 = (bf16[384,256]{1,0:T(8,128)(2,1)S(1)}, bf16[384,256]{1,0:T(8,128)(2,1)}, u32[]{:S(2)}) copy-start(bf16[384,256]{1,0:T(8,128)(2,1)} %constant.11.clone.table) | copy-start | bytes 589828
  16.1 3.1 %collective-permute-start.7 = (f32[24,128]{1,0:T(8,128)S(1)}, f32[24,128]{1,0:T(8,128)S(1)}, u32[]{:S(2)}, u32[]{:S(2)}) collective-permute-start(f32[24,128]{1,0:T(8,128)S(1)} %get-tuple-element.36), channel_id=1, source_target_pairs={{0,1},{1,0},{2,3},{3,2},{4,5},{5,4},{6,7},{7,6},{8,9},{9,8},{10,11... | collective-permute-start | bytes 36872 | tf_op jit(solution)/shard_map/ppermute | solution.py:564
  16.3 3.7 %collective-permute-start.8 = (f32[24,128]{1,0:T(8,128)S(1)}, f32[24,128]{1,0:T(8,128)S(1)}, u32[]{:S(2)}, u32[]{:S(2)}) collective-permute-start(f32[24,128]{1,0:T(8,128)S(1)} %get-tuple-element.37), channel_id=1, source_target_pairs={{0,2},{1,3},{2,0},{3,1},{4,6},{5,7},{6,4},{7,5},{8,10},{9,11},{10,... | collective-permute-start | bytes 36872 | tf_op jit(solution)/shard_map/ppermute | solution.py:564
  17.2 3.1 %collective-permute-start.9 = (f32[24,128]{1,0:T(8,128)S(1)}, f32[24,128]{1,0:T(8,128)S(1)}, u32[]{:S(2)}, u32[]{:S(2)}) collective-permute-start(f32[24,128]{1,0:T(8,128)S(1)} %get-tuple-element.38), channel_id=1, source_target_pairs={{0,3},{1,2},{2,1},{3,0},{4,7},{5,6},{6,5},{7,4},{8,11},{9,10},{10,... | collective-permute-start | bytes 36872 | tf_op jit(solution)/shard_map/ppermute | solution.py:564
